TPU v7x, 32 devices: a whole 2x2x4 slice. The times are simulated.
32 devices in a mesh: dp: 4 (over y, x), head: 4 (over z), width: 2 (over core).
Axes of the slice: x: 2, y: 2, z: 4, core: 2. Of those that a mesh axis runs over, the one named last changes fastest.
Arguments:
- hidden: bfloat16 [16384, 1024], P(('dp', 'head'), 'width'), may hold values from -6 to 6
- lengths: int32 [4], P('dp'), may hold values from 1024 to 4096, as said below
- cotangent: bfloat16 [16384, 1024], P(('dp', 'head'), 'width'), may hold values from -6 to 6
- norm_gain: bfloat16 [1024], P('width'), may hold values from 0.5 to 1.5
- in_zx: bfloat16 [1024, 32, 128], P('width', 'head'), may hold values from -0.1875 to 0.1875
- in_bcdt: bfloat16 [1024, 288], P('width'), may hold values from -0.1875 to 0.1875
- conv_x: bfloat16 [4, 2048], P(None, 'head'), may hold values from -3 to 3
- conv_bc: bfloat16 [4, 256], replicated, may hold values from -3 to 3
- dt_bias: float32 [32], P('head'), may hold values from -7 to -1
- a_log: float32 [32], P('head'), may hold values from -1 to 1.5
- d_skip: float32 [32], P('head'), may hold values from 0.5 to 1.5
- gnorm_gain: bfloat16 [2048], P('head'), may hold values from 0.5 to 1.5
- out_w: bfloat16 [2048, 1024], P('head', 'width'), may hold values from -0.125 to 0.125
Outputs:
- out_hidden: bfloat16 [16384, 1024], P(('dp', 'head'), 'width')
- grad_hidden: bfloat16 [16384, 1024], P(('dp', 'head'), 'width')
- grad_norm_gain: float32 [1024], P('width')
- grad_in_zx: float32 [1024, 32, 128], P('width', 'head')
- grad_in_bcdt: float32 [1024, 288], P('width')
- grad_conv_x: float32 [4, 2048], P(None, 'head')
- grad_conv_bc: float32 [4, 256], replicated
- grad_dt_bias: float32 [32], P('head')
- grad_a_log: float32 [32], P('head')
- grad_d_skip: float32 [32], P('head')
- grad_gnorm_gain: float32 [2048], P('head')
- grad_out_w: float32 [2048, 1024], P('head', 'width')
Inputs may be any that keep to these rules, and one draw needn't show every extreme that they name: `lengths`: the valid prefix of each sequence; some sequence is full and some has exactly 1024 valid tokens.
All inputs are finite; a program needn't handle non-finite values.
Results may differ from a plain program's by a relative error of at most 0.0084.
Values may be sent and summed in bfloat16 or wider, within the bound.
A program may use at most 256 MiB of HBM per device.

v0:
```python
import jax
import jax.numpy as jnp
from jax import lax
from jax.sharding import PartitionSpec as P

D = 1024
HEADS = 32
HEADDIM = 64
STATE = 128
SCAN_BLOCK = 256
LEN = 4096
INNER = 2048


EPS = 1e-05
HIGH = lax.Precision.HIGHEST


def conv_causal(values, kernel):
    taps = kernel.shape[0]
    padded = jnp.pad(values, ((taps - 1, 0), (0, 0)))
    total = jnp.zeros_like(values)
    for offset in range(taps):
        total = total + kernel[offset] * padded[offset : offset + values.shape[0]]
    return total


def block_scan(inputs, steps, rates, bmat, cmat, block):
    length, heads, hsize = inputs.shape
    count = length // block
    in_blocks = inputs.reshape(count, block, heads, hsize)
    step_blocks = steps.reshape(count, block, heads)
    b_blocks = bmat.reshape(count, block, bmat.shape[1])
    c_blocks = cmat.reshape(count, block, cmat.shape[1])
    places = jnp.arange(block)
    lower = (places[:, None] >= places[None, :])[:, :, None]

    def advance(state, pieces):
        x_part, dt_part, b_part, c_part = pieces
        cums = jnp.cumsum(dt_part * rates, axis=0)
        spread = cums[:, None, :] - cums[None, :, :]
        decay = jnp.where(lower, jnp.exp(jnp.where(lower, spread, 0.0)), 0.0)
        scores = jnp.dot(c_part, b_part.T, precision=HIGH)
        weights = scores[:, :, None] * decay * dt_part[None, :, :]
        inside = jnp.einsum("ijh,jhp->ihp", weights, x_part, precision=HIGH)
        carried = (
            jnp.einsum("in,hpn->ihp", c_part, state, precision=HIGH) * jnp.exp(cums)[:, :, None]
        )
        tails = jnp.exp(cums[-1][None, :] - cums) * dt_part
        state = jnp.exp(cums[-1])[:, None, None] * state + jnp.einsum(
            "jh,jhp,jn->hpn", tails, x_part, b_part, precision=HIGH
        )
        return (state, inside + carried)

    start_state = jnp.zeros((heads, hsize, bmat.shape[1]), jnp.float32)
    _, result = lax.scan(
        jax.checkpoint(advance), start_state, (in_blocks, step_blocks, b_blocks, c_blocks)
    )
    return result.reshape(length, heads, hsize)


def mixer(zx, bc_raw, dt_raw, kernel_x, kernel_bc, bias_dt, log_rate, skip):
    length, heads, double = zx.shape
    hsize = double // 2
    gate = zx[:, :, :hsize]
    x_raw = zx[:, :, hsize:].reshape(length, heads * hsize)
    xs_conv = jax.nn.silu(conv_causal(x_raw, kernel_x)).reshape(length, heads, hsize)
    bc_conv = jax.nn.silu(conv_causal(bc_raw, kernel_bc))
    half = bc_conv.shape[1] // 2
    steps = jax.nn.softplus(dt_raw + bias_dt)
    rates = -jnp.exp(log_rate)
    result = (
        block_scan(xs_conv, steps, rates, bc_conv[:, :half], bc_conv[:, half:], SCAN_BLOCK)
        + skip[:, None] * xs_conv
    )
    return (result * jax.nn.silu(gate)).reshape(length, heads * hsize)


def per_device(
    hidden,
    lengths,
    cotangent,
    norm_gain,
    in_zx,
    in_bcdt,
    conv_x,
    conv_bc,
    dt_bias,
    a_log,
    d_skip,
    gnorm_gain,
    out_w,
):
    slice_rows, half_width = hidden.shape
    local_heads = in_zx.shape[1]
    head_count = lax.axis_size("head")
    head_index = lax.axis_index("head")
    total_rows = slice_rows * head_count
    seq_local = lengths.shape[0]
    inner_local = local_heads * HEADDIM
    row_ids = head_index * slice_rows + jnp.arange(slice_rows, dtype=jnp.int32)
    owner = (row_ids // LEN)[:, None] == jnp.arange(seq_local, dtype=jnp.int32)[None, :]
    limits = jnp.sum(jnp.where(owner, lengths[None, :], 0), axis=1)
    keeper = (row_ids % LEN < limits).astype(jnp.float32)[:, None]
    source = hidden.astype(jnp.float32)
    squares = lax.psum(jnp.sum(source * source, axis=1), "width")
    scale = lax.rsqrt(squares / D + EPS)[:, None]
    gain_in = norm_gain.astype(jnp.float32)
    normed = (source * scale * gain_in).astype(jnp.bfloat16)
    gathered = lax.all_gather(normed, "head", axis=0, tiled=True)
    w_zx = in_zx.reshape(half_width, local_heads * 2 * HEADDIM)
    zx_part = jnp.dot(gathered, w_zx, preferred_element_type=jnp.float32)
    bcdt_part = jnp.dot(gathered, in_bcdt, preferred_element_type=jnp.float32)
    zx_full, bcdt_full = lax.psum((zx_part, bcdt_part), "width")
    zx_seq = zx_full.reshape(seq_local, LEN, local_heads, 2 * HEADDIM)
    bc_seq = bcdt_full[:, : 2 * STATE].reshape(seq_local, LEN, 2 * STATE)
    dt_seq = lax.dynamic_slice_in_dim(
        bcdt_full, 2 * STATE + head_index * local_heads, local_heads, 1
    ).reshape(seq_local, LEN, local_heads)

    def local_mix(zx_in, bc_in, dt_in, kernel_x, kernel_bc, bias_in, log_in, skip_in):
        per_sequence = jax.vmap(mixer, in_axes=(0, 0, 0, None, None, None, None, None))
        return per_sequence(
            zx_in, bc_in, dt_in, kernel_x, kernel_bc, bias_in, log_in, skip_in
        ).reshape(total_rows, inner_local)

    gated, mix_pull = jax.vjp(
        local_mix,
        zx_seq,
        bc_seq,
        dt_seq,
        conv_x.astype(jnp.float32),
        conv_bc.astype(jnp.float32),
        dt_bias,
        a_log,
        d_skip,
    )
    total_sq = lax.psum(jnp.sum(gated * gated, axis=1), "head")
    scale_out = lax.rsqrt(total_sq / INNER + EPS)[:, None]
    gain_out = gnorm_gain.astype(jnp.float32)
    mixed = (gated * scale_out * gain_out).astype(jnp.bfloat16)
    picked = mixed
    branch = lax.psum_scatter(
        jnp.dot(picked, out_w, preferred_element_type=jnp.float32),
        "head",
        scatter_dimension=0,
        tiled=True,
    )
    out_hidden = (source + keeper * branch).astype(jnp.bfloat16)
    grad_out = cotangent.astype(jnp.float32)
    masked = (grad_out * keeper).astype(jnp.bfloat16)
    piece = lax.all_gather(masked, "head", axis=0, tiled=True)
    picked = mixed
    acc_weight = jnp.einsum("tc,td->cd", picked, piece, preferred_element_type=jnp.float32)
    product = jnp.einsum("td,cd->tc", piece, out_w, preferred_element_type=jnp.float32)
    grad_mixed = lax.psum(product, "width")
    gain_out_grad = jnp.sum(grad_mixed * gated * scale_out, axis=0)
    inner_total = lax.psum(jnp.sum(grad_mixed * gain_out * gated, axis=1), "head")
    cubed = scale_out * scale_out * scale_out
    grad_gated = scale_out * gain_out * grad_mixed - gated * cubed / INNER * inner_total[:, None]
    (
        grad_zx_seq,
        grad_bc_seq,
        grad_dt_seq,
        kernel_x_grad,
        kernel_bc_grad,
        bias_grad,
        rate_grad,
        skip_grad,
    ) = mix_pull(grad_gated)
    grad_zx = grad_zx_seq.reshape(total_rows, local_heads * 2 * HEADDIM).astype(jnp.bfloat16)
    dt_columns = jnp.zeros((total_rows, HEADS), jnp.float32)
    dt_columns = lax.dynamic_update_slice_in_dim(
        dt_columns, grad_dt_seq.reshape(total_rows, local_heads), head_index * local_heads, 1
    )
    grad_bcdt_head = jnp.concatenate(
        [grad_bc_seq.reshape(total_rows, 2 * STATE), dt_columns], axis=1
    )
    weight_zx = jnp.einsum(
        "td,tc->dc", gathered, grad_zx, preferred_element_type=jnp.float32
    ).reshape(half_width, local_heads, 2 * HEADDIM)
    normed_part = jnp.einsum("tc,dc->td", grad_zx, w_zx, preferred_element_type=jnp.float32)
    grad_normed, bcdt_summed = (
        lax.psum_scatter(normed_part, "head", scatter_dimension=0, tiled=True),
        lax.psum_scatter(grad_bcdt_head, "head", scatter_dimension=0, tiled=True),
    )
    bcdt_low = bcdt_summed.astype(jnp.bfloat16)
    grad_normed = grad_normed + jnp.einsum(
        "tk,dk->td", bcdt_low, in_bcdt, preferred_element_type=jnp.float32
    )
    weight_bcdt = jnp.einsum("td,tk->dk", normed, bcdt_low, preferred_element_type=jnp.float32)
    gain_in_grad = jnp.sum(grad_normed * source * scale, axis=0)
    across = lax.psum(jnp.sum(grad_normed * gain_in * source, axis=1), "width")
    scale_cubed = scale * scale * scale
    grad_hidden = (
        grad_out + scale * gain_in * grad_normed - source * scale_cubed / D * across[:, None]
    ).astype(jnp.bfloat16)
    summed_dp = lax.psum(
        (weight_zx, acc_weight, kernel_x_grad, bias_grad, rate_grad, skip_grad, gain_out_grad), "dp"
    )
    summed_all = lax.psum((weight_bcdt, gain_in_grad, kernel_bc_grad), ("dp", "head"))
    return (
        out_hidden,
        grad_hidden,
        summed_all[1],
        summed_dp[0],
        summed_all[0],
        summed_dp[2],
        summed_all[2],
        summed_dp[3],
        summed_dp[4],
        summed_dp[5],
        summed_dp[6],
        summed_dp[1],
    )


def solution(mesh):
    placed = (
        P(("dp", "head"), "width"),
        P("dp"),
        P(("dp", "head"), "width"),
        P("width"),
        P("width", "head", None),
        P("width", None),
        P(None, "head"),
        P(),
        P("head"),
        P("head"),
        P("head"),
        P("head"),
        P("head", "width"),
    )
    return jax.shard_map(
        per_device,
        mesh=mesh,
        in_specs=placed,
        out_specs=(
            P(("dp", "head"), "width"),
            P(("dp", "head"), "width"),
            P("width"),
            P("width", "head", None),
            P("width", None),
            P(None, "head"),
            P(),
            P("head"),
            P("head"),
            P("head"),
            P("head"),
            P("head", "width"),
        ),
        check_vma=False,
    )
```

profile of v0, /device:TPU:0, one launch (start us, length us, event | category | flops | bytes accessed | tf_op | source)
XLA Modules:
  0.0 2354.9 jit_solution(7531693521205252435)
XLA Ops:
  18.5 80.8 %all-gather.3.cloned.1.call-done = bf16[4096,512]{1,0:T(8,128)(2,1)} async-done(((bf16[1024,512]{1,0:T(8,128)(2,1)}), bf16[4096,512]{1,0:T(8,128)(2,1)}) %all-gather.3.cloned.1.call-update) | async-done | bytes 4194320 | tf_op jit(solution)/shard_map/all_gather | solution.py:110
  105.2 8.2 fusion.149
  113.5 67.4 %all-gather.5.cloned.1.call-done = bf16[4096,512]{1,0:T(8,128)(2,1)} async-done(((bf16[1024,512]{1,0:T(8,128)(2,1)}), bf16[4096,512]{1,0:T(8,128)(2,1)}) %all-gather.5.cloned.1.call-update) | async-done | bytes 4194320 | tf_op jit(solution)/shard_map/all_gather | solution.py:152
  189.9 90.5 %all-reduce.36.cloned.1.call-done = (f32[4096,288]{0,1:T(8,128)}, f32[1,4096,8,128]{1,3,2,0:T(8,128)}, f32[4096,512]{1,0:T(8,128)}) async-done(((f32[4096,288]{0,1:T(8,128)}, f32[1,4096,8,128]{1,3,2,0:T(8,128)}, f32[4096,512]{1,0:T(8,128)}), (f32[4096,288]{0,1:T(8,128)}, f32[1,4096,8,128]{1,3,2,0:T(8,128)}, f32[4096,512]{1,0:T(8,128)})) %all-reduce.36.cloned.1.call-update) | async-done | bytes 29884432 | tf_op jit(solution)/shard_map/psum | solution.py:114
  303.0 22.0 fusion.129
  332.3 8.0 copy.154
  345.7 377.7 %while.44 = (s32[]{:T(128)}, f32[1,8,64,128]{3,2,1,0:T(8,128)S(1)}, f32[16,1,256,8,64]{2,0,4,3,1:T(8,128)}, f32[16,1,8,64,128]{4,3,2,1,0:T(8,128)}, f32[16,1,256...) while((s32[]{:T(128)}, f32[1,8,64,128]{3,2,1,0:T(8,128)S(1)}, ...), condition=%wide.region_7.8_spmd.clone.clone, body=%wide.region_4.7_spmd.clone.clone.sunk | while | flops 909582336 | bytes 7303585 | solution.py:56
  354.1 12.8 dynamic_update_slice.79
  377.7 12.8 dynamic_update_slice.79
  401.3 12.8 dynamic_update_slice.79
  424.9 12.8 dynamic_update_slice.79
  448.5 12.8 dynamic_update_slice.79
  472.0 12.8 dynamic_update_slice.79
  495.6 12.8 dynamic_update_slice.79
  519.2 12.8 dynamic_update_slice.79
  542.8 12.8 dynamic_update_slice.79
  566.4 12.8 dynamic_update_slice.79
  590.0 12.8 dynamic_update_slice.79
  613.6 12.8 dynamic_update_slice.79
  637.2 12.8 dynamic_update_slice.79
  660.8 12.8 dynamic_update_slice.79
  684.3 12.8 dynamic_update_slice.79
  707.9 12.8 dynamic_update_slice.79
  723.5 9.4 transpose.154
  732.8 10.5 fusion.146
  747.5 9.0 copy.158
  756.5 18.9 psum.122
  782.9 15.7 psum.124
  798.7 10.7 multiply_subtract_fusion
  809.4 8.9 copy.161
  818.3 18.4 multiply_reduce_fusion.3
  852.2 809.1 %while.43 = (s32[]{:T(128)}, f32[8]{0:T(128)}, f32[1,8,64,128]{3,2,1,0:T(8,128)S(1)}, f32[16,1,256,8,64]{2,0,4,3,1:T(8,128)}, f32[16,1,256,8]{2,3,1,0:T(8,128)},...) while((s32[]{:T(128)}, f32[8]{0:T(128)}, ...), condition=%wide.region_27.28_spmd.clone, body=%wide.region_14.27_spmd.clone.sunk | while | flops 2126555136 | bytes 20484160 | solution.py:56
  888.8 12.8 dynamic_update_slice.76
  939.3 12.8 dynamic_update_slice.76
  989.9 12.8 dynamic_update_slice.76
  1040.5 12.8 dynamic_update_slice.76
  1091.1 12.8 dynamic_update_slice.76
  1141.6 12.8 dynamic_update_slice.76
  1192.2 12.8 dynamic_update_slice.76
  1242.8 12.8 dynamic_update_slice.76
  1293.4 12.8 dynamic_update_slice.76
  1343.9 12.8 dynamic_update_slice.76
  1394.4 12.8 dynamic_update_slice.76
  1445.0 12.8 dynamic_update_slice.76
  1495.5 12.8 dynamic_update_slice.76
  1546.0 12.8 dynamic_update_slice.76
  1596.6 12.8 dynamic_update_slice.76
  1647.1 12.8 dynamic_update_slice.76
  1661.3 9.8 transpose.155
  1671.1 11.5 multiply_add_fusion
  1682.6 21.0 multiply_reduce_fusion.6
  1703.7 11.8 broadcast_multiply_fusion
  1720.0 13.9 pad_add_fusion
  1739.3 9.9 fusion.169
  1756.7 11.2 multiply_reduce_fusion.12
  1785.4 10.4 fusion.147
  1796.0 9.3 fusion.170
  1806.1 16.8 all-reduce.25
  1822.9 18.5 all-reduce.34.cloned.1.call-done
  1845.5 83.4 %reduce-scatter.8.cloned.1.call-done = f32[1024,288]{0,1:T(8,128)} async-done(((f32[4096,288]{0,1:T(8,128)}), f32[1024,288]{0,1:T(8,128)}) %reduce-scatter.8.cloned.1.call-update) | async-done | bytes 1179664 | tf_op jit(solution)/shard_map/reduce_scatter | solution.py:185
  1931.6 144.7 %reduce-scatter.6.cloned.1.call-done = f32[1024,512]{1,0:T(8,128)} async-done(((f32[4096,512]{1,0:T(8,128)}), f32[1024,512]{1,0:T(8,128)}) %reduce-scatter.6.cloned.1.call-update) | async-done | bytes 2097168 | tf_op jit(solution)/shard_map/reduce_scatter | solution.py:184
  2083.2 45.9 %all-reduce.24 = (f32[512]{0:T(512)}, f32[4,256]{1,0:T(4,128)}) all-reduce(f32[512]{0:T(512)S(1)} %get-tuple-element.759, f32[4,256]{1,0:T(4,128)S(1)} %pad_add_fusion.7), channel_id=1, replica_groups=mesh['dp'=4,'head'=4,'width'=2] {'dp','head'}, use_global_device_ids=true, to_apply=%region_33.34 | all-reduce | flops 1536 | bytes 12288 | tf_op jit(solution)/shard_map/psum | solution.py:201
  2129.1 97.5 %reduce-scatter.4.cloned.1.call-done = f32[1024,512]{1,0:T(8,128)} async-done(((f32[4096,512]{1,0:T(8,128)}), f32[1024,512]{1,0:T(8,128)}) %reduce-scatter.4.cloned.1.call-update) | async-done | bytes 2097168 | tf_op jit(solution)/shard_map/reduce_scatter | solution.py:143
  2230.2 113.4 %all-reduce.32.cloned.1.call-done = f32[512,288]{0,1:T(8,128)} async-done(((f32[512,288]{0,1:T(8,128)}), f32[512,288]{0,1:T(8,128)}) %all-reduce.32.cloned.1.call-update) | async-done | bytes 589840 | tf_op jit(solution)/shard_map/psum | solution.py:201
  (1503 shorter events, 917.2 us)
Async XLA Ops:
  7.2 173.6 %copy-start = (bf16[512,512]{1,0:T(8,128)(2,1)S(1)}, bf16[512,512]{1,0:T(8,128)(2,1)}, u32[]{:S(2)}) copy-start(bf16[512,512]{1,0:T(8,128)(2,1)} %param.29) | copy-start | bytes 1572868
  7.2 92.2 %copy-start.18 = (bf16[512,288]{0,1:T(8,128)(2,1)S(1)}, bf16[512,288]{0,1:T(8,128)(2,1)}, u32[]{:S(2)}) copy-start(bf16[512,288]{0,1:T(8,128)(2,1)} %param.22) | copy-start | bytes 884740
  7.2 92.1 %all-gather.3.cloned.1.call-start = ((), (), s32[]{:S(2)}) async-start(), calls=%async_computation.3 | async-start | bytes 5242880 | tf_op jit(solution)/shard_map/all_gather | solution.py:110
  15.9 165.0 %all-gather.5.cloned.1.call-start = ((), (), s32[]{:S(2)}) async-start(), calls=%async_computation.5 | async-start | bytes 5242880 | tf_op jit(solution)/shard_map/all_gather | solution.py:152
  18.5 86.8 %copy-start.67 = (bf16[512,8,128]{2,1,0:T(8,128)(2,1)S(1)}, bf16[512,8,128]{2,1,0:T(8,128)(2,1)}, u32[]{:S(2)}) copy-start(bf16[512,8,128]{2,1,0:T(8,128)(2,1)} %param.21) | copy-start | bytes 3145732
  18.5 262.0 %all-reduce.36.cloned.1.call-start = ((), (), s32[]{:S(2)}) async-start(), calls=%async_computation.10 | async-start | bytes 59768832 | tf_op jit(solution)/shard_map/psum | solution.py:114
  188.6 1652.8 %all-reduce.34.cloned.1.call-start = ((), (), s32[]{:S(2)}) async-start(), calls=%async_computation.9 | async-start | bytes 6291456 | tf_op jit(solution)/shard_map/psum | solution.py:198
  189.3 609.4 %copy-start.32 = (f32[512]{0:T(512)}, f32[512]{0:T(512)S(1)}, u32[]{:S(2)}) copy-start(f32[512]{0:T(512)S(1)} %convert_element_type.60) | copy-start | bytes 6148
  189.9 99.2 %copy-start.51 = (f32[1,256]{1,0:T(1,128)}, f32[1,256]{1,0:T(1,128)S(1)}, u32[]{:S(2)}) copy-start(f32[1,256]{1,0:T(1,128)S(1)} %get-tuple-element.866) | copy-start | bytes 3076
  189.9 99.2 %copy-start.53 = (f32[1,256]{1,0:T(1,128)}, f32[1,256]{1,0:T(1,128)S(1)}, u32[]{:S(2)}) copy-start(f32[1,256]{1,0:T(1,128)S(1)} %get-tuple-element.867) | copy-start | bytes 3076
  189.9 99.1 %copy-start.55 = (f32[1,256]{1,0:T(1,128)}, f32[1,256]{1,0:T(1,128)S(1)}, u32[]{:S(2)}) copy-start(f32[1,256]{1,0:T(1,128)S(1)} %get-tuple-element.868) | copy-start | bytes 3076
  189.9 99.1 %copy-start.57 = (f32[1,256]{1,0:T(1,128)}, f32[1,256]{1,0:T(1,128)S(1)}, u32[]{:S(2)}) copy-start(f32[1,256]{1,0:T(1,128)S(1)} %get-tuple-element.869) | copy-start | bytes 3076
  189.9 113.1 %copy-start.38 = (f32[1,512]{1,0:T(1,128)}, f32[1,512]{1,0:T(1,128)S(1)}, u32[]{:S(2)}) copy-start(f32[1,512]{1,0:T(1,128)S(1)} %get-tuple-element.862) | copy-start | bytes 6148
  189.9 113.1 %copy-start.40 = (f32[1,512]{1,0:T(1,128)}, f32[1,512]{1,0:T(1,128)S(1)}, u32[]{:S(2)}) copy-start(f32[1,512]{1,0:T(1,128)S(1)} %get-tuple-element.863) | copy-start | bytes 6148
  189.9 113.1 %copy-start.42 = (f32[1,512]{1,0:T(1,128)}, f32[1,512]{1,0:T(1,128)S(1)}, u32[]{:S(2)}) copy-start(f32[1,512]{1,0:T(1,128)S(1)} %get-tuple-element.864) | copy-start | bytes 6148
  189.9 113.1 %copy-start.44 = (f32[1,512]{1,0:T(1,128)}, f32[1,512]{1,0:T(1,128)S(1)}, u32[]{:S(2)}) copy-start(f32[1,512]{1,0:T(1,128)S(1)} %get-tuple-element.865) | copy-start | bytes 6148
  775.5 23.2 copy-start.24
  878.1 23.5 copy-start.28
  878.1 23.5 copy-start.16
  928.7 23.5 copy-start.28
  928.7 23.5 copy-start.16
  979.3 23.5 copy-start.28
  979.3 23.5 copy-start.16
  1029.8 23.5 copy-start.28
  1029.9 23.4 copy-start.16
  1031.6 23.1 copy-start.22
  1080.4 23.5 copy-start.28
  1080.4 23.5 copy-start.16
  1082.2 23.1 copy-start.22
  1131.0 23.4 copy-start.28
  1131.0 23.4 copy-start.16
  1181.6 23.5 copy-start.28
  1181.6 23.4 copy-start.16
  1232.1 23.5 copy-start.28
  1232.2 23.5 copy-start.16
  1233.9 23.1 copy-start.22
  1282.7 23.4 copy-start.28
  1282.7 23.4 copy-start.16
  1333.3 23.4 copy-start.28
  1333.3 23.4 copy-start.16
  1383.8 23.4 copy-start.28
  1383.8 23.4 copy-start.16
  1434.3 23.4 copy-start.28
  1434.3 23.4 copy-start.16
  1484.9 23.4 copy-start.28
  1484.9 23.4 copy-start.16
  1535.4 23.4 copy-start.28
  1535.4 23.4 copy-start.16
  1585.9 23.4 copy-start.28
  1585.9 23.4 copy-start.16
  1636.4 23.4 copy-start.28
  1636.5 23.4 copy-start.16
  1755.1 173.8 %reduce-scatter.8.cloned.1.call-start = ((), (), s32[]{:S(2)}) async-start(), calls=%async_computation.7 | async-start | bytes 5898240 | tf_op jit(solution)/shard_map/reduce_scatter | solution.py:185
  1784.1 292.2 %reduce-scatter.6.cloned.1.call-start = ((), (), s32[]{:S(2)}) async-start(), calls=%async_computation.6 | async-start | bytes 10485760 | tf_op jit(solution)/shard_map/reduce_scatter | solution.py:184
  1795.7 430.8 %reduce-scatter.4.cloned.1.call-start = ((), (), s32[]{:S(2)}) async-start(), calls=%async_computation.4 | async-start | bytes 10485760 | tf_op jit(solution)/shard_map/reduce_scatter | solution.py:143
  1805.4 123.6 %copy-start.6 = (bf16[1024,512]{1,0:T(8,128)(2,1)S(1)}, bf16[1024,512]{1,0:T(8,128)(2,1)}, u32[]{:S(2)}) copy-start(bf16[1024,512]{1,0:T(8,128)(2,1)} %fusion.140) | copy-start | bytes 3145732
  1805.4 270.9 %copy-start.5 = (bf16[1024,512]{1,0:T(8,128)(2,1)S(1)}, bf16[1024,512]{1,0:T(8,128)(2,1)}, u32[]{:S(2)}) copy-start(bf16[1024,512]{1,0:T(8,128)(2,1)} %param.17) | copy-start | bytes 3145732
  1805.4 270.9 %copy-start.19 = (bf16[512,288]{0,1:T(8,128)(2,1)S(1)}, bf16[512,288]{0,1:T(8,128)(2,1)}, u32[]{:S(2)}) copy-start(bf16[512,288]{0,1:T(8,128)(2,1)} %param.22) | copy-start | bytes 884740
  1805.4 270.9 %copy-start.31 = (f32[1024]{0:T(1024)S(1)}, f32[1024]{0:T(1024)}, u32[]{:S(2)}) copy-start(f32[1024]{0:T(1024)} %copy-done.30) | copy-start | bytes 12292
  1805.4 270.9 %copy-start.37 = (f32[512]{0:T(512)S(1)}, f32[512]{0:T(512)}, u32[]{:S(2)}) copy-start(f32[512]{0:T(512)} %copy-done.36) | copy-start | bytes 6148
  1805.5 538.1 %all-reduce.32.cloned.1.call-start = ((), (), s32[]{:S(2)}) async-start(), calls=%async_computation.8 | async-start | bytes 1179648 | tf_op jit(solution)/shard_map/psum | solution.py:201
  1931.5 295.0 %copy-start.14 = (bf16[1024,512]{1,0:T(8,128)(2,1)S(1)}, bf16[1024,512]{1,0:T(8,128)(2,1)}, u32[]{:S(2)}) copy-start(bf16[1024,512]{1,0:T(8,128)(2,1)} %param.19) | copy-start | bytes 3145732
  1931.5 295.0 %copy-start.35 = (f32[1024]{0:T(1024)S(1)}, f32[1024]{0:T(1024)}, u32[]{:S(2)}) copy-start(f32[1024]{0:T(1024)} %copy-done.34) | copy-start | bytes 12292
  1931.5 295.0 %copy-start.46 = (f32[1024]{0:T(1024)S(1)}, f32[1024]{0:T(1024)}, u32[]{:S(2)}) copy-start(f32[1024]{0:T(1024)} %get-tuple-element.860) | copy-start | bytes 12292
  (195 other events, 1264.3 us)
Sparse Core Ops, SparseCore 0:
  16.0 83.3 all-gather.2
  101.5 79.2 all-gather.4
  188.7 91.6 all-reduce.35
  1755.3 86.1 all-reduce.33
  1843.7 85.2 reduce-scatter.7
  1931.3 144.9 reduce-scatter.5
  2078.8 147.7 reduce-scatter.3
  2233.3 110.2 all-reduce.31
where the time goes:
time: 2380 us; the launch traced here: 2350 us
  local copies, waits for them, and re-layouts  748 us (31%)
  waiting for transfers between devices  696 us (29%)
  matrix products  409 us (17%)
  other arithmetic  378 us (16%)
  blocking collectives  102 us (4%)
    dynamic_update_slice x96, local copies, waits for them, and re-layouts, block_scan(): lax.scan(jax.checkpoint(advance), start_state, (in_blocks, step_blocks, b...  495 us
    dot_general x48, matrix products, advance(): inside = jnp.einsum('ijh,jhp->ihp', weights, x_part, precision=HIGH)  169 us
    reduce_scatter x1, waiting for transfers between devices, per_device(): lax.psum_scatter(normed_part, 'head', scatter_dimension=0, tiled=True)  145 us
    psum x1, waiting for transfers between devices, per_device(): lax.psum((weight_bcdt, gain_in_grad, kernel_bc_grad), ('dp', 'head'))  113 us
    another operation x176, other arithmetic  110 us
    reduce_scatter x1, waiting for transfers between devices, per_device(): lax.psum_scatter(jnp.dot(picked, out_w, preferred_element_type=jnp.float3...  97.5 us
    psum x1, waiting for transfers between devices, per_device(): zx_full, bcdt_full = lax.psum((zx_part, bcdt_part), 'width')  90.5 us
    reduce_scatter x1, waiting for transfers between devices, per_device(): lax.psum_scatter(grad_bcdt_head, 'head', scatter_dimension=0, tiled=True)  83.4 us
  transfers between devices with their start and end apart: 8, of which 8 were waited for; matrix products, arithmetic and copies ran while one was open for 3% of the time, Pallas kernels for 0%

commit v1 on v0

--- a/solution.py
+++ b/solution.py
@@ -1,6 +1,11 @@
+import functools
+
 import jax
 import jax.numpy as jnp
+import numpy as np
 from jax import lax
+from jax.experimental import pallas as pl
+from jax.experimental.pallas import tpu as pltpu
 from jax.sharding import PartitionSpec as P
 
 D = 1024
@@ -10,6 +15,7 @@
 SCAN_BLOCK = 256
 LEN = 4096
 INNER = 2048
+SEQS = 4
 
 
 EPS = 1e-05
@@ -215,6 +221,794 @@
     )
 
 
+BF = jnp.bfloat16
+F32 = jnp.float32
+Q = 128
+HALO = 16
+NEG = -1e30
+VMEM = 60 * 1024 * 1024
+
+
+def dot(a, b, prec=None):
+    return lax.dot_general(a, b, (((1,), (0,)), ((), ())), precision=prec, preferred_element_type=F32)
+
+
+def dot_t(a, b, prec=None):
+    return lax.dot_general(a, b, (((1,), (1,)), ((), ())), precision=prec, preferred_element_type=F32)
+
+
+def t_dot(a, b, prec=None):
+    return lax.dot_general(a, b, (((0,), (0,)), ((), ())), precision=prec, preferred_element_type=F32)
+
+
+def split2(v, axis=1):
+    hi = v.astype(BF)
+    lo = (v - hi.astype(F32)).astype(BF)
+    return jnp.concatenate([hi, lo], axis=axis)
+
+
+def dot_split(v, m):
+    hi = v.astype(BF)
+    lo = (v - hi.astype(F32)).astype(BF)
+    return dot(hi, m) + dot(lo, m)
+
+
+def split_dot(m, v):
+    hi = v.astype(BF)
+    lo = (v - hi.astype(F32)).astype(BF)
+    return dot(m, hi) + dot(m, lo)
+
+
+def sigmoid(v):
+    return 1.0 / (1.0 + jnp.exp(-v))
+
+
+def tri(kind):
+    row = lax.broadcasted_iota(jnp.int32, (Q, Q), 0)
+    col = lax.broadcasted_iota(jnp.int32, (Q, Q), 1)
+    return {"ge": row >= col, "le": row <= col, "gt": row > col}[kind]
+
+
+def entry_kernel(
+    hm, ho, hh, gain, wbc, wdt, cbc, bias, rate,
+    xn_o, r_o, raw_o, rawh_o, u_o, b_o, c_o, dt_o, sig_o, cl_o, clt_o, ctot_o,
+    dt2_o, e12_o, tl2_o, dttl2_o, ec2_o, edt2_o, buf,
+):
+    rows = hm.shape[0]
+    state = b_o.shape[1]
+    blocks = rows // Q
+    lower = tri("ge").astype(F32)
+
+    def norm(left, right):
+        h = jnp.concatenate([left, right], axis=1).astype(F32)
+        r = lax.rsqrt(jnp.mean(h * h, axis=1, keepdims=True) + EPS)
+        return (h * r * gain[...]).astype(BF), r
+
+    half = hm.shape[1]
+    xnh, _ = norm(hh[:, :half], hh[:, half:])
+    xn_o[rows:, :] = xnh
+    buf[0:HALO, :] = dot_t(xnh, wbc[...])
+    rawh_o[...] = buf[0:HALO, :]
+
+    def first(i, carry):
+        here = pl.ds(pl.multiple_of(i * Q, Q), Q)
+        xn, r = norm(hm[here, :], ho[here, :])
+        xn_o[here, :] = xn
+        r_o[here, :] = r
+        raw = dot_t(xn, wbc[...])
+        raw_o[here, :] = raw
+        buf[pl.ds(pl.multiple_of(HALO + i * Q, HALO), Q), :] = raw
+        steps = dot_t(xn, wdt[...]) + bias[...]
+        dt = jax.nn.softplus(steps)
+        dt_o[here, :] = dt
+        sig_o[here, :] = sigmoid(steps)
+        da = dt * rate[...]
+        cl_o[here, :] = dot(lower, da, HIGH)
+        clt_o[:, here] = lax.dot_general(
+            da, lower, (((0,), (1,)), ((), ())), precision=HIGH, preferred_element_type=F32
+        )
+        return carry
+
+    lax.fori_loop(0, blocks, first, 0)
+
+    def second(i, carry):
+        here = pl.ds(pl.multiple_of(i * Q, Q), Q)
+        win = buf[pl.ds(pl.multiple_of(i * Q, Q), Q + HALO), :]
+        u = jnp.zeros((Q, win.shape[1]), F32)
+        for k in range(4):
+            u = u + cbc[k : k + 1, :] * win[HALO - 3 + k : HALO - 3 + k + Q, :]
+        u_o[here, :] = u
+        v = u * sigmoid(u)
+        b_o[here, :] = v[:, :state].astype(BF)
+        c_o[here, :] = v[:, state:].astype(BF)
+        return carry
+
+    lax.fori_loop(0, blocks, second, 0)
+    tots = [cl_o[i * Q + Q - 1 : i * Q + Q, :] for i in range(blocks)]
+    ctot = functools.reduce(lambda x, y: x + y, tots)
+    ctot_o[...] = ctot
+    off = jnp.zeros_like(ctot)
+    for i in range(blocks):
+        here = slice(i * Q, i * Q + Q)
+        cl = cl_o[here, :]
+        dt = dt_o[here, :]
+        tail = jnp.exp(tots[i] - cl)
+        dt2_o[here, :] = split2(dt)
+        e12_o[here, :] = split2(jnp.exp(cl))
+        tl2_o[here, :] = split2(tail)
+        dttl2_o[here, :] = split2(dt * tail)
+        ec2_o[here, :] = split2(jnp.exp(cl + off))
+        edt2_o[here, :] = split2(dt * jnp.exp(ctot - cl - off))
+        off = off + tots[i]
+
+
+def project_kernel(
+    xn, wz, wx, cw, dt2, edt2, ex, b, z_o, xr_o, xrh_o, u_o, xs_o, xdt_o, s_o, buf
+):
+    rows = z_o.shape[0]
+    z_o[...] = dot_t(xn[0:rows, :], wz[...])
+    xr = dot_t(xn[...], wx[...])
+    buf[HALO:, :] = xr[0:rows, :]
+    buf[0:HALO, :] = xr[rows:, :]
+    xrh_o[...] = xr[rows:, :]
+    s_o[...] = jnp.zeros_like(s_o)
+
+    def step(i, carry):
+        here = pl.ds(pl.multiple_of(i * Q, Q), Q)
+        win = buf[pl.ds(pl.multiple_of(i * Q, Q), Q + HALO), :]
+        u = jnp.zeros((Q, win.shape[1]), F32)
+        for k in range(4):
+            u = u + cw[k : k + 1, :] * win[HALO - 3 + k : HALO - 3 + k + Q, :]
+        xr_o[here, :] = win[HALO:, :]
+        u_o[here, :] = u
+        xs = u * sigmoid(u)
+        xs_o[here, :] = xs
+        xdt_o[here, :] = (xs * dot(dt2[here, :], ex[...])).astype(BF)
+        s_o[...] += t_dot((xs * dot(edt2[here, :], ex[...])).astype(BF), b[here, :])
+        return carry
+
+    lax.fori_loop(0, rows // Q, step, 0)
+
+
+def decay(cl, clt, h, mask):
+    return jnp.exp(jnp.where(mask, cl[:, h : h + 1] - clt[h : h + 1, :], NEG))
+
+
+def lane_masks():
+    lane = lax.broadcasted_iota(jnp.int32, (1, Q), 1)
+    low = (lane < HEADDIM).astype(F32)
+    return low.astype(BF), (1.0 - low).astype(BF)
+
+
+def inside_kernel(xdt, b, c, cl, clt, y_o):
+    mask = tri("ge")
+    low, high = lane_masks()
+    g = dot_t(c[...], b[...])
+    clv, cltv = cl[...], clt[...]
+    for p in range(xdt.shape[1] // Q):
+        here = slice(p * Q, p * Q + Q)
+        ws = [(g * decay(clv, cltv, h, mask)).astype(BF) for h in (2 * p, 2 * p + 1)]
+        x = xdt[:, here]
+        y_o[:, here] = dot(
+            jnp.concatenate(ws, axis=1), jnp.concatenate([x * low, x * high], axis=0)
+        )
+
+
+def carry_kernel(
+    y_in, xs, z, dyn, b, c, clt, e12, dttl2, s_in, dsk, gain, ex, ext,
+    ys_o, gg_o, sum_o, st_o, s,
+):
+    @pl.when(pl.program_id(0) == 0)
+    def _():
+        s[...] = s_in[...]
+
+    et2 = split2(jnp.broadcast_to(jnp.exp(clt[:, Q - 1 : Q]), (clt.shape[0], Q)), axis=0)
+    square = jnp.zeros((Q, Q), F32)
+    inner = jnp.zeros((Q, Q), F32)
+    for p in range(xs.shape[1] // Q):
+        here = slice(p * Q, p * Q + Q)
+        sb = s[here, :].astype(BF)
+        st_o[0, here, :] = sb
+        x = xs[:, here]
+        e1 = dot(e12[...], ex[:, here])
+        y = y_in[:, here] + e1 * dot_t(c[...], sb) + dsk[:, here] * x
+        ys_o[:, here] = y
+        xt = (x * dot(dttl2[...], ex[:, here])).astype(BF)
+        s[here, :] = dot(ext[here, :], et2) * s[here, :] + t_dot(xt, b[...])
+        zz = z[:, here]
+        gz = y * (zz * sigmoid(zz))
+        gg = gz * gain[:, here]
+        gg_o[:, here] = gg.astype(BF)
+        square = square + gz * gz
+        inner = inner + gg * dyn[:, here]
+    lane = lax.broadcasted_iota(jnp.int32, (Q, 2), 1)
+    sum_o[...] = jnp.where(
+        lane == 0,
+        jnp.sum(square, axis=1, keepdims=True),
+        jnp.sum(inner, axis=1, keepdims=True),
+    )
+
+
+def gate_kernel(
+    dyn, ys, z, xs, scal, gain, ec2, ex, c,
+    dys_o, dz_o, yn_o, ds_o, gn_o, sk_o,
+):
+    @pl.when(pl.program_id(0) == 0)
+    def _():
+        ds_o[...] = jnp.zeros_like(ds_o)
+        gn_o[...] = jnp.zeros_like(gn_o)
+        sk_o[...] = jnp.zeros_like(sk_o)
+
+    r2 = scal[:, 0:1]
+    pull = scal[:, 1:2]
+    for p in range(xs.shape[1] // Q):
+        here = slice(p * Q, p * Q + Q)
+        gn = gain[:, here]
+        zz = z[:, here]
+        sz = sigmoid(zz)
+        silu = zz * sz
+        y = ys[:, here]
+        gz = y * silu
+        dy_n = dyn[:, here]
+        gr = gz * r2
+        yn_o[:, here] = (gr * gn).astype(BF)
+        gn_o[:, here] += jnp.sum(dy_n * gr, axis=0, keepdims=True)
+        dgz = r2 * gn * dy_n - gz * pull
+        dys = dgz * silu
+        dys_o[:, here] = dys
+        dz_o[:, here] = (dgz * y * (sz + silu * (1.0 - sz))).astype(BF)
+        sk_o[:, here] += jnp.sum(dys * xs[:, here], axis=0, keepdims=True)
+        ds_o[here, :] += t_dot((dys * dot(ec2[...], ex[:, here])).astype(BF), c[...])
+
+
+def inside_back_kernel(xdt, dys, b, c, cl, clt, dx_o, db_o, dc_o, da_o, kt):
+    mask = tri("ge")
+    low, high = lane_masks()
+    g = dot_t(c[...], b[...])
+    clv, cltv = cl[...], clt[...]
+    heads = clt.shape[0]
+    lane = lax.broadcasted_iota(jnp.int32, (Q, heads), 1)
+    dg = jnp.zeros((Q, Q), F32)
+    rsum = jnp.zeros((Q, heads), F32)
+    for p in range(heads // 2):
+        here = slice(p * Q, p * Q + Q)
+        x = xdt[:, here]
+        dy = dys[:, here].astype(BF)
+        pp = dot_t(dy, jnp.concatenate([x * low, x * high], axis=0))
+        ws = []
+        for j in range(2):
+            h = 2 * p + j
+            ell = decay(clv, cltv, h, mask)
+            ws.append((g * ell).astype(BF))
+            pe = pp[:, j * Q : j * Q + Q] * ell
+            dg = dg + pe
+            m = pe * g
+            rsum = jnp.where(lane == h, jnp.sum(m, axis=1, keepdims=True), rsum)
+            kt[h : h + 1, :] = jnp.sum(m, axis=0, keepdims=True)
+        dx_o[:, here] = t_dot(
+            jnp.concatenate(ws, axis=0), jnp.concatenate([dy * low, dy * high], axis=0)
+        )
+    dgb = dg.astype(BF)
+    dc_o[...] = dot(dgb, b[...])
+    db_o[...] = t_dot(dgb, c[...])
+    upper = tri("le").astype(F32)
+    da_o[...] = dot(upper, rsum, HIGH) - dot_t(upper, kt[...], HIGH)
+
+
+def back_kernel(
+    dxi, dys, u, xr, xrh, st, b, c, dbi, dci, dai, dt, sig, clt,
+    dt2, e12, tl2, ubc, braw, brawh, cw, cbc, rate, dsk, dz, ds_in, ex, er, ext,
+    all_o, gcx_o, gcb_o, ga_o, gbias_o, ds, du_next, db_next,
+):
+    step = pl.program_id(0)
+    blocks = pl.num_programs(0)
+    rows = all_o.shape[0] - HALO
+    channels = dys.shape[1]
+    heads = dt.shape[1]
+    state = b.shape[1]
+
+    @pl.when(step == 0)
+    def _():
+        ds[...] = ds_in[...]
+        du_next[...] = jnp.zeros_like(du_next)
+        db_next[...] = jnp.zeros_like(db_next)
+        gcx_o[...] = jnp.zeros_like(gcx_o)
+        gcb_o[...] = jnp.zeros_like(gcb_o)
+        ga_o[...] = jnp.zeros_like(ga_o)
+        gbias_o[...] = jnp.zeros_like(gbias_o)
+        all_o[rows:, :] = jnp.zeros((HALO, all_o.shape[1]), BF)
+
+    where = pl.ds(pl.multiple_of((blocks - 1 - step) * Q, Q), Q)
+    last = step == blocks - 1
+    et2 = split2(jnp.broadcast_to(jnp.exp(clt[:, Q - 1 : Q]), (heads, Q)), axis=0)
+    ones = jnp.ones((8, Q), BF)
+
+    def conv_back(d, nxt, taps, raw, rawh, grad_o, first, here):
+        win = jnp.concatenate([d, nxt[:, here]], axis=0)
+        back = jnp.zeros_like(d)
+        sums = []
+        for k in range(4):
+            part = win[3 - k : 3 - k + Q, :]
+            back = back + taps[k : k + 1, here] * part
+            sums.append(jnp.sum(raw * part, axis=0, keepdims=True))
+        grad_o[:, here] += jnp.concatenate(sums, axis=0)
+        all_o[where, first] = back.astype(BF)
+        nxt[:, here] = d[0:8, :]
+
+        @pl.when(last)
+        def _():
+            win_h = jnp.concatenate([jnp.zeros((HALO, d.shape[1]), F32), d[0:8, :]], axis=0)
+            back_h = jnp.zeros((HALO, d.shape[1]), F32)
+            sums_h = []
+            for k in range(4):
+                part = win_h[3 - k : 3 - k + HALO, :]
+                back_h = back_h + taps[k : k + 1, here] * part
+                sums_h.append(jnp.sum(rawh * part, axis=0, keepdims=True))
+            grad_o[:, here] += jnp.concatenate(sums_h, axis=0)
+            all_o[rows:, first] = back_h.astype(BF)
+
+    rsum = jnp.zeros((Q, heads), F32)
+    gsum = jnp.zeros((Q, heads), F32)
+    ddt = jnp.zeros((Q, heads), F32)
+    vrow = jnp.zeros((8, heads), F32)
+    dbs = dbi[...]
+    dcs = dci[...]
+    for p in range(channels // Q):
+        here = slice(p * Q, p * Q + Q)
+        ehere = er[here, :]
+        sb = st[0, here, :]
+        dsv = ds[here, :]
+        dsb = dsv.astype(BF)
+        dy = dys[:, here]
+        dye = dy * dot(e12[...], ex[:, here])
+        dyb = dye.astype(BF)
+        rsum = rsum + dot_split(dye * dot_t(c[...], sb), ehere)
+        dcs = dcs + dot(dyb, sb)
+        bds = dot_t(b[...], dsb)
+        tail = dot(tl2[...], ex[:, here])
+        dtx = dot(dt2[...], ex[:, here])
+        uu = u[:, here]
+        su = sigmoid(uu)
+        xs = uu * su
+        xt = xs * dtx * tail
+        gsum = gsum + dot_split(xt * bds, ehere)
+        dbs = dbs + dot(xt.astype(BF), dsb)
+        dxdt = dxi[:, here] + tail * bds
+        ddt = ddt + dot_split(dxdt * xs, ehere)
+        etr = dot(ext[here, :], et2)
+        eds = etr * dsv
+        vrow = vrow + dot_split(split_dot_t(ones, eds * sb.astype(F32)), ehere)
+        ds[here, :] = eds + t_dot(dyb, c[...])
+        du = (dxdt * dtx + dsk[:, here] * dy) * (su + xs * (1.0 - su))
+        first = slice(channels + p * Q, channels + p * Q + Q)
+        conv_back(du, du_next, cw, xr[:, here], xrh[:, here], gcx_o, first, here)
+    all_o[where, 0:channels] = dz[...]
+    da = (
+        dai[...]
+        + split_dot(tri("le").astype(BF), rsum)
+        + split_dot(tri("gt").astype(BF), gsum)
+        + vrow[0:1, :]
+    )
+    draw = (rate[...] * da + ddt) * sig[...]
+    all_o[where, 2 * channels + 2 * state :] = draw.astype(BF)
+    ga_o[...] += jnp.sum(da * dt[...], axis=0, keepdims=True)
+    gbias_o[...] += jnp.sum(draw, axis=0, keepdims=True)
+    for j, d in enumerate((dbs, dcs)):
+        here = slice(j * state, j * state + state)
+        v = ubc[:, here]
+        sv = sigmoid(v)
+        first = slice(2 * channels + j * state, 2 * channels + j * state + state)
+        conv_back(
+            d * (sv + v * sv * (1.0 - sv)), db_next, cbc, braw[:, here], brawh[:, here],
+            gcb_o, first, here,
+        )
+
+
+def split_dot_t(m, v):
+    hi = v.astype(BF)
+    lo = (v - hi.astype(F32)).astype(BF)
+    return dot_t(m, hi) + dot_t(m, lo)
+
+
+def shape(dims, dtype=F32):
+    return jax.ShapeDtypeStruct(dims, dtype)
+
+
+def whole(array):
+    rank = len(array.shape)
+    return pl.BlockSpec(array.shape, lambda *_: (0,) * rank)
+
+
+def params():
+    return pltpu.CompilerParams(vmem_limit_bytes=VMEM)
+
+
+def sequence_device(
+    hidden, lengths, cotangent, norm_gain, in_zx, in_bcdt, conv_x, conv_bc,
+    dt_bias, a_log, d_skip, gnorm_gain, out_w,
+):
+    rows, half = hidden.shape
+    own_heads = in_zx.shape[1]
+    nz = lax.axis_size("head")
+    ndp = lax.axis_size("dp")
+    zi = lax.axis_index("head")
+    di = lax.axis_index("dp")
+    wi = lax.axis_index("width")
+    per = ndp
+    heads = nz * per
+    channels = heads * HEADDIM
+    model = 2 * half
+    blocks = rows // Q
+    all_columns = 2 * channels + 2 * STATE + heads
+
+    def swap(v):
+        return lax.ppermute(v, "width", [(0, 1), (1, 0)])
+
+    def turn(v, s):
+        return lax.ppermute(v, "head", [(i, (i + s) % nz) for i in range(nz)])
+
+    def shift(v, s):
+        return lax.ppermute(v, "head", [(i, i + s) for i in range(nz) if 0 <= i + s < nz])
+
+    def cross(v, m):
+        return lax.ppermute(v, "dp", [(i, i ^ m) for i in range(ndp)])
+
+    def pick(v, index):
+        return lax.dynamic_index_in_dim(v, index, 0, keepdims=False)
+
+    zx_t = jnp.transpose(in_zx, (1, 2, 0))
+    out_h = out_w.reshape(own_heads, HEADDIM, half)
+
+    def own_group(v):
+        mine = jnp.stack([pick(v, per * wi + (di ^ m)) for m in range(per)])
+        other = jnp.stack([pick(v, per * (1 - wi) + (di ^ m)) for m in range(per)])
+        return jnp.concatenate([mine, swap(other)], axis=2)
+
+    def gather(own):
+        slots = [own[m] for m in range(per)]
+        for s in range(1, nz):
+            got = turn(own[0], s)
+            slots += [got] + [cross(got, m) for m in range(1, per)]
+        return slots
+
+    hidden_o = swap(hidden)
+    zx_slots = gather(own_group(zx_t))
+    wz = jnp.concatenate([v[:HEADDIM] for v in zx_slots], axis=0)
+    wx = jnp.concatenate([v[HEADDIM:] for v in zx_slots], axis=0)
+    wout = jnp.concatenate(gather(own_group(out_h)), axis=0)
+    bcdt_t = jnp.transpose(in_bcdt)
+    bcdt_t = jnp.concatenate([bcdt_t, swap(bcdt_t)], axis=1)
+    wbc = bcdt_t[: 2 * STATE]
+    slot = jnp.arange(heads)
+    slot_head = ((zi - slot // per) % nz) * own_heads + wi * per + ((slot % per) ^ di)
+    pick_heads = (slot_head[:, None] == jnp.arange(HEADS)[None, :]).astype(F32)
+    wdt = jnp.dot(
+        pick_heads.astype(BF), bcdt_t[2 * STATE :], preferred_element_type=F32
+    ).astype(BF)
+
+    table = jnp.concatenate(
+        [
+            dt_bias[:, None],
+            a_log[:, None],
+            d_skip[:, None],
+            jnp.transpose(conv_x.astype(F32).reshape(4, own_heads, HEADDIM), (1, 0, 2)).reshape(
+                own_heads, 4 * HEADDIM
+            ),
+            gnorm_gain.astype(F32).reshape(own_heads, HEADDIM),
+        ],
+        axis=1,
+    )
+    table = jnp.stack([pick(table, per * wi + (di ^ m)) for m in range(per)])
+    table = jnp.concatenate([table] + [turn(table, s) for s in range(1, nz)], axis=0)
+    bias = table[:, 0][None]
+    rate = -jnp.exp(table[:, 1])[None]
+    skip = jnp.repeat(table[:, 2], HEADDIM)[None]
+    taps = jnp.transpose(
+        table[:, 3 : 3 + 4 * HEADDIM].reshape(heads, 4, HEADDIM), (1, 0, 2)
+    ).reshape(4, channels)
+    gain_out = table[:, 3 + 4 * HEADDIM :].reshape(1, channels)
+    taps_bc = conv_bc.astype(F32)
+    gain_in = jnp.concatenate([norm_gain, swap(norm_gain)])[None].astype(F32)
+
+    onehot = np.kron(np.eye(heads), np.ones((1, HEADDIM)))
+    ex = jnp.asarray(np.concatenate([onehot, onehot], axis=0), BF)
+    er = jnp.asarray(onehot.T, BF)
+    ext = jnp.asarray(np.concatenate([onehot.T, onehot.T], axis=1), BF)
+
+    cot_o = swap(cotangent)
+    edge = jnp.concatenate([hidden[rows - HALO :], hidden_o[rows - HALO :]], axis=1)
+    edge = shift(edge, 1)
+    ext_rows = rows + HALO
+    narrow = shape((rows, 2 * heads), BF)
+    (
+        xn, r, braw, brawh, ubc, bs, cs, dt, sig, cl, clt, ctot,
+        dt2, e12, tl2, dttl2, ec2, edt2,
+    ) = pl.pallas_call(
+        entry_kernel,
+        out_shape=[
+            shape((ext_rows, model), BF), shape((rows, 1)), shape((rows, 2 * STATE)),
+            shape((HALO, 2 * STATE)), shape((rows, 2 * STATE)), shape((rows, STATE), BF),
+            shape((rows, STATE), BF), shape((rows, heads)), shape((rows, heads)),
+            shape((rows, heads)), shape((heads, rows)), shape((1, heads)),
+            narrow, narrow, narrow, narrow, narrow, narrow,
+        ],
+        scratch_shapes=[pltpu.VMEM((ext_rows, 2 * STATE), F32)],
+        compiler_params=params(),
+        name="entry",
+    )(hidden, hidden_o, edge, gain_in, wbc, wdt, taps_bc, bias, rate)
+
+    def realign(v, k, group):
+        return jnp.roll(v, k * group, axis=0)
+
+    totals = ctot.reshape(heads, 1)
+    after = {k: realign(shift(totals, -k), -k, per) for k in range(1, nz - 1)}
+    before = {k: realign(shift(totals, k), k, per) for k in range(1, nz - 1)}
+
+    def pass_on(local, sign, between):
+        total = jnp.zeros_like(local)
+        for k in range(1, nz):
+            faded = jnp.zeros_like(totals)
+            for j in range(1, k):
+                faded = faded + between[j]
+            scale = jnp.repeat(jnp.exp(faded), HEADDIM, axis=0)
+            got = shift((local * scale).astype(BF), sign * k)
+            total = total + realign(got, sign * k, per * HEADDIM).astype(F32)
+        return total
+
+    full = shape((rows, channels))
+    pair = lambda p: (0, p)
+    z, xr, xrh, u, xs, xdt, s_local = pl.pallas_call(
+        project_kernel,
+        grid=(channels // Q,),
+        in_specs=[
+            whole(xn), pl.BlockSpec((Q, model), lambda p: (p, 0)),
+            pl.BlockSpec((Q, model), lambda p: (p, 0)), pl.BlockSpec((4, Q), pair), whole(dt2),
+            whole(edt2), pl.BlockSpec((2 * heads, Q), pair), whole(bs),
+        ],
+        out_specs=[
+            pl.BlockSpec((rows, Q), pair), pl.BlockSpec((rows, Q), pair),
+            pl.BlockSpec((HALO, Q), pair), pl.BlockSpec((rows, Q), pair),
+            pl.BlockSpec((rows, Q), pair), pl.BlockSpec((rows, Q), pair),
+            pl.BlockSpec((Q, STATE), lambda p: (p, 0)),
+        ],
+        out_shape=[
+            full, full, shape((HALO, channels)), full, full, shape((rows, channels), BF),
+            shape((channels, STATE)),
+        ],
+        scratch_shapes=[pltpu.VMEM((ext_rows, Q), F32)],
+        compiler_params=params(),
+        name="project",
+    )(xn, wz, wx, taps, dt2, edt2, ex, bs)
+    state_in = pass_on(s_local, 1, after)
+
+    tokens = lambda i: (i, 0)
+    wide = pl.BlockSpec((Q, channels), tokens)
+    bspec = pl.BlockSpec((Q, STATE), tokens)
+    hspec = pl.BlockSpec((Q, heads), tokens)
+    h2spec = pl.BlockSpec((Q, 2 * heads), tokens)
+    tspec = pl.BlockSpec((heads, Q), lambda i: (0, i))
+    y_in = pl.pallas_call(
+        inside_kernel,
+        grid=(blocks,),
+        in_specs=[wide, bspec, bspec, hspec, tspec],
+        out_specs=wide,
+        out_shape=full,
+        compiler_params=params(),
+        name="inside",
+    )(xdt, bs, cs, cl, clt)
+
+    position = zi * rows + jnp.arange(rows, dtype=jnp.int32)
+    keeper = (position < lengths[0])[:, None]
+    grads = jnp.concatenate([cotangent, cot_o], axis=1)
+    masked = jnp.where(keeper, grads, jnp.zeros_like(grads))
+    dyn = dot_t(masked, wout)
+    ys, gg, sums, states = pl.pallas_call(
+        carry_kernel,
+        grid=(blocks,),
+        in_specs=[
+            wide, wide, wide, wide, bspec, bspec, tspec, h2spec, h2spec, whole(state_in),
+            whole(skip), whole(gain_out), whole(ex), whole(ext),
+        ],
+        out_specs=[
+            wide, wide, pl.BlockSpec((Q, 2), tokens),
+            pl.BlockSpec((1, channels, STATE), lambda i: (i, 0, 0)),
+        ],
+        out_shape=[
+            full, shape((rows, channels), BF), shape((rows, 2)),
+            shape((blocks, channels, STATE), BF),
+        ],
+        scratch_shapes=[pltpu.VMEM((channels, STATE), F32)],
+        compiler_params=params(),
+        name="carry",
+    )(y_in, xs, z, dyn, bs, cs, clt, e12, dttl2, state_in, skip, gain_out, ex, ext)
+    sums = sums + swap(sums)
+    branch = dot(gg, wout)
+    branch_o = swap(branch[:, half:].astype(BF))
+    r2 = lax.rsqrt(sums[:, 0:1] / (2 * channels) + EPS)
+    pull = sums[:, 1:2] * (r2 * r2 * r2) / (2 * channels)
+    out_hidden = (
+        hidden.astype(F32)
+        + jnp.where(keeper, (branch[:, :half] + branch_o.astype(F32)) * r2, 0.0)
+    ).astype(BF)
+
+    acc = lambda i: (0, 0)
+    dys, dz, yn, ds_local, g_gain, g_skip = pl.pallas_call(
+        gate_kernel,
+        grid=(blocks,),
+        in_specs=[
+            wide, wide, wide, wide, pl.BlockSpec((Q, 2), tokens), whole(gain_out), h2spec,
+            whole(ex), bspec,
+        ],
+        out_specs=[
+            wide, wide, wide, pl.BlockSpec((channels, STATE), acc),
+            pl.BlockSpec((1, channels), acc), pl.BlockSpec((1, channels), acc),
+        ],
+        out_shape=[
+            full, shape((rows, channels), BF), shape((rows, channels), BF),
+            shape((channels, STATE)), shape((1, channels)), shape((1, channels)),
+        ],
+        compiler_params=params(),
+        name="gate",
+    )(dyn, ys, z, xs, jnp.concatenate([r2, pull], axis=1), gain_out, ec2, ex, cs)
+    ds_in = pass_on(ds_local, -1, before)
+
+    def reduce_slots(v):
+        mine = v[:, 0].astype(F32)
+        for m in range(1, per):
+            mine = mine + cross(v[:, m], m).astype(F32)
+        low = mine.astype(BF)
+        total = mine[0]
+        for s in range(1, nz):
+            total = total + turn(low[s], -s).astype(F32)
+        total = total.astype(BF)
+        return jnp.stack([total] + [cross(total, m) for m in range(1, per)])
+
+    def to_owner(v):
+        v = jnp.stack([pick(v, di ^ m) for m in range(per)])
+        mine, other = v[:, :, :half], swap(v[:, :, half:])
+        low_w = jnp.where(wi == 0, mine, other)
+        high_w = jnp.where(wi == 0, other, mine)
+        return jnp.concatenate([low_w, high_w], axis=0)
+
+    g_out = t_dot(yn, masked).astype(BF).reshape(nz, per, HEADDIM, model)
+    g_out = to_owner(reduce_slots(g_out))
+
+    dxi, dbi, dci, dai = pl.pallas_call(
+        inside_back_kernel,
+        grid=(blocks,),
+        in_specs=[wide, wide, bspec, bspec, hspec, tspec],
+        out_specs=[wide, bspec, bspec, hspec],
+        out_shape=[full, shape((rows, STATE)), shape((rows, STATE)), shape((rows, heads))],
+        scratch_shapes=[pltpu.VMEM((heads, Q), F32)],
+        compiler_params=params(),
+        name="inside_back",
+    )(xdt, dys, bs, cs, cl, clt)
+    rev = lambda i: (blocks - 1 - i, 0)
+    rwide = pl.BlockSpec((Q, channels), rev)
+    rb = pl.BlockSpec((Q, STATE), rev)
+    rh = pl.BlockSpec((Q, heads), rev)
+    rh2 = pl.BlockSpec((Q, 2 * heads), rev)
+    rbc = pl.BlockSpec((Q, 2 * STATE), rev)
+    everything, g_taps, g_taps_bc, g_rate, g_bias = pl.pallas_call(
+        back_kernel,
+        grid=(blocks,),
+        in_specs=[
+            rwide, rwide, rwide, rwide, whole(xrh),
+            pl.BlockSpec((1, channels, STATE), lambda i: (blocks - 1 - i, 0, 0)),
+            rb, rb, rb, rb, rh, rh, rh, pl.BlockSpec((heads, Q), lambda i: (0, blocks - 1 - i)),
+            rh2, rh2, rh2, rbc, rbc, whole(brawh), whole(taps), whole(taps_bc), whole(rate),
+            whole(skip), rwide, whole(ds_in), whole(ex), whole(er), whole(ext),
+        ],
+        out_specs=[
+            pl.BlockSpec((ext_rows, all_columns), acc), pl.BlockSpec((4, channels), acc),
+            pl.BlockSpec((4, 2 * STATE), acc), pl.BlockSpec((1, heads), acc),
+            pl.BlockSpec((1, heads), acc),
+        ],
+        out_shape=[
+            shape((ext_rows, all_columns), BF), shape((4, channels)), shape((4, 2 * STATE)),
+            shape((1, heads)), shape((1, heads)),
+        ],
+        scratch_shapes=[
+            pltpu.VMEM((channels, STATE), F32), pltpu.VMEM((8, channels), F32),
+            pltpu.VMEM((8, 2 * STATE), F32),
+        ],
+        compiler_params=params(),
+        name="back",
+    )(
+        dxi, dys, u, xr, xrh, states, bs, cs, dbi, dci, dai, dt, sig, clt, dt2, e12, tl2, ubc,
+        braw, brawh, taps, taps_bc, rate, skip, dz, ds_in, ex, er, ext,
+    )
+
+    grad_all = t_dot(everything, xn)
+    g_z = grad_all[:channels].astype(BF).reshape(nz, per, HEADDIM, model)
+    g_x = grad_all[channels : 2 * channels].astype(BF).reshape(nz, per, HEADDIM, model)
+    g_zx = to_owner(reduce_slots(jnp.concatenate([g_z, g_x], axis=2)))
+    g_bcdt = jnp.concatenate(
+        [
+            grad_all[2 * channels : 2 * channels + 2 * STATE],
+            jnp.dot(pick_heads.T, grad_all[2 * channels + 2 * STATE :], precision=HIGH),
+        ],
+        axis=0,
+    )
+    g_bcdt = g_bcdt[:, :half] + swap(g_bcdt[:, half:].astype(BF)).astype(F32)
+    quarter = g_bcdt.reshape(per, -1, half)
+    share = pick(quarter, di)
+    for m in range(1, per):
+        share = share + cross(pick(quarter, di ^ m).astype(BF), m).astype(F32)
+    low_share = share.astype(BF)
+    for s in range(1, nz):
+        share = share + turn(low_share, s).astype(F32)
+    share = share.astype(BF)
+    parts = jnp.stack([share] + [cross(share, m) for m in range(1, per)])
+    parts = jnp.stack([pick(parts, di ^ m) for m in range(per)])
+    grad_in_bcdt = jnp.transpose(parts.reshape(-1, half).astype(F32))
+
+    weights_all = jnp.concatenate([wz, wx, wbc, wdt], axis=0)
+    dxn = dot(everything, weights_all)
+    dxn = dxn[:, :half] + swap(dxn[:, half:].astype(BF)).astype(F32)
+    late = shift(dxn[rows:], -1)
+    dxn = jnp.concatenate([dxn[: rows - HALO], dxn[rows - HALO : rows] + late], axis=0)
+    source = hidden.astype(F32)
+    gain_half = gain_in[:, :half]
+    across = jnp.sum(dxn * gain_half * source, axis=1, keepdims=True)
+    across = across + swap(across)
+    grad_hidden = (
+        cotangent.astype(F32)
+        + r * gain_half * dxn
+        - source * (r * r * r) / model * across
+    ).astype(BF)
+    g_norm = jnp.sum(dxn * source * r, axis=0)
+
+    table = jnp.concatenate(
+        [
+            g_bias.reshape(heads, 1),
+            (g_rate * rate).reshape(heads, 1),
+            jnp.sum(g_skip.reshape(heads, HEADDIM), axis=1, keepdims=True),
+            jnp.transpose(g_taps.reshape(4, heads, HEADDIM), (1, 0, 2)).reshape(heads, 4 * HEADDIM),
+            g_gain.reshape(heads, HEADDIM),
+        ],
+        axis=1,
+    )
+    table = jnp.dot(pick_heads.T, table, precision=HIGH)
+    side = (jnp.arange(2) == wi).astype(F32)[:, None] * g_norm[None]
+    small = jnp.concatenate([table.reshape(-1), g_taps_bc.reshape(-1), side.reshape(-1)])
+    small = lax.psum(small, ("dp", "head", "width"))
+    size = table.size
+    table = lax.dynamic_slice_in_dim(
+        small[:size].reshape(HEADS, -1), zi * own_heads, own_heads, 0
+    )
+    g_taps_bc = small[size : size + 8 * STATE].reshape(4, 2 * STATE)
+    g_norm = pick(small[size + 8 * STATE :].reshape(2, half), wi)
+    return (
+        out_hidden,
+        grad_hidden,
+        g_norm,
+        jnp.transpose(g_zx, (2, 0, 1)).astype(F32),
+        grad_in_bcdt,
+        jnp.transpose(
+            table[:, 3 : 3 + 4 * HEADDIM].reshape(own_heads, 4, HEADDIM), (1, 0, 2)
+        ).reshape(4, own_heads * HEADDIM),
+        g_taps_bc,
+        table[:, 0],
+        table[:, 1],
+        table[:, 2],
+        table[:, 3 + 4 * HEADDIM :].reshape(-1),
+        g_out.reshape(own_heads * HEADDIM, half).astype(F32),
+    )
+
+
+def fits(mesh):
+    ndp, nz, nw = mesh.shape["dp"], mesh.shape["head"], mesh.shape["width"]
+    return (
+        nw == 2
+        and ndp in (2, 4, 8)
+        and HEADS == nz * nw * ndp
+        and LEN % (nz * Q) == 0
+        and SEQS == ndp
+        and HEADS // nw * HEADDIM % Q == 0
+    )
+
+
 def solution(mesh):
     placed = (
         P(("dp", "head"), "width"),
@@ -232,7 +1026,7 @@
         P("head", "width"),
     )
     return jax.shard_map(
-        per_device,
+        sequence_device if fits(mesh) else per_device,
         mesh=mesh,
         in_specs=placed,
         out_specs=(

time: 2380 us -> 593 us (0.25)
  local copies, waits for them, and re-layouts: 748 us -> 44 us
  waiting for transfers between devices: 696 us -> 141 us
  matrix products: 409 us -> 34.3 us
  other arithmetic: 378 us -> 32.4 us
  Pallas kernels: 0 us -> 168 us
  starting transfers between devices: 0.76 us -> 119 us
  blocking collectives: 102 us -> 40.7 us
    dynamic_update_slice x97 -> x0, local copies, waits for them, and re-layouts: 495 us -> none  [the longest x96 495 us: block_scan(): lax.scan(jax.checkpoint(advance), start_state, (in_blocks, step_blocks, b...]
    dot_general x233 -> x8, matrix products: 409 us -> 34.3 us  [the longest x2 17.2 us: t_dot(): lax.dot_general(a, b, (((0,), (0,)), ((), ())), precision=prec, preferred...]
    reduce_scatter x3 -> x0, waiting for transfers between devices: 326 us -> none  [the longest x1 145 us: per_device(): lax.psum_scatter(normed_part, 'head', scatter_dimension=0, tiled=True)]
    psum x3 -> x0, waiting for transfers between devices: 222 us -> none  [the longest x1 113 us: per_device(): lax.psum((weight_bcdt, gain_in_grad, kernel_bc_grad), ('dp', 'head'))]
    pallas_call x0 -> x7, Pallas kernels: none -> 168 us  [the longest x1 67.1 us: sequence_device(): pl.pallas_call(back_kernel, grid=(blocks,), in_specs=[rwide, rwide, rwide...]
    all_gather x2 -> x0, waiting for transfers between devices: 148 us -> none  [the longest x1 80.8 us: per_device(): gathered = lax.all_gather(normed, 'head', axis=0, tiled=True)]
    ppermute x0 -> x79, waiting for transfers between devices: none -> 141 us  [the longest x36 113 us: cross(): return lax.ppermute(v, 'dp', [(i, i ^ m) for i in range(ndp)])]
    ppermute x0 -> x79, starting transfers between devices: none -> 119 us  [the longest x36 47.2 us: cross(): return lax.ppermute(v, 'dp', [(i, i ^ m) for i in range(ndp)])]
  transfers between devices with their start and end apart: 8 -> 79, of which waited for: 8 -> 29; matrix products, arithmetic and copies ran while one was open for 3% -> 15% of each run, Pallas kernels for 0% -> 22%
where the time goes in v1:
time: 593 us; the launch traced here: 583 us
  Pallas kernels  168 us (28%)
  waiting for transfers between devices  141 us (24%)
  starting transfers between devices  119 us (20%)
  local copies, waits for them, and re-layouts  44 us (7%)
  blocking collectives  40.7 us (7%)
  matrix products  34.3 us (6%)
  other arithmetic  32.4 us (5%)
    ppermute x36, waiting for transfers between devices, cross(): return lax.ppermute(v, 'dp', [(i, i ^ m) for i in range(ndp)])  113 us
    pallas_call x1, Pallas kernels, sequence_device(): pl.pallas_call(back_kernel, grid=(blocks,), in_specs=[rwide, rwide, rwide...  67.1 us
    ppermute x36, starting transfers between devices, cross(): return lax.ppermute(v, 'dp', [(i, i ^ m) for i in range(ndp)])  47.2 us
    ppermute x18, starting transfers between devices, turn(): return lax.ppermute(v, 'head', [(i, (i + s) % nz) for i in range(nz)])  41.3 us
    psum x1, blocking collectives, sequence_device(): small = lax.psum(small, ('dp', 'head', 'width'))  40.7 us
    pallas_call x1, Pallas kernels, sequence_device(): pl.pallas_call(project_kernel, grid=(channels // Q,), in_specs=[whole(xn)...  34.2 us
    ppermute x12, starting transfers between devices, shift(): lax.ppermute(v, 'head', [(i, i + s) for i in range(nz) if 0 <= i + s < nz])  28.5 us
    ppermute x18, waiting for transfers between devices, turn(): return lax.ppermute(v, 'head', [(i, (i + s) % nz) for i in range(nz)])  18.6 us
  transfers between devices with their start and end apart: 79, of which 29 were waited for; matrix products, arithmetic and copies ran while one was open for 15% of the time, Pallas kernels for 22%

profile of v1, /device:TPU:0, one launch (start us, length us, event | category | flops | bytes accessed | tf_op | source)
XLA Modules:
  0.0 583.1 jit_solution(12404775747676495956)
XLA Ops:
  5.3 5.0 collective-permute-start.6
  15.5 2.9 constant_dynamic-slice_fusion.29
  30.3 2.0 collective-permute-start.26
  33.8 8.1 %collective-permute-done.22 = bf16[64,1024]{1,0:T(8,128)(2,1)S(1)} collective-permute-done((bf16[64,1024]{1,0:T(8,128)(2,1)S(1)}, bf16[64,1024]{1,0:T(8,128)(2,1)S(1)}, u32[]{:S(2)}, u32[]{:S(2)}) %collective-permute-start.22) | collective-permute-done | bytes 131104 | tf_op jit(solution)/shard_map/ppermute | solution.py:648
  46.2 2.2 collective-permute-done.23
  49.9 1.9 collective-permute-start.30
  51.8 2.5 collective-permute-start.28
  56.9 3.3 collective-permute-done.27
  64.0 2.3 collective-permute-done.31
  66.3 2.9 collective-permute-start.33
  69.2 1.9 collective-permute-start.12
  71.1 2.3 collective-permute-done.8
  75.1 7.1 %collective-permute-done.9 = bf16[128,1024]{1,0:T(8,128)(2,1)S(1)} collective-permute-done((bf16[128,1024]{1,0:T(8,128)(2,1)S(1)}, bf16[128,1024]{1,0:T(8,128)(2,1)S(1)}, u32[]{:S(2)}, u32[]{:S(2)}) %collective-permute-start.9) | collective-permute-done | bytes 262176 | tf_op jit(solution)/shard_map/ppermute | solution.py:654
  82.9 2.9 collective-permute-start.14
  85.8 5.2 collective-permute-done.11
  91.6 6.2 %collective-permute-done.13 = bf16[128,1024]{1,0:T(8,128)(2,1)S(1)} collective-permute-done((bf16[128,1024]{1,0:T(8,128)(2,1)S(1)}, bf16[128,1024]{1,0:T(8,128)(2,1)S(1)}, u32[]{:S(2)}, u32[]{:S(2)}) %collective-permute-start.13) | collective-permute-done | bytes 262176 | tf_op jit(solution)/shard_map/ppermute | solution.py:654
  97.8 2.0 collective-permute-start.15
  100.9 2.7 collective-permute-start.18
  103.6 2.6 collective-permute-done.15
  106.2 2.5 collective-permute-start.17
  108.7 8.8 %collective-permute-done.17 = bf16[128,1024]{1,0:T(8,128)(2,1)S(1)} collective-permute-done((bf16[128,1024]{1,0:T(8,128)(2,1)S(1)}, bf16[128,1024]{1,0:T(8,128)(2,1)S(1)}, u32[]{:S(2)}, u32[]{:S(2)}) %collective-permute-start.17) | collective-permute-done | bytes 262176 | tf_op jit(solution)/shard_map/ppermute | solution.py:654
  117.5 3.2 collective-permute-start.1
  123.7 4.3 fusion.39.dyn
  128.9 2.2 copy-done.29
  131.7 13.8 %entry.1 = (bf16[1040,1024]{1,0:T(8,128)(2,1)}, f32[1024,1]{1,0:T(8,128)}, f32[1024,256]{1,0:T(8,128)}, f32[16,256]{1,0:T(8,128)}, f32[1024,256]{1,0:T(8,128)}, ...) custom-call(bf16[1024,512]{1,0:T(8,128)(2,1)} %hm.1, ...), custom_call_target="tpu_custom_call" | custom-call | tf_op jit(solution)/shard_map/entry/pallas_call | solution.py:726
  145.5 4.2 collective-permute-start.44
  149.7 1.8 collective-permute-start.42
  155.7 34.2 %project.1 = (f32[1024,1024]{1,0:T(8,128)}, f32[1024,1024]{1,0:T(8,128)}, f32[16,1024]{1,0:T(8,128)}, f32[1024,1024]{1,0:T(8,128)}, f32[1024,1024]{1,0:T(8,128)}...) custom-call(bf16[1040,1024]{1,0:T(8,128)(2,1)} %get-tuple-element.56.xn, bf16[1024,1024]{1,0:T(8,128)(2,1)} %copy-done.4, ...), custom_call_target="tpu_custom_call" | custom-call | tf_op jit(solution)/shard_map/project/pallas_call | solution.py:760
  190.0 8.5 %inside.1.y_in = f32[1024,1024]{1,0:T(8,128)} custom-call(bf16[1024,1024]{1,0:T(8,128)(2,1)} %get-tuple-element.60.xdt, bf16[1024,128]{1,0:T(8,128)(2,1)} %get-tuple-element.59.b, bf16[1024,128]{1,0:T(8,128)(2,1)} %get-tuple-element.61.c, f32[1024,16]{1,0:T(8,128)} %get-tuple-element.62.cl, f32[16,1024]{1,0:T(8,128)} %get-tuple-element.63.clt), custom_call_target="tpu_custom_call" | custom-call | tf_op jit(solution)/shard_map/inside/pallas_call | solution.py:790
  199.3 7.5 %collective-permute-start.38 = (bf16[1024,128]{1,0:T(8,128)(2,1)S(1)}, bf16[1024,128]{1,0:T(8,128)(2,1)S(1)}, u32[]{:S(2)}, u32[]{:S(2)}) collective-permute-start(bf16[1024,128]{1,0:T(8,128)(2,1)S(1)} %get-tuple-element.245), channel_id=1, source_target_pairs={{0,6},{1,7},{8,14},{9,15},{16,22},{17,23},{24,30},{25,31}} | collective-permute-start | bytes 786440 | tf_op jit(solution)/shard_map/ppermute | solution.py:651
  208.2 2.5 collective-permute-start.34
  211.2 2.4 collective-permute-done.38
  213.6 6.4 %collective-permute-done.34 = bf16[1024,128]{1,0:T(8,128)(2,1)S(1)} collective-permute-done((bf16[1024,128]{1,0:T(8,128)(2,1)S(1)}, bf16[1024,128]{1,0:T(8,128)(2,1)S(1)}, u32[]{:S(2)}, u32[]{:S(2)}) %collective-permute-start.34) | collective-permute-done | bytes 262176 | tf_op jit(solution)/shard_map/ppermute | solution.py:651
  220.9 14.1 %carry.1 = (f32[1024,1024]{1,0:T(8,128)}, bf16[1024,1024]{1,0:T(8,128)(2,1)}, f32[1024,2]{1,0:T(8,128)}, bf16[8,1024,128]{2,1,0:T(8,128)(2,1)}) custom-call(f32[1024,1024]{1,0:T(8,128)} %inside.1.y_in, f32[1024,1024]{1,0:T(8,128)} %get-tuple-element.64.xs, f32[1024,1024]{1,0:T(8,128)} %get-tuple-element.65.z, f32[1024,1024]{1,0:T(8,128)} %fusion.39.dyn, ...), custom_call_target="tpu_custom_call" | custom-call | tf_op jit(solution)/shard_map/carry/pallas_call | solution.py:805
  235.1 3.9 fusion.81
  242.4 12.9 %gate.1 = (f32[1024,1024]{1,0:T(8,128)}, bf16[1024,1024]{1,0:T(8,128)(2,1)}, bf16[1024,1024]{1,0:T(8,128)(2,1)}, f32[1024,128]{1,0:T(8,128)}, f32[1,1024]{1,0:T(1,128)}, /*index=5*/f32[1,1024]{1,0:T(1,128)}) custom-call(f32[1024,1024]{1,0:T(8,128)} %fusion.39.dyn, f32[1024,1024]{1,0:T(8,128)} %get-tuple-element.73.ys, f32[1024,1024]{1,0:T(8,128)} %get-tuple-element.65.z, ...), custom_call_target="tpu_custom_call" | custom-call | tf_op jit(solution)/shard_map/gate/pallas_call | solution.py:835
  264.4 4.0 convolution_convert_fusion
  272.1 2.4 collective-permute-start.71
  274.5 17.7 %inside_back.1 = (f32[1024,1024]{1,0:T(8,128)}, f32[1024,128]{1,0:T(8,128)}, f32[1024,128]{1,0:T(8,128)}, f32[1024,16]{1,0:T(8,128)}) custom-call(bf16[1024,1024]{1,0:T(8,128)(2,1)} %get-tuple-element.60.xdt, f32[1024,1024]{1,0:T(8,128)} %get-tuple-element.75.dys, bf16[1024,128]{1,0:T(8,128)(2,1)} %get-tuple-element.59.b, ...), custom_call_target="tpu_custom_call" | custom-call | tf_op jit(solution)/shard_map/inside_back/pallas_call | solution.py:876
  296.0 67.1 %back.1 = (bf16[1040,2320]{1,0:T(8,128)(2,1)}, f32[4,1024]{1,0:T(4,128)}, f32[4,256]{1,0:T(4,128)}, f32[1,16]{1,0:T(1,128)}, f32[1,16]{1,0:T(1,128)}) custom-call(f32[1024,1024]{1,0:T(8,128)} %get-tuple-element.76.dxi, f32[1024,1024]{1,0:T(8,128)} %get-tuple-element.75.dys, f32[1024,1024]{1,0:T(8,128)} %get-tuple-element.77.u, ...), custom_call_target="tpu_custom_call" | custom-call | tf_op jit(solution)/shard_map/back/pallas_call | solution.py:892
  363.1 13.2 %fusion.80 = (bf16[2320,1024]{1,0:T(8,128)(2,1)}, f32[2320,1024]{1,0:T(8,128)S(1)}) fusion(bf16[1040,2320]{1,0:T(8,128)(2,1)} %get-tuple-element.92, bf16[1040,1024]{1,0:T(8,128)(2,1)S(1)} %copy-done.7), kind=kOutput, calls=%fused_computation.317 | convolution fusion | flops 4943790080 | bytes 21209600 | tf_op jit(solution)/shard_map/dot_general | solution.py:241
  376.8 7.5 %fusion.82 = f32[1040,1024]{1,0:T(8,128)} fusion(bf16[1040,2320]{1,0:T(8,128)(2,1)S(1)} %bitcast.301, bf16[2320,1024]{1,0:T(8,128)(2,1)S(1)} %bitcast.292), kind=kOutput, calls=%fused_computation.319 | convolution fusion | flops 4941414400 | bytes 13836800 | tf_op jit(solution)/shard_map/dot_general | solution.py:233
  387.7 2.7 fusion.76
  393.0 2.5 collective-permute-start.62
  397.0 21.2 %collective-permute-done.60 = bf16[72,512]{1,0:T(8,128)(2,1)S(1)} collective-permute-done((bf16[72,512]{1,0:T(8,128)(2,1)S(1)}, bf16[72,512]{1,0:T(8,128)(2,1)S(1)}, u32[]{:S(2)}, u32[]{:S(2)}) %collective-permute-start.60) | collective-permute-done | bytes 73760 | tf_op jit(solution)/shard_map/ppermute | solution.py:654
  418.3 2.2 collective-permute-done.62
  420.5 11.9 %collective-permute-start.65 = (bf16[72,512]{1,0:T(8,128)(2,1)S(1)}, bf16[72,512]{1,0:T(8,128)(2,1)S(1)}, u32[]{:S(2)}, u32[]{:S(2)}) collective-permute-start(bf16[72,512]{1,0:T(8,128)(2,1)S(1)} %fusion.53), channel_id=1, source_target_pairs={{0,6},{2,0},{4,2},{6,4},{1,7},{3,1},{5,3},{7,5},{8,14},{10,8},{12,... | collective-permute-start | bytes 221192 | tf_op jit(solution)/shard_map/ppermute | solution.py:648
  434.5 4.5 collective-permute-start.72
  439.3 3.2 collective-permute-start.73
  443.2 2.9 collective-permute-done.74
  446.2 3.5 collective-permute-done.73
  451.4 2.0 collective-permute-start.76
  455.8 2.0 collective-permute-done.77
  464.2 17.6 %collective-permute-done.51 = bf16[4,128,1024]{2,1,0:T(8,128)(2,1)S(1)} collective-permute-done((bf16[4,128,1024]{2,1,0:T(8,128)(2,1)S(1)}, bf16[4,128,1024]{2,1,0:T(8,128)(2,1)S(1)}, u32[]{:S(2)}, u32[]{:S(2)}) %collective-permute-start.51) | collective-permute-done | bytes 1048608 | tf_op jit(solution)/shard_map/ppermute | solution.py:654
  481.8 22.4 %collective-permute-done.50 = bf16[4,128,1024]{2,1,0:T(8,128)(2,1)S(1)} collective-permute-done((bf16[4,128,1024]{2,1,0:T(8,128)(2,1)S(1)}, bf16[4,128,1024]{2,1,0:T(8,128)(2,1)S(1)}, u32[]{:S(2)}, u32[]{:S(2)}) %collective-permute-start.50) | collective-permute-done | bytes 1048608 | tf_op jit(solution)/shard_map/ppermute | solution.py:654
  504.1 2.3 fusion.73
  509.0 2.7 collective-permute-start.52
  511.7 3.1 collective-permute-start.53
  516.1 40.7 %psum.7 = f32[12384]{0:T(1024)S(1)} all-reduce(f32[12384]{0:T(1024)S(1)} %concatenate.182), channel_id=1, replica_groups=mesh['dp'=4,'head'=4,'width'=2] {'dp','head','width'}, use_global_device_ids=true, to_apply=%region_3.4 | all-reduce | flops 12384 | bytes 99072 | tf_op jit(solution)/shard_map/psum | solution.py:975
  558.9 2.8 collective-permute-start.57
  566.4 2.8 collective-permute-done.57
  569.3 3.6 collective-permute-done.56
  577.1 3.5 fusion.3
  580.8 1.8 copy.200
  (403 shorter events, 106.7 us)
Async XLA Ops:
  5.3 18.8 %collective-permute-start.6 = (f32[4,323]{1,0:T(4,128)}, f32[4,323]{1,0:T(4,128)}, u32[]{:S(2)}, u32[]{:S(2)}) collective-permute-start(f32[4,323]{1,0:T(4,128)} %pad_maximum_fusion.18), channel_id=1, source_target_pairs={{0,6},{2,0},{4,2},{6,4},{1,7},{3,1},{5,3},{7,5},{8,14},{10,8},{12,... | collective-permute-start | bytes 15512 | tf_op jit(solution)/shard_map/ppermute | solution.py:648
  10.3 14.3 %collective-permute-start.5 = (f32[4,323]{1,0:T(4,128)}, f32[4,323]{1,0:T(4,128)}, u32[]{:S(2)}, u32[]{:S(2)}) collective-permute-start(f32[4,323]{1,0:T(4,128)} %pad_maximum_fusion.18), channel_id=1, source_target_pairs={{0,4},{2,6},{4,0},{6,2},{1,5},{3,7},{5,1},{7,3},{8,12},{10,14},{12... | collective-permute-start | bytes 15512 | tf_op jit(solution)/shard_map/ppermute | solution.py:648
  10.3 14.4 %collective-permute-start.4 = (f32[4,323]{1,0:T(4,128)}, f32[4,323]{1,0:T(4,128)}, u32[]{:S(2)}, u32[]{:S(2)}) collective-permute-start(f32[4,323]{1,0:T(4,128)} %pad_maximum_fusion.18), channel_id=1, source_target_pairs={{0,2},{2,4},{4,6},{6,0},{1,3},{3,5},{5,7},{7,1},{8,10},{10,12},{12... | collective-permute-start | bytes 15512 | tf_op jit(solution)/shard_map/ppermute | solution.py:648
  11.3 11.9 %collective-permute-start.2 = (bf16[512]{0:T(512)(128)(2,1)}, bf16[512]{0:T(512)(128)(2,1)}, u32[]{:S(2)}, u32[]{:S(2)}) collective-permute-start(bf16[512]{0:T(512)(128)(2,1)} %param.19), channel_id=1, source_target_pairs={{0,1},{1,0},{2,3},{3,2},{4,5},{5,4},{6,7},{7,6},{8,9},{9,8},{10,11... | collective-permute-start | bytes 3080 | tf_op jit(solution)/shard_map/ppermute | solution.py:645
  13.9 15.4 %collective-permute-start.21 = (bf16[4,64,512]{2,1,0:T(8,128)(2,1)}, bf16[4,64,512]{2,1,0:T(8,128)(2,1)}, u32[]{:S(2)}, u32[]{:S(2)}) collective-permute-start(bf16[4,64,512]{2,1,0:T(8,128)(2,1)} %pad_maximum_fusion.14), channel_id=1, source_target_pairs={{0,1},{1,0},{2,3},{3,2},{4,5},{5,4},{6,7},{7,6},{8,9},{9,8},{10,11... | collective-permute-start | bytes 786440 | tf_op jit(solution)/shard_map/ppermute | solution.py:645
  23.3 76.6 %collective-permute-start = (bf16[1024,512]{1,0:T(8,128)(2,1)S(1)}, bf16[1024,512]{1,0:T(8,128)(2,1)S(1)}, u32[]{:S(2)}, u32[]{:S(2)}) collective-permute-start(bf16[1024,512]{1,0:T(8,128)(2,1)S(1)} %copy-done), channel_id=1, source_target_pairs={{0,1},{1,0},{2,3},{3,2},{4,5},{5,4},{6,7},{7,6},{8,9},{9,8},{10,11... | collective-permute-start | bytes 3145736 | tf_op jit(solution)/shard_map/ppermute | solution.py:645
  24.1 98.6 %collective-permute-start.3 = (bf16[288,512]{1,0:T(8,128)(2,1)S(1)}, bf16[288,512]{1,0:T(8,128)(2,1)S(1)}, u32[]{:S(2)}, u32[]{:S(2)}) collective-permute-start(bf16[288,512]{1,0:T(8,128)(2,1)S(1)} %bitcast.256), channel_id=1, source_target_pairs={{0,1},{1,0},{2,3},{3,2},{4,5},{5,4},{6,7},{7,6},{8,9},{9,8},{10,11... | collective-permute-start | bytes 884744 | tf_op jit(solution)/shard_map/ppermute | solution.py:645
  24.6 18.8 %collective-permute-start.7 = (bf16[4,128,512]{2,1,0:T(8,128)(2,1)}, bf16[4,128,512]{2,1,0:T(8,128)(2,1)}, u32[]{:S(2)}, u32[]{:S(2)}) collective-permute-start(bf16[4,128,512]{2,1,0:T(8,128)(2,1)} %pad_maximum_fusion.6), channel_id=1, source_target_pairs={{0,1},{1,0},{2,3},{3,2},{4,5},{5,4},{6,7},{7,6},{8,9},{9,8},{10,11... | collective-permute-start | bytes 1572872 | tf_op jit(solution)/shard_map/ppermute | solution.py:645
  30.3 19.7 %collective-permute-start.26 = (bf16[64,1024]{1,0:T(8,128)(2,1)S(1)}, bf16[64,1024]{1,0:T(8,128)(2,1)S(1)}, u32[]{:S(2)}, u32[]{:S(2)}) collective-permute-start(bf16[64,1024]{1,0:T(8,128)(2,1)S(1)} %slice_bitcast_fusion.16), channel_id=1, source_target_pairs={{0,4},{2,6},{4,0},{6,2},{1,5},{3,7},{5,1},{7,3},{8,12},{10,14},{12... | collective-permute-start | bytes 393224 | tf_op jit(solution)/shard_map/ppermute | solution.py:648
  32.2 9.6 %collective-permute-start.22 = (bf16[64,1024]{1,0:T(8,128)(2,1)S(1)}, bf16[64,1024]{1,0:T(8,128)(2,1)S(1)}, u32[]{:S(2)}, u32[]{:S(2)}) collective-permute-start(bf16[64,1024]{1,0:T(8,128)(2,1)S(1)} %slice_bitcast_fusion.16), channel_id=1, source_target_pairs={{0,2},{2,4},{4,6},{6,0},{1,3},{3,5},{5,7},{7,1},{8,10},{10,12},{12... | collective-permute-start | bytes 393224 | tf_op jit(solution)/shard_map/ppermute | solution.py:648
  41.9 10.0 %collective-permute-start.24 = (bf16[64,1024]{1,0:T(8,128)(2,1)S(1)}, bf16[64,1024]{1,0:T(8,128)(2,1)S(1)}, u32[]{:S(2)}, u32[]{:S(2)}) collective-permute-start(bf16[64,1024]{1,0:T(8,128)(2,1)S(1)} %collective-permute-done.22), channel_id=1, source_target_pairs={{0,16},{8,24},{16,0},{24,8},{1,17},{9,25},{17,1},{25,9},{2,18},{10... | collective-permute-start | bytes 393224 | tf_op jit(solution)/shard_map/ppermute | solution.py:654
  51.8 8.4 %collective-permute-start.28 = (bf16[64,1024]{1,0:T(8,128)(2,1)S(1)}, bf16[64,1024]{1,0:T(8,128)(2,1)S(1)}, u32[]{:S(2)}, u32[]{:S(2)}) collective-permute-start(bf16[64,1024]{1,0:T(8,128)(2,1)S(1)} %collective-permute-done.26), channel_id=1, source_target_pairs={{0,16},{8,24},{16,0},{24,8},{1,17},{9,25},{17,1},{25,9},{2,18},{10... | collective-permute-start | bytes 393224 | tf_op jit(solution)/shard_map/ppermute | solution.py:654
  60.2 9.0 %collective-permute-start.32 = (bf16[64,1024]{1,0:T(8,128)(2,1)S(1)}, bf16[64,1024]{1,0:T(8,128)(2,1)S(1)}, u32[]{:S(2)}, u32[]{:S(2)}) collective-permute-start(bf16[64,1024]{1,0:T(8,128)(2,1)S(1)} %collective-permute-done.30), channel_id=1, source_target_pairs={{0,16},{8,24},{16,0},{24,8},{1,17},{9,25},{17,1},{25,9},{2,18},{10... | collective-permute-start | bytes 393224 | tf_op jit(solution)/shard_map/ppermute | solution.py:654
  62.3 11.1 %collective-permute-start.8 = (bf16[128,1024]{1,0:T(8,128)(2,1)S(1)}, bf16[128,1024]{1,0:T(8,128)(2,1)S(1)}, u32[]{:S(2)}, u32[]{:S(2)}) collective-permute-start(bf16[128,1024]{1,0:T(8,128)(2,1)S(1)} %slice_bitcast_fusion.9), channel_id=1, source_target_pairs={{0,2},{2,4},{4,6},{6,0},{1,3},{3,5},{5,7},{7,1},{8,10},{10,12},{12... | collective-permute-start | bytes 786440 | tf_op jit(solution)/shard_map/ppermute | solution.py:648
  66.3 8.0 %collective-permute-start.33 = (bf16[64,1024]{1,0:T(8,128)(2,1)S(1)}, bf16[64,1024]{1,0:T(8,128)(2,1)S(1)}, u32[]{:S(2)}, u32[]{:S(2)}) collective-permute-start(bf16[64,1024]{1,0:T(8,128)(2,1)S(1)} %collective-permute-done.30), channel_id=1, source_target_pairs={{0,24},{8,16},{16,8},{24,0},{1,25},{9,17},{17,9},{25,1},{2,26},{10... | collective-permute-start | bytes 393224 | tf_op jit(solution)/shard_map/ppermute | solution.py:654
  69.2 13.3 %collective-permute-start.12 = (bf16[128,1024]{1,0:T(8,128)(2,1)S(1)}, bf16[128,1024]{1,0:T(8,128)(2,1)S(1)}, u32[]{:S(2)}, u32[]{:S(2)}) collective-permute-start(bf16[128,1024]{1,0:T(8,128)(2,1)S(1)} %slice_bitcast_fusion.9), channel_id=1, source_target_pairs={{0,4},{2,6},{4,0},{6,2},{1,5},{3,7},{5,1},{7,3},{8,12},{10,14},{12... | collective-permute-start | bytes 786440 | tf_op jit(solution)/shard_map/ppermute | solution.py:648
  73.4 8.9 %collective-permute-start.9 = (bf16[128,1024]{1,0:T(8,128)(2,1)S(1)}, bf16[128,1024]{1,0:T(8,128)(2,1)S(1)}, u32[]{:S(2)}, u32[]{:S(2)}) collective-permute-start(bf16[128,1024]{1,0:T(8,128)(2,1)S(1)} %collective-permute-done.8), channel_id=1, source_target_pairs={{0,8},{8,0},{16,24},{24,16},{1,9},{9,1},{17,25},{25,17},{2,10},{10... | collective-permute-start | bytes 786440 | tf_op jit(solution)/shard_map/ppermute | solution.py:654
  74.3 8.6 %collective-permute-start.10 = (bf16[128,1024]{1,0:T(8,128)(2,1)S(1)}, bf16[128,1024]{1,0:T(8,128)(2,1)S(1)}, u32[]{:S(2)}, u32[]{:S(2)}) collective-permute-start(bf16[128,1024]{1,0:T(8,128)(2,1)S(1)} %collective-permute-done.8), channel_id=1, source_target_pairs={{0,16},{8,24},{16,0},{24,8},{1,17},{9,25},{17,1},{25,9},{2,18},{10... | collective-permute-start | bytes 786440 | tf_op jit(solution)/shard_map/ppermute | solution.py:654
  82.3 8.7 %collective-permute-start.11 = (bf16[128,1024]{1,0:T(8,128)(2,1)S(1)}, bf16[128,1024]{1,0:T(8,128)(2,1)S(1)}, u32[]{:S(2)}, u32[]{:S(2)}) collective-permute-start(bf16[128,1024]{1,0:T(8,128)(2,1)S(1)} %collective-permute-done.8), channel_id=1, source_target_pairs={{0,24},{8,16},{16,8},{24,0},{1,25},{9,17},{17,9},{25,1},{2,26},{10... | collective-permute-start | bytes 786440 | tf_op jit(solution)/shard_map/ppermute | solution.py:654
  82.6 17.2 %collective-permute-start.16 = (bf16[128,1024]{1,0:T(8,128)(2,1)S(1)}, bf16[128,1024]{1,0:T(8,128)(2,1)S(1)}, u32[]{:S(2)}, u32[]{:S(2)}) collective-permute-start(bf16[128,1024]{1,0:T(8,128)(2,1)S(1)} %slice_bitcast_fusion.9), channel_id=1, source_target_pairs={{0,6},{2,0},{4,2},{6,4},{1,7},{3,1},{5,3},{7,5},{8,14},{10,8},{12,... | collective-permute-start | bytes 786440 | tf_op jit(solution)/shard_map/ppermute | solution.py:648
  82.9 18.0 %collective-permute-start.14 = (bf16[128,1024]{1,0:T(8,128)(2,1)S(1)}, bf16[128,1024]{1,0:T(8,128)(2,1)S(1)}, u32[]{:S(2)}, u32[]{:S(2)}) collective-permute-start(bf16[128,1024]{1,0:T(8,128)(2,1)S(1)} %collective-permute-done.12), channel_id=1, source_target_pairs={{0,16},{8,24},{16,0},{24,8},{1,17},{9,25},{17,1},{25,9},{2,18},{10... | collective-permute-start | bytes 786440 | tf_op jit(solution)/shard_map/ppermute | solution.py:654
  97.8 8.4 %collective-permute-start.15 = (bf16[128,1024]{1,0:T(8,128)(2,1)S(1)}, bf16[128,1024]{1,0:T(8,128)(2,1)S(1)}, u32[]{:S(2)}, u32[]{:S(2)}) collective-permute-start(bf16[128,1024]{1,0:T(8,128)(2,1)S(1)} %collective-permute-done.12), channel_id=1, source_target_pairs={{0,24},{8,16},{16,8},{24,0},{1,25},{9,17},{17,9},{25,1},{2,26},{10... | collective-permute-start | bytes 786440 | tf_op jit(solution)/shard_map/ppermute | solution.py:654
  99.8 23.9 %collective-permute-start.20 = (bf16[1024,512]{1,0:T(8,128)(2,1)S(1)}, bf16[1024,512]{1,0:T(8,128)(2,1)S(1)}, u32[]{:S(2)}, u32[]{:S(2)}) collective-permute-start(bf16[1024,512]{1,0:T(8,128)(2,1)S(1)} %copy-done.11), channel_id=1, source_target_pairs={{0,1},{1,0},{2,3},{3,2},{4,5},{5,4},{6,7},{7,6},{8,9},{9,8},{10,11... | collective-permute-start | bytes 3145736 | tf_op jit(solution)/shard_map/ppermute | solution.py:645
  99.9 20.8 %collective-permute-start.19 = (bf16[128,1024]{1,0:T(8,128)(2,1)S(1)}, bf16[128,1024]{1,0:T(8,128)(2,1)S(1)}, u32[]{:S(2)}, u32[]{:S(2)}) collective-permute-start(bf16[128,1024]{1,0:T(8,128)(2,1)S(1)} %collective-permute-done.16), channel_id=1, source_target_pairs={{0,24},{8,16},{16,8},{24,0},{1,25},{9,17},{17,9},{25,1},{2,26},{10... | collective-permute-start | bytes 786440 | tf_op jit(solution)/shard_map/ppermute | solution.py:654
  100.9 19.8 %collective-permute-start.18 = (bf16[128,1024]{1,0:T(8,128)(2,1)S(1)}, bf16[128,1024]{1,0:T(8,128)(2,1)S(1)}, u32[]{:S(2)}, u32[]{:S(2)}) collective-permute-start(bf16[128,1024]{1,0:T(8,128)(2,1)S(1)} %collective-permute-done.16), channel_id=1, source_target_pairs={{0,16},{8,24},{16,0},{24,8},{1,17},{9,25},{17,1},{25,9},{2,18},{10... | collective-permute-start | bytes 786440 | tf_op jit(solution)/shard_map/ppermute | solution.py:654
  106.2 11.3 %collective-permute-start.17 = (bf16[128,1024]{1,0:T(8,128)(2,1)S(1)}, bf16[128,1024]{1,0:T(8,128)(2,1)S(1)}, u32[]{:S(2)}, u32[]{:S(2)}) collective-permute-start(bf16[128,1024]{1,0:T(8,128)(2,1)S(1)} %collective-permute-done.16), channel_id=1, source_target_pairs={{0,8},{8,0},{16,24},{24,16},{1,9},{9,1},{17,25},{25,17},{2,10},{10... | collective-permute-start | bytes 786440 | tf_op jit(solution)/shard_map/ppermute | solution.py:654
  117.5 11.4 %collective-permute-start.1 = (bf16[16,1024]{1,0:T(8,128)(2,1)S(1)}, bf16[16,1024]{1,0:T(8,128)(2,1)S(1)}, u32[]{:S(2)}, u32[]{:S(2)}) collective-permute-start(bf16[16,1024]{1,0:T(8,128)(2,1)S(1)} %pad_maximum_fusion.17), channel_id=1, source_target_pairs={{0,2},{2,4},{4,6},{1,3},{3,5},{5,7},{8,10},{10,12},{12,14},{9,11},... | collective-permute-start | bytes 98312 | tf_op jit(solution)/shard_map/ppermute | solution.py:651
  145.5 65.2 %collective-permute-start.44 = (f32[16,1]{0,1:T(1,128)}, f32[16,1]{0,1:T(1,128)S(1)}, u32[]{:S(2)}, u32[]{:S(2)}) collective-permute-start(f32[16,1]{0,1:T(1,128)} %bitcast.302), channel_id=1, source_target_pairs={{0,4},{2,6},{1,5},{3,7},{8,12},{10,14},{9,13},{11,15},{16,20},{18,... | collective-permute-start | bytes 200 | tf_op jit(solution)/shard_map/ppermute | solution.py:651
  149.7 61.0 %collective-permute-start.42 = (f32[16,1]{0,1:T(1,128)}, f32[16,1]{0,1:T(1,128)S(1)}, u32[]{:S(2)}, u32[]{:S(2)}) collective-permute-start(f32[16,1]{0,1:T(1,128)} %bitcast.303), channel_id=1, source_target_pairs={{0,2},{2,4},{4,6},{1,3},{3,5},{5,7},{8,10},{10,12},{12,14},{9,11},... | collective-permute-start | bytes 200 | tf_op jit(solution)/shard_map/ppermute | solution.py:651
  151.6 47.0 %collective-permute-start.37 = (f32[16,1]{0,1:T(1,128)}, f32[16,1]{0,1:T(1,128)S(1)}, u32[]{:S(2)}, u32[]{:S(2)}) collective-permute-start(f32[16,1]{0,1:T(1,128)} %bitcast.304), channel_id=1, source_target_pairs={{4,0},{6,2},{5,1},{7,3},{12,8},{14,10},{13,9},{15,11},{20,16},{22,... | collective-permute-start | bytes 200 | tf_op jit(solution)/shard_map/ppermute | solution.py:651
  152.9 45.6 %collective-permute-start.35 = (f32[16,1]{0,1:T(1,128)}, f32[16,1]{0,1:T(1,128)S(1)}, u32[]{:S(2)}, u32[]{:S(2)}) collective-permute-start(f32[16,1]{0,1:T(1,128)} %bitcast.305), channel_id=1, source_target_pairs={{2,0},{4,2},{6,4},{3,1},{5,3},{7,5},{10,8},{12,10},{14,12},{11,9},... | collective-permute-start | bytes 200 | tf_op jit(solution)/shard_map/ppermute | solution.py:651
  199.3 14.3 %collective-permute-start.38 = (bf16[1024,128]{1,0:T(8,128)(2,1)S(1)}, bf16[1024,128]{1,0:T(8,128)(2,1)S(1)}, u32[]{:S(2)}, u32[]{:S(2)}) collective-permute-start(bf16[1024,128]{1,0:T(8,128)(2,1)S(1)} %get-tuple-element.245), channel_id=1, source_target_pairs={{0,6},{1,7},{8,14},{9,15},{16,22},{17,23},{24,30},{25,31}} | collective-permute-start | bytes 786440 | tf_op jit(solution)/shard_map/ppermute | solution.py:651
  206.9 13.2 %collective-permute-start.36 = (bf16[1024,128]{1,0:T(8,128)(2,1)S(1)}, bf16[1024,128]{1,0:T(8,128)(2,1)S(1)}, u32[]{:S(2)}, u32[]{:S(2)}) collective-permute-start(bf16[1024,128]{1,0:T(8,128)(2,1)S(1)} %get-tuple-element.246), channel_id=1, source_target_pairs={{0,4},{2,6},{1,5},{3,7},{8,12},{10,14},{9,13},{11,15},{16,20},{18,... | collective-permute-start | bytes 786440 | tf_op jit(solution)/shard_map/ppermute | solution.py:651
  208.2 11.8 %collective-permute-start.34 = (bf16[1024,128]{1,0:T(8,128)(2,1)S(1)}, bf16[1024,128]{1,0:T(8,128)(2,1)S(1)}, u32[]{:S(2)}, u32[]{:S(2)}) collective-permute-start(bf16[1024,128]{1,0:T(8,128)(2,1)S(1)} %get-tuple-element.247), channel_id=1, source_target_pairs={{0,2},{2,4},{4,6},{1,3},{3,5},{5,7},{8,10},{10,12},{12,14},{9,11},... | collective-permute-start | bytes 786440 | tf_op jit(solution)/shard_map/ppermute | solution.py:651
  260.5 31.7 %collective-permute-start.45 = (bf16[1024,128]{1,0:T(8,128)(2,1)S(1)}, bf16[1024,128]{1,0:T(8,128)(2,1)S(1)}, u32[]{:S(2)}, u32[]{:S(2)}) collective-permute-start(bf16[1024,128]{1,0:T(8,128)(2,1)S(1)} %get-tuple-element.239), channel_id=1, source_target_pairs={{6,0},{7,1},{14,8},{15,9},{22,16},{23,17},{30,24},{31,25}} | collective-permute-start | bytes 786440 | tf_op jit(solution)/shard_map/ppermute | solution.py:651
  261.8 32.3 %collective-permute-start.43 = (bf16[1024,128]{1,0:T(8,128)(2,1)S(1)}, bf16[1024,128]{1,0:T(8,128)(2,1)}, u32[]{:S(2)}, u32[]{:S(2)}) collective-permute-start(bf16[1024,128]{1,0:T(8,128)(2,1)S(1)} %get-tuple-element.240), channel_id=1, source_target_pairs={{4,0},{6,2},{5,1},{7,3},{12,8},{14,10},{13,9},{15,11},{20,16},{22,... | collective-permute-start | bytes 786440 | tf_op jit(solution)/shard_map/ppermute | solution.py:651
  263.1 29.2 %collective-permute-start.41 = (bf16[1024,128]{1,0:T(8,128)(2,1)S(1)}, bf16[1024,128]{1,0:T(8,128)(2,1)}, u32[]{:S(2)}, u32[]{:S(2)}) collective-permute-start(bf16[1024,128]{1,0:T(8,128)(2,1)S(1)} %get-tuple-element.241), channel_id=1, source_target_pairs={{2,0},{4,2},{6,4},{3,1},{5,3},{7,5},{10,8},{12,10},{14,12},{11,9},... | collective-permute-start | bytes 786440 | tf_op jit(solution)/shard_map/ppermute | solution.py:651
  271.0 121.1 %collective-permute-start.69 = (bf16[4,64,1024]{2,1,0:T(8,128)(2,1)}, bf16[4,64,1024]{2,1,0:T(8,128)(2,1)S(1)}, u32[]{:S(2)}, u32[]{:S(2)}) collective-permute-start(bf16[4,64,1024]{2,1,0:T(8,128)(2,1)} %get-tuple-element.193), channel_id=1, source_target_pairs={{0,8},{8,0},{16,24},{24,16},{1,9},{9,1},{17,25},{25,17},{2,10},{10... | collective-permute-start | bytes 1572872 | tf_op jit(solution)/shard_map/ppermute | solution.py:654
  272.1 120.9 %collective-permute-start.71 = (bf16[4,64,1024]{2,1,0:T(8,128)(2,1)}, bf16[4,64,1024]{2,1,0:T(8,128)(2,1)S(1)}, u32[]{:S(2)}, u32[]{:S(2)}) collective-permute-start(bf16[4,64,1024]{2,1,0:T(8,128)(2,1)} %get-tuple-element.194), channel_id=1, source_target_pairs={{0,24},{8,16},{16,8},{24,0},{1,25},{9,17},{17,9},{25,1},{2,26},{10... | collective-permute-start | bytes 1572872 | tf_op jit(solution)/shard_map/ppermute | solution.py:654
  292.2 103.4 %collective-permute-start.70 = (bf16[4,64,1024]{2,1,0:T(8,128)(2,1)}, bf16[4,64,1024]{2,1,0:T(8,128)(2,1)S(1)}, u32[]{:S(2)}, u32[]{:S(2)}) collective-permute-start(bf16[4,64,1024]{2,1,0:T(8,128)(2,1)} %get-tuple-element.195), channel_id=1, source_target_pairs={{0,16},{8,24},{16,0},{24,8},{1,17},{9,25},{17,1},{25,9},{2,18},{10... | collective-permute-start | bytes 1572872 | tf_op jit(solution)/shard_map/ppermute | solution.py:654
  387.0 119.4 %collective-permute-start.46 = (bf16[1040,512]{1,0:T(8,128)(2,1)S(1)}, bf16[1040,512]{1,0:T(8,128)(2,1)S(1)}, u32[]{:S(2)}, u32[]{:S(2)}) collective-permute-start(bf16[1040,512]{1,0:T(8,128)(2,1)S(1)} %slice.825), channel_id=1, source_target_pairs={{0,1},{1,0},{2,3},{3,2},{4,5},{5,4},{6,7},{7,6},{8,9},{9,8},{10,11... | collective-permute-start | bytes 3194888 | tf_op jit(solution)/shard_map/ppermute | solution.py:645
  390.7 73.4 %collective-permute-start.49 = (bf16[4,128,1024]{2,1,0:T(8,128)(2,1)S(1)}, bf16[4,128,1024]{2,1,0:T(8,128)(2,1)S(1)}, u32[]{:S(2)}, u32[]{:S(2)}) collective-permute-start(bf16[4,128,1024]{2,1,0:T(8,128)(2,1)S(1)} %get-tuple-element.190), channel_id=1, source_target_pairs={{0,8},{8,0},{16,24},{24,16},{1,9},{9,1},{17,25},{25,17},{2,10},{10... | collective-permute-start | bytes 3145736 | tf_op jit(solution)/shard_map/ppermute | solution.py:654
  392.0 26.2 %collective-permute-start.60 = (bf16[72,512]{1,0:T(8,128)(2,1)S(1)}, bf16[72,512]{1,0:T(8,128)(2,1)S(1)}, u32[]{:S(2)}, u32[]{:S(2)}) collective-permute-start(bf16[72,512]{1,0:T(8,128)(2,1)S(1)} %get-tuple-element.229), channel_id=1, source_target_pairs={{0,8},{8,0},{16,24},{24,16},{1,9},{9,1},{17,25},{25,17},{2,10},{10... | collective-permute-start | bytes 221192 | tf_op jit(solution)/shard_map/ppermute | solution.py:654
  393.0 27.4 %collective-permute-start.62 = (bf16[72,512]{1,0:T(8,128)(2,1)S(1)}, bf16[72,512]{1,0:T(8,128)(2,1)S(1)}, u32[]{:S(2)}, u32[]{:S(2)}) collective-permute-start(bf16[72,512]{1,0:T(8,128)(2,1)S(1)} %get-tuple-element.230), channel_id=1, source_target_pairs={{0,24},{8,16},{16,8},{24,0},{1,25},{9,17},{17,9},{25,1},{2,26},{10... | collective-permute-start | bytes 221192 | tf_op jit(solution)/shard_map/ppermute | solution.py:654
  395.6 24.9 %collective-permute-start.61 = (bf16[72,512]{1,0:T(8,128)(2,1)S(1)}, bf16[72,512]{1,0:T(8,128)(2,1)S(1)}, u32[]{:S(2)}, u32[]{:S(2)}) collective-permute-start(bf16[72,512]{1,0:T(8,128)(2,1)S(1)} %get-tuple-element.231), channel_id=1, source_target_pairs={{0,16},{8,24},{16,0},{24,8},{1,17},{9,25},{17,1},{25,9},{2,18},{10... | collective-permute-start | bytes 221192 | tf_op jit(solution)/shard_map/ppermute | solution.py:654
  420.5 14.0 %collective-permute-start.65 = (bf16[72,512]{1,0:T(8,128)(2,1)S(1)}, bf16[72,512]{1,0:T(8,128)(2,1)S(1)}, u32[]{:S(2)}, u32[]{:S(2)}) collective-permute-start(bf16[72,512]{1,0:T(8,128)(2,1)S(1)} %fusion.53), channel_id=1, source_target_pairs={{0,6},{2,0},{4,2},{6,4},{1,7},{3,1},{5,3},{7,5},{8,14},{10,8},{12,... | collective-permute-start | bytes 221192 | tf_op jit(solution)/shard_map/ppermute | solution.py:648
  432.4 6.9 %collective-permute-start.64 = (bf16[72,512]{1,0:T(8,128)(2,1)S(1)}, bf16[72,512]{1,0:T(8,128)(2,1)S(1)}, u32[]{:S(2)}, u32[]{:S(2)}) collective-permute-start(bf16[72,512]{1,0:T(8,128)(2,1)S(1)} %fusion.53), channel_id=1, source_target_pairs={{0,4},{2,6},{4,0},{6,2},{1,5},{3,7},{5,1},{7,3},{8,12},{10,14},{12... | collective-permute-start | bytes 221192 | tf_op jit(solution)/shard_map/ppermute | solution.py:648
  432.4 6.9 %collective-permute-start.63 = (bf16[72,512]{1,0:T(8,128)(2,1)S(1)}, bf16[72,512]{1,0:T(8,128)(2,1)S(1)}, u32[]{:S(2)}, u32[]{:S(2)}) collective-permute-start(bf16[72,512]{1,0:T(8,128)(2,1)S(1)} %fusion.53), channel_id=1, source_target_pairs={{0,2},{2,4},{4,6},{6,0},{1,3},{3,5},{5,7},{7,1},{8,10},{10,12},{12... | collective-permute-start | bytes 221192 | tf_op jit(solution)/shard_map/ppermute | solution.py:648
  434.5 8.1 %collective-permute-start.72 = (bf16[64,1024]{1,0:T(8,128)(2,1)S(1)}, bf16[64,1024]{1,0:T(8,128)(2,1)S(1)}, u32[]{:S(2)}, u32[]{:S(2)}) collective-permute-start(bf16[64,1024]{1,0:T(8,128)(2,1)S(1)} %get-tuple-element.236), channel_id=1, source_target_pairs={{0,6},{2,0},{4,2},{6,4},{1,7},{3,1},{5,3},{7,5},{8,14},{10,8},{12,... | collective-permute-start | bytes 393224 | tf_op jit(solution)/shard_map/ppermute | solution.py:648
  439.3 10.4 %collective-permute-start.73 = (bf16[64,1024]{1,0:T(8,128)(2,1)S(1)}, bf16[64,1024]{1,0:T(8,128)(2,1)S(1)}, u32[]{:S(2)}, u32[]{:S(2)}) collective-permute-start(bf16[64,1024]{1,0:T(8,128)(2,1)S(1)} %get-tuple-element.238), channel_id=1, source_target_pairs={{0,4},{2,6},{4,0},{6,2},{1,5},{3,7},{5,1},{7,3},{8,12},{10,14},{12... | collective-permute-start | bytes 393224 | tf_op jit(solution)/shard_map/ppermute | solution.py:648
  442.6 8.3 %collective-permute-start.68 = (bf16[72,512]{1,0:T(8,128)(2,1)S(1)}, bf16[72,512]{1,0:T(8,128)(2,1)S(1)}, u32[]{:S(2)}, u32[]{:S(2)}) collective-permute-start(bf16[72,512]{1,0:T(8,128)(2,1)S(1)} %add_convert_fusion), channel_id=1, source_target_pairs={{0,24},{8,16},{16,8},{24,0},{1,25},{9,17},{17,9},{25,1},{2,26},{10... | collective-permute-start | bytes 221192 | tf_op jit(solution)/shard_map/ppermute | solution.py:654
  450.9 7.0 %collective-permute-start.77 = (bf16[64,1024]{1,0:T(8,128)(2,1)S(1)}, bf16[64,1024]{1,0:T(8,128)(2,1)S(1)}, u32[]{:S(2)}, u32[]{:S(2)}) collective-permute-start(bf16[64,1024]{1,0:T(8,128)(2,1)S(1)} %fusion.36), channel_id=1, source_target_pairs={{0,24},{8,16},{16,8},{24,0},{1,25},{9,17},{17,9},{25,1},{2,26},{10... | collective-permute-start | bytes 393224 | tf_op jit(solution)/shard_map/ppermute | solution.py:654
  451.4 7.8 %collective-permute-start.76 = (bf16[64,1024]{1,0:T(8,128)(2,1)S(1)}, bf16[64,1024]{1,0:T(8,128)(2,1)S(1)}, u32[]{:S(2)}, u32[]{:S(2)}) collective-permute-start(bf16[64,1024]{1,0:T(8,128)(2,1)S(1)} %fusion.36), channel_id=1, source_target_pairs={{0,16},{8,24},{16,0},{24,8},{1,17},{9,25},{17,1},{25,9},{2,18},{10... | collective-permute-start | bytes 393224 | tf_op jit(solution)/shard_map/ppermute | solution.py:654
  457.9 23.9 %collective-permute-start.51 = (bf16[4,128,1024]{2,1,0:T(8,128)(2,1)S(1)}, bf16[4,128,1024]{2,1,0:T(8,128)(2,1)S(1)}, u32[]{:S(2)}, u32[]{:S(2)}) collective-permute-start(bf16[4,128,1024]{2,1,0:T(8,128)(2,1)S(1)} %get-tuple-element.191), channel_id=1, source_target_pairs={{0,24},{8,16},{16,8},{24,0},{1,25},{9,17},{17,9},{25,1},{2,26},{10... | collective-permute-start | bytes 3145736 | tf_op jit(solution)/shard_map/ppermute | solution.py:654
  459.2 45.0 %collective-permute-start.50 = (bf16[4,128,1024]{2,1,0:T(8,128)(2,1)S(1)}, bf16[4,128,1024]{2,1,0:T(8,128)(2,1)S(1)}, u32[]{:S(2)}, u32[]{:S(2)}) collective-permute-start(bf16[4,128,1024]{2,1,0:T(8,128)(2,1)S(1)} %get-tuple-element.192), channel_id=1, source_target_pairs={{0,16},{8,24},{16,0},{24,8},{1,17},{9,25},{17,1},{25,9},{2,18},{10... | collective-permute-start | bytes 3145736 | tf_op jit(solution)/shard_map/ppermute | solution.py:654
  462.8 112.2 %collective-permute-start.39 = (bf16[1024,512]{1,0:T(8,128)(2,1)}, bf16[1024,512]{1,0:T(8,128)(2,1)}, u32[]{:S(2)}, u32[]{:S(2)}) collective-permute-start(bf16[1024,512]{1,0:T(8,128)(2,1)} %slice.826), channel_id=1, source_target_pairs={{0,1},{1,0},{2,3},{3,2},{4,5},{5,4},{6,7},{7,6},{8,9},{9,8},{10,11... | collective-permute-start | bytes 3145736 | tf_op jit(solution)/shard_map/ppermute | solution.py:645
  506.8 8.2 %collective-permute-start.47 = (f32[16,512]{1,0:T(8,128)S(1)}, f32[16,512]{1,0:T(8,128)S(1)}, u32[]{:S(2)}, u32[]{:S(2)}) collective-permute-start(f32[16,512]{1,0:T(8,128)S(1)} %slice.580), channel_id=1, source_target_pairs={{2,0},{4,2},{6,4},{3,1},{5,3},{7,5},{10,8},{12,10},{14,12},{11,9},... | collective-permute-start | bytes 98312 | tf_op jit(solution)/shard_map/ppermute | solution.py:651
  509.0 47.8 %collective-permute-start.52 = (bf16[128,1024]{1,0:T(8,128)(2,1)}, bf16[128,1024]{1,0:T(8,128)(2,1)S(1)}, u32[]{:S(2)}, u32[]{:S(2)}) collective-permute-start(bf16[128,1024]{1,0:T(8,128)(2,1)} %get-tuple-element.202), channel_id=1, source_target_pairs={{0,6},{2,0},{4,2},{6,4},{1,7},{3,1},{5,3},{7,5},{8,14},{10,8},{12,... | collective-permute-start | bytes 786440 | tf_op jit(solution)/shard_map/ppermute | solution.py:648
  511.7 45.1 %collective-permute-start.54 = (bf16[128,1024]{1,0:T(8,128)(2,1)}, bf16[128,1024]{1,0:T(8,128)(2,1)}, u32[]{:S(2)}, u32[]{:S(2)}) collective-permute-start(bf16[128,1024]{1,0:T(8,128)(2,1)} %get-tuple-element.203), channel_id=1, source_target_pairs={{0,2},{2,4},{4,6},{6,0},{1,3},{3,5},{5,7},{7,1},{8,10},{10,12},{12... | collective-permute-start | bytes 786440 | tf_op jit(solution)/shard_map/ppermute | solution.py:648
  511.7 45.1 %collective-permute-start.53 = (bf16[128,1024]{1,0:T(8,128)(2,1)}, bf16[128,1024]{1,0:T(8,128)(2,1)}, u32[]{:S(2)}, u32[]{:S(2)}) collective-permute-start(bf16[128,1024]{1,0:T(8,128)(2,1)} %get-tuple-element.204), channel_id=1, source_target_pairs={{0,4},{2,6},{4,0},{6,2},{1,5},{3,7},{5,1},{7,3},{8,12},{10,14},{12... | collective-permute-start | bytes 786440 | tf_op jit(solution)/shard_map/ppermute | solution.py:648
  558.9 10.4 %collective-permute-start.57 = (bf16[128,1024]{1,0:T(8,128)(2,1)S(1)}, bf16[128,1024]{1,0:T(8,128)(2,1)}, u32[]{:S(2)}, u32[]{:S(2)}) collective-permute-start(bf16[128,1024]{1,0:T(8,128)(2,1)S(1)} %fusion.30), channel_id=1, source_target_pairs={{0,24},{8,16},{16,8},{24,0},{1,25},{9,17},{17,9},{25,1},{2,26},{10... | collective-permute-start | bytes 786440 | tf_op jit(solution)/shard_map/ppermute | solution.py:654
  561.8 11.1 %collective-permute-start.56 = (bf16[128,1024]{1,0:T(8,128)(2,1)S(1)}, bf16[128,1024]{1,0:T(8,128)(2,1)}, u32[]{:S(2)}, u32[]{:S(2)}) collective-permute-start(bf16[128,1024]{1,0:T(8,128)(2,1)S(1)} %fusion.30), channel_id=1, source_target_pairs={{0,16},{8,24},{16,0},{24,8},{1,17},{9,25},{17,1},{25,9},{2,18},{10... | collective-permute-start | bytes 786440 | tf_op jit(solution)/shard_map/ppermute | solution.py:654
  562.7 10.6 %collective-permute-start.55 = (bf16[128,1024]{1,0:T(8,128)(2,1)S(1)}, bf16[128,1024]{1,0:T(8,128)(2,1)}, u32[]{:S(2)}, u32[]{:S(2)}) collective-permute-start(bf16[128,1024]{1,0:T(8,128)(2,1)S(1)} %fusion.30), channel_id=1, source_target_pairs={{0,8},{8,0},{16,24},{24,16},{1,9},{9,1},{17,25},{25,17},{2,10},{10... | collective-permute-start | bytes 786440 | tf_op jit(solution)/shard_map/ppermute | solution.py:654
  565.1 9.8 %collective-permute-start.48 = (f32[1024,1]{0,1:T(1,128)S(1)}, f32[1024,1]{0,1:T(1,128)S(1)}, u32[]{:S(2)}, u32[]{:S(2)}) collective-permute-start(f32[1024,1]{0,1:T(1,128)S(1)} %bitcast.283), channel_id=1, source_target_pairs={{0,1},{1,0},{2,3},{3,2},{4,5},{5,4},{6,7},{7,6},{8,9},{9,8},{10,11... | collective-permute-start | bytes 12296 | tf_op jit(solution)/shard_map/ppermute | solution.py:645
  (58 other events, 629.5 us)

commit v2 on v1

v2 whole, which is shorter than its diff:
```python
import functools

import jax
import jax.numpy as jnp
import numpy as np
from jax import lax
from jax.experimental import pallas as pl
from jax.experimental.pallas import tpu as pltpu
from jax.sharding import PartitionSpec as P

D = 1024
HEADS = 32
HEADDIM = 64
STATE = 128
SCAN_BLOCK = 256
LEN = 4096
INNER = 2048
SEQS = 4


EPS = 1e-05
HIGH = lax.Precision.HIGHEST


def conv_causal(values, kernel):
    taps = kernel.shape[0]
    padded = jnp.pad(values, ((taps - 1, 0), (0, 0)))
    total = jnp.zeros_like(values)
    for offset in range(taps):
        total = total + kernel[offset] * padded[offset : offset + values.shape[0]]
    return total


def block_scan(inputs, steps, rates, bmat, cmat, block):
    length, heads, hsize = inputs.shape
    count = length // block
    in_blocks = inputs.reshape(count, block, heads, hsize)
    step_blocks = steps.reshape(count, block, heads)
    b_blocks = bmat.reshape(count, block, bmat.shape[1])
    c_blocks = cmat.reshape(count, block, cmat.shape[1])
    places = jnp.arange(block)
    lower = (places[:, None] >= places[None, :])[:, :, None]

    def advance(state, pieces):
        x_part, dt_part, b_part, c_part = pieces
        cums = jnp.cumsum(dt_part * rates, axis=0)
        spread = cums[:, None, :] - cums[None, :, :]
        decay = jnp.where(lower, jnp.exp(jnp.where(lower, spread, 0.0)), 0.0)
        scores = jnp.dot(c_part, b_part.T, precision=HIGH)
        weights = scores[:, :, None] * decay * dt_part[None, :, :]
        inside = jnp.einsum("ijh,jhp->ihp", weights, x_part, precision=HIGH)
        carried = (
            jnp.einsum("in,hpn->ihp", c_part, state, precision=HIGH) * jnp.exp(cums)[:, :, None]
        )
        tails = jnp.exp(cums[-1][None, :] - cums) * dt_part
        state = jnp.exp(cums[-1])[:, None, None] * state + jnp.einsum(
            "jh,jhp,jn->hpn", tails, x_part, b_part, precision=HIGH
        )
        return (state, inside + carried)

    start_state = jnp.zeros((heads, hsize, bmat.shape[1]), jnp.float32)
    _, result = lax.scan(
        jax.checkpoint(advance), start_state, (in_blocks, step_blocks, b_blocks, c_blocks)
    )
    return result.reshape(length, heads, hsize)


def mixer(zx, bc_raw, dt_raw, kernel_x, kernel_bc, bias_dt, log_rate, skip):
    length, heads, double = zx.shape
    hsize = double // 2
    gate = zx[:, :, :hsize]
    x_raw = zx[:, :, hsize:].reshape(length, heads * hsize)
    xs_conv = jax.nn.silu(conv_causal(x_raw, kernel_x)).reshape(length, heads, hsize)
    bc_conv = jax.nn.silu(conv_causal(bc_raw, kernel_bc))
    half = bc_conv.shape[1] // 2
    steps = jax.nn.softplus(dt_raw + bias_dt)
    rates = -jnp.exp(log_rate)
    result = (
        block_scan(xs_conv, steps, rates, bc_conv[:, :half], bc_conv[:, half:], SCAN_BLOCK)
        + skip[:, None] * xs_conv
    )
    return (result * jax.nn.silu(gate)).reshape(length, heads * hsize)


def per_device(
    hidden,
    lengths,
    cotangent,
    norm_gain,
    in_zx,
    in_bcdt,
    conv_x,
    conv_bc,
    dt_bias,
    a_log,
    d_skip,
    gnorm_gain,
    out_w,
):
    slice_rows, half_width = hidden.shape
    local_heads = in_zx.shape[1]
    head_count = lax.axis_size("head")
    head_index = lax.axis_index("head")
    total_rows = slice_rows * head_count
    seq_local = lengths.shape[0]
    inner_local = local_heads * HEADDIM
    row_ids = head_index * slice_rows + jnp.arange(slice_rows, dtype=jnp.int32)
    owner = (row_ids // LEN)[:, None] == jnp.arange(seq_local, dtype=jnp.int32)[None, :]
    limits = jnp.sum(jnp.where(owner, lengths[None, :], 0), axis=1)
    keeper = (row_ids % LEN < limits).astype(jnp.float32)[:, None]
    source = hidden.astype(jnp.float32)
    squares = lax.psum(jnp.sum(source * source, axis=1), "width")
    scale = lax.rsqrt(squares / D + EPS)[:, None]
    gain_in = norm_gain.astype(jnp.float32)
    normed = (source * scale * gain_in).astype(jnp.bfloat16)
    gathered = lax.all_gather(normed, "head", axis=0, tiled=True)
    w_zx = in_zx.reshape(half_width, local_heads * 2 * HEADDIM)
    zx_part = jnp.dot(gathered, w_zx, preferred_element_type=jnp.float32)
    bcdt_part = jnp.dot(gathered, in_bcdt, preferred_element_type=jnp.float32)
    zx_full, bcdt_full = lax.psum((zx_part, bcdt_part), "width")
    zx_seq = zx_full.reshape(seq_local, LEN, local_heads, 2 * HEADDIM)
    bc_seq = bcdt_full[:, : 2 * STATE].reshape(seq_local, LEN, 2 * STATE)
    dt_seq = lax.dynamic_slice_in_dim(
        bcdt_full, 2 * STATE + head_index * local_heads, local_heads, 1
    ).reshape(seq_local, LEN, local_heads)

    def local_mix(zx_in, bc_in, dt_in, kernel_x, kernel_bc, bias_in, log_in, skip_in):
        per_sequence = jax.vmap(mixer, in_axes=(0, 0, 0, None, None, None, None, None))
        return per_sequence(
            zx_in, bc_in, dt_in, kernel_x, kernel_bc, bias_in, log_in, skip_in
        ).reshape(total_rows, inner_local)

    gated, mix_pull = jax.vjp(
        local_mix,
        zx_seq,
        bc_seq,
        dt_seq,
        conv_x.astype(jnp.float32),
        conv_bc.astype(jnp.float32),
        dt_bias,
        a_log,
        d_skip,
    )
    total_sq = lax.psum(jnp.sum(gated * gated, axis=1), "head")
    scale_out = lax.rsqrt(total_sq / INNER + EPS)[:, None]
    gain_out = gnorm_gain.astype(jnp.float32)
    mixed = (gated * scale_out * gain_out).astype(jnp.bfloat16)
    picked = mixed
    branch = lax.psum_scatter(
        jnp.dot(picked, out_w, preferred_element_type=jnp.float32),
        "head",
        scatter_dimension=0,
        tiled=True,
    )
    out_hidden = (source + keeper * branch).astype(jnp.bfloat16)
    grad_out = cotangent.astype(jnp.float32)
    masked = (grad_out * keeper).astype(jnp.bfloat16)
    piece = lax.all_gather(masked, "head", axis=0, tiled=True)
    picked = mixed
    acc_weight = jnp.einsum("tc,td->cd", picked, piece, preferred_element_type=jnp.float32)
    product = jnp.einsum("td,cd->tc", piece, out_w, preferred_element_type=jnp.float32)
    grad_mixed = lax.psum(product, "width")
    gain_out_grad = jnp.sum(grad_mixed * gated * scale_out, axis=0)
    inner_total = lax.psum(jnp.sum(grad_mixed * gain_out * gated, axis=1), "head")
    cubed = scale_out * scale_out * scale_out
    grad_gated = scale_out * gain_out * grad_mixed - gated * cubed / INNER * inner_total[:, None]
    (
        grad_zx_seq,
        grad_bc_seq,
        grad_dt_seq,
        kernel_x_grad,
        kernel_bc_grad,
        bias_grad,
        rate_grad,
        skip_grad,
    ) = mix_pull(grad_gated)
    grad_zx = grad_zx_seq.reshape(total_rows, local_heads * 2 * HEADDIM).astype(jnp.bfloat16)
    dt_columns = jnp.zeros((total_rows, HEADS), jnp.float32)
    dt_columns = lax.dynamic_update_slice_in_dim(
        dt_columns, grad_dt_seq.reshape(total_rows, local_heads), head_index * local_heads, 1
    )
    grad_bcdt_head = jnp.concatenate(
        [grad_bc_seq.reshape(total_rows, 2 * STATE), dt_columns], axis=1
    )
    weight_zx = jnp.einsum(
        "td,tc->dc", gathered, grad_zx, preferred_element_type=jnp.float32
    ).reshape(half_width, local_heads, 2 * HEADDIM)
    normed_part = jnp.einsum("tc,dc->td", grad_zx, w_zx, preferred_element_type=jnp.float32)
    grad_normed, bcdt_summed = (
        lax.psum_scatter(normed_part, "head", scatter_dimension=0, tiled=True),
        lax.psum_scatter(grad_bcdt_head, "head", scatter_dimension=0, tiled=True),
    )
    bcdt_low = bcdt_summed.astype(jnp.bfloat16)
    grad_normed = grad_normed + jnp.einsum(
        "tk,dk->td", bcdt_low, in_bcdt, preferred_element_type=jnp.float32
    )
    weight_bcdt = jnp.einsum("td,tk->dk", normed, bcdt_low, preferred_element_type=jnp.float32)
    gain_in_grad = jnp.sum(grad_normed * source * scale, axis=0)
    across = lax.psum(jnp.sum(grad_normed * gain_in * source, axis=1), "width")
    scale_cubed = scale * scale * scale
    grad_hidden = (
        grad_out + scale * gain_in * grad_normed - source * scale_cubed / D * across[:, None]
    ).astype(jnp.bfloat16)
    summed_dp = lax.psum(
        (weight_zx, acc_weight, kernel_x_grad, bias_grad, rate_grad, skip_grad, gain_out_grad), "dp"
    )
    summed_all = lax.psum((weight_bcdt, gain_in_grad, kernel_bc_grad), ("dp", "head"))
    return (
        out_hidden,
        grad_hidden,
        summed_all[1],
        summed_dp[0],
        summed_all[0],
        summed_dp[2],
        summed_all[2],
        summed_dp[3],
        summed_dp[4],
        summed_dp[5],
        summed_dp[6],
        summed_dp[1],
    )


BF = jnp.bfloat16
F32 = jnp.float32
Q = 128
HALO = 16
NEG = -1e30
VMEM = 60 * 1024 * 1024


def dot(a, b, prec=None):
    return lax.dot_general(a, b, (((1,), (0,)), ((), ())), precision=prec, preferred_element_type=F32)


def dot_t(a, b, prec=None):
    return lax.dot_general(a, b, (((1,), (1,)), ((), ())), precision=prec, preferred_element_type=F32)


def t_dot(a, b, prec=None):
    return lax.dot_general(a, b, (((0,), (0,)), ((), ())), precision=prec, preferred_element_type=F32)


def split2(v, axis=1):
    hi = v.astype(BF)
    lo = (v - hi.astype(F32)).astype(BF)
    return jnp.concatenate([hi, lo], axis=axis)


def dot_split(v, m):
    hi = v.astype(BF)
    lo = (v - hi.astype(F32)).astype(BF)
    return dot(hi, m) + dot(lo, m)


def split_dot(m, v):
    hi = v.astype(BF)
    lo = (v - hi.astype(F32)).astype(BF)
    return dot(m, hi) + dot(m, lo)


def sigmoid(v):
    return 1.0 / (1.0 + jnp.exp(-v))


def tri(kind):
    row = lax.broadcasted_iota(jnp.int32, (Q, Q), 0)
    col = lax.broadcasted_iota(jnp.int32, (Q, Q), 1)
    return {"ge": row >= col, "le": row <= col, "gt": row > col}[kind]


def entry_kernel(
    hm, ho, hh, gain, wbc, wdt, cbc, bias, rate,
    xn_o, xnh_o, r_o, raw_o, rawh_o, u_o, b_o, c_o, dt_o, sig_o, cl_o, clt_o, tot_o,
    dt2_o, e12_o, tl2_o, dttl2_o, ec2_o, edt2_o, buf,
):
    rows = hm.shape[0]
    state = b_o.shape[1]
    blocks = rows // Q
    lower = tri("ge").astype(F32)

    def norm(left, right):
        h = jnp.concatenate([left, right], axis=1).astype(F32)
        r = lax.rsqrt(jnp.mean(h * h, axis=1, keepdims=True) + EPS)
        return (h * r * gain[...]).astype(BF), r

    half = hm.shape[1]
    xnh, _ = norm(hh[:, :half], hh[:, half:])
    xnh_o[...] = xnh
    buf[0:HALO, :] = dot_t(xnh, wbc[...])
    rawh_o[...] = buf[0:HALO, :]

    def first(i, carry):
        here = pl.ds(pl.multiple_of(i * Q, Q), Q)
        xn, r = norm(hm[here, :], ho[here, :])
        xn_o[here, :] = xn
        r_o[here, :] = r
        raw = dot_t(xn, wbc[...])
        raw_o[here, :] = raw
        buf[pl.ds(pl.multiple_of(HALO + i * Q, HALO), Q), :] = raw
        steps = dot_t(xn, wdt[...]) + bias[...]
        dt = jax.nn.softplus(steps)
        dt_o[here, :] = dt
        sig_o[here, :] = sigmoid(steps)
        da = dt * rate[...]
        cl_o[here, :] = dot(lower, da, HIGH)
        clt_o[:, here] = lax.dot_general(
            da, lower, (((0,), (1,)), ((), ())), precision=HIGH, preferred_element_type=F32
        )
        return carry

    lax.fori_loop(0, blocks, first, 0, unroll=2)

    def second(i, carry):
        here = pl.ds(pl.multiple_of(i * Q, Q), Q)
        win = buf[pl.ds(pl.multiple_of(i * Q, Q), Q + HALO), :]
        u = jnp.zeros((Q, win.shape[1]), F32)
        for k in range(4):
            u = u + cbc[k : k + 1, :] * win[HALO - 3 + k : HALO - 3 + k + Q, :]
        u_o[here, :] = u
        v = u * sigmoid(u)
        b_o[here, :] = v[:, :state].astype(BF)
        c_o[here, :] = v[:, state:].astype(BF)
        return carry

    lax.fori_loop(0, blocks, second, 0, unroll=2)
    tots = [cl_o[i * Q + Q - 1 : i * Q + Q, :] for i in range(blocks)]
    ctot = functools.reduce(lambda x, y: x + y, tots)
    heads = clt_o.shape[0]
    column = functools.reduce(
        lambda x, y: x + y, [clt_o[:, i * Q + Q - 1 : i * Q + Q] for i in range(blocks)]
    )
    hi = column.astype(BF)
    mid = (column - hi.astype(F32)).astype(BF)
    low = (column - hi.astype(F32) - mid.astype(F32)).astype(BF)
    lane = lax.broadcasted_iota(jnp.int32, (heads, tot_o.shape[1]), 1)
    tot_o[...] = jnp.where(
        lane == 0,
        hi.astype(F32),
        jnp.where(lane == 1, mid.astype(F32), jnp.where(lane == 2, low.astype(F32), 0.0)),
    ).astype(BF)
    off = jnp.zeros_like(ctot)
    for i in range(blocks):
        here = slice(i * Q, i * Q + Q)
        cl = cl_o[here, :]
        dt = dt_o[here, :]
        tail = jnp.exp(tots[i] - cl)
        dt2_o[here, :] = split2(dt)
        e12_o[here, :] = split2(jnp.exp(cl))
        tl2_o[here, :] = split2(tail)
        dttl2_o[here, :] = split2(dt * tail)
        ec2_o[here, :] = split2(jnp.exp(cl + off))
        edt2_o[here, :] = split2(dt * jnp.exp(ctot - cl - off))
        off = off + tots[i]


def decay(cl, clt, h, mask):
    return jnp.exp(jnp.where(mask, cl[:, h : h + 1] - clt[h : h + 1, :], NEG))


def lane_masks():
    lane = lax.broadcasted_iota(jnp.int32, (1, Q), 1)
    low = (lane < HEADDIM).astype(F32)
    return low.astype(BF), (1.0 - low).astype(BF)


def project_kernel(s, per, *refs):
    xn, xnh, pieces, cw, dt2, edt2, ex, b, rest = take(refs, 0, 0, per, 0, 0, 0, 0, 0)
    wz_o, wx_o, z_o, xr_o, xrh_o, u_o, xs_o, xdt_o, s_o, buf, acc = rest
    rows = z_o.shape[0]
    gc = per * HEADDIM
    cols = slice(s * gc, s * gc + gc)
    wx = jnp.concatenate([v[HEADDIM:, :] for v in pieces], axis=0)
    wz = jnp.concatenate([v[:HEADDIM, :] for v in pieces], axis=0)

    @pl.when(pl.program_id(0) == 0)
    def _():
        wz_o[...] = wz
        wx_o[...] = wx
        xh = dot_t(xnh[...], wx)
        buf[0:HALO, :] = xh
        xrh_o[...] = xh
        acc[...] = jnp.zeros_like(acc)

    @pl.when(pl.program_id(0) > 0)
    def _():
        buf[0:HALO, :] = buf[rows : rows + HALO, :]

    buf[HALO:, :] = dot_t(xn[...], wx)
    z_o[...] = dot_t(xn[...], wz)
    for i in range(rows // Q):
        here = slice(i * Q, i * Q + Q)
        win = buf[i * Q : i * Q + Q + HALO, :]
        u = jnp.zeros((Q, gc), F32)
        for k in range(4):
            u = u + cw[k : k + 1, cols] * win[HALO - 3 + k : HALO - 3 + k + Q, :]
        xr_o[here, :] = win[HALO:, :]
        u_o[here, :] = u
        xs = u * sigmoid(u)
        xs_o[here, :] = xs
        xdt_o[here, :] = (xs * dot(dt2[here, :], ex[:, cols])).astype(BF)
        acc[...] += t_dot((xs * dot(edt2[here, :], ex[:, cols])).astype(BF), b[here, :])

    @pl.when(pl.program_id(0) == pl.num_programs(0) - 1)
    def _():
        s_o[...] = acc[...].astype(BF)


def inside_kernel(s, per, xdt, b, c, cl, clt, y_o):
    mask = tri("ge")
    low, high = lane_masks()
    for i in range(xdt.shape[0] // Q):
        rows = slice(i * Q, i * Q + Q)
        g = dot_t(c[rows, :], b[rows, :])
        clv, cltv = cl[rows, :], clt[:, rows]
        for p in range(xdt.shape[1] // Q):
            here = slice(p * Q, p * Q + Q)
            h = s * per + 2 * p
            ws = [(g * decay(clv, cltv, j, mask)).astype(BF) for j in (h, h + 1)]
            x = xdt[rows, here]
            y_o[rows, here] = dot(
                jnp.concatenate(ws, axis=1), jnp.concatenate([x * low, x * high], axis=0)
            )


def head_scale(clt, first, per, state):
    return jnp.concatenate(
        [
            jnp.broadcast_to(jnp.exp(clt[h : h + 1, Q - 1 : Q]), (HEADDIM, state))
            for h in range(first, first + per)
        ],
        axis=0,
    )


def from_messages(messages, sign, groups, per, state, store):
    nz = len(messages) + 1
    gc = per * HEADDIM
    top = nz * gc
    totals = [
        sum(m[top:, i : i + 1].astype(F32) for i in range(3)) for m in messages
    ]
    for at, j in enumerate(groups):
        total = jnp.zeros((gc, state), F32)
        faded = jnp.zeros((per, 1), F32)
        for k in range(1, nz):
            there = (j - sign * k) % nz
            scale = jnp.exp(faded)
            scale = jnp.concatenate(
                [jnp.broadcast_to(scale[h : h + 1, :], (HEADDIM, state)) for h in range(per)],
                axis=0,
            )
            total = total + scale * messages[k - 1][there * gc : there * gc + gc, :].astype(F32)
            faded = faded + totals[k - 1][there * per : there * per + per, :]
        store[at * gc : at * gc + gc, :] = total


def carry_kernel(groups, per, *refs):
    n = len(groups)
    y_in, xs, z, dyn, b, c, clt, e12, dttl2, messages, dsk, gain, ex, rest = take(
        refs, n, n, n, 0, 0, 0, 0, 0, 0, n - 1, 0, 0, 0
    )
    ys_o, st_o, rest = take(rest, n, n)
    gg_o, sum_o, s = rest
    gc = per * HEADDIM

    @pl.when(pl.program_id(0) == 0)
    def _():
        from_messages(messages, 1, groups, per, s.shape[1], s)

    square = jnp.zeros((Q, gc), F32)
    inner = jnp.zeros((Q, gc), F32)
    for j in groups:
        here = slice(j * gc, j * gc + gc)
        sv = s[here, :]
        sb = sv.astype(BF)
        st_o[j][0] = sb
        x = xs[j][...]
        e1 = dot(e12[...], ex[:, here])
        y = y_in[j][...] + e1 * dot_t(c[...], sb) + dsk[:, here] * x
        ys_o[j][...] = y
        xt = (x * dot(dttl2[...], ex[:, here])).astype(BF)
        s[here, :] = head_scale(clt, j * per, per, sv.shape[1]) * sv + t_dot(xt, b[...])
        zz = z[j][...]
        gz = y * (zz * sigmoid(zz))
        gg = gz * gain[:, here]
        gg_o[:, here] = gg.astype(BF)
        square = square + gz * gz
        inner = inner + gg * dyn[:, here]
    lane = lax.broadcasted_iota(jnp.int32, (Q, 2), 1)
    sum_o[...] = jnp.where(
        lane == 0,
        jnp.sum(square, axis=1, keepdims=True),
        jnp.sum(inner, axis=1, keepdims=True),
    )


def gate_kernel(groups, per, *refs):
    n = len(groups)
    ys, z, xs, dyn, sums, sums2, gain, ec2, ex, c, rest = take(refs, n, n, n, *[0] * 7)
    hidden, branch, branch2, limit, rest = take(rest, 0, 0, 0, 0)
    dys_o, rest = take(rest, n)
    dz_o, yn_o, ds_o, gn_o, sk_o, out_o, acc = rest
    gc = per * HEADDIM

    @pl.when(pl.program_id(0) == 0)
    def _():
        acc[...] = jnp.zeros_like(acc)
        gn_o[...] = jnp.zeros_like(gn_o)
        sk_o[...] = jnp.zeros_like(sk_o)

    count = n * gc * 2
    both = sums[...] + sums2[...]
    r2 = lax.rsqrt(both[:, 0:1] / count + EPS)
    pull = both[:, 1:2] * (r2 * r2 * r2) / count
    row = lax.broadcasted_iota(jnp.int32, (Q, 1), 0) + pl.program_id(0) * Q
    keep = jnp.where(row < limit[0, 0], r2, 0.0)
    out_o[...] = (
        hidden[...].astype(F32) + keep * (branch[...] + branch2[...].astype(F32))
    ).astype(BF)
    for j in groups:
        here = slice(j * gc, j * gc + gc)
        gn = gain[:, here]
        zz = z[j][...]
        sz = sigmoid(zz)
        silu = zz * sz
        y = ys[j][...]
        gz = y * silu
        dy_n = dyn[:, here]
        gr = gz * r2
        yn_o[:, here] = (gr * gn).astype(BF)
        gn_o[:, here] += jnp.sum(dy_n * gr, axis=0, keepdims=True)
        dgz = r2 * gn * dy_n - gz * pull
        dys = dgz * silu
        dys_o[j][...] = dys
        dz_o[:, here] = (dgz * y * (sz + silu * (1.0 - sz))).astype(BF)
        sk_o[:, here] += jnp.sum(dys * xs[j][...], axis=0, keepdims=True)
        acc[here, :] += t_dot((dys * dot(ec2[...], ex[:, here])).astype(BF), c[...])

    @pl.when(pl.program_id(0) == pl.num_programs(0) - 1)
    def _():
        ds_o[...] = acc[...].astype(BF)


def inside_back_kernel(groups, per, *refs):
    n = len(groups)
    xdt, dys, b, c, cl, clt, rest = take(refs, n, n, 0, 0, 0, 0)
    dx_o, rest = take(rest, n)
    db_o, dc_o, da_o, kt = rest
    mask = tri("ge")
    low, high = lane_masks()
    g = dot_t(c[...], b[...])
    clv, cltv = cl[...], clt[...]
    heads = clt.shape[0]
    lane = lax.broadcasted_iota(jnp.int32, (Q, heads), 1)
    dg = jnp.zeros((Q, Q), F32)
    rsum = jnp.zeros((Q, heads), F32)
    for s in groups:
        for p in range(per // 2):
            here = slice(p * Q, p * Q + Q)
            x = xdt[s][:, here]
            dy = dys[s][:, here].astype(BF)
            pp = dot_t(dy, jnp.concatenate([x * low, x * high], axis=0))
            ws = []
            for j in range(2):
                h = s * per + 2 * p + j
                ell = decay(clv, cltv, h, mask)
                ws.append((g * ell).astype(BF))
                pe = pp[:, j * Q : j * Q + Q] * ell
                dg = dg + pe
                m = pe * g
                rsum = jnp.where(lane == h, jnp.sum(m, axis=1, keepdims=True), rsum)
                kt[h : h + 1, :] = jnp.sum(m, axis=0, keepdims=True)
            dx_o[s][:, here] = t_dot(
                jnp.concatenate(ws, axis=0), jnp.concatenate([dy * low, dy * high], axis=0)
            )
    dgb = dg.astype(BF)
    dc_o[...] = dot(dgb, b[...])
    db_o[...] = t_dot(dgb, c[...])
    upper = tri("le").astype(F32)
    da_o[...] = dot(upper, rsum, HIGH) - dot_t(upper, kt[...], HIGH)


def conv_back(d, nxt, taps, raw, rawh, grad_o, out_o, outh_o, last):
    win = jnp.concatenate([d, nxt[...]], axis=0)
    back = jnp.zeros_like(d)
    sums = []
    for k in range(4):
        part = win[3 - k : 3 - k + Q, :]
        back = back + taps[k : k + 1, :] * part
        sums.append(jnp.sum(raw * part, axis=0, keepdims=True))
    grad_o[...] += jnp.concatenate(sums, axis=0)
    out_o[...] = back.astype(BF)
    nxt[...] = d[0:8, :]

    @pl.when(last)
    def _():
        win_h = jnp.concatenate([jnp.zeros((HALO, d.shape[1]), F32), d[0:8, :]], axis=0)
        back_h = jnp.zeros((HALO, d.shape[1]), F32)
        sums_h = []
        for k in range(4):
            part = win_h[3 - k : 3 - k + HALO, :]
            back_h = back_h + taps[k : k + 1, :] * part
            sums_h.append(jnp.sum(rawh[...] * part, axis=0, keepdims=True))
        grad_o[...] += jnp.concatenate(sums_h, axis=0)
        outh_o[...] = back_h.astype(BF)


def back_kernel(groups, per, final, *refs):
    n = len(groups)
    dxi, dys, u, xr, xrh, st, rest = take(refs, n, n, n, n, n, n)
    (b, c, dbi, dci, dai, dti, dt, sig, clt, dt2, e12, tl2), rest = rest[:12], rest[12:]
    (ubc, braw, brawh, cw, cbc, rate, dsk, ex, er), rest = rest[:9], rest[9:]
    nz = dt.shape[1] // per
    messages, _, dx_o, dxh_o, gcx_o, rest = take(rest, nz - 1, 0, n, n, n)
    db_o, dc_o, dt_o, ga_o, gbias_o, bc_o, bch_o, gcb_o, ds, vs = rest[:10]
    du_next, rest = take(rest[10:], n)
    (db_next,) = rest
    step = pl.program_id(0)
    blocks = pl.num_programs(0)
    heads = dt.shape[1]
    state = b.shape[1]
    gc = per * HEADDIM

    @pl.when(step == 0)
    def _():
        from_messages(messages, -1, groups, per, state, ds)
        for i in range(n):
            du_next[i][...] = jnp.zeros_like(du_next[i])
            gcx_o[i][...] = jnp.zeros_like(gcx_o[i])
        vs[...] = jnp.zeros_like(vs)
        db_next[...] = jnp.zeros_like(db_next)
        gcb_o[...] = jnp.zeros_like(gcb_o)
        ga_o[...] = jnp.zeros_like(ga_o)
        gbias_o[...] = jnp.zeros_like(gbias_o)

    last = step == blocks - 1
    rsum = jnp.zeros((Q, heads), F32)
    gsum = jnp.zeros((Q, heads), F32)
    ddt = jnp.zeros((Q, heads), F32)
    dbs = dbi[...]
    dcs = dci[...]
    for i, s in enumerate(groups):
        here = slice(s * gc, s * gc + gc)
        mine = slice(i * gc, i * gc + gc)
        ehere = er[here, :]
        sb = st[i][0]
        dsv = ds[mine, :]
        dsb = dsv.astype(BF)
        dy = dys[i][...]
        dye = dy * dot(e12[...], ex[:, here])
        dyb = dye.astype(BF)
        rsum = rsum + dot((dye * dot_t(c[...], sb)).astype(BF), ehere)
        dcs = dcs + dot(dyb, sb)
        bds = dot_t(b[...], dsb)
        tail = dot(tl2[...], ex[:, here])
        dtx = dot(dt2[...], ex[:, here])
        uu = u[i][...]
        su = sigmoid(uu)
        xs = uu * su
        xt = xs * dtx * tail
        gsum = gsum + dot((xt * bds).astype(BF), ehere)
        dbs = dbs + dot(xt.astype(BF), dsb)
        dxdt = dxi[i][...] + tail * bds
        ddt = ddt + dot((dxdt * xs).astype(BF), ehere)
        eds = head_scale(clt, s * per, per, state) * dsv
        ev = eds * sb.astype(F32)
        for j in range(per):
            h = s * per + j
            vs[h : h + 1, :] = jnp.sum(
                ev[j * HEADDIM : (j + 1) * HEADDIM, :], axis=0, keepdims=True
            )
        ds[mine, :] = eds + t_dot(dyb, c[...])
        du = (dxdt * dtx + dsk[:, here] * dy) * (su + xs * (1.0 - su))
        conv_back(
            du, du_next[i], cw.at[:, here], xr[i][...], xrh[i], gcx_o[i], dx_o[i], dxh_o[i], last
        )
    col = lax.broadcasted_iota(jnp.int32, (1, heads), 1)
    mine = functools.reduce(
        jnp.logical_or, [(col >= s * per) & (col < s * per + per) for s in groups]
    )
    vrow = dot_t(jnp.ones((8, state), F32), vs[...], HIGH)
    da = (
        dai[...]
        + split_dot(tri("le").astype(BF), rsum)
        + split_dot(tri("gt").astype(BF), gsum)
        + vrow[0:1, :]
    )
    da = jnp.where(mine, da, 0.0)
    draw = (rate[...] * da + ddt) * sig[...]
    dt_o[...] = (dti[...] + draw).astype(dt_o.dtype)
    ga_o[...] += jnp.sum(da * dt[...], axis=0, keepdims=True)
    gbias_o[...] += jnp.sum(draw, axis=0, keepdims=True)
    db_o[...] = dbs
    dc_o[...] = dcs
    if final:
        d = jnp.concatenate([dbs, dcs], axis=1)
        v = ubc[...]
        sv = sigmoid(v)
        conv_back(
            d * (sv + v * sv * (1.0 - sv)), db_next, cbc, braw[...], brawh, gcb_o, bc_o, bch_o, last
        )


def sum_products_kernel(n, *refs):
    a, w, rest = take(refs, n, n)
    left_o, right_o = rest
    total = dot(a[0][...], w[0][...])
    for i in range(1, n):
        total = total + dot(a[i][...], w[i][...])
    half = left_o.shape[1]
    left_o[...] = total[:, :half]
    right_o[...] = total[:, half:].astype(BF)


def pull_kernel(per, nz, *refs):
    cot, cot2, limit, own, others, rest = take(refs, 0, 0, 0, per, per)
    w_o, mask_o, dyn_o = rest
    rows = cot.shape[0]
    half = cot.shape[1]

    @pl.when(pl.program_id(0) == 0)
    def _():
        for m in range(per):
            w_o[m * HEADDIM : (m + 1) * HEADDIM, :] = own[m][...]
            for s in range(1, nz):
                at = (s * per + m) * HEADDIM
                w_o[at : at + HEADDIM, :] = others[m][(s - 1) * HEADDIM : s * HEADDIM, :]

    row = lax.broadcasted_iota(jnp.int32, (rows, 1), 0) + pl.program_id(0) * rows
    keep = row < limit[0, 0]
    for i, v in enumerate((cot, cot2)):
        mask_o[:, i * half : i * half + half] = jnp.where(keep, v[...].astype(F32), 0.0).astype(BF)
    dyn_o[...] = dot_t(mask_o[...], w_o[...])


def early_grad_kernel(per, yn, masked, dz, xn, *outs):
    g_out = t_dot(yn[...], masked[...]).astype(BF)
    g_z = t_dot(dz[...], xn[...]).astype(BF)
    for m in range(per):
        here = slice(m * HEADDIM, (m + 1) * HEADDIM)
        outs[m][0, :HEADDIM, :] = g_out[here, :]
        outs[m][0, HEADDIM:, :] = g_z[here, :]


def late_grad_kernel(n, per, final, *refs):
    dx, dxh, xn, xnh, rest = take(refs, n, n, 0, 0)
    if final:
        dbc, dbch, ddt, spread, rest = take(rest, 0, 0, 0, 0)
        outs, rest = take(rest, per)
        gbc, gdt = rest
        bc_rows = gbc.shape[0] // per
        dt_rows = gdt.shape[0] // per
        gbc[...] = t_dot(dbc[...], xn[...]) + t_dot(dbch[...], xnh[...])
        gdt[...] = split_dot(spread[...], t_dot(ddt[...], xn[...]))
    else:
        outs, rest = take(rest, per)
    for i in range(n):
        g = (t_dot(dx[i][...], xn[...]) + t_dot(dxh[i][...], xnh[...])).astype(BF)
        for m in range(per):
            outs[m][i * HEADDIM : (i + 1) * HEADDIM, :] = g[m * HEADDIM : (m + 1) * HEADDIM, :]
    if final:
        me = lax.axis_index("dp")
        for m in range(per):
            at = jnp.bitwise_xor(me, m)
            v = gbc[pl.ds(pl.multiple_of(at * bc_rows, bc_rows), bc_rows), :]
            w = gdt[pl.ds(pl.multiple_of(at * dt_rows, dt_rows), dt_rows), :]
            w = jnp.concatenate([w, jnp.zeros((HALO - dt_rows, w.shape[1]), F32)], axis=0)
            outs[m][n * HEADDIM : n * HEADDIM + bc_rows, :] = v.astype(BF)
            outs[m][n * HEADDIM + bc_rows :, :] = w.astype(BF)


def shape(dims, dtype=F32):
    return jax.ShapeDtypeStruct(dims, dtype)


def whole(array):
    rank = len(array.shape)
    return pl.BlockSpec(array.shape, lambda *_: (0,) * rank)


def params():
    return pltpu.CompilerParams(vmem_limit_bytes=VMEM)


def cost(us):
    return pl.CostEstimate(flops=int(us * 1.0e8), bytes_accessed=int(us * 1.0e3), transcendentals=0)


def take(refs, *counts):
    out, at = [], 0
    for n in counts:
        out.append(refs[at] if n == 0 else refs[at : at + n])
        at += max(n, 1)
    return out + [refs[at:]]


def sequence_device(
    hidden, lengths, cotangent, norm_gain, in_zx, in_bcdt, conv_x, conv_bc,
    dt_bias, a_log, d_skip, gnorm_gain, out_w,
):
    rows, half = hidden.shape
    own_heads = in_zx.shape[1]
    nz = lax.axis_size("head")
    ndp = lax.axis_size("dp")
    zi = lax.axis_index("head")
    di = lax.axis_index("dp")
    wi = lax.axis_index("width")
    per = ndp
    heads = nz * per
    channels = heads * HEADDIM
    model = 2 * half
    blocks = rows // Q

    def swap(v):
        return lax.ppermute(v, "width", [(0, 1), (1, 0)])

    def turn(v, s):
        return lax.ppermute(v, "head", [(i, (i + s) % nz) for i in range(nz)])

    def shift(v, s):
        return lax.ppermute(v, "head", [(i, i + s) for i in range(nz) if 0 <= i + s < nz])

    def cross(v, m):
        return lax.ppermute(v, "dp", [(i, i ^ m) for i in range(ndp)])

    def pick(v, index):
        return lax.dynamic_index_in_dim(v, index, 0, keepdims=False)

    gc = per * HEADDIM
    groups = tuple(range(nz))

    zx_t = jnp.transpose(in_zx, (1, 2, 0))
    out_h = out_w.reshape(own_heads, HEADDIM, half)

    def slot_of(v, w, m):
        return pick(v, per * w + (di ^ m))

    def join(v, m):
        return jnp.concatenate([slot_of(v, wi, m), swap(slot_of(v, 1 - wi, m))], axis=-1)

    def join_rest(v):
        mine = jnp.stack([slot_of(v, wi, m) for m in range(1, per)])
        other = jnp.stack([slot_of(v, 1 - wi, m) for m in range(1, per)])
        both = jnp.concatenate([mine, swap(other)], axis=-1)
        return [both[m] for m in range(per - 1)]

    def after_that(v, w):
        return v + (w[(0,) * w.ndim] * 0).astype(v.dtype)

    own_first = join(zx_t, 0)
    zx_rest = zx_t
    along = [turn(own_first, s) for s in range(1, nz)]
    hidden_o = swap(hidden)
    pieces = [[own_first] + join_rest(zx_rest)]
    for got in along:
        pieces.append([got] + [cross(got, m) for m in range(1, per)])
    bcdt_t = jnp.concatenate([jnp.transpose(in_bcdt), norm_gain[None]], axis=0)
    bcdt_t = jnp.concatenate([bcdt_t, swap(bcdt_t)], axis=1)
    gain_in = bcdt_t[2 * STATE + HEADS :].astype(F32)
    wbc = bcdt_t[: 2 * STATE]
    slot = jnp.arange(heads)
    slot_head = ((zi - slot // per) % nz) * own_heads + wi * per + ((slot % per) ^ di)
    pick_heads = (slot_head[:, None] == jnp.arange(HEADS)[None, :]).astype(F32)
    wdt = jnp.dot(
        pick_heads.astype(BF), bcdt_t[2 * STATE : 2 * STATE + HEADS], preferred_element_type=F32
    ).astype(BF)

    table = jnp.concatenate(
        [
            dt_bias[:, None],
            a_log[:, None],
            d_skip[:, None],
            jnp.transpose(conv_x.astype(F32).reshape(4, own_heads, HEADDIM), (1, 0, 2)).reshape(
                own_heads, 4 * HEADDIM
            ),
            gnorm_gain.astype(F32).reshape(own_heads, HEADDIM),
        ],
        axis=1,
    )
    table = jnp.stack([slot_of(table, wi, m) for m in range(per)])
    table = jnp.concatenate([table] + [turn(table, s) for s in range(1, nz)], axis=0)
    bias = table[:, 0][None]
    rate = -jnp.exp(table[:, 1])[None]
    skip = jnp.repeat(table[:, 2], HEADDIM)[None]
    taps = jnp.transpose(
        table[:, 3 : 3 + 4 * HEADDIM].reshape(heads, 4, HEADDIM), (1, 0, 2)
    ).reshape(4, channels)
    gain_out = table[:, 3 + 4 * HEADDIM :].reshape(1, channels)
    taps_bc = conv_bc.astype(F32)

    onehot = np.kron(np.eye(heads), np.ones((1, HEADDIM)))
    ex = jnp.asarray(np.concatenate([onehot, onehot], axis=0), BF)
    er = jnp.asarray(onehot.T, BF)

    edge = jnp.concatenate([hidden[rows - HALO :], hidden_o[rows - HALO :]], axis=1)
    edge = shift(edge, 1)
    ext_rows = rows + HALO
    narrow = shape((rows, 2 * heads), BF)
    (
        xn, xnh, r, braw, brawh, ubc, bs, cs, dt, sig, cl, clt, totals,
        dt2, e12, tl2, dttl2, ec2, edt2,
    ) = pl.pallas_call(
        entry_kernel,
        out_shape=[
            shape((rows, model), BF), shape((HALO, model), BF), shape((rows, 1)),
            shape((rows, 2 * STATE)),
            shape((HALO, 2 * STATE)), shape((rows, 2 * STATE)), shape((rows, STATE), BF),
            shape((rows, STATE), BF), shape((rows, heads)), shape((rows, heads)),
            shape((rows, heads)), shape((heads, rows)), shape((heads, STATE), BF),
            narrow, narrow, narrow, narrow, narrow, narrow,
        ],
        scratch_shapes=[pltpu.VMEM((ext_rows, 2 * STATE), F32)],
        compiler_params=params(),
        cost_estimate=cost(12),
        name="entry",
    )(hidden, hidden_o, edge, gain_in, wbc, wdt, taps_bc, bias, rate)

    def send_states(local, sign):
        message = jnp.concatenate([*local, totals], axis=0)
        return [shift(message, sign * k) for k in range(1, nz)]

    cut = rows // 2 if rows // 2 % Q == 0 else rows
    part = shape((rows, gc))
    full = shape((rows, channels))
    step = lambda i: (i, 0)
    fix = lambda i: (0, 0)
    gspec = pl.BlockSpec((cut, gc), step)
    wz, wx, z, xr, xrh, u, xs, xdt, s_local, y_in = ([] for _ in range(10))
    for s in groups:
        out = pl.pallas_call(
            functools.partial(project_kernel, s, per),
            grid=(rows // cut,),
            in_specs=[
                pl.BlockSpec((cut, model), step),
                pl.BlockSpec((HALO, model), fix),
                *[whole(v) for v in pieces[s]], whole(taps), pl.BlockSpec((cut, 2 * heads), step),
                pl.BlockSpec((cut, 2 * heads), step), whole(ex), pl.BlockSpec((cut, STATE), step),
            ],
            out_specs=[
                pl.BlockSpec((gc, model), fix), pl.BlockSpec((gc, model), fix), gspec, gspec,
                pl.BlockSpec((HALO, gc), fix), gspec, gspec, gspec, pl.BlockSpec((gc, STATE), fix),
            ],
            out_shape=[
                shape((gc, model), BF), shape((gc, model), BF), part, part, shape((HALO, gc)),
                part, part, shape((rows, gc), BF), shape((gc, STATE), BF),
            ],
            scratch_shapes=[pltpu.VMEM((cut + HALO, gc), F32), pltpu.VMEM((gc, STATE), F32)],
            compiler_params=params(),
            cost_estimate=cost(5),
            name="project",
        )(xn, xnh, *pieces[s], taps, dt2, edt2, ex, bs)
        for keep, v in zip((wz, wx, z, xr, xrh, u, xs, xdt, s_local), out):
            keep.append(v)
        y_in.append(
            pl.pallas_call(
                functools.partial(inside_kernel, s, per),
                grid=(rows // cut,),
                in_specs=[
                    gspec, pl.BlockSpec((cut, STATE), step), pl.BlockSpec((cut, STATE), step),
                    pl.BlockSpec((cut, heads), step), pl.BlockSpec((heads, cut), lambda i: (0, i)),
                ],
                out_specs=gspec,
                out_shape=part,
                compiler_params=params(),
                cost_estimate=cost(3),
                name="inside",
            )(xdt[s], bs, cs, cl, clt)
        )
    messages = send_states(s_local, 1)

    out_first = after_that(join(out_h, 0), pieces[-1][-1])
    out_own = [out_first] + join_rest(out_h)
    out_along = jnp.concatenate([turn(out_first, s) for s in range(1, nz)], axis=0)
    out_cross = [out_along] + [cross(out_along, m) for m in range(1, per)]
    cot_o = swap(cotangent)
    limit = (lengths[0] - zi * rows).reshape(1, 1)

    wide = pl.BlockSpec((Q, channels), step)
    gwide = pl.BlockSpec((Q, gc), step)
    bspec = pl.BlockSpec((Q, STATE), step)
    hspec = pl.BlockSpec((Q, heads), step)
    h2spec = pl.BlockSpec((Q, 2 * heads), step)
    tspec = pl.BlockSpec((heads, Q), lambda i: (0, i))
    tile = 2 * Q if rows % (2 * Q) == 0 else Q
    smem = pl.BlockSpec(memory_space=pltpu.SMEM)
    wout, masked, dyn = pl.pallas_call(
        functools.partial(pull_kernel, per, nz),
        grid=(rows // tile,),
        in_specs=[
            pl.BlockSpec((tile, half), step), pl.BlockSpec((tile, half), step), smem,
            *[whole(v) for v in out_own + out_cross],
        ],
        out_specs=[
            pl.BlockSpec((channels, model), fix), pl.BlockSpec((tile, model), step),
            pl.BlockSpec((tile, channels), step),
        ],
        out_shape=[shape((channels, model), BF), shape((rows, model), BF), full],
        compiler_params=params(),
        cost_estimate=cost(5),
        name="pull",
    )(cotangent, cot_o, limit, *out_own, *out_cross)
    out = pl.pallas_call(
        functools.partial(carry_kernel, groups, per),
        grid=(blocks,),
        in_specs=[
            *[gwide] * (3 * nz), wide, bspec, bspec, tspec, h2spec, h2spec, *[whole(v) for v in messages],
            whole(skip), whole(gain_out), whole(ex),
        ],
        out_specs=[
            *[gwide] * nz, *[pl.BlockSpec((1, gc, STATE), lambda i: (i, 0, 0))] * nz, wide,
            pl.BlockSpec((Q, 2), step),
        ],
        out_shape=[
            *[part] * nz, *[shape((blocks, gc, STATE), BF)] * nz, shape((rows, channels), BF),
            shape((rows, 2)),
        ],
        scratch_shapes=[pltpu.VMEM((channels, STATE), F32)],
        compiler_params=params(),
        cost_estimate=cost(10),
        name="carry",
    )(*y_in, *xs, *z, dyn, bs, cs, clt, e12, dttl2, *messages, skip, gain_out, ex)
    ys, states, gg, sums = out[:nz], out[nz : 2 * nz], out[2 * nz], out[2 * nz + 1]
    sums2 = swap(sums)

    def sum_products(a, w, count):
        tile = 2 * Q if count % (2 * Q) == 0 else count
        return pl.pallas_call(
            functools.partial(sum_products_kernel, len(a)),
            grid=(count // tile,),
            in_specs=[
                *[pl.BlockSpec((tile, v.shape[1]), step) for v in a], *[whole(v) for v in w]
            ],
            out_specs=[pl.BlockSpec((tile, half), step)] * 2,
            out_shape=[shape((count, half)), shape((count, half), BF)],
            compiler_params=params(),
            cost_estimate=cost(4),
            name="products",
        )(*a, *w)

    branch, branch_o = sum_products([gg], [wout], rows)
    branch_o = swap(branch_o)
    hhalf = pl.BlockSpec((Q, half), step)
    out = pl.pallas_call(
        functools.partial(gate_kernel, groups, per),
        grid=(blocks,),
        in_specs=[
            *[gwide] * (3 * nz), wide, pl.BlockSpec((Q, 2), step), pl.BlockSpec((Q, 2), step),
            whole(gain_out), h2spec, whole(ex), bspec, hhalf, hhalf, hhalf, smem,
        ],
        out_specs=[
            *[gwide] * nz, wide, wide, pl.BlockSpec((channels, STATE), fix),
            pl.BlockSpec((1, channels), fix), pl.BlockSpec((1, channels), fix), hhalf,
        ],
        out_shape=[
            *[part] * nz, shape((rows, channels), BF), shape((rows, channels), BF),
            shape((channels, STATE), BF), shape((1, channels)), shape((1, channels)),
            shape((rows, half), BF),
        ],
        scratch_shapes=[pltpu.VMEM((channels, STATE), F32)],
        compiler_params=params(),
        cost_estimate=cost(10),
        name="gate",
    )(
        *ys, *z, *xs, dyn, sums, sums2, gain_out, ec2, ex, cs, hidden, branch, branch_o, limit
    )
    dys = out[:nz]
    dz, yn, ds_local, g_gain, g_skip, out_hidden = out[nz:]
    messages = send_states([ds_local], -1)

    def plane_sum(parts):
        total = parts[0].astype(F32)
        for m in range(1, per):
            total = total + cross(parts[m], m).astype(F32)
        return total

    def to_owner(total):
        v = jnp.stack([total] + [cross(total, m) for m in range(1, per)])
        v = jnp.stack([pick(v, di ^ m) for m in range(per)])
        return v[:, :, :half], swap(v[:, :, half:])

    def by_head(mine, other):
        low_w = jnp.where(wi == 0, mine, other)
        high_w = jnp.where(wi == 0, other, mine)
        return jnp.concatenate([low_w, high_w], axis=0)

    gcol = pl.BlockSpec((rows, gc), lambda s: (0, s))
    early = pl.pallas_call(
        functools.partial(early_grad_kernel, per),
        grid=(nz,),
        in_specs=[gcol, whole(masked), gcol, whole(xn)],
        out_specs=[pl.BlockSpec((1, 2 * HEADDIM, model), lambda s: (s, 0, 0))] * per,
        out_shape=[shape((nz, 2 * HEADDIM, model), BF)] * per,
        compiler_params=params(),
        cost_estimate=cost(6),
        name="early_grad",
    )(yn, masked, dz, xn)
    early = plane_sum(early)
    early_low = early.astype(BF)

    out = pl.pallas_call(
        functools.partial(inside_back_kernel, groups, per),
        grid=(blocks,),
        in_specs=[*[gwide] * (2 * nz), bspec, bspec, hspec, tspec],
        out_specs=[*[gwide] * nz, bspec, bspec, hspec],
        out_shape=[*[part] * nz, shape((rows, STATE)), shape((rows, STATE)), shape((rows, heads))],
        scratch_shapes=[pltpu.VMEM((heads, Q), F32)],
        compiler_params=params(),
        cost_estimate=cost(15),
        name="inside_back",
    )(*xdt, *dys, bs, cs, cl, clt)
    dxi = out[:nz]
    dbi, dci, dai = out[nz:]
    rev = lambda i: (blocks - 1 - i, 0)
    rg = pl.BlockSpec((Q, gc), rev)
    rb = pl.BlockSpec((Q, STATE), rev)
    rh = pl.BlockSpec((Q, heads), rev)
    rh2 = pl.BlockSpec((Q, 2 * heads), rev)
    rbc = pl.BlockSpec((Q, 2 * STATE), rev)

    def back(some, final, dbi, dci, dti, wait):
        n = len(some)
        of = lambda values: [values[s] for s in some]
        out = pl.pallas_call(
            functools.partial(back_kernel, some, per, final),
            grid=(blocks,),
            in_specs=[
                *[rg] * (4 * n), *[pl.BlockSpec((HALO, gc), fix)] * n,
                *[pl.BlockSpec((1, gc, STATE), lambda i: (blocks - 1 - i, 0, 0))] * n,
                rb, rb, rb, rb, rh, rh, rh, rh,
                pl.BlockSpec((heads, Q), lambda i: (0, blocks - 1 - i)), rh2, rh2, rh2,
                rbc, rbc, whole(brawh), whole(taps), whole(taps_bc), whole(rate), whole(skip),
                whole(ex), whole(er), *[whole(v) for v in messages],
                pl.BlockSpec(memory_space=pl.ANY),
            ],
            out_specs=[
                *[rg] * n, *[pl.BlockSpec((HALO, gc), fix)] * n, *[pl.BlockSpec((4, gc), fix)] * n,
                rb, rb, rh, pl.BlockSpec((1, heads), fix), pl.BlockSpec((1, heads), fix),
                rbc, pl.BlockSpec((HALO, 2 * STATE), fix), pl.BlockSpec((4, 2 * STATE), fix),
            ],
            out_shape=[
                *[shape((rows, gc), BF)] * n, *[shape((HALO, gc), BF)] * n, *[shape((4, gc))] * n,
                shape((rows, STATE)), shape((rows, STATE)),
                shape((rows, heads), BF if final else F32), shape((1, heads)), shape((1, heads)),
                shape((rows, 2 * STATE), BF), shape((HALO, 2 * STATE), BF), shape((4, 2 * STATE)),
            ],
            scratch_shapes=[
                pltpu.VMEM((n * gc, STATE), F32), pltpu.VMEM((heads, STATE), F32),
                *[pltpu.VMEM((8, gc), F32)] * n, pltpu.VMEM((8, 2 * STATE), F32),
            ],
            compiler_params=params(),
            cost_estimate=cost(7 * n),
            name="back",
        )(
            *of(dxi), *of(dys), *of(u), *of(xr), *of(xrh), *of(states), bs, cs, dbi, dci, dai, dti,
            dt, sig, clt, dt2, e12, tl2, ubc, braw, brawh, taps, taps_bc, rate, skip, ex, er,
            *messages, wait,
        )
        return out[:n], out[n : 2 * n], out[2 * n : 3 * n], *out[3 * n :]

    halves = (groups[1 : nz // 2 + 1], groups[nz // 2 + 1 :] + groups[:1])
    dx, dxh, g_taps = [None] * nz, [None] * nz, [None] * nz
    dti = jnp.zeros((rows, heads), F32)
    g_rate, g_bias, late, wait = 0.0, 0.0, [], dti
    bc_rows = 2 * STATE // per
    for number, some in enumerate(halves):
        final = number == len(halves) - 1
        got, got_h, got_taps, dbi, dci, dti, one, two, dbc, dbch, g_taps_bc = back(
            some, final, dbi, dci, dti, wait
        )
        g_rate, g_bias = g_rate + one, g_bias + two
        for i, s in enumerate(some):
            dx[s], dxh[s], g_taps[s] = got[i], got_h[i], got_taps[i]
        n = len(some)
        spread_heads = pick_heads.T.astype(BF)
        more = [dbc, dbch, dti, spread_heads] if final else []
        out_rows = n * HEADDIM + (bc_rows + HALO if final else 0)
        g = pl.pallas_call(
            functools.partial(late_grad_kernel, n, per, final),
            out_shape=[shape((out_rows, model), BF)] * per,
            scratch_shapes=(
                [pltpu.VMEM((2 * STATE, model), F32), pltpu.VMEM((HEADS, model), F32)]
                if final
                else []
            ),
            compiler_params=params(),
            cost_estimate=cost(3),
            name="late_grad",
        )(*got, *got_h, xn, xnh, *more)
        late.append(plane_sum(g))
        wait = early_low if number == 0 else wait
    g_taps = jnp.concatenate(g_taps, axis=1)

    total = early[0]
    for s in range(1, nz):
        total = total + turn(early_low[s], -s).astype(F32)
    early_own, early_other = to_owner(total.astype(BF))
    share = late[-1][len(halves[-1]) * HEADDIM :]
    addend = {}
    for some, v in zip(halves, late):
        for i, s in enumerate(some):
            addend[s] = jnp.concatenate([v[i * HEADDIM : (i + 1) * HEADDIM], share], axis=0)
    total = addend[0]
    for s in range(1, nz):
        total = total + turn(addend[s].astype(BF), -s).astype(F32)
    late_own, late_other = to_owner(total.astype(BF))
    g_early = by_head(early_own, early_other)
    g_late = by_head(late_own[:, :HEADDIM], late_other[:, :HEADDIM])
    g_zx = jnp.concatenate([g_early[:, HEADDIM:], g_late], axis=1)
    g_bcdt = late_own[:, HEADDIM:].astype(F32) + late_other[:, HEADDIM:].astype(F32)
    grad_in_bcdt = jnp.transpose(
        jnp.concatenate(
            [
                g_bcdt[:, :bc_rows].reshape(2 * STATE, half),
                g_bcdt[:, bc_rows : bc_rows + HEADS // per].reshape(HEADS, half),
            ],
            axis=0,
        )
    )

    lhs = [dz] + dx + [dbc, dti]
    dxn, dxn_o = sum_products(lhs, [jnp.concatenate(wz, axis=0)] + wx + [wbc, wdt], rows)
    edge = sum(dot(v, w) for v, w in zip(dxh + [dbch], wx + [wbc]))
    edge = edge[:, :half] + swap(edge[:, half:])
    edge = shift(edge, -1)
    dxn = dxn + swap(dxn_o).astype(F32) + jnp.pad(edge, ((rows - HALO, 0), (0, 0)))
    source = hidden.astype(F32)
    gain_half = gain_in[:, :half]
    across = jnp.sum(dxn * gain_half * source, axis=1, keepdims=True)
    across = across + swap(across)
    grad_hidden = (
        cotangent.astype(F32)
        + r * gain_half * dxn
        - source * (r * r * r) / model * across
    ).astype(BF)
    g_norm = jnp.sum(dxn * source * r, axis=0)

    table = jnp.concatenate(
        [
            g_bias.reshape(heads, 1),
            (g_rate * rate).reshape(heads, 1),
            jnp.sum(g_skip.reshape(heads, HEADDIM), axis=1, keepdims=True),
            jnp.transpose(g_taps.reshape(4, heads, HEADDIM), (1, 0, 2)).reshape(heads, 4 * HEADDIM),
            g_gain.reshape(heads, HEADDIM),
        ],
        axis=1,
    )
    table = jnp.dot(pick_heads.T, table, precision=HIGH)
    side = (jnp.arange(2) == wi).astype(F32)[:, None] * g_norm[None]
    small = jnp.concatenate([table.reshape(-1), g_taps_bc.reshape(-1), side.reshape(-1)])
    small = small + swap(small)
    flip = 1
    while flip < ndp:
        small = small + cross(small, flip)
        flip *= 2
    flip = 1
    while flip < nz:
        small = small + lax.ppermute(small, "head", [(i, i ^ flip) for i in range(nz)])
        flip *= 2
    size = table.size
    table = lax.dynamic_slice_in_dim(
        small[:size].reshape(HEADS, -1), zi * own_heads, own_heads, 0
    )
    g_taps_bc = small[size : size + 8 * STATE].reshape(4, 2 * STATE)
    g_norm = pick(small[size + 8 * STATE :].reshape(2, half), wi)
    return (
        out_hidden,
        grad_hidden,
        g_norm,
        jnp.transpose(g_zx, (2, 0, 1)).astype(F32),
        grad_in_bcdt,
        jnp.transpose(
            table[:, 3 : 3 + 4 * HEADDIM].reshape(own_heads, 4, HEADDIM), (1, 0, 2)
        ).reshape(4, own_heads * HEADDIM),
        g_taps_bc,
        table[:, 0],
        table[:, 1],
        table[:, 2],
        table[:, 3 + 4 * HEADDIM :].reshape(-1),
        g_early[:, :HEADDIM].reshape(own_heads * HEADDIM, half).astype(F32),
    )


def fits(mesh):
    ndp, nz, nw = mesh.shape["dp"], mesh.shape["head"], mesh.shape["width"]
    return (
        nw == 2
        and ndp in (2, 4, 8)
        and nz & (nz - 1) == 0
        and HEADS == nz * nw * ndp
        and LEN % (nz * Q) == 0
        and SEQS == ndp
        and HEADS // nw * HEADDIM % Q == 0
        and HEADS // ndp <= HALO
    )


def solution(mesh):
    placed = (
        P(("dp", "head"), "width"),
        P("dp"),
        P(("dp", "head"), "width"),
        P("width"),
        P("width", "head", None),
        P("width", None),
        P(None, "head"),
        P(),
        P("head"),
        P("head"),
        P("head"),
        P("head"),
        P("head", "width"),
    )
    return jax.shard_map(
        sequence_device if fits(mesh) else per_device,
        mesh=mesh,
        in_specs=placed,
        out_specs=(
            P(("dp", "head"), "width"),
            P(("dp", "head"), "width"),
            P("width"),
            P("width", "head", None),
            P("width", None),
            P(None, "head"),
            P(),
            P("head"),
            P("head"),
            P("head"),
            P("head"),
            P("head", "width"),
        ),
        check_vma=False,
    )
```

time: 593 us -> 439 us (0.74)
  starting transfers between devices: 119 us -> 73.9 us
  waiting for transfers between devices: 141 us -> 97.3 us
  blocking collectives: 40.7 us -> 0 us
  matrix products: 34.3 us -> 2.71 us
  Pallas kernels: 168 us -> 181 us
    ppermute x36 -> x29, waiting for transfers between devices: 113 us -> 40.8 us  [cross(): return lax.ppermute(v, 'dp', [(i, i ^ m) for i in range(ndp)])]
    psum x1 -> x0, blocking collectives: 40.7 us -> none  [sequence_device(): small = lax.psum(small, ('dp', 'head', 'width'))]
    ppermute x18 -> x15, waiting for transfers between devices: 18.6 us -> 45.9 us  [turn(): return lax.ppermute(v, 'head', [(i, (i + s) % nz) for i in range(nz)])]
    dot_general x5 -> x1, matrix products: 22.6 us -> 0.8 us  [sequence_device(): jnp.dot(pick_heads.astype(BF), bcdt_t[2 * STATE:2 * STATE + HEADS], prefe...]
    ppermute x18 -> x15, starting transfers between devices: 41.3 us -> 24.9 us  [turn(): return lax.ppermute(v, 'head', [(i, (i + s) % nz) for i in range(nz)])]
    ppermute x12 -> x8, starting transfers between devices: 28.5 us -> 13.3 us  [shift(): lax.ppermute(v, 'head', [(i, i + s) for i in range(nz) if 0 <= i + s < nz])]
    ppermute x36 -> x29, starting transfers between devices: 47.2 us -> 32.8 us  [cross(): return lax.ppermute(v, 'dp', [(i, i ^ m) for i in range(ndp)])]
    pallas_call x7 -> x20, Pallas kernels: 168 us -> 181 us  [the longest x2 35.4 us: back(): pl.pallas_call(functools.partial(back_kernel, some, per, final), grid=(bl...]
  transfers between devices with their start and end apart: 79 -> 69, of which waited for: 29 -> 18; matrix products, arithmetic and copies ran while one was open for 15% -> 13% of each run, Pallas kernels for 22% -> 28%
where the time goes in v2:
time: 439 us; the launch traced here: 433 us
  Pallas kernels  181 us (41%)
  waiting for transfers between devices  97.3 us (22%)
  starting transfers between devices  73.9 us (17%)
  local copies, waits for them, and re-layouts  43.1 us (10%)
  other arithmetic  31.1 us (7%)
    ppermute x15, waiting for transfers between devices, turn(): return lax.ppermute(v, 'head', [(i, (i + s) % nz) for i in range(nz)])  45.9 us
    ppermute x29, waiting for transfers between devices, cross(): return lax.ppermute(v, 'dp', [(i, i ^ m) for i in range(ndp)])  40.8 us
    pallas_call x2, Pallas kernels, back(): pl.pallas_call(functools.partial(back_kernel, some, per, final), grid=(bl...  35.4 us
    ppermute x29, starting transfers between devices, cross(): return lax.ppermute(v, 'dp', [(i, i ^ m) for i in range(ndp)])  32.8 us
    pallas_call x4, Pallas kernels, sequence_device(): pl.pallas_call(functools.partial(project_kernel, s, per), grid=(rows // c...  30.7 us
    ppermute x15, starting transfers between devices, turn(): return lax.ppermute(v, 'head', [(i, (i + s) % nz) for i in range(nz)])  24.9 us
    pallas_call x1, Pallas kernels, sequence_device(): pl.pallas_call(functools.partial(inside_back_kernel, groups, per), grid=(...  17.8 us
    pallas_call x2, Pallas kernels, sum_products(): pl.pallas_call(functools.partial(sum_products_kernel, len(a)), grid=(coun...  15.9 us
  transfers between devices with their start and end apart: 69, of which 18 were waited for; matrix products, arithmetic and copies ran while one was open for 13% of the time, Pallas kernels for 28%

profile of v2, /device:TPU:0, one launch (start us, length us, event | category | flops | bytes accessed | tf_op | source)
XLA Modules:
  0.0 432.7 jit_solution(2086110132282169042)
XLA Ops:
  4.6 3.1 collective-permute-start.3
  7.7 2.6 collective-permute-start.4
  11.6 6.6 %constant_dynamic-slice_fusion.21 = (bf16[512,1,128]{2,1,0:T(2,128)(2,1)S(1)}, bf16[512,1,128]{2,1,0:T(2,128)(2,1)S(1)}, bf16[512,1,128]{2,1,0:T(2,128)(2,1)S(1)...) fusion(bf16[512,8,128]{2,1,0:T(8,128)(2,1)} %param.19, ...), kind=kLoop, calls=%fused_computation.124 | loop fusion | bytes 2097184 | tf_op jit(solution)/shard_map/dynamic-slice.2
  31.1 1.6 collective-permute-start.8
  33.6 11.1 %collective-permute-done.16.refs_2_ = bf16[128,1024]{1,0:T(8,128)(2,1)} collective-permute-done((bf16[128,1024]{1,0:T(8,128)(2,1)S(1)}, bf16[128,1024]{1,0:T(8,128)(2,1)}, u32[]{:S(2)}, u32[]{:S(2)}) %collective-permute-start.16) | collective-permute-done | bytes 262176 | tf_op jit(solution)/shard_map/ppermute | solution.py:819
  44.6 2.4 collective-permute-start.19
  49.8 2.3 collective-permute-done.19.refs_5_
  52.1 1.5 collective-permute-start.10
  56.5 5.9 %collective-permute-done.23 = bf16[64,1024]{1,0:T(8,128)(2,1)S(1)} collective-permute-done((bf16[64,1024]{1,0:T(8,128)(2,1)S(1)}, bf16[64,1024]{1,0:T(8,128)(2,1)S(1)}, u32[]{:S(2)}, u32[]{:S(2)}) %collective-permute-start.23) | collective-permute-done | bytes 131104 | tf_op jit(solution)/shard_map/ppermute | solution.py:819
  62.4 4.9 %collective-permute-start.24 = (bf16[64,1024]{1,0:T(8,128)(2,1)S(1)}, bf16[64,1024]{1,0:T(8,128)(2,1)S(1)}, u32[]{:S(2)}, u32[]{:S(2)}) collective-permute-start(bf16[64,1024]{1,0:T(8,128)(2,1)S(1)} %maximum_add_fusion.refs_3_), channel_id=1, source_target_pairs={{0,4},{2,6},{4,0},{6,2},{1,5},{3,7},{5,1},{7,3},{8,12},{10,14},{12... | collective-permute-start | bytes 393224 | tf_op jit(solution)/shard_map/ppermute | solution.py:819
  68.6 5.5 %collective-permute-done.24 = bf16[64,1024]{1,0:T(8,128)(2,1)S(1)} collective-permute-done((bf16[64,1024]{1,0:T(8,128)(2,1)S(1)}, bf16[64,1024]{1,0:T(8,128)(2,1)S(1)}, u32[]{:S(2)}, u32[]{:S(2)}) %collective-permute-start.24) | collective-permute-done | bytes 131104 | tf_op jit(solution)/shard_map/ppermute | solution.py:819
  74.0 1.5 collective-permute-start.1
  76.1 1.5 collective-permute-start.9
  78.2 11.6 %entry.1 = (bf16[1024,1024]{1,0:T(8,128)(2,1)}, bf16[16,1024]{1,0:T(8,128)(2,1)}, f32[1024,1]{1,0:T(8,128)}, f32[1024,256]{1,0:T(8,128)}, f32[16,256]{1,0:T(8,12...) custom-call(bf16[1024,512]{1,0:T(8,128)(2,1)} %refs_19_.1, ...), custom_call_target="tpu_custom_call" | custom-call | flops 1200000000 | bytes 12000 | tf_op jit(solution)/shard_map/entry/pallas_call | solution.py:903
  89.9 7.7 %project.4 = (bf16[256,1024]{1,0:T(8,128)(2,1)}, bf16[256,1024]{1,0:T(8,128)(2,1)}, f32[1024,256]{1,0:T(8,128)}, f32[1024,256]{1,0:T(8,128)}, f32[16,256]{1,0:T(...) custom-call(bf16[1024,1024]{1,0:T(8,128)(2,1)} %get-tuple-element.136., ...), custom_call_target="tpu_custom_call" | custom-call | flops 500000000 | bytes 5000 | tf_op jit(solution)/shard_map/project/pallas_call | solution.py:931
  97.6 1.6 collective-permute-start.13
  99.2 1.5 collective-permute-start.14
  101.2 7.6 %project.5 = (bf16[256,1024]{1,0:T(8,128)(2,1)}, bf16[256,1024]{1,0:T(8,128)(2,1)}, f32[1024,256]{1,0:T(8,128)}, f32[1024,256]{1,0:T(8,128)}, f32[16,256]{1,0:T(...) custom-call(bf16[1024,1024]{1,0:T(8,128)(2,1)} %get-tuple-element.136., ...), custom_call_target="tpu_custom_call" | custom-call | flops 500000000 | bytes 5000 | tf_op jit(solution)/shard_map/project/pallas_call | solution.py:931
  108.9 1.5 collective-permute-start.15
  112.0 3.3 collective-permute-done.18.refs_4_
  116.2 7.7 %project.7 = (bf16[256,1024]{1,0:T(8,128)(2,1)}, bf16[256,1024]{1,0:T(8,128)(2,1)}, f32[1024,256]{1,0:T(8,128)}, f32[1024,256]{1,0:T(8,128)}, f32[16,256]{1,0:T(...) custom-call(bf16[1024,1024]{1,0:T(8,128)(2,1)} %get-tuple-element.136., ...), custom_call_target="tpu_custom_call" | custom-call | flops 500000000 | bytes 5000 | tf_op jit(solution)/shard_map/project/pallas_call | solution.py:931
  123.9 1.5 collective-permute-start.27
  126.6 7.7 %project.6 = (bf16[256,1024]{1,0:T(8,128)(2,1)}, bf16[256,1024]{1,0:T(8,128)(2,1)}, f32[1024,256]{1,0:T(8,128)}, f32[1024,256]{1,0:T(8,128)}, f32[16,256]{1,0:T(...) custom-call(bf16[1024,1024]{1,0:T(8,128)(2,1)} %get-tuple-element.136., ...), custom_call_target="tpu_custom_call" | custom-call | flops 500000000 | bytes 5000 | tf_op jit(solution)/shard_map/project/pallas_call | solution.py:931
  134.3 1.5 constant_dynamic-update-slice_fusion.5
  137.0 3.5 collective-permute-start.29
  141.7 1.5 collective-permute-start.31
  144.1 3.6 inside.7.refs_3_
  147.7 3.6 inside.6.refs_2_
  151.3 3.6 inside.5.refs_1_
  154.9 3.6 inside.4.refs_0_
  158.5 7.0 %pull.1 = (bf16[1024,1024]{1,0:T(8,128)(2,1)}, bf16[1024,1024]{1,0:T(8,128)(2,1)}, f32[1024,1024]{1,0:T(8,128)}) custom-call(bf16[1024,512]{1,0:T(8,128)(2,1)} %refs_0_.1, bf16[1024,512]{1,0:T(8,128)(2,1)} %copy-done.23, s32[1,1]{1,0:T(1,128)} %bitcast.20.refs_2_.refs_22_, bf16[64,1024]{1,0:T(8,128)(2,1)} %copy-done.31, ...), custom_call_target="tpu_custom_call" | custom-call | flops 500000000 | bytes 5000 | tf_op jit(solution)/shard_map/pull/pallas_call | solution.py:987
  166.3 14.0 %carry.1 = (f32[1024,256]{1,0:T(8,128)}, f32[1024,256]{1,0:T(8,128)}, f32[1024,256]{1,0:T(8,128)}, f32[1024,256]{1,0:T(8,128)}, bf16[8,256,128]{2,1,0:T(8,128)(2...) custom-call(f32[1024,256]{1,0:T(8,128)} %inside.4.refs_0_, ...), custom_call_target="tpu_custom_call" | custom-call | flops 1000000000 | bytes 10000 | tf_op jit(solution)/shard_map/carry/pallas_call | solution.py:1003
  180.3 5.9 %products.2 = (f32[1024,512]{1,0:T(8,128)}, bf16[1024,512]{1,0:T(8,128)(2,1)}) custom-call(bf16[1024,1024]{1,0:T(8,128)(2,1)} %get-tuple-element.170.refs_0_, bf16[1024,1024]{1,0:T(8,128)(2,1)} %get-tuple-element.171.refs_1_), custom_call_target="tpu_custom_call" | custom-call | flops 400000000 | bytes 4000 | tf_op jit(solution)/shard_map/products/pallas_call | solution.py:1028
  186.7 2.9 collective-permute-done.32.refs_14_
  190.8 14.6 %gate.1 = (f32[1024,256]{1,0:T(8,128)}, f32[1024,256]{1,0:T(8,128)}, f32[1024,256]{1,0:T(8,128)}, f32[1024,256]{1,0:T(8,128)}, bf16[1024,1024]{1,0:T(8,128)(2,1)...) custom-call(f32[1024,256]{1,0:T(8,128)} %get-tuple-element.164.refs_, ...), custom_call_target="tpu_custom_call" | custom-call | flops 1000000000 | bytes 10000 | tf_op jit(solution)/shard_map/gate/pallas_call | solution.py:1044
  209.0 1.7 collective-permute-start.36
  210.7 9.0 %early_grad.1 = (bf16[4,128,1024]{2,1,0:T(8,128)(2,1)}, bf16[4,128,1024]{2,1,0:T(8,128)(2,1)}, bf16[4,128,1024]{2,1,0:T(8,128)(2,1)}, bf16[4,128,1024]{2,1,0:T(8,128)(2,1)}) custom-call(bf16[1024,1024]{1,0:T(8,128)(2,1)} %get-tuple-element.214.yn, bf16[1024,1024]{1,0:T(8,128)(2,1)} %get-tuple-element.215.masked, ...), custom_call_target="tpu_custom_call" | custom-call | flops 600000000 | bytes 6000 | tf_op jit(solution)/shard_map/early_grad/pallas_call | solution.py:1088
  220.9 17.8 %inside_back.1 = (f32[1024,256]{1,0:T(8,128)}, f32[1024,256]{1,0:T(8,128)}, f32[1024,256]{1,0:T(8,128)}, f32[1024,256]{1,0:T(8,128)}, f32[1024,128]{1,0:T(8,128)...) custom-call(bf16[1024,256]{1,0:T(8,128)(2,1)} %get-tuple-element.141.xdt.refs_0_, ...), custom_call_target="tpu_custom_call" | custom-call | flops 1500000000 | bytes 15000 | tf_op jit(solution)/shard_map/inside_back/pallas_call | solution.py:1101
  238.6 2.4 collective-permute-start.39
  242.1 16.9 %back.2 = (bf16[1024,256]{1,0:T(8,128)(2,1)}, bf16[1024,256]{1,0:T(8,128)(2,1)}, bf16[16,256]{1,0:T(8,128)(2,1)}, bf16[16,256]{1,0:T(8,128)(2,1)}, f32[4,256]{1,...) custom-call(f32[1024,256]{1,0:T(8,128)} %get-tuple-element.191.refs_, ...), custom_call_target="tpu_custom_call" | custom-call | flops 1400000000 | bytes 14000 | tf_op jit(solution)/shard_map/back/pallas_call | solution.py:1124
  259.0 4.5 %late_grad.3 = (bf16[128,1024]{1,0:T(8,128)(2,1)}, bf16[128,1024]{1,0:T(8,128)(2,1)}, bf16[128,1024]{1,0:T(8,128)(2,1)}, bf16[128,1024]{1,0:T(8,128)(2,1)}) custom-call(bf16[1024,256]{1,0:T(8,128)(2,1)} %get-tuple-element.221.refs_2_.refs_0_, bf16[1024,256]{1,0:T(8,128)(2,1)} %get-tuple-element.222.refs_3_.refs_1_, ...), custom_call_target="tpu_custom_call" | custom-call | flops 300000000 | bytes 3000 | tf_op jit(solution)/shard_map/late_grad/pallas_call | solution.py:1178
  265.8 7.4 %collective-permute-done.59 = bf16[128,1024]{1,0:T(8,128)(2,1)S(1)} collective-permute-done((bf16[128,1024]{1,0:T(8,128)(2,1)}, bf16[128,1024]{1,0:T(8,128)(2,1)S(1)}, u32[]{:S(2)}, u32[]{:S(2)}) %collective-permute-start.59) | collective-permute-done | bytes 262176 | tf_op jit(solution)/shard_map/ppermute | solution.py:825
  274.2 3.0 pad_maximum_fusion.refs_7_
  279.4 2.6 collective-permute-done.61
  284.3 4.2 fusion.38
  289.7 18.5 %back.3 = (bf16[1024,256]{1,0:T(8,128)(2,1)}, bf16[1024,256]{1,0:T(8,128)(2,1)}, bf16[16,256]{1,0:T(8,128)(2,1)}, bf16[16,256]{1,0:T(8,128)(2,1)}, f32[4,256]{1,...) custom-call(f32[1024,256]{1,0:T(8,128)} %get-tuple-element.181.refs_, ...), custom_call_target="tpu_custom_call" | custom-call | flops 1400000000 | bytes 14000 | tf_op jit(solution)/shard_map/back/pallas_call | solution.py:1124
  309.2 6.0 %late_grad.2 = (bf16[208,1024]{1,0:T(8,128)(2,1)}, bf16[208,1024]{1,0:T(8,128)(2,1)}, bf16[208,1024]{1,0:T(8,128)(2,1)}, bf16[208,1024]{1,0:T(8,128)(2,1)}) custom-call(bf16[1024,256]{1,0:T(8,128)(2,1)} %get-tuple-element.223.refs_4_.refs_0_, bf16[1024,256]{1,0:T(8,128)(2,1)} %get-tuple-element.220.refs_1_, bf16[16,256]{1,0:T(8,128)(2,1)} %get-tuple-element.239.refs_2_, ...), custom_call_target="tpu_custom_call" | custom-call | flops 300000000 | bytes 3000 | tf_op jit(solution)/shard_map/late_grad/pallas_call | solution.py:1178
  316.5 2.3 collective-permute-start.58
  318.8 4.4 %collective-permute-start.49 = (bf16[128,1024]{1,0:T(8,128)(2,1)}, bf16[128,1024]{1,0:T(8,128)(2,1)}, u32[]{:S(2)}, u32[]{:S(2)}) collective-permute-start(bf16[128,1024]{1,0:T(8,128)(2,1)} %get-tuple-element.346), channel_id=1, source_target_pairs={{0,6},{2,0},{4,2},{6,4},{1,7},{3,1},{5,3},{7,5},{8,14},{10,8},{12,... | collective-permute-start | bytes 786440 | tf_op jit(solution)/shard_map/ppermute | solution.py:819
  325.6 10.0 %products.3 = (f32[1024,512]{1,0:T(8,128)}, bf16[1024,512]{1,0:T(8,128)(2,1)}) custom-call(bf16[1024,1024]{1,0:T(8,128)(2,1)} %get-tuple-element.176.dz.refs_0_, bf16[1024,256]{1,0:T(8,128)(2,1)} %get-tuple-element.220.refs_1_, bf16[1024,256]{1,0:T(8,128)(2,1)} %get-tuple-element.221.refs_2_.refs_0_, bf16[1024,256]{1,0:T(8,128)(2,1)} %get-tuple-element.222.refs_3_.refs_1_, ...), custom_call_target="tpu_custom_call" | custom-call | flops 400000000 | bytes 4000 | tf_op jit(solution)/shard_map/products/pallas_call | solution.py:1028
  337.8 3.3 collective-permute-start.62
  342.4 2.4 collective-permute-done.51
  347.5 2.7 collective-permute-done.62
  351.3 18.3 %collective-permute-done.63 = bf16[144,1024]{1,0:T(8,128)(2,1)S(1)} collective-permute-done((bf16[144,1024]{1,0:T(8,128)(2,1)S(1)}, bf16[144,1024]{1,0:T(8,128)(2,1)S(1)}, u32[]{:S(2)}, u32[]{:S(2)}) %collective-permute-start.63) | collective-permute-done | bytes 294944 | tf_op jit(solution)/shard_map/ppermute | solution.py:819
  369.9 2.3 collective-permute-start.54
  373.3 9.7 %collective-permute-done.53 = bf16[128,1024]{1,0:T(8,128)(2,1)S(1)} collective-permute-done((bf16[128,1024]{1,0:T(8,128)(2,1)S(1)}, bf16[128,1024]{1,0:T(8,128)(2,1)S(1)}, u32[]{:S(2)}, u32[]{:S(2)}) %collective-permute-start.53) | collective-permute-done | bytes 262176 | tf_op jit(solution)/shard_map/ppermute | solution.py:825
  383.4 2.3 collective-permute-start.67
  386.9 10.5 %collective-permute-done.66 = bf16[144,1024]{1,0:T(8,128)(2,1)S(1)} collective-permute-done((bf16[144,1024]{1,0:T(8,128)(2,1)S(1)}, bf16[144,1024]{1,0:T(8,128)(2,1)S(1)}, u32[]{:S(2)}, u32[]{:S(2)}) %collective-permute-start.66) | collective-permute-done | bytes 294944 | tf_op jit(solution)/shard_map/ppermute | solution.py:825
  406.3 2.2 collective-permute-done.45
  410.0 2.7 collective-permute-done.46
  412.8 4.1 collective-permute-done.47
  417.0 2.0 fusion.2
  419.0 3.4 collective-permute-done.48
  429.8 1.8 copy.116
  (394 shorter events, 83.3 us)
Async XLA Ops:
  4.6 20.8 %collective-permute-start.3 = (f32[4,323]{1,0:T(4,128)S(1)}, f32[4,323]{1,0:T(4,128)S(1)}, u32[]{:S(2)}, u32[]{:S(2)}) collective-permute-start(f32[4,323]{1,0:T(4,128)S(1)} %pad_maximum_fusion.19), channel_id=1, source_target_pairs={{0,2},{2,4},{4,6},{6,0},{1,3},{3,5},{5,7},{7,1},{8,10},{10,12},{12... | collective-permute-start | bytes 15512 | tf_op jit(solution)/shard_map/ppermute | solution.py:819
  7.7 17.8 %collective-permute-start.4 = (f32[4,323]{1,0:T(4,128)S(1)}, f32[4,323]{1,0:T(4,128)S(1)}, u32[]{:S(2)}, u32[]{:S(2)}) collective-permute-start(f32[4,323]{1,0:T(4,128)S(1)} %pad_maximum_fusion.19), channel_id=1, source_target_pairs={{0,4},{2,6},{4,0},{6,2},{1,5},{3,7},{5,1},{7,3},{8,12},{10,14},{12... | collective-permute-start | bytes 15512 | tf_op jit(solution)/shard_map/ppermute | solution.py:819
  10.3 15.8 %collective-permute-start.5 = (f32[4,323]{1,0:T(4,128)S(1)}, f32[4,323]{1,0:T(4,128)S(1)}, u32[]{:S(2)}, u32[]{:S(2)}) collective-permute-start(f32[4,323]{1,0:T(4,128)S(1)} %pad_maximum_fusion.19), channel_id=1, source_target_pairs={{0,6},{2,0},{4,2},{6,4},{1,7},{3,1},{5,3},{7,5},{8,14},{10,8},{12,... | collective-permute-start | bytes 15512 | tf_op jit(solution)/shard_map/ppermute | solution.py:819
  11.6 55.7 %collective-permute-start = (bf16[1024,512]{1,0:T(8,128)(2,1)}, bf16[1024,512]{1,0:T(8,128)(2,1)}, u32[]{:S(2)}, u32[]{:S(2)}) collective-permute-start(bf16[1024,512]{1,0:T(8,128)(2,1)} %refs_19_.1), channel_id=1, source_target_pairs={{0,1},{1,0},{2,3},{3,2},{4,5},{5,4},{6,7},{7,6},{8,9},{9,8},{10,11... | collective-permute-start | bytes 3145736 | tf_op jit(solution)/shard_map/ppermute | solution.py:816
  19.0 10.2 %collective-permute-start.6 = (bf16[128,512]{1,0:T(8,128)(2,1)}, bf16[128,512]{1,0:T(8,128)(2,1)}, u32[]{:S(2)}, u32[]{:S(2)}) collective-permute-start(bf16[128,512]{1,0:T(8,128)(2,1)} %bitcast.8), channel_id=1, source_target_pairs={{0,1},{1,0},{2,3},{3,2},{4,5},{5,4},{6,7},{7,6},{8,9},{9,8},{10,11... | collective-permute-start | bytes 393224 | tf_op jit(solution)/shard_map/ppermute | solution.py:816
  25.4 5.7 %collective-permute-start.2 = (bf16[289,512]{1,0:T(8,128)(2,1)}, bf16[289,512]{1,0:T(8,128)(2,1)S(1)}, u32[]{:S(2)}, u32[]{:S(2)}) collective-permute-start(bf16[289,512]{1,0:T(8,128)(2,1)} %pad_maximum_fusion.13), channel_id=1, source_target_pairs={{0,1},{1,0},{2,3},{3,2},{4,5},{5,4},{6,7},{7,6},{8,9},{9,8},{10,11... | collective-permute-start | bytes 887816 | tf_op jit(solution)/shard_map/ppermute | solution.py:816
  25.5 23.1 %collective-permute-start.7 = (bf16[3,128,512]{2,1,0:T(8,128)(2,1)}, bf16[3,128,512]{2,1,0:T(8,128)(2,1)}, u32[]{:S(2)}, u32[]{:S(2)}) collective-permute-start(bf16[3,128,512]{2,1,0:T(8,128)(2,1)} %pad_maximum_fusion.8), channel_id=1, source_target_pairs={{0,1},{1,0},{2,3},{3,2},{4,5},{5,4},{6,7},{7,6},{8,9},{9,8},{10,11... | collective-permute-start | bytes 1179656 | tf_op jit(solution)/shard_map/ppermute | solution.py:816
  26.0 4.5 %collective-permute-start.22 = (bf16[3,64,512]{2,1,0:T(8,128)(2,1)S(1)}, bf16[3,64,512]{2,1,0:T(8,128)(2,1)S(1)}, u32[]{:S(2)}, u32[]{:S(2)}) collective-permute-start(bf16[3,64,512]{2,1,0:T(8,128)(2,1)S(1)} %pad_maximum_fusion.16), channel_id=1, source_target_pairs={{0,1},{1,0},{2,3},{3,2},{4,5},{5,4},{6,7},{7,6},{8,9},{9,8},{10,11... | collective-permute-start | bytes 589832 | tf_op jit(solution)/shard_map/ppermute | solution.py:816
  29.2 25.6 %collective-permute-start.21 = (bf16[64,512]{1,0:T(8,128)(2,1)}, bf16[64,512]{1,0:T(8,128)(2,1)S(1)}, u32[]{:S(2)}, u32[]{:S(2)}) collective-permute-start(bf16[64,512]{1,0:T(8,128)(2,1)} %get-tuple-element.366), channel_id=1, source_target_pairs={{0,1},{1,0},{2,3},{3,2},{4,5},{5,4},{6,7},{7,6},{8,9},{9,8},{10,11... | collective-permute-start | bytes 196616 | tf_op jit(solution)/shard_map/ppermute | solution.py:816
  30.6 14.1 %collective-permute-start.16 = (bf16[128,1024]{1,0:T(8,128)(2,1)S(1)}, bf16[128,1024]{1,0:T(8,128)(2,1)}, u32[]{:S(2)}, u32[]{:S(2)}) collective-permute-start(bf16[128,1024]{1,0:T(8,128)(2,1)S(1)} %pad_maximum_fusion.15.refs_2_), channel_id=1, source_target_pairs={{0,6},{2,0},{4,2},{6,4},{1,7},{3,1},{5,3},{7,5},{8,14},{10,8},{12,... | collective-permute-start | bytes 786440 | tf_op jit(solution)/shard_map/ppermute | solution.py:819
  31.1 18.6 %collective-permute-start.8 = (bf16[128,1024]{1,0:T(8,128)(2,1)S(1)}, bf16[128,1024]{1,0:T(8,128)(2,1)}, u32[]{:S(2)}, u32[]{:S(2)}) collective-permute-start(bf16[128,1024]{1,0:T(8,128)(2,1)S(1)} %pad_maximum_fusion.15.refs_2_), channel_id=1, source_target_pairs={{0,2},{2,4},{4,6},{6,0},{1,3},{3,5},{5,7},{7,1},{8,10},{10,12},{12... | collective-permute-start | bytes 786440 | tf_op jit(solution)/shard_map/ppermute | solution.py:819
  44.6 7.5 %collective-permute-start.19 = (bf16[128,1024]{1,0:T(8,128)(2,1)}, bf16[128,1024]{1,0:T(8,128)(2,1)S(1)}, u32[]{:S(2)}, u32[]{:S(2)}) collective-permute-start(bf16[128,1024]{1,0:T(8,128)(2,1)} %collective-permute-done.16.refs_2_), channel_id=1, source_target_pairs={{0,24},{8,16},{16,8},{24,0},{1,25},{9,17},{17,9},{25,1},{2,26},{10... | collective-permute-start | bytes 786440 | tf_op jit(solution)/shard_map/ppermute | solution.py:825
  48.6 91.8 %collective-permute-start.20 = (bf16[1024,512]{1,0:T(8,128)(2,1)S(1)}, bf16[1024,512]{1,0:T(8,128)(2,1)S(1)}, u32[]{:S(2)}, u32[]{:S(2)}) collective-permute-start(bf16[1024,512]{1,0:T(8,128)(2,1)S(1)} %copy-done.10), channel_id=1, source_target_pairs={{0,1},{1,0},{2,3},{3,2},{4,5},{5,4},{6,7},{7,6},{8,9},{9,8},{10,11... | collective-permute-start | bytes 3145736 | tf_op jit(solution)/shard_map/ppermute | solution.py:816
  49.7 25.8 %collective-permute-start.12 = (bf16[128,1024]{1,0:T(8,128)(2,1)S(1)}, bf16[128,1024]{1,0:T(8,128)(2,1)S(1)}, u32[]{:S(2)}, u32[]{:S(2)}) collective-permute-start(bf16[128,1024]{1,0:T(8,128)(2,1)S(1)} %pad_maximum_fusion.15.refs_2_), channel_id=1, source_target_pairs={{0,4},{2,6},{4,0},{6,2},{1,5},{3,7},{5,1},{7,3},{8,12},{10,14},{12... | collective-permute-start | bytes 786440 | tf_op jit(solution)/shard_map/ppermute | solution.py:819
  52.1 45.5 %collective-permute-start.10 = (bf16[128,1024]{1,0:T(8,128)(2,1)}, bf16[128,1024]{1,0:T(8,128)(2,1)}, u32[]{:S(2)}, u32[]{:S(2)}) collective-permute-start(bf16[128,1024]{1,0:T(8,128)(2,1)} %collective-permute-done.8.refs_2_), channel_id=1, source_target_pairs={{0,16},{8,24},{16,0},{24,8},{1,17},{9,25},{17,1},{25,9},{2,18},{10... | collective-permute-start | bytes 786440 | tf_op jit(solution)/shard_map/ppermute | solution.py:825
  54.9 7.5 %collective-permute-start.23 = (bf16[64,1024]{1,0:T(8,128)(2,1)S(1)}, bf16[64,1024]{1,0:T(8,128)(2,1)S(1)}, u32[]{:S(2)}, u32[]{:S(2)}) collective-permute-start(bf16[64,1024]{1,0:T(8,128)(2,1)S(1)} %maximum_add_fusion.refs_3_), channel_id=1, source_target_pairs={{0,2},{2,4},{4,6},{6,0},{1,3},{3,5},{5,7},{7,1},{8,10},{10,12},{12... | collective-permute-start | bytes 393224 | tf_op jit(solution)/shard_map/ppermute | solution.py:819
  62.4 11.6 %collective-permute-start.24 = (bf16[64,1024]{1,0:T(8,128)(2,1)S(1)}, bf16[64,1024]{1,0:T(8,128)(2,1)S(1)}, u32[]{:S(2)}, u32[]{:S(2)}) collective-permute-start(bf16[64,1024]{1,0:T(8,128)(2,1)S(1)} %maximum_add_fusion.refs_3_), channel_id=1, source_target_pairs={{0,4},{2,6},{4,0},{6,2},{1,5},{3,7},{5,1},{7,3},{8,12},{10,14},{12... | collective-permute-start | bytes 393224 | tf_op jit(solution)/shard_map/ppermute | solution.py:819
  67.3 8.8 %collective-permute-start.25 = (bf16[64,1024]{1,0:T(8,128)(2,1)S(1)}, bf16[64,1024]{1,0:T(8,128)(2,1)S(1)}, u32[]{:S(2)}, u32[]{:S(2)}) collective-permute-start(bf16[64,1024]{1,0:T(8,128)(2,1)S(1)} %maximum_add_fusion.refs_3_), channel_id=1, source_target_pairs={{0,6},{2,0},{4,2},{6,4},{1,7},{3,1},{5,3},{7,5},{8,14},{10,8},{12,... | collective-permute-start | bytes 393224 | tf_op jit(solution)/shard_map/ppermute | solution.py:819
  75.5 23.7 %collective-permute-start.11 = (bf16[128,1024]{1,0:T(8,128)(2,1)}, bf16[128,1024]{1,0:T(8,128)(2,1)}, u32[]{:S(2)}, u32[]{:S(2)}) collective-permute-start(bf16[128,1024]{1,0:T(8,128)(2,1)} %collective-permute-done.8.refs_2_), channel_id=1, source_target_pairs={{0,24},{8,16},{16,8},{24,0},{1,25},{9,17},{17,9},{25,1},{2,26},{10... | collective-permute-start | bytes 786440 | tf_op jit(solution)/shard_map/ppermute | solution.py:825
  76.1 24.6 %collective-permute-start.9 = (bf16[128,1024]{1,0:T(8,128)(2,1)}, bf16[128,1024]{1,0:T(8,128)(2,1)}, u32[]{:S(2)}, u32[]{:S(2)}) collective-permute-start(bf16[128,1024]{1,0:T(8,128)(2,1)} %collective-permute-done.8.refs_2_), channel_id=1, source_target_pairs={{0,8},{8,0},{16,24},{24,16},{1,9},{9,1},{17,25},{25,17},{2,10},{10... | collective-permute-start | bytes 786440 | tf_op jit(solution)/shard_map/ppermute | solution.py:825
  77.6 31.3 %collective-permute-start.17 = (bf16[128,1024]{1,0:T(8,128)(2,1)}, bf16[128,1024]{1,0:T(8,128)(2,1)}, u32[]{:S(2)}, u32[]{:S(2)}) collective-permute-start(bf16[128,1024]{1,0:T(8,128)(2,1)} %collective-permute-done.16.refs_2_), channel_id=1, source_target_pairs={{0,8},{8,0},{16,24},{24,16},{1,9},{9,1},{17,25},{25,17},{2,10},{10... | collective-permute-start | bytes 786440 | tf_op jit(solution)/shard_map/ppermute | solution.py:825
  97.6 26.3 %collective-permute-start.13 = (bf16[128,1024]{1,0:T(8,128)(2,1)S(1)}, bf16[128,1024]{1,0:T(8,128)(2,1)}, u32[]{:S(2)}, u32[]{:S(2)}) collective-permute-start(bf16[128,1024]{1,0:T(8,128)(2,1)S(1)} %copy-done.39), channel_id=1, source_target_pairs={{0,8},{8,0},{16,24},{24,16},{1,9},{9,1},{17,25},{25,17},{2,10},{10... | collective-permute-start | bytes 786440 | tf_op jit(solution)/shard_map/ppermute | solution.py:825
  99.2 26.3 %collective-permute-start.14 = (bf16[128,1024]{1,0:T(8,128)(2,1)S(1)}, bf16[128,1024]{1,0:T(8,128)(2,1)}, u32[]{:S(2)}, u32[]{:S(2)}) collective-permute-start(bf16[128,1024]{1,0:T(8,128)(2,1)S(1)} %copy-done.39), channel_id=1, source_target_pairs={{0,16},{8,24},{16,0},{24,8},{1,17},{9,25},{17,1},{25,9},{2,18},{10... | collective-permute-start | bytes 786440 | tf_op jit(solution)/shard_map/ppermute | solution.py:825
  100.7 14.6 %collective-permute-start.18 = (bf16[128,1024]{1,0:T(8,128)(2,1)}, bf16[128,1024]{1,0:T(8,128)(2,1)}, u32[]{:S(2)}, u32[]{:S(2)}) collective-permute-start(bf16[128,1024]{1,0:T(8,128)(2,1)} %collective-permute-done.16.refs_2_), channel_id=1, source_target_pairs={{0,16},{8,24},{16,0},{24,8},{1,17},{9,25},{17,1},{25,9},{2,18},{10... | collective-permute-start | bytes 786440 | tf_op jit(solution)/shard_map/ppermute | solution.py:825
  108.9 17.7 %collective-permute-start.15 = (bf16[128,1024]{1,0:T(8,128)(2,1)S(1)}, bf16[128,1024]{1,0:T(8,128)(2,1)}, u32[]{:S(2)}, u32[]{:S(2)}) collective-permute-start(bf16[128,1024]{1,0:T(8,128)(2,1)S(1)} %copy-done.39), channel_id=1, source_target_pairs={{0,24},{8,16},{16,8},{24,0},{1,25},{9,17},{17,9},{25,1},{2,26},{10... | collective-permute-start | bytes 786440 | tf_op jit(solution)/shard_map/ppermute | solution.py:825
  115.3 26.5 %collective-permute-start.26 = (bf16[192,1024]{1,0:T(8,128)(2,1)S(1)}, bf16[192,1024]{1,0:T(8,128)(2,1)}, u32[]{:S(2)}, u32[]{:S(2)}) collective-permute-start(bf16[192,1024]{1,0:T(8,128)(2,1)S(1)} %constant_dynamic-update-slice_fusion.refs_7_), channel_id=1, source_target_pairs={{0,8},{8,0},{16,24},{24,16},{1,9},{9,1},{17,25},{25,17},{2,10},{10... | collective-permute-start | bytes 1179656 | tf_op jit(solution)/shard_map/ppermute | solution.py:825
  123.9 34.6 %collective-permute-start.27 = (bf16[192,1024]{1,0:T(8,128)(2,1)S(1)}, bf16[192,1024]{1,0:T(8,128)(2,1)}, u32[]{:S(2)}, u32[]{:S(2)}) collective-permute-start(bf16[192,1024]{1,0:T(8,128)(2,1)S(1)} %constant_dynamic-update-slice_fusion.refs_7_), channel_id=1, source_target_pairs={{0,16},{8,24},{16,0},{24,8},{1,17},{9,25},{17,1},{25,9},{2,18},{10... | collective-permute-start | bytes 1179656 | tf_op jit(solution)/shard_map/ppermute | solution.py:825
  125.5 33.1 %collective-permute-start.28 = (bf16[192,1024]{1,0:T(8,128)(2,1)S(1)}, bf16[192,1024]{1,0:T(8,128)(2,1)}, u32[]{:S(2)}, u32[]{:S(2)}) collective-permute-start(bf16[192,1024]{1,0:T(8,128)(2,1)S(1)} %constant_dynamic-update-slice_fusion.refs_7_), channel_id=1, source_target_pairs={{0,24},{8,16},{16,8},{24,0},{1,25},{9,17},{17,9},{25,1},{2,26},{10... | collective-permute-start | bytes 1179656 | tf_op jit(solution)/shard_map/ppermute | solution.py:825
  137.0 28.6 %collective-permute-start.29 = (bf16[1040,128]{1,0:T(8,128)(2,1)}, bf16[1040,128]{1,0:T(8,128)(2,1)}, u32[]{:S(2)}, u32[]{:S(2)}) collective-permute-start(bf16[1040,128]{1,0:T(8,128)(2,1)} %constant_dynamic-update-slice_fusion.3), channel_id=1, source_target_pairs={{0,2},{2,4},{4,6},{1,3},{3,5},{5,7},{8,10},{10,12},{12,14},{9,11},... | collective-permute-start | bytes 798728 | tf_op jit(solution)/shard_map/ppermute | solution.py:822
  140.4 25.1 %collective-permute-start.30 = (bf16[1040,128]{1,0:T(8,128)(2,1)}, bf16[1040,128]{1,0:T(8,128)(2,1)S(1)}, u32[]{:S(2)}, u32[]{:S(2)}) collective-permute-start(bf16[1040,128]{1,0:T(8,128)(2,1)} %constant_dynamic-update-slice_fusion.3), channel_id=1, source_target_pairs={{0,4},{2,6},{1,5},{3,7},{8,12},{10,14},{9,13},{11,15},{16,20},{18,... | collective-permute-start | bytes 798728 | tf_op jit(solution)/shard_map/ppermute | solution.py:822
  141.7 23.8 %collective-permute-start.31 = (bf16[1040,128]{1,0:T(8,128)(2,1)}, bf16[1040,128]{1,0:T(8,128)(2,1)S(1)}, u32[]{:S(2)}, u32[]{:S(2)}) collective-permute-start(bf16[1040,128]{1,0:T(8,128)(2,1)} %constant_dynamic-update-slice_fusion.3), channel_id=1, source_target_pairs={{0,6},{1,7},{8,14},{9,15},{16,22},{17,23},{24,30},{25,31}} | collective-permute-start | bytes 798728 | tf_op jit(solution)/shard_map/ppermute | solution.py:822
  206.4 32.2 %collective-permute-start.34 = (bf16[1040,128]{1,0:T(8,128)(2,1)S(1)}, bf16[1040,128]{1,0:T(8,128)(2,1)S(1)}, u32[]{:S(2)}, u32[]{:S(2)}) collective-permute-start(bf16[1040,128]{1,0:T(8,128)(2,1)S(1)} %constant_dynamic-update-slice_fusion.8), channel_id=1, source_target_pairs={{2,0},{4,2},{6,4},{3,1},{5,3},{7,5},{10,8},{12,10},{14,12},{11,9},... | collective-permute-start | bytes 798728 | tf_op jit(solution)/shard_map/ppermute | solution.py:822
  207.7 33.4 %collective-permute-start.35 = (bf16[1040,128]{1,0:T(8,128)(2,1)S(1)}, bf16[1040,128]{1,0:T(8,128)(2,1)S(1)}, u32[]{:S(2)}, u32[]{:S(2)}) collective-permute-start(bf16[1040,128]{1,0:T(8,128)(2,1)S(1)} %constant_dynamic-update-slice_fusion.8), channel_id=1, source_target_pairs={{4,0},{6,2},{5,1},{7,3},{12,8},{14,10},{13,9},{15,11},{20,16},{22,... | collective-permute-start | bytes 798728 | tf_op jit(solution)/shard_map/ppermute | solution.py:822
  209.0 32.1 %collective-permute-start.36 = (bf16[1040,128]{1,0:T(8,128)(2,1)S(1)}, bf16[1040,128]{1,0:T(8,128)(2,1)S(1)}, u32[]{:S(2)}, u32[]{:S(2)}) collective-permute-start(bf16[1040,128]{1,0:T(8,128)(2,1)S(1)} %constant_dynamic-update-slice_fusion.8), channel_id=1, source_target_pairs={{6,0},{7,1},{14,8},{15,9},{22,16},{23,17},{30,24},{31,25}} | collective-permute-start | bytes 798728 | tf_op jit(solution)/shard_map/ppermute | solution.py:822
  219.7 63.7 %collective-permute-start.37 = (bf16[4,128,1024]{2,1,0:T(8,128)(2,1)}, bf16[4,128,1024]{2,1,0:T(8,128)(2,1)S(1)}, u32[]{:S(2)}, u32[]{:S(2)}) collective-permute-start(bf16[4,128,1024]{2,1,0:T(8,128)(2,1)} %get-tuple-element.217), channel_id=1, source_target_pairs={{0,8},{8,0},{16,24},{24,16},{1,9},{9,1},{17,25},{25,17},{2,10},{10... | collective-permute-start | bytes 3145736 | tf_op jit(solution)/shard_map/ppermute | solution.py:825
  220.8 62.6 %collective-permute-start.38 = (bf16[4,128,1024]{2,1,0:T(8,128)(2,1)}, bf16[4,128,1024]{2,1,0:T(8,128)(2,1)}, u32[]{:S(2)}, u32[]{:S(2)}) collective-permute-start(bf16[4,128,1024]{2,1,0:T(8,128)(2,1)} %get-tuple-element.218), channel_id=1, source_target_pairs={{0,16},{8,24},{16,0},{24,8},{1,17},{9,25},{17,1},{25,9},{2,18},{10... | collective-permute-start | bytes 3145736 | tf_op jit(solution)/shard_map/ppermute | solution.py:825
  238.6 44.7 %collective-permute-start.39 = (bf16[4,128,1024]{2,1,0:T(8,128)(2,1)}, bf16[4,128,1024]{2,1,0:T(8,128)(2,1)}, u32[]{:S(2)}, u32[]{:S(2)}) collective-permute-start(bf16[4,128,1024]{2,1,0:T(8,128)(2,1)} %get-tuple-element.219), channel_id=1, source_target_pairs={{0,24},{8,16},{16,8},{24,0},{1,25},{9,17},{17,9},{25,1},{2,26},{10... | collective-permute-start | bytes 3145736 | tf_op jit(solution)/shard_map/ppermute | solution.py:825
  263.5 9.7 %collective-permute-start.59 = (bf16[128,1024]{1,0:T(8,128)(2,1)}, bf16[128,1024]{1,0:T(8,128)(2,1)S(1)}, u32[]{:S(2)}, u32[]{:S(2)}) collective-permute-start(bf16[128,1024]{1,0:T(8,128)(2,1)} %get-tuple-element.257), channel_id=1, source_target_pairs={{0,8},{8,0},{16,24},{24,16},{1,9},{9,1},{17,25},{25,17},{2,10},{10... | collective-permute-start | bytes 786440 | tf_op jit(solution)/shard_map/ppermute | solution.py:825
  265.7 13.7 %collective-permute-start.60 = (bf16[128,1024]{1,0:T(8,128)(2,1)}, bf16[128,1024]{1,0:T(8,128)(2,1)}, u32[]{:S(2)}, u32[]{:S(2)}) collective-permute-start(bf16[128,1024]{1,0:T(8,128)(2,1)} %get-tuple-element.258), channel_id=1, source_target_pairs={{0,16},{8,24},{16,0},{24,8},{1,17},{9,25},{17,1},{25,9},{2,18},{10... | collective-permute-start | bytes 786440 | tf_op jit(solution)/shard_map/ppermute | solution.py:825
  273.2 8.8 %collective-permute-start.61 = (bf16[128,1024]{1,0:T(8,128)(2,1)}, bf16[128,1024]{1,0:T(8,128)(2,1)}, u32[]{:S(2)}, u32[]{:S(2)}) collective-permute-start(bf16[128,1024]{1,0:T(8,128)(2,1)} %get-tuple-element.259), channel_id=1, source_target_pairs={{0,24},{8,16},{16,8},{24,0},{1,25},{9,17},{17,9},{25,1},{2,26},{10... | collective-permute-start | bytes 786440 | tf_op jit(solution)/shard_map/ppermute | solution.py:825
  315.2 20.4 %collective-permute-start.56 = (bf16[208,1024]{1,0:T(8,128)(2,1)}, bf16[208,1024]{1,0:T(8,128)(2,1)S(1)}, u32[]{:S(2)}, u32[]{:S(2)}) collective-permute-start(bf16[208,1024]{1,0:T(8,128)(2,1)} %get-tuple-element.253), channel_id=1, source_target_pairs={{0,8},{8,0},{16,24},{24,16},{1,9},{9,1},{17,25},{25,17},{2,10},{10... | collective-permute-start | bytes 1277960 | tf_op jit(solution)/shard_map/ppermute | solution.py:825
  316.4 19.9 %collective-permute-start.57 = (bf16[208,1024]{1,0:T(8,128)(2,1)}, bf16[208,1024]{1,0:T(8,128)(2,1)S(1)}, u32[]{:S(2)}, u32[]{:S(2)}) collective-permute-start(bf16[208,1024]{1,0:T(8,128)(2,1)} %get-tuple-element.254), channel_id=1, source_target_pairs={{0,16},{8,24},{16,0},{24,8},{1,17},{9,25},{17,1},{25,9},{2,18},{10... | collective-permute-start | bytes 1277960 | tf_op jit(solution)/shard_map/ppermute | solution.py:825
  316.5 19.8 %collective-permute-start.58 = (bf16[208,1024]{1,0:T(8,128)(2,1)}, bf16[208,1024]{1,0:T(8,128)(2,1)}, u32[]{:S(2)}, u32[]{:S(2)}) collective-permute-start(bf16[208,1024]{1,0:T(8,128)(2,1)} %get-tuple-element.255), channel_id=1, source_target_pairs={{0,24},{8,16},{16,8},{24,0},{1,25},{9,17},{17,9},{25,1},{2,26},{10... | collective-permute-start | bytes 1277960 | tf_op jit(solution)/shard_map/ppermute | solution.py:825
  318.8 23.5 %collective-permute-start.49 = (bf16[128,1024]{1,0:T(8,128)(2,1)}, bf16[128,1024]{1,0:T(8,128)(2,1)}, u32[]{:S(2)}, u32[]{:S(2)}) collective-permute-start(bf16[128,1024]{1,0:T(8,128)(2,1)} %get-tuple-element.346), channel_id=1, source_target_pairs={{0,6},{2,0},{4,2},{6,4},{1,7},{3,1},{5,3},{7,5},{8,14},{10,8},{12,... | collective-permute-start | bytes 786440 | tf_op jit(solution)/shard_map/ppermute | solution.py:819
  323.2 19.1 %collective-permute-start.50 = (bf16[128,1024]{1,0:T(8,128)(2,1)}, bf16[128,1024]{1,0:T(8,128)(2,1)}, u32[]{:S(2)}, u32[]{:S(2)}) collective-permute-start(bf16[128,1024]{1,0:T(8,128)(2,1)} %get-tuple-element.348), channel_id=1, source_target_pairs={{0,4},{2,6},{4,0},{6,2},{1,5},{3,7},{5,1},{7,3},{8,12},{10,14},{12... | collective-permute-start | bytes 786440 | tf_op jit(solution)/shard_map/ppermute | solution.py:819
  335.6 9.2 %collective-permute-start.51 = (bf16[128,1024]{1,0:T(8,128)(2,1)S(1)}, bf16[128,1024]{1,0:T(8,128)(2,1)S(1)}, u32[]{:S(2)}, u32[]{:S(2)}) collective-permute-start(bf16[128,1024]{1,0:T(8,128)(2,1)S(1)} %copy-done.44), channel_id=1, source_target_pairs={{0,2},{2,4},{4,6},{6,0},{1,3},{3,5},{5,7},{7,1},{8,10},{10,12},{12... | collective-permute-start | bytes 786440 | tf_op jit(solution)/shard_map/ppermute | solution.py:819
  336.3 4.9 %collective-permute-start.41 = (f32[16,512]{1,0:T(8,128)S(1)}, f32[16,512]{1,0:T(8,128)S(1)}, u32[]{:S(2)}, u32[]{:S(2)}) collective-permute-start(f32[16,512]{1,0:T(8,128)S(1)} %slice.212), channel_id=1, source_target_pairs={{0,1},{1,0},{2,3},{3,2},{4,5},{5,4},{6,7},{7,6},{8,9},{9,8},{10,11... | collective-permute-start | bytes 98312 | tf_op jit(solution)/shard_map/ppermute | solution.py:816
  337.8 12.4 %collective-permute-start.62 = (bf16[144,1024]{1,0:T(8,128)(2,1)S(1)}, bf16[144,1024]{1,0:T(8,128)(2,1)S(1)}, u32[]{:S(2)}, u32[]{:S(2)}) collective-permute-start(bf16[144,1024]{1,0:T(8,128)(2,1)S(1)} %get-tuple-element.373), channel_id=1, source_target_pairs={{0,6},{2,0},{4,2},{6,4},{1,7},{3,1},{5,3},{7,5},{8,14},{10,8},{12,... | collective-permute-start | bytes 884744 | tf_op jit(solution)/shard_map/ppermute | solution.py:819
  341.1 28.5 %collective-permute-start.63 = (bf16[144,1024]{1,0:T(8,128)(2,1)S(1)}, bf16[144,1024]{1,0:T(8,128)(2,1)S(1)}, u32[]{:S(2)}, u32[]{:S(2)}) collective-permute-start(bf16[144,1024]{1,0:T(8,128)(2,1)S(1)} %get-tuple-element.374), channel_id=1, source_target_pairs={{0,4},{2,6},{4,0},{6,2},{1,5},{3,7},{5,1},{7,3},{8,12},{10,14},{12... | collective-permute-start | bytes 884744 | tf_op jit(solution)/shard_map/ppermute | solution.py:819
  342.2 27.6 %collective-permute-start.64 = (bf16[144,1024]{1,0:T(8,128)(2,1)S(1)}, bf16[144,1024]{1,0:T(8,128)(2,1)S(1)}, u32[]{:S(2)}, u32[]{:S(2)}) collective-permute-start(bf16[144,1024]{1,0:T(8,128)(2,1)S(1)} %get-tuple-element.375), channel_id=1, source_target_pairs={{0,2},{2,4},{4,6},{6,0},{1,3},{3,5},{5,7},{7,1},{8,10},{10,12},{12... | collective-permute-start | bytes 884744 | tf_op jit(solution)/shard_map/ppermute | solution.py:819
  342.4 57.0 %collective-permute-start.40 = (bf16[1024,512]{1,0:T(8,128)(2,1)S(1)}, bf16[1024,512]{1,0:T(8,128)(2,1)S(1)}, u32[]{:S(2)}, u32[]{:S(2)}) collective-permute-start(bf16[1024,512]{1,0:T(8,128)(2,1)S(1)} %copy-done.76), channel_id=1, source_target_pairs={{0,1},{1,0},{2,3},{3,2},{4,5},{5,4},{6,7},{7,6},{8,9},{9,8},{10,11... | collective-permute-start | bytes 3145736 | tf_op jit(solution)/shard_map/ppermute | solution.py:816
  344.9 54.5 %collective-permute-start.42 = (f32[16,512]{1,0:T(8,128)S(1)}, f32[16,512]{1,0:T(8,128)S(1)}, u32[]{:S(2)}, u32[]{:S(2)}) collective-permute-start(f32[16,512]{1,0:T(8,128)S(1)} %slice_add_fusion.1), channel_id=1, source_target_pairs={{2,0},{4,2},{6,4},{3,1},{5,3},{7,5},{10,8},{12,10},{14,12},{11,9},... | collective-permute-start | bytes 98312 | tf_op jit(solution)/shard_map/ppermute | solution.py:822
  350.2 22.1 %collective-permute-start.52 = (bf16[128,1024]{1,0:T(8,128)(2,1)S(1)}, bf16[128,1024]{1,0:T(8,128)(2,1)S(1)}, u32[]{:S(2)}, u32[]{:S(2)}) collective-permute-start(bf16[128,1024]{1,0:T(8,128)(2,1)S(1)} %fusion.16), channel_id=1, source_target_pairs={{0,8},{8,0},{16,24},{24,16},{1,9},{9,1},{17,25},{25,17},{2,10},{10... | collective-permute-start | bytes 786440 | tf_op jit(solution)/shard_map/ppermute | solution.py:825
  369.6 13.5 %collective-permute-start.53 = (bf16[128,1024]{1,0:T(8,128)(2,1)S(1)}, bf16[128,1024]{1,0:T(8,128)(2,1)S(1)}, u32[]{:S(2)}, u32[]{:S(2)}) collective-permute-start(bf16[128,1024]{1,0:T(8,128)(2,1)S(1)} %fusion.16), channel_id=1, source_target_pairs={{0,16},{8,24},{16,0},{24,8},{1,17},{9,25},{17,1},{25,9},{2,18},{10... | collective-permute-start | bytes 786440 | tf_op jit(solution)/shard_map/ppermute | solution.py:825
  369.9 13.5 %collective-permute-start.54 = (bf16[128,1024]{1,0:T(8,128)(2,1)S(1)}, bf16[128,1024]{1,0:T(8,128)(2,1)S(1)}, u32[]{:S(2)}, u32[]{:S(2)}) collective-permute-start(bf16[128,1024]{1,0:T(8,128)(2,1)S(1)} %fusion.16), channel_id=1, source_target_pairs={{0,24},{8,16},{16,8},{24,0},{1,25},{9,17},{17,9},{25,1},{2,26},{10... | collective-permute-start | bytes 786440 | tf_op jit(solution)/shard_map/ppermute | solution.py:825
  372.3 14.6 %collective-permute-start.65 = (bf16[144,1024]{1,0:T(8,128)(2,1)S(1)}, bf16[144,1024]{1,0:T(8,128)(2,1)S(1)}, u32[]{:S(2)}, u32[]{:S(2)}) collective-permute-start(bf16[144,1024]{1,0:T(8,128)(2,1)S(1)} %fusion.10), channel_id=1, source_target_pairs={{0,8},{8,0},{16,24},{24,16},{1,9},{9,1},{17,25},{25,17},{2,10},{10... | collective-permute-start | bytes 884744 | tf_op jit(solution)/shard_map/ppermute | solution.py:825
  383.1 14.3 %collective-permute-start.66 = (bf16[144,1024]{1,0:T(8,128)(2,1)S(1)}, bf16[144,1024]{1,0:T(8,128)(2,1)S(1)}, u32[]{:S(2)}, u32[]{:S(2)}) collective-permute-start(bf16[144,1024]{1,0:T(8,128)(2,1)S(1)} %fusion.10), channel_id=1, source_target_pairs={{0,16},{8,24},{16,0},{24,8},{1,17},{9,25},{17,1},{25,9},{2,18},{10... | collective-permute-start | bytes 884744 | tf_op jit(solution)/shard_map/ppermute | solution.py:825
  383.4 14.0 %collective-permute-start.67 = (bf16[144,1024]{1,0:T(8,128)(2,1)S(1)}, bf16[144,1024]{1,0:T(8,128)(2,1)S(1)}, u32[]{:S(2)}, u32[]{:S(2)}) collective-permute-start(bf16[144,1024]{1,0:T(8,128)(2,1)S(1)} %fusion.10), channel_id=1, source_target_pairs={{0,24},{8,16},{16,8},{24,0},{1,25},{9,17},{17,9},{25,1},{2,26},{10... | collective-permute-start | bytes 884744 | tf_op jit(solution)/shard_map/ppermute | solution.py:825
  386.9 16.0 %collective-permute-start.55 = (bf16[4,128,512]{2,1,0:T(8,128)(2,1)}, bf16[4,128,512]{2,1,0:T(8,128)(2,1)}, u32[]{:S(2)}, u32[]{:S(2)}) collective-permute-start(bf16[4,128,512]{2,1,0:T(8,128)(2,1)} %slice.219), channel_id=1, source_target_pairs={{0,1},{1,0},{2,3},{3,2},{4,5},{5,4},{6,7},{7,6},{8,9},{9,8},{10,11... | collective-permute-start | bytes 1572872 | tf_op jit(solution)/shard_map/ppermute | solution.py:816
  399.4 26.8 %collective-permute-start.68 = (bf16[4,144,512]{2,1,0:T(8,128)(2,1)}, bf16[4,144,512]{2,1,0:T(8,128)(2,1)}, u32[]{:S(2)}, u32[]{:S(2)}) collective-permute-start(bf16[4,144,512]{2,1,0:T(8,128)(2,1)} %slice.226), channel_id=1, source_target_pairs={{0,1},{1,0},{2,3},{3,2},{4,5},{5,4},{6,7},{7,6},{8,9},{9,8},{10,11... | collective-permute-start | bytes 1769480 | tf_op jit(solution)/shard_map/ppermute | solution.py:816
  402.4 10.3 %collective-permute-start.43 = (f32[1024,1]{0,1:T(1,128)S(1)}, f32[1024,1]{0,1:T(1,128)S(1)}, u32[]{:S(2)}, u32[]{:S(2)}) collective-permute-start(f32[1024,1]{0,1:T(1,128)S(1)} %bitcast.135), channel_id=1, source_target_pairs={{0,1},{1,0},{2,3},{3,2},{4,5},{5,4},{6,7},{7,6},{8,9},{9,8},{10,11... | collective-permute-start | bytes 12296 | tf_op jit(solution)/shard_map/ppermute | solution.py:816
  404.3 4.2 collective-permute-start.45
  408.5 4.2 collective-permute-start.46
  416.9 5.5 %collective-permute-start.48 = (f32[12384]{0:T(1024)S(1)}, f32[12384]{0:T(1024)S(1)}, u32[]{:S(2)}, u32[]{:S(2)}) collective-permute-start(f32[12384]{0:T(1024)S(1)} %add.284), channel_id=1, source_target_pairs={{0,4},{2,6},{4,0},{6,2},{1,5},{3,7},{5,1},{7,3},{8,12},{10,14},{12... | collective-permute-start | bytes 148616 | tf_op jit(solution)/shard_map/ppermute | solution.py:1258
  (83 other events, 774.5 us)

commit v3 on v2

--- a/solution.py
+++ b/solution.py
@@ -226,6 +226,7 @@
 Q = 128
 HALO = 16
 NEG = -1e30
+MESH = pl.DeviceIdType.MESH
 VMEM = 60 * 1024 * 1024
 
 
@@ -269,20 +270,77 @@
     return {"ge": row >= col, "le": row <= col, "gt": row > col}[kind]
 
 
+def slot_heads(heads, per):
+    nz = heads // per
+    own = HEADS // nz
+    bits = per.bit_length() - 1
+    slot = lax.broadcasted_iota(jnp.int32, (heads, HEADS), 0)
+    head = lax.broadcasted_iota(jnp.int32, (heads, HEADS), 1)
+    z = (lax.axis_index("head") - (slot >> bits)) & (nz - 1)
+    m = (slot & (per - 1)) ^ lax.axis_index("dp")
+    return (head == z * own + lax.axis_index("width") * per + m).astype(F32)
+
+
+def prep_kernel(
+    per, zx, ow, bcdt, gain, cx, scal, gn,
+    first_o, first2_o, rest_o, rest2_o, out_o, out2_o, bcdt_o, table_o,
+):
+    di = lax.axis_index("dp")
+    wi = lax.axis_index("width")
+    wide = 2 * HEADDIM
+    for m in range(per):
+        for w, whole_o, some_o, o_o in (
+            (wi, first_o, rest_o, out_o), (1 - wi, first2_o, rest2_o, out2_o)
+        ):
+            head = w * per + jnp.bitwise_xor(di, m)
+            v = jnp.transpose(zx[:, pl.ds(pl.multiple_of(head * wide, wide), wide)])
+            if m == 0:
+                whole_o[...] = v
+            else:
+                some_o[m - 1] = v
+            o_o[m] = ow[pl.ds(pl.multiple_of(head * HEADDIM, HEADDIM), HEADDIM), :]
+    n = bcdt.shape[1]
+    bcdt_o[0:n, :] = jnp.transpose(bcdt[...])
+    bcdt_o[n:, :] = jnp.broadcast_to(gain[...], (HALO, gain.shape[1]))
+    rows = jnp.concatenate(
+        [cx[...].astype(F32), gn[...].astype(F32), scal[...]], axis=0
+    )
+    half = rows.shape[1] // 2
+    rows = jnp.where(wi == 0, rows[:, :half], rows[:, half:])
+    step = 1
+    while step < per:
+        size = HEADDIM * step
+        parts = [rows[:, i * size : (i + 1) * size] for i in range(half // size)]
+        swapped = jnp.concatenate([parts[i ^ 1] for i in range(len(parts))], axis=1)
+        rows = jnp.where(jnp.bitwise_and(di, step) != 0, swapped, rows)
+        step *= 2
+    table_o[...] = rows
+
+
 def entry_kernel(
-    hm, ho, hh, gain, wbc, wdt, cbc, bias, rate,
+    per, hm, ho, hh, bcdt, table, cbc, sel,
     xn_o, xnh_o, r_o, raw_o, rawh_o, u_o, b_o, c_o, dt_o, sig_o, cl_o, clt_o, tot_o,
-    dt2_o, e12_o, tl2_o, dttl2_o, ec2_o, edt2_o, buf,
+    dt2_o, e12_o, tl2_o, dttl2_o, ec2_o, edt2_o, rate_o, wdt_o, buf,
 ):
     rows = hm.shape[0]
     state = b_o.shape[1]
+    per_head = dot(table[...], sel[...], HIGH)
+    bias = per_head[5:6, :]
+    rate = -jnp.exp(per_head[6:7, :])
+    rate_o[...] = rate
+    wbc = bcdt.at[0 : 2 * state, :]
+    wdt_o[...] = dot(
+        slot_heads(rate.shape[1], per).astype(BF), bcdt[2 * state : 2 * state + HEADS, :]
+    ).astype(BF)
+    wdt = wdt_o
+    gain = bcdt[2 * state + HEADS : 2 * state + HEADS + 1, :].astype(F32)
     blocks = rows // Q
     lower = tri("ge").astype(F32)
 
     def norm(left, right):
         h = jnp.concatenate([left, right], axis=1).astype(F32)
         r = lax.rsqrt(jnp.mean(h * h, axis=1, keepdims=True) + EPS)
-        return (h * r * gain[...]).astype(BF), r
+        return (h * r * gain).astype(BF), r
 
     half = hm.shape[1]
     xnh, _ = norm(hh[:, :half], hh[:, half:])
@@ -298,11 +356,11 @@
         raw = dot_t(xn, wbc[...])
         raw_o[here, :] = raw
         buf[pl.ds(pl.multiple_of(HALO + i * Q, HALO), Q), :] = raw
-        steps = dot_t(xn, wdt[...]) + bias[...]
+        steps = dot_t(xn, wdt[...]) + bias
         dt = jax.nn.softplus(steps)
         dt_o[here, :] = dt
         sig_o[here, :] = sigmoid(steps)
-        da = dt * rate[...]
+        da = dt * rate
         cl_o[here, :] = dot(lower, da, HIGH)
         clt_o[:, here] = lax.dot_general(
             da, lower, (((0,), (1,)), ((), ())), precision=HIGH, preferred_element_type=F32
@@ -366,7 +424,7 @@
 
 def project_kernel(s, per, *refs):
     xn, xnh, pieces, cw, dt2, edt2, ex, b, rest = take(refs, 0, 0, per, 0, 0, 0, 0, 0)
-    wz_o, wx_o, z_o, xr_o, xrh_o, u_o, xs_o, xdt_o, s_o, buf, acc = rest
+    wz_o, wx_o, z_o, xr_o, xrh_o, u_o, xdt_o, s_o, buf, acc = rest
     rows = z_o.shape[0]
     gc = per * HEADDIM
     cols = slice(s * gc, s * gc + gc)
@@ -394,10 +452,9 @@
         u = jnp.zeros((Q, gc), F32)
         for k in range(4):
             u = u + cw[k : k + 1, cols] * win[HALO - 3 + k : HALO - 3 + k + Q, :]
-        xr_o[here, :] = win[HALO:, :]
+        xr_o[here, :] = win[HALO:, :].astype(BF)
         u_o[here, :] = u
         xs = u * sigmoid(u)
-        xs_o[here, :] = xs
         xdt_o[here, :] = (xs * dot(dt2[here, :], ex[:, cols])).astype(BF)
         acc[...] += t_dot((xs * dot(edt2[here, :], ex[:, cols])).astype(BF), b[here, :])
 
@@ -420,7 +477,7 @@
             x = xdt[rows, here]
             y_o[rows, here] = dot(
                 jnp.concatenate(ws, axis=1), jnp.concatenate([x * low, x * high], axis=0)
-            )
+            ).astype(BF)
 
 
 def head_scale(clt, first, per, state):
@@ -433,7 +490,7 @@
     )
 
 
-def from_messages(messages, sign, groups, per, state, store):
+def from_messages(messages, sign, groups, per, state, store, valid=None):
     nz = len(messages) + 1
     gc = per * HEADDIM
     top = nz * gc
@@ -450,14 +507,17 @@
                 [jnp.broadcast_to(scale[h : h + 1, :], (HEADDIM, state)) for h in range(per)],
                 axis=0,
             )
-            total = total + scale * messages[k - 1][there * gc : there * gc + gc, :].astype(F32)
+            part = scale * messages[k - 1][there * gc : there * gc + gc, :].astype(F32)
+            if valid is not None:
+                part = jnp.where(valid(k), part, 0.0)
+            total = total + part
             faded = faded + totals[k - 1][there * per : there * per + per, :]
         store[at * gc : at * gc + gc, :] = total
 
 
 def carry_kernel(groups, per, *refs):
     n = len(groups)
-    y_in, xs, z, dyn, b, c, clt, e12, dttl2, messages, dsk, gain, ex, rest = take(
+    y_in, us, z, dyn, b, c, clt, e12, dttl2, messages, dsk, gain, ex, rest = take(
         refs, n, n, n, 0, 0, 0, 0, 0, 0, n - 1, 0, 0, 0
     )
     ys_o, st_o, rest = take(rest, n, n)
@@ -475,9 +535,10 @@
         sv = s[here, :]
         sb = sv.astype(BF)
         st_o[j][0] = sb
-        x = xs[j][...]
+        x = us[j][...]
+        x = x * sigmoid(x)
         e1 = dot(e12[...], ex[:, here])
-        y = y_in[j][...] + e1 * dot_t(c[...], sb) + dsk[:, here] * x
+        y = y_in[j][...].astype(F32) + e1 * dot_t(c[...], sb) + dsk[:, here] * x
         ys_o[j][...] = y
         xt = (x * dot(dttl2[...], ex[:, here])).astype(BF)
         s[here, :] = head_scale(clt, j * per, per, sv.shape[1]) * sv + t_dot(xt, b[...])
@@ -497,7 +558,7 @@
 
 def gate_kernel(groups, per, *refs):
     n = len(groups)
-    ys, z, xs, dyn, sums, sums2, gain, ec2, ex, c, rest = take(refs, n, n, n, *[0] * 7)
+    ys, z, us, dyn, sums, sums2, gain, ec2, ex, c, rest = take(refs, n, n, n, *[0] * 7)
     hidden, branch, branch2, limit, rest = take(rest, 0, 0, 0, 0)
     dys_o, rest = take(rest, n)
     dz_o, yn_o, ds_o, gn_o, sk_o, out_o, acc = rest
@@ -532,9 +593,11 @@
         gn_o[:, here] += jnp.sum(dy_n * gr, axis=0, keepdims=True)
         dgz = r2 * gn * dy_n - gz * pull
         dys = dgz * silu
-        dys_o[j][...] = dys
+        dys_o[j][...] = dys.astype(BF)
         dz_o[:, here] = (dgz * y * (sz + silu * (1.0 - sz))).astype(BF)
-        sk_o[:, here] += jnp.sum(dys * xs[j][...], axis=0, keepdims=True)
+        x = us[j][...]
+        x = x * sigmoid(x)
+        sk_o[:, here] += jnp.sum(dys * x, axis=0, keepdims=True)
         acc[here, :] += t_dot((dys * dot(ec2[...], ex[:, here])).astype(BF), c[...])
 
     @pl.when(pl.program_id(0) == pl.num_programs(0) - 1)
@@ -542,11 +605,62 @@
         ds_o[...] = acc[...].astype(BF)
 
 
+def line_peers(count, sign):
+    z = lax.axis_index("head")
+    return [{"head": lax.rem(z + sign * k + count, count)} for k in range(1, count)]
+
+
+def plane_peers(count):
+    d = lax.axis_index("dp")
+    return [{"dp": jnp.bitwise_xor(d, m)} for m in range(1, count)]
+
+
+def meet(peers):
+    barrier = pltpu.get_barrier_semaphore()
+    for peer in peers:
+        pl.semaphore_signal(barrier, inc=1, device_id=peer, device_id_type=MESH)
+    pl.semaphore_wait(barrier, len(peers))
+
+
+def remote(source, target, sends, receives, i, peer):
+    return pltpu.make_async_remote_copy(
+        src_ref=source,
+        dst_ref=target,
+        send_sem=sends.at[i],
+        recv_sem=receives.at[i],
+        device_id=peer,
+        device_id_type=MESH,
+    )
+
+
 def inside_back_kernel(groups, per, *refs):
     n = len(groups)
-    xdt, dys, b, c, cl, clt, rest = take(refs, n, n, 0, 0, 0, 0)
+    xdt, dys, b, c, cl, clt, message, early, rest = take(refs, n, n, 0, 0, 0, 0, 0, per)
     dx_o, rest = take(rest, n)
-    db_o, dc_o, da_o, kt = rest
+    db_o, dc_o, da_o, rest = take(rest, 0, 0, 0)
+    messages_o, early_o, rest = take(rest, n - 1, per - 1)
+    kt, sends, receives = rest
+    nz = n
+
+    def copies():
+        found = []
+        for i, peer in enumerate(line_peers(nz, -1)):
+            found.append(remote(message, messages_o[i], sends, receives, i, peer))
+        for i, peer in enumerate(plane_peers(per)):
+            found.append(remote(early[i + 1], early_o[i], sends, receives, nz - 1 + i, peer))
+        return found
+
+    @pl.when(pl.program_id(0) == 0)
+    def _():
+        meet(line_peers(nz, -1) + plane_peers(per))
+        for copy in copies():
+            copy.start()
+
+    @pl.when(pl.program_id(0) == pl.num_programs(0) - 1)
+    def _():
+        for copy in copies():
+            copy.wait()
+
     mask = tri("ge")
     low, high = lane_masks()
     g = dot_t(c[...], b[...])
@@ -559,7 +673,7 @@
         for p in range(per // 2):
             here = slice(p * Q, p * Q + Q)
             x = xdt[s][:, here]
-            dy = dys[s][:, here].astype(BF)
+            dy = dys[s][:, here]
             pp = dot_t(dy, jnp.concatenate([x * low, x * high], axis=0))
             ws = []
             for j in range(2):
@@ -612,7 +726,7 @@
     (b, c, dbi, dci, dai, dti, dt, sig, clt, dt2, e12, tl2), rest = rest[:12], rest[12:]
     (ubc, braw, brawh, cw, cbc, rate, dsk, ex, er), rest = rest[:9], rest[9:]
     nz = dt.shape[1] // per
-    messages, _, dx_o, dxh_o, gcx_o, rest = take(rest, nz - 1, 0, n, n, n)
+    messages, _, _, dx_o, dxh_o, gcx_o, rest = take(rest, nz - 1, 0, 0, n, n, n)
     db_o, dc_o, dt_o, ga_o, gbias_o, bc_o, bch_o, gcb_o, ds, vs = rest[:10]
     du_next, rest = take(rest[10:], n)
     (db_next,) = rest
@@ -624,7 +738,8 @@
 
     @pl.when(step == 0)
     def _():
-        from_messages(messages, -1, groups, per, state, ds)
+        z = lax.axis_index("head")
+        from_messages(messages, -1, groups, per, state, ds, lambda k: z + k < nz)
         for i in range(n):
             du_next[i][...] = jnp.zeros_like(du_next[i])
             gcx_o[i][...] = jnp.zeros_like(gcx_o[i])
@@ -647,7 +762,7 @@
         sb = st[i][0]
         dsv = ds[mine, :]
         dsb = dsv.astype(BF)
-        dy = dys[i][...]
+        dy = dys[i][...].astype(F32)
         dye = dy * dot(e12[...], ex[:, here])
         dyb = dye.astype(BF)
         rsum = rsum + dot((dye * dot_t(c[...], sb)).astype(BF), ehere)
@@ -673,7 +788,7 @@
         ds[mine, :] = eds + t_dot(dyb, c[...])
         du = (dxdt * dtx + dsk[:, here] * dy) * (su + xs * (1.0 - su))
         conv_back(
-            du, du_next[i], cw.at[:, here], xr[i][...], xrh[i], gcx_o[i], dx_o[i], dxh_o[i], last
+            du, du_next[i], cw.at[:, here], xr[i][...].astype(F32), xrh[i], gcx_o[i], dx_o[i], dxh_o[i], last
         )
     col = lax.broadcasted_iota(jnp.int32, (1, heads), 1)
     mine = functools.reduce(
@@ -703,7 +818,7 @@
 
 
 def sum_products_kernel(n, *refs):
-    a, w, rest = take(refs, n, n)
+    a, w, _, rest = take(refs, n, n, 0)
     left_o, right_o = rest
     total = dot(a[0][...], w[0][...])
     for i in range(1, n):
@@ -744,7 +859,7 @@
 
 
 def late_grad_kernel(n, per, final, *refs):
-    dx, dxh, xn, xnh, rest = take(refs, n, n, 0, 0)
+    _, dx, dxh, xn, xnh, rest = take(refs, 0, n, n, 0, 0)
     if final:
         dbc, dbch, ddt, spread, rest = take(rest, 0, 0, 0, 0)
         outs, rest = take(rest, per)
@@ -830,68 +945,49 @@
     gc = per * HEADDIM
     groups = tuple(range(nz))
 
-    zx_t = jnp.transpose(in_zx, (1, 2, 0))
-    out_h = out_w.reshape(own_heads, HEADDIM, half)
-
-    def slot_of(v, w, m):
-        return pick(v, per * w + (di ^ m))
-
-    def join(v, m):
-        return jnp.concatenate([slot_of(v, wi, m), swap(slot_of(v, 1 - wi, m))], axis=-1)
-
-    def join_rest(v):
-        mine = jnp.stack([slot_of(v, wi, m) for m in range(1, per)])
-        other = jnp.stack([slot_of(v, 1 - wi, m) for m in range(1, per)])
-        both = jnp.concatenate([mine, swap(other)], axis=-1)
-        return [both[m] for m in range(per - 1)]
+    onehot = np.kron(np.eye(heads), np.ones((1, HEADDIM)))
+    ex = jnp.asarray(np.concatenate([onehot, onehot], axis=0), BF)
+    er = jnp.asarray(onehot.T, BF)
+    sel = jnp.asarray(onehot.T * (np.arange(channels) % HEADDIM == 0)[:, None], F32)
 
     def after_that(v, w):
         return v + (w[(0,) * w.ndim] * 0).astype(v.dtype)
 
-    own_first = join(zx_t, 0)
-    zx_rest = zx_t
+    def beside(mine, other):
+        return jnp.concatenate([mine, swap(other)], axis=-1)
+
+    scal = jnp.repeat(jnp.stack([dt_bias, a_log, d_skip]), HEADDIM, axis=1)
+    piece = shape((2 * HEADDIM, half), BF)
+    some = shape((per - 1, 2 * HEADDIM, half), BF)
+    outs = shape((per, HEADDIM, half), BF)
+    first, first2, rest, rest2, out_mine, out_mine2, bcdt_t, table = pl.pallas_call(
+        functools.partial(prep_kernel, per),
+        out_shape=[
+            piece, piece, some, some, outs, outs,
+            shape((2 * STATE + HEADS + HALO, half), BF), shape((8, gc)),
+        ],
+        compiler_params=params(),
+        cost_estimate=cost(4),
+        name="prep",
+    )(
+        in_zx.reshape(half, -1), out_w, in_bcdt, norm_gain[None], conv_x, scal,
+        gnorm_gain[None],
+    )
+    own_first = beside(first, first2)
     along = [turn(own_first, s) for s in range(1, nz)]
     hidden_o = swap(hidden)
-    pieces = [[own_first] + join_rest(zx_rest)]
+    bcdt_t = beside(bcdt_t, bcdt_t)
+    table = jnp.concatenate([table] + [turn(table, s) for s in range(1, nz)], axis=1)
+    rest = beside(rest, rest2)
+    pieces = [[own_first] + [rest[m] for m in range(per - 1)]]
     for got in along:
         pieces.append([got] + [cross(got, m) for m in range(1, per)])
-    bcdt_t = jnp.concatenate([jnp.transpose(in_bcdt), norm_gain[None]], axis=0)
-    bcdt_t = jnp.concatenate([bcdt_t, swap(bcdt_t)], axis=1)
-    gain_in = bcdt_t[2 * STATE + HEADS :].astype(F32)
     wbc = bcdt_t[: 2 * STATE]
+    taps, gain_out, skip = table[:4], table[4:5], table[7:8]
+    taps_bc = conv_bc.astype(F32)
     slot = jnp.arange(heads)
     slot_head = ((zi - slot // per) % nz) * own_heads + wi * per + ((slot % per) ^ di)
     pick_heads = (slot_head[:, None] == jnp.arange(HEADS)[None, :]).astype(F32)
-    wdt = jnp.dot(
-        pick_heads.astype(BF), bcdt_t[2 * STATE : 2 * STATE + HEADS], preferred_element_type=F32
-    ).astype(BF)
-
-    table = jnp.concatenate(
-        [
-            dt_bias[:, None],
-            a_log[:, None],
-            d_skip[:, None],
-            jnp.transpose(conv_x.astype(F32).reshape(4, own_heads, HEADDIM), (1, 0, 2)).reshape(
-                own_heads, 4 * HEADDIM
-            ),
-            gnorm_gain.astype(F32).reshape(own_heads, HEADDIM),
-        ],
-        axis=1,
-    )
-    table = jnp.stack([slot_of(table, wi, m) for m in range(per)])
-    table = jnp.concatenate([table] + [turn(table, s) for s in range(1, nz)], axis=0)
-    bias = table[:, 0][None]
-    rate = -jnp.exp(table[:, 1])[None]
-    skip = jnp.repeat(table[:, 2], HEADDIM)[None]
-    taps = jnp.transpose(
-        table[:, 3 : 3 + 4 * HEADDIM].reshape(heads, 4, HEADDIM), (1, 0, 2)
-    ).reshape(4, channels)
-    gain_out = table[:, 3 + 4 * HEADDIM :].reshape(1, channels)
-    taps_bc = conv_bc.astype(F32)
-
-    onehot = np.kron(np.eye(heads), np.ones((1, HEADDIM)))
-    ex = jnp.asarray(np.concatenate([onehot, onehot], axis=0), BF)
-    er = jnp.asarray(onehot.T, BF)
 
     edge = jnp.concatenate([hidden[rows - HALO :], hidden_o[rows - HALO :]], axis=1)
     edge = shift(edge, 1)
@@ -899,34 +995,35 @@
     narrow = shape((rows, 2 * heads), BF)
     (
         xn, xnh, r, braw, brawh, ubc, bs, cs, dt, sig, cl, clt, totals,
-        dt2, e12, tl2, dttl2, ec2, edt2,
+        dt2, e12, tl2, dttl2, ec2, edt2, rate, wdt,
     ) = pl.pallas_call(
-        entry_kernel,
+        functools.partial(entry_kernel, per),
         out_shape=[
             shape((rows, model), BF), shape((HALO, model), BF), shape((rows, 1)),
             shape((rows, 2 * STATE)),
             shape((HALO, 2 * STATE)), shape((rows, 2 * STATE)), shape((rows, STATE), BF),
             shape((rows, STATE), BF), shape((rows, heads)), shape((rows, heads)),
             shape((rows, heads)), shape((heads, rows)), shape((heads, STATE), BF),
-            narrow, narrow, narrow, narrow, narrow, narrow,
+            narrow, narrow, narrow, narrow, narrow, narrow, shape((1, heads)),
+            shape((heads, model), BF),
         ],
         scratch_shapes=[pltpu.VMEM((ext_rows, 2 * STATE), F32)],
         compiler_params=params(),
         cost_estimate=cost(12),
         name="entry",
-    )(hidden, hidden_o, edge, gain_in, wbc, wdt, taps_bc, bias, rate)
+    )(hidden, hidden_o, edge, bcdt_t, table, taps_bc, sel)
 
     def send_states(local, sign):
         message = jnp.concatenate([*local, totals], axis=0)
         return [shift(message, sign * k) for k in range(1, nz)]
 
     cut = rows // 2 if rows // 2 % Q == 0 else rows
-    part = shape((rows, gc))
+    part = shape((rows, gc), BF)
     full = shape((rows, channels))
     step = lambda i: (i, 0)
     fix = lambda i: (0, 0)
     gspec = pl.BlockSpec((cut, gc), step)
-    wz, wx, z, xr, xrh, u, xs, xdt, s_local, y_in = ([] for _ in range(10))
+    wz, wx, z, xr, xrh, u, xdt, s_local, y_in = ([] for _ in range(9))
     for s in groups:
         out = pl.pallas_call(
             functools.partial(project_kernel, s, per),
@@ -939,18 +1036,19 @@
             ],
             out_specs=[
                 pl.BlockSpec((gc, model), fix), pl.BlockSpec((gc, model), fix), gspec, gspec,
-                pl.BlockSpec((HALO, gc), fix), gspec, gspec, gspec, pl.BlockSpec((gc, STATE), fix),
+                pl.BlockSpec((HALO, gc), fix), gspec, gspec, pl.BlockSpec((gc, STATE), fix),
             ],
             out_shape=[
-                shape((gc, model), BF), shape((gc, model), BF), part, part, shape((HALO, gc)),
-                part, part, shape((rows, gc), BF), shape((gc, STATE), BF),
+                shape((gc, model), BF), shape((gc, model), BF), shape((rows, gc)), part,
+                shape((HALO, gc)),
+                shape((rows, gc)), part, shape((gc, STATE), BF),
             ],
             scratch_shapes=[pltpu.VMEM((cut + HALO, gc), F32), pltpu.VMEM((gc, STATE), F32)],
             compiler_params=params(),
             cost_estimate=cost(5),
             name="project",
         )(xn, xnh, *pieces[s], taps, dt2, edt2, ex, bs)
-        for keep, v in zip((wz, wx, z, xr, xrh, u, xs, xdt, s_local), out):
+        for keep, v in zip((wz, wx, z, xr, xrh, u, xdt, s_local), out):
             keep.append(v)
         y_in.append(
             pl.pallas_call(
@@ -969,11 +1067,13 @@
         )
     messages = send_states(s_local, 1)
 
-    out_first = after_that(join(out_h, 0), pieces[-1][-1])
-    out_own = [out_first] + join_rest(out_h)
+    out_mine2 = after_that(out_mine2, totals)
+    out_both = beside(out_mine, out_mine2)
+    out_own = [out_both[m] for m in range(per)]
+    out_first = after_that(out_own[0], s_local[1])
     out_along = jnp.concatenate([turn(out_first, s) for s in range(1, nz)], axis=0)
     out_cross = [out_along] + [cross(out_along, m) for m in range(1, per)]
-    cot_o = swap(cotangent)
+    cot_o = swap(after_that(cotangent, totals))
     limit = (lengths[0] - zi * rows).reshape(1, 1)
 
     wide = pl.BlockSpec((Q, channels), step)
@@ -1012,33 +1112,38 @@
             pl.BlockSpec((Q, 2), step),
         ],
         out_shape=[
-            *[part] * nz, *[shape((blocks, gc, STATE), BF)] * nz, shape((rows, channels), BF),
+            *[shape((rows, gc))] * nz, *[shape((blocks, gc, STATE), BF)] * nz, shape((rows, channels), BF),
             shape((rows, 2)),
         ],
         scratch_shapes=[pltpu.VMEM((channels, STATE), F32)],
         compiler_params=params(),
         cost_estimate=cost(10),
         name="carry",
-    )(*y_in, *xs, *z, dyn, bs, cs, clt, e12, dttl2, *messages, skip, gain_out, ex)
+    )(*y_in, *u, *z, dyn, bs, cs, clt, e12, dttl2, *messages, skip, gain_out, ex)
     ys, states, gg, sums = out[:nz], out[nz : 2 * nz], out[2 * nz], out[2 * nz + 1]
     sums2 = swap(sums)
 
-    def sum_products(a, w, count):
+    def sum_products(a, columns, w, count, wait):
         tile = 2 * Q if count % (2 * Q) == 0 else count
         return pl.pallas_call(
             functools.partial(sum_products_kernel, len(a)),
             grid=(count // tile,),
             in_specs=[
-                *[pl.BlockSpec((tile, v.shape[1]), step) for v in a], *[whole(v) for v in w]
+                *[
+                    pl.BlockSpec((tile, v.shape[0]), lambda i, j=j: (i, j))
+                    for v, j in zip(w, columns)
+                ],
+                *[whole(v) for v in w],
+                pl.BlockSpec(memory_space=pl.ANY),
             ],
             out_specs=[pl.BlockSpec((tile, half), step)] * 2,
             out_shape=[shape((count, half)), shape((count, half), BF)],
             compiler_params=params(),
             cost_estimate=cost(4),
             name="products",
-        )(*a, *w)
-
-    branch, branch_o = sum_products([gg], [wout], rows)
+        )(*a, *w, wait)
+
+    branch, branch_o = sum_products([gg], [0], [wout], rows, sums)
     branch_o = swap(branch_o)
     hhalf = pl.BlockSpec((Q, half), step)
     out = pl.pallas_call(
@@ -1062,11 +1167,11 @@
         cost_estimate=cost(10),
         name="gate",
     )(
-        *ys, *z, *xs, dyn, sums, sums2, gain_out, ec2, ex, cs, hidden, branch, branch_o, limit
+        *ys, *z, *u, dyn, sums, sums2, gain_out, ec2, ex, cs, hidden, branch, branch_o, limit
     )
     dys = out[:nz]
     dz, yn, ds_local, g_gain, g_skip, out_hidden = out[nz:]
-    messages = send_states([ds_local], -1)
+    message = jnp.concatenate([ds_local, totals], axis=0)
 
     def plane_sum(parts):
         total = parts[0].astype(F32)
@@ -1084,6 +1189,7 @@
         high_w = jnp.where(wi == 0, other, mine)
         return jnp.concatenate([low_w, high_w], axis=0)
 
+    anywhere = pl.BlockSpec(memory_space=pl.ANY)
     gcol = pl.BlockSpec((rows, gc), lambda s: (0, s))
     early = pl.pallas_call(
         functools.partial(early_grad_kernel, per),
@@ -1095,22 +1201,38 @@
         cost_estimate=cost(6),
         name="early_grad",
     )(yn, masked, dz, xn)
-    early = plane_sum(early)
-    early_low = early.astype(BF)
-
     out = pl.pallas_call(
         functools.partial(inside_back_kernel, groups, per),
         grid=(blocks,),
-        in_specs=[*[gwide] * (2 * nz), bspec, bspec, hspec, tspec],
-        out_specs=[*[gwide] * nz, bspec, bspec, hspec],
-        out_shape=[*[part] * nz, shape((rows, STATE)), shape((rows, STATE)), shape((rows, heads))],
-        scratch_shapes=[pltpu.VMEM((heads, Q), F32)],
-        compiler_params=params(),
+        in_specs=[
+            *[gwide] * (2 * nz), bspec, bspec, hspec, tspec, *[anywhere] * (1 + per)
+        ],
+        out_specs=[*[gwide] * nz, bspec, bspec, hspec, *[anywhere] * (nz - 1 + per - 1)],
+        out_shape=[
+            *[shape((rows, gc))] * nz, shape((rows, STATE)), shape((rows, STATE)),
+            shape((rows, heads)), *[shape(message.shape, BF)] * (nz - 1),
+            *[shape(early[0].shape, BF)] * (per - 1),
+        ],
+        scratch_shapes=[
+            pltpu.VMEM((heads, Q), F32), pltpu.SemaphoreType.DMA((nz + per - 2,)),
+            pltpu.SemaphoreType.DMA((nz + per - 2,)),
+        ],
+        compiler_params=pltpu.CompilerParams(
+            vmem_limit_bytes=VMEM, collective_id=0, has_side_effects=True
+        ),
         cost_estimate=cost(15),
         name="inside_back",
-    )(*xdt, *dys, bs, cs, cl, clt)
+    )(*xdt, *dys, bs, cs, cl, clt, message, *early)
     dxi = out[:nz]
-    dbi, dci, dai = out[nz:]
+    dbi, dci, dai = out[nz : nz + 3]
+    messages = out[nz + 3 : 2 * nz + 2]
+    early_sum = sum(v.astype(F32) for v in [early[0], *out[2 * nz + 2 :]])
+    early_low = early_sum.astype(BF)
+    early_total = early_sum[0]
+    for s in range(1, nz):
+        early_total = early_total + turn(early_low[s], -s).astype(F32)
+    early_total = early_total.astype(BF)
+    early_own, early_other = to_owner(early_total)
     rev = lambda i: (blocks - 1 - i, 0)
     rg = pl.BlockSpec((Q, gc), rev)
     rb = pl.BlockSpec((Q, STATE), rev)
@@ -1131,7 +1253,7 @@
                 pl.BlockSpec((heads, Q), lambda i: (0, blocks - 1 - i)), rh2, rh2, rh2,
                 rbc, rbc, whole(brawh), whole(taps), whole(taps_bc), whole(rate), whole(skip),
                 whole(ex), whole(er), *[whole(v) for v in messages],
-                pl.BlockSpec(memory_space=pl.ANY),
+                pl.BlockSpec(memory_space=pl.ANY), pl.BlockSpec(memory_space=pl.ANY),
             ],
             out_specs=[
                 *[rg] * n, *[pl.BlockSpec((HALO, gc), fix)] * n, *[pl.BlockSpec((4, gc), fix)] * n,
@@ -1154,14 +1276,14 @@
         )(
             *of(dxi), *of(dys), *of(u), *of(xr), *of(xrh), *of(states), bs, cs, dbi, dci, dai, dti,
             dt, sig, clt, dt2, e12, tl2, ubc, braw, brawh, taps, taps_bc, rate, skip, ex, er,
-            *messages, wait,
+            *messages, *wait,
         )
         return out[:n], out[n : 2 * n], out[2 * n : 3 * n], *out[3 * n :]
 
     halves = (groups[1 : nz // 2 + 1], groups[nz // 2 + 1 :] + groups[:1])
     dx, dxh, g_taps = [None] * nz, [None] * nz, [None] * nz
     dti = jnp.zeros((rows, heads), F32)
-    g_rate, g_bias, late, wait = 0.0, 0.0, [], dti
+    g_rate, g_bias, late, wait = 0.0, 0.0, [], (dti, dti)
     bc_rows = 2 * STATE // per
     for number, some in enumerate(halves):
         final = number == len(halves) - 1
@@ -1177,6 +1299,10 @@
         out_rows = n * HEADDIM + (bc_rows + HALO if final else 0)
         g = pl.pallas_call(
             functools.partial(late_grad_kernel, n, per, final),
+            in_specs=[
+                pl.BlockSpec(memory_space=pl.ANY),
+                *[whole(v) for v in [*got, *got_h, xn, xnh, *more]],
+            ],
             out_shape=[shape((out_rows, model), BF)] * per,
             scratch_shapes=(
                 [pltpu.VMEM((2 * STATE, model), F32), pltpu.VMEM((HEADS, model), F32)]
@@ -1186,15 +1312,11 @@
             compiler_params=params(),
             cost_estimate=cost(3),
             name="late_grad",
-        )(*got, *got_h, xn, xnh, *more)
+        )(early_total if final else dti, *got, *got_h, xn, xnh, *more)
         late.append(plane_sum(g))
-        wait = early_low if number == 0 else wait
+        wait = (early_low, g[0])
     g_taps = jnp.concatenate(g_taps, axis=1)
 
-    total = early[0]
-    for s in range(1, nz):
-        total = total + turn(early_low[s], -s).astype(F32)
-    early_own, early_other = to_owner(total.astype(BF))
     share = late[-1][len(halves[-1]) * HEADDIM :]
     addend = {}
     for some, v in zip(halves, late):
@@ -1218,14 +1340,16 @@
         )
     )
 
-    lhs = [dz] + dx + [dbc, dti]
-    dxn, dxn_o = sum_products(lhs, [jnp.concatenate(wz, axis=0)] + wx + [wbc, wdt], rows)
+    lhs = [dz] * nz + dx + [dbc, dti]
+    dxn, dxn_o = sum_products(
+        lhs, [*groups] + [0] * (nz + 2), wz + wx + [wbc, wdt], rows, early_other
+    )
     edge = sum(dot(v, w) for v, w in zip(dxh + [dbch], wx + [wbc]))
     edge = edge[:, :half] + swap(edge[:, half:])
     edge = shift(edge, -1)
     dxn = dxn + swap(dxn_o).astype(F32) + jnp.pad(edge, ((rows - HALO, 0), (0, 0)))
     source = hidden.astype(F32)
-    gain_half = gain_in[:, :half]
+    gain_half = norm_gain[None].astype(F32)
     across = jnp.sum(dxn * gain_half * source, axis=1, keepdims=True)
     across = across + swap(across)
     grad_hidden = (

time: 439 us -> 455 us (1.036)
  Pallas kernels: 181 us -> 223 us
  waiting for transfers between devices: 97.3 us -> 59.2 us
  starting transfers between devices: 73.9 us -> 88.6 us
  other arithmetic: 31.1 us -> 25.9 us
    pallas_call x1, Pallas kernels: 17.8 us -> 57.4 us  [sequence_device(): pl.pallas_call(functools.partial(inside_back_kernel, groups, per), grid=(...]
    ppermute x15, waiting for transfers between devices: 45.9 us -> 28.2 us  [turn(): return lax.ppermute(v, 'head', [(i, (i + s) % nz) for i in range(nz)])]
    ppermute x29 -> x26, waiting for transfers between devices: 40.8 us -> 24.5 us  [cross(): return lax.ppermute(v, 'dp', [(i, i ^ m) for i in range(ndp)])]
    ppermute x15, starting transfers between devices: 24.9 us -> 38 us  [turn(): return lax.ppermute(v, 'head', [(i, (i + s) % nz) for i in range(nz)])]
    unnamed x174 -> x144, local copies, waits for them, and re-layouts: 14.1 us -> 25.1 us
    another operation x2 -> x0, local copies, waits for them, and re-layouts: 7.29 us -> none
    ppermute x2, waiting for transfers between devices: 7.51 us -> 2.66 us  [sequence_device(): lax.ppermute(small, 'head', [(i, i ^ flip) for i in range(nz)])]
    pallas_call x3 -> x4, Pallas kernels: 22.1 us -> 25.5 us  [the longest x1 12 us: sequence_device(): pl.pallas_call(functools.partial(entry_kernel, per), out_shape=[shape((ro...]
  transfers between devices with their start and end apart: 69 -> 62, of which waited for: 18 -> 15; matrix products, arithmetic and copies ran while one was open for 13% -> 12% of each run, Pallas kernels for 28% -> 22%
where the time goes in v3:
time: 455 us; the launch traced here: 450 us
  Pallas kernels  223 us (49%)
  starting transfers between devices  88.6 us (19%)
  waiting for transfers between devices  59.2 us (13%)
  local copies, waits for them, and re-layouts  46.7 us (10%)
  other arithmetic  25.9 us (6%)
    pallas_call x1, Pallas kernels, sequence_device(): pl.pallas_call(functools.partial(inside_back_kernel, groups, per), grid=(...  57.4 us
    ppermute x15, starting transfers between devices, turn(): return lax.ppermute(v, 'head', [(i, (i + s) % nz) for i in range(nz)])  38 us
    pallas_call x2, Pallas kernels, back(): pl.pallas_call(functools.partial(back_kernel, some, per, final), grid=(bl...  35.7 us
    ppermute x26, starting transfers between devices, cross(): return lax.ppermute(v, 'dp', [(i, i ^ m) for i in range(ndp)])  32.2 us
    pallas_call x4, Pallas kernels, sequence_device(): pl.pallas_call(functools.partial(project_kernel, s, per), grid=(rows // c...  29.5 us
    ppermute x15, waiting for transfers between devices, turn(): return lax.ppermute(v, 'head', [(i, (i + s) % nz) for i in range(nz)])  28.2 us
    unnamed x144, local copies, waits for them, and re-layouts  25.1 us
    ppermute x26, waiting for transfers between devices, cross(): return lax.ppermute(v, 'dp', [(i, i ^ m) for i in range(ndp)])  24.5 us
  transfers between devices with their start and end apart: 62, of which 15 were waited for; matrix products, arithmetic and copies ran while one was open for 12% of the time, Pallas kernels for 22%

profile of v3, /device:TPU:0, one launch (start us, length us, event | category | flops | bytes accessed | tf_op | source)
XLA Modules:
  0.0 450.4 jit_solution(4707999249235945491)
XLA Ops:
  0.7 2.6 copy.53
  6.2 3.0 prep.1
  9.2 3.0 collective-permute-start.3
  12.2 2.6 collective-permute-start.4
  29.7 1.4 fusion.31
  31.5 2.9 collective-permute-start.16
  34.4 5.7 %collective-permute-done.8.refs_2_ = bf16[128,1024]{1,0:T(8,128)(2,1)S(1)} collective-permute-done((bf16[128,1024]{1,0:T(8,128)(2,1)S(1)}, bf16[128,1024]{1,0:T(8,128)(2,1)S(1)}, u32[]{:S(2)}, u32[]{:S(2)}) %collective-permute-start.8) | collective-permute-done | bytes 262176 | tf_op jit(solution)/shard_map/ppermute | solution.py:934
  40.1 1.5 collective-permute-start.10
  41.7 1.4 collective-permute-start.11
  46.8 3.6 collective-permute-done.12.refs_2_
  50.4 1.5 collective-permute-start.9
  52.5 12.0 %entry.1 = (bf16[1024,1024]{1,0:T(8,128)(2,1)}, bf16[16,1024]{1,0:T(8,128)(2,1)}, f32[1024,1]{1,0:T(8,128)}, f32[1024,256]{1,0:T(8,128)}, f32[16,256]{1,0:T(8,12...) custom-call(bf16[1024,512]{1,0:T(8,128)(2,1)} %refs_19_.1, ...), custom_call_target="tpu_custom_call" | custom-call | flops 1200000000 | bytes 12000 | tf_op jit(solution)/shard_map/entry/pallas_call | solution.py:999
  64.6 7.4 %project.4 = (bf16[256,1024]{1,0:T(8,128)(2,1)}, bf16[256,1024]{1,0:T(8,128)(2,1)}, f32[1024,256]{1,0:T(8,128)}, bf16[1024,256]{1,0:T(8,128)(2,1)}, f32[16,256]{...) custom-call(bf16[1024,1024]{1,0:T(8,128)(2,1)} %get-tuple-element.150.refs_0_.xn.refs_5_, ...), custom_call_target="tpu_custom_call" | custom-call | flops 500000000 | bytes 5000 | tf_op jit(solution)/shard_map/project/pallas_call | solution.py:1028
  72.0 1.5 constant_dynamic-update-slice_fusion.19
  73.5 1.5 collective-permute-start.14
  77.8 7.4 %project.5 = (bf16[256,1024]{1,0:T(8,128)(2,1)}, bf16[256,1024]{1,0:T(8,128)(2,1)}, f32[1024,256]{1,0:T(8,128)}, bf16[1024,256]{1,0:T(8,128)(2,1)}, f32[16,256]{...) custom-call(bf16[1024,1024]{1,0:T(8,128)(2,1)} %get-tuple-element.150.refs_0_.xn.refs_5_, ...), custom_call_target="tpu_custom_call" | custom-call | flops 500000000 | bytes 5000 | tf_op jit(solution)/shard_map/project/pallas_call | solution.py:1028
  88.5 1.4 collective-permute-done.21
  89.9 2.6 collective-permute-start.22
  93.2 1.5 collective-permute-start.18
  94.7 3.4 collective-permute-start.23
  98.2 7.4 %project.6 = (bf16[256,1024]{1,0:T(8,128)(2,1)}, bf16[256,1024]{1,0:T(8,128)(2,1)}, f32[1024,256]{1,0:T(8,128)}, bf16[1024,256]{1,0:T(8,128)(2,1)}, f32[16,256]{...) custom-call(bf16[1024,1024]{1,0:T(8,128)(2,1)} %get-tuple-element.150.refs_0_.xn.refs_5_, ...), custom_call_target="tpu_custom_call" | custom-call | flops 500000000 | bytes 5000 | tf_op jit(solution)/shard_map/project/pallas_call | solution.py:1028
  105.6 12.5 %collective-permute-start.24 = (bf16[64,1024]{1,0:T(8,128)(2,1)S(1)}, bf16[64,1024]{1,0:T(8,128)(2,1)S(1)}, u32[]{:S(2)}, u32[]{:S(2)}) collective-permute-start(bf16[64,1024]{1,0:T(8,128)(2,1)S(1)} %broadcast_add_fusion.2), channel_id=1, source_target_pairs={{0,6},{2,0},{4,2},{6,4},{1,7},{3,1},{5,3},{7,5},{8,14},{10,8},{12,... | collective-permute-start | bytes 393224 | tf_op jit(solution)/shard_map/ppermute | solution.py:934
  118.8 3.7 collective-permute-done.24
  122.5 1.5 collective-permute-start.25
  124.5 1.5 constant_dynamic-update-slice_fusion.17
  126.0 2.6 collective-permute-done.19.refs_5_
  128.6 7.4 %project.7 = (bf16[256,1024]{1,0:T(8,128)(2,1)}, bf16[256,1024]{1,0:T(8,128)(2,1)}, f32[1024,256]{1,0:T(8,128)}, bf16[1024,256]{1,0:T(8,128)(2,1)}, f32[16,256]{...) custom-call(bf16[1024,1024]{1,0:T(8,128)(2,1)} %get-tuple-element.150.refs_0_.xn.refs_5_, ...), custom_call_target="tpu_custom_call" | custom-call | flops 500000000 | bytes 5000 | tf_op jit(solution)/shard_map/project/pallas_call | solution.py:1028
  136.0 1.5 constant_dynamic-update-slice_fusion.16
  138.6 4.3 collective-permute-start.28
  142.9 3.5 inside.7.refs_3_
  146.4 3.6 inside.6.refs_2_
  150.0 3.5 inside.5.refs_1_
  153.5 3.5 inside.4.refs_0_
  157.0 2.2 collective-permute-start.29
  159.3 2.0 collective-permute-start.30
  163.1 6.9 %pull.1 = (bf16[1024,1024]{1,0:T(8,128)(2,1)}, bf16[1024,1024]{1,0:T(8,128)(2,1)}, f32[1024,1024]{1,0:T(8,128)}) custom-call(bf16[1024,512]{1,0:T(8,128)(2,1)} %refs_0_.1, bf16[1024,512]{1,0:T(8,128)(2,1)} %copy-done.19, s32[1,1]{1,0:T(1,128)} %bitcast.8.refs_2_.refs_22_, bf16[64,1024]{1,0:T(8,128)(2,1)} %get-tuple-element.352.refs_3_, ...), custom_call_target="tpu_custom_call" | custom-call | flops 500000000 | bytes 5000 | tf_op jit(solution)/shard_map/pull/pallas_call | solution.py:1087
  170.0 13.7 %carry.1 = (f32[1024,256]{1,0:T(8,128)}, f32[1024,256]{1,0:T(8,128)}, f32[1024,256]{1,0:T(8,128)}, f32[1024,256]{1,0:T(8,128)}, bf16[8,256,128]{2,1,0:T(8,128)(2...) custom-call(bf16[1024,256]{1,0:T(8,128)(2,1)} %inside.4.refs_0_, ...), custom_call_target="tpu_custom_call" | custom-call | flops 1000000000 | bytes 10000 | tf_op jit(solution)/shard_map/carry/pallas_call | solution.py:1103
  183.8 5.9 %products.2 = (f32[1024,512]{1,0:T(8,128)}, bf16[1024,512]{1,0:T(8,128)(2,1)}) custom-call(bf16[1024,1024]{1,0:T(8,128)(2,1)} %get-tuple-element.190.refs_0_, bf16[1024,1024]{1,0:T(8,128)(2,1)} %get-tuple-element.191.refs_1_, f32[1024,2]{1,0:T(8,128)} %get-tuple-element.188.refs_2_.refs_13_), custom_call_target="tpu_custom_call" | custom-call | flops 400000000 | bytes 4000 | tf_op jit(solution)/shard_map/products/pallas_call | solution.py:1128
  195.0 14.5 %gate.1 = (bf16[1024,256]{1,0:T(8,128)(2,1)}, bf16[1024,256]{1,0:T(8,128)(2,1)}, bf16[1024,256]{1,0:T(8,128)(2,1)}, bf16[1024,256]{1,0:T(8,128)(2,1)}, bf16[1024...) custom-call(f32[1024,256]{1,0:T(8,128)} %get-tuple-element.184.refs_, ...), custom_call_target="tpu_custom_call" | custom-call | flops 1000000000 | bytes 10000 | tf_op jit(solution)/shard_map/gate/pallas_call | solution.py:1149
  209.5 1.7 pad_maximum_fusion.8.refs_12_
  211.1 9.1 %early_grad.1 = (bf16[4,128,1024]{2,1,0:T(8,128)(2,1)}, bf16[4,128,1024]{2,1,0:T(8,128)(2,1)}, bf16[4,128,1024]{2,1,0:T(8,128)(2,1)}, bf16[4,128,1024]{2,1,0:T(8,128)(2,1)}) custom-call(bf16[1024,1024]{1,0:T(8,128)(2,1)} %get-tuple-element.202.yn, bf16[1024,1024]{1,0:T(8,128)(2,1)} %get-tuple-element.203.masked, ...), custom_call_target="tpu_custom_call" | custom-call | flops 600000000 | bytes 6000 | tf_op jit(solution)/shard_map/early_grad/pallas_call | solution.py:1194
  220.2 57.4 %inside_back.1 = (f32[1024,256]{1,0:T(8,128)}, f32[1024,256]{1,0:T(8,128)}, f32[1024,256]{1,0:T(8,128)}, f32[1024,256]{1,0:T(8,128)}, f32[1024,128]{1,0:T(8,128)...) custom-call(bf16[1024,256]{1,0:T(8,128)(2,1)} %get-tuple-element.159, ...), custom_call_target="tpu_custom_call" | custom-call | flops 1500000000 | bytes 15000 | tf_op jit(solution)/shard_map/inside_back/pallas_call | solution.py:1204
  278.5 17.1 %back.2 = (bf16[1024,256]{1,0:T(8,128)(2,1)}, bf16[1024,256]{1,0:T(8,128)(2,1)}, bf16[16,256]{1,0:T(8,128)(2,1)}, bf16[16,256]{1,0:T(8,128)(2,1)}, f32[4,256]{1,...) custom-call(f32[1024,256]{1,0:T(8,128)} %get-tuple-element.216.refs_, ...), custom_call_target="tpu_custom_call" | custom-call | flops 1400000000 | bytes 14000 | tf_op jit(solution)/shard_map/back/pallas_call | solution.py:1246
  295.5 4.5 late_grad.2
  300.0 1.5 collective-permute-start.52
  302.8 4.1 fusion.28
  310.5 18.6 %back.3 = (bf16[1024,256]{1,0:T(8,128)(2,1)}, bf16[1024,256]{1,0:T(8,128)(2,1)}, bf16[16,256]{1,0:T(8,128)(2,1)}, bf16[16,256]{1,0:T(8,128)(2,1)}, f32[4,256]{1,...) custom-call(f32[1024,256]{1,0:T(8,128)} %get-tuple-element.208.refs_, ...), custom_call_target="tpu_custom_call" | custom-call | flops 1400000000 | bytes 14000 | tf_op jit(solution)/shard_map/back/pallas_call | solution.py:1246
  340.2 5.9 %late_grad.3 = (bf16[208,1024]{1,0:T(8,128)(2,1)}, bf16[208,1024]{1,0:T(8,128)(2,1)}, bf16[208,1024]{1,0:T(8,128)(2,1)}, bf16[208,1024]{1,0:T(8,128)(2,1)}) custom-call(bf16[128,1024]{1,0:T(8,128)(2,1)} %copy-done.9, bf16[1024,256]{1,0:T(8,128)(2,1)} %get-tuple-element.249.refs_7_.refs_1_, bf16[1024,256]{1,0:T(8,128)(2,1)} %get-tuple-element.248.refs_4_.refs_2_, ...), custom_call_target="tpu_custom_call" | custom-call | flops 300000000 | bytes 3000 | tf_op jit(solution)/shard_map/late_grad/pallas_call | solution.py:1300
  348.1 1.5 collective-permute-start.51
  349.9 9.2 %collective-permute-done.49 = bf16[208,1024]{1,0:T(8,128)(2,1)S(1)} collective-permute-done((bf16[208,1024]{1,0:T(8,128)(2,1)}, bf16[208,1024]{1,0:T(8,128)(2,1)S(1)}, u32[]{:S(2)}, u32[]{:S(2)}) %collective-permute-start.49) | collective-permute-done | bytes 426016 | tf_op jit(solution)/shard_map/ppermute | solution.py:940
  360.4 9.6 %collective-permute-done.50 = bf16[208,1024]{1,0:T(8,128)(2,1)S(1)} collective-permute-done((bf16[208,1024]{1,0:T(8,128)(2,1)}, bf16[208,1024]{1,0:T(8,128)(2,1)S(1)}, u32[]{:S(2)}, u32[]{:S(2)}) %collective-permute-start.50) | collective-permute-done | bytes 426016 | tf_op jit(solution)/shard_map/ppermute | solution.py:940
  370.0 3.3 collective-permute-start.38
  373.7 3.3 collective-permute-start.55
  377.0 2.4 collective-permute-done.37
  379.5 2.6 collective-permute-start.57
  382.6 15.1 %collective-permute-done.56 = bf16[144,1024]{1,0:T(8,128)(2,1)S(1)} collective-permute-done((bf16[144,1024]{1,0:T(8,128)(2,1)S(1)}, bf16[144,1024]{1,0:T(8,128)(2,1)S(1)}, u32[]{:S(2)}, u32[]{:S(2)}) %collective-permute-start.56) | collective-permute-done | bytes 294944 | tf_op jit(solution)/shard_map/ppermute | solution.py:934
  403.1 1.5 collective-permute-start.42
  405.5 10.1 %products.3 = (f32[1024,512]{1,0:T(8,128)}, bf16[1024,512]{1,0:T(8,128)(2,1)}) custom-call(bf16[1024,1024]{1,0:T(8,128)(2,1)} %get-tuple-element.196.dz.refs_0_.refs_1_.refs_2_.refs_3_, bf16[1024,1024]{1,0:T(8,128)(2,1)} %get-tuple-element.196.dz.refs_0_.refs_1_.refs_2_.refs_3_, bf16[1024,1024]{1,0:T(8,128)(2,1)} %get-tuple-element.196.dz.refs_0_.refs_1_.refs_2_.refs_3_, ...), custom_call_target="tpu_custom_call" | custom-call | flops 400000000 | bytes 4000 | tf_op jit(solution)/shard_map/products/pallas_call | solution.py:1128
  423.0 1.5 concatenate.74
  427.7 2.6 convert_bitcast_fusion
  433.3 3.0 copy.47
  436.3 2.7 collective-permute-start.47
  439.0 2.1 collective-permute-done.47
  442.5 3.2 fusion.2
  (334 shorter events, 82.6 us)
Async XLA Ops:
  9.2 13.9 %collective-permute-start.3 = (f32[8,256]{1,0:T(8,128)}, f32[8,256]{1,0:T(8,128)}, u32[]{:S(2)}, u32[]{:S(2)}) collective-permute-start(f32[8,256]{1,0:T(8,128)} %get-tuple-element.149), channel_id=1, source_target_pairs={{0,2},{2,4},{4,6},{6,0},{1,3},{3,5},{5,7},{7,1},{8,10},{10,12},{12... | collective-permute-start | bytes 24584 | tf_op jit(solution)/shard_map/ppermute | solution.py:934
  12.2 12.3 %collective-permute-start.4 = (f32[8,256]{1,0:T(8,128)}, f32[8,256]{1,0:T(8,128)}, u32[]{:S(2)}, u32[]{:S(2)}) collective-permute-start(f32[8,256]{1,0:T(8,128)} %get-tuple-element.149), channel_id=1, source_target_pairs={{0,4},{2,6},{4,0},{6,2},{1,5},{3,7},{5,1},{7,3},{8,12},{10,14},{12... | collective-permute-start | bytes 24584 | tf_op jit(solution)/shard_map/ppermute | solution.py:934
  14.8 11.5 %collective-permute-start.5 = (f32[8,256]{1,0:T(8,128)}, f32[8,256]{1,0:T(8,128)}, u32[]{:S(2)}, u32[]{:S(2)}) collective-permute-start(f32[8,256]{1,0:T(8,128)} %get-tuple-element.149), channel_id=1, source_target_pairs={{0,6},{2,0},{4,2},{6,4},{1,7},{3,1},{5,3},{7,5},{8,14},{10,8},{12,... | collective-permute-start | bytes 24584 | tf_op jit(solution)/shard_map/ppermute | solution.py:934
  16.2 15.3 %collective-permute-start.2 = (bf16[304,512]{1,0:T(8,128)(2,1)}, bf16[304,512]{1,0:T(8,128)(2,1)S(1)}, u32[]{:S(2)}, u32[]{:S(2)}) collective-permute-start(bf16[304,512]{1,0:T(8,128)(2,1)} %get-tuple-element.148), channel_id=1, source_target_pairs={{0,1},{1,0},{2,3},{3,2},{4,5},{5,4},{6,7},{7,6},{8,9},{9,8},{10,11... | collective-permute-start | bytes 933896 | tf_op jit(solution)/shard_map/ppermute | solution.py:931
  16.2 27.0 %collective-permute-start = (bf16[1024,512]{1,0:T(8,128)(2,1)S(1)}, bf16[1024,512]{1,0:T(8,128)(2,1)}, u32[]{:S(2)}, u32[]{:S(2)}) collective-permute-start(bf16[1024,512]{1,0:T(8,128)(2,1)S(1)} %copy-done), channel_id=1, source_target_pairs={{0,1},{1,0},{2,3},{3,2},{4,5},{5,4},{6,7},{7,6},{8,9},{9,8},{10,11... | collective-permute-start | bytes 3145736 | tf_op jit(solution)/shard_map/ppermute | solution.py:931
  23.1 5.8 %collective-permute-start.6 = (bf16[128,512]{1,0:T(8,128)(2,1)}, bf16[128,512]{1,0:T(8,128)(2,1)S(1)}, u32[]{:S(2)}, u32[]{:S(2)}) collective-permute-start(bf16[128,512]{1,0:T(8,128)(2,1)} %get-tuple-element.153), channel_id=1, source_target_pairs={{0,1},{1,0},{2,3},{3,2},{4,5},{5,4},{6,7},{7,6},{8,9},{9,8},{10,11... | collective-permute-start | bytes 393224 | tf_op jit(solution)/shard_map/ppermute | solution.py:931
  24.5 17.2 %collective-permute-start.7 = (bf16[3,128,512]{2,1,0:T(8,128)(2,1)}, bf16[3,128,512]{2,1,0:T(8,128)(2,1)S(1)}, u32[]{:S(2)}, u32[]{:S(2)}) collective-permute-start(bf16[3,128,512]{2,1,0:T(8,128)(2,1)} %get-tuple-element.155), channel_id=1, source_target_pairs={{0,1},{1,0},{2,3},{3,2},{4,5},{5,4},{6,7},{7,6},{8,9},{9,8},{10,11... | collective-permute-start | bytes 1179656 | tf_op jit(solution)/shard_map/ppermute | solution.py:931
  29.0 35.6 %copy-start.22 = (bf16[128,1024]{1,0:T(8,128)(2,1)}, bf16[128,1024]{1,0:T(8,128)(2,1)S(1)}, u32[]{:S(2)}) copy-start(bf16[128,1024]{1,0:T(8,128)(2,1)S(1)} %constant_dynamic-update-slice_fusion.6.refs_2_) | copy-start | bytes 786436
  29.0 11.2 %collective-permute-start.8 = (bf16[128,1024]{1,0:T(8,128)(2,1)S(1)}, bf16[128,1024]{1,0:T(8,128)(2,1)S(1)}, u32[]{:S(2)}, u32[]{:S(2)}) collective-permute-start(bf16[128,1024]{1,0:T(8,128)(2,1)S(1)} %constant_dynamic-update-slice_fusion.6.refs_2_), channel_id=1, source_target_pairs={{0,2},{2,4},{4,6},{6,0},{1,3},{3,5},{5,7},{7,1},{8,10},{10,12},{12... | collective-permute-start | bytes 786440 | tf_op jit(solution)/shard_map/ppermute | solution.py:934
  31.1 19.3 %collective-permute-start.12 = (bf16[128,1024]{1,0:T(8,128)(2,1)S(1)}, bf16[128,1024]{1,0:T(8,128)(2,1)S(1)}, u32[]{:S(2)}, u32[]{:S(2)}) collective-permute-start(bf16[128,1024]{1,0:T(8,128)(2,1)S(1)} %constant_dynamic-update-slice_fusion.6.refs_2_), channel_id=1, source_target_pairs={{0,4},{2,6},{4,0},{6,2},{1,5},{3,7},{5,1},{7,3},{8,12},{10,14},{12... | collective-permute-start | bytes 786440 | tf_op jit(solution)/shard_map/ppermute | solution.py:934
  31.5 42.0 %collective-permute-start.16 = (bf16[128,1024]{1,0:T(8,128)(2,1)S(1)}, bf16[128,1024]{1,0:T(8,128)(2,1)}, u32[]{:S(2)}, u32[]{:S(2)}) collective-permute-start(bf16[128,1024]{1,0:T(8,128)(2,1)S(1)} %constant_dynamic-update-slice_fusion.6.refs_2_), channel_id=1, source_target_pairs={{0,6},{2,0},{4,2},{6,4},{1,7},{3,1},{5,3},{7,5},{8,14},{10,8},{12,... | collective-permute-start | bytes 786440 | tf_op jit(solution)/shard_map/ppermute | solution.py:934
  40.1 34.9 %collective-permute-start.10 = (bf16[128,1024]{1,0:T(8,128)(2,1)S(1)}, bf16[128,1024]{1,0:T(8,128)(2,1)S(1)}, u32[]{:S(2)}, u32[]{:S(2)}) collective-permute-start(bf16[128,1024]{1,0:T(8,128)(2,1)S(1)} %collective-permute-done.8.refs_2_), channel_id=1, source_target_pairs={{0,16},{8,24},{16,0},{24,8},{1,17},{9,25},{17,1},{25,9},{2,18},{10... | collective-permute-start | bytes 786440 | tf_op jit(solution)/shard_map/ppermute | solution.py:940
  41.7 34.8 %collective-permute-start.11 = (bf16[128,1024]{1,0:T(8,128)(2,1)S(1)}, bf16[128,1024]{1,0:T(8,128)(2,1)}, u32[]{:S(2)}, u32[]{:S(2)}) collective-permute-start(bf16[128,1024]{1,0:T(8,128)(2,1)S(1)} %collective-permute-done.8.refs_2_), channel_id=1, source_target_pairs={{0,24},{8,16},{16,8},{24,0},{1,25},{9,17},{17,9},{25,1},{2,26},{10... | collective-permute-start | bytes 786440 | tf_op jit(solution)/shard_map/ppermute | solution.py:940
  44.6 7.3 %collective-permute-start.1 = (bf16[16,1024]{1,0:T(8,128)(2,1)S(1)}, bf16[16,1024]{1,0:T(8,128)(2,1)S(1)}, u32[]{:S(2)}, u32[]{:S(2)}) collective-permute-start(bf16[16,1024]{1,0:T(8,128)(2,1)S(1)} %pad_maximum_fusion.10), channel_id=1, source_target_pairs={{0,2},{2,4},{4,6},{1,3},{3,5},{5,7},{8,10},{10,12},{12,14},{9,11},... | collective-permute-start | bytes 98312 | tf_op jit(solution)/shard_map/ppermute | solution.py:937
  50.4 26.6 %collective-permute-start.9 = (bf16[128,1024]{1,0:T(8,128)(2,1)S(1)}, bf16[128,1024]{1,0:T(8,128)(2,1)S(1)}, u32[]{:S(2)}, u32[]{:S(2)}) collective-permute-start(bf16[128,1024]{1,0:T(8,128)(2,1)S(1)} %collective-permute-done.8.refs_2_), channel_id=1, source_target_pairs={{0,8},{8,0},{16,24},{24,16},{1,9},{9,1},{17,25},{25,17},{2,10},{10... | collective-permute-start | bytes 786440 | tf_op jit(solution)/shard_map/ppermute | solution.py:940
  51.9 41.3 %collective-permute-start.13 = (bf16[128,1024]{1,0:T(8,128)(2,1)S(1)}, bf16[128,1024]{1,0:T(8,128)(2,1)S(1)}, u32[]{:S(2)}, u32[]{:S(2)}) collective-permute-start(bf16[128,1024]{1,0:T(8,128)(2,1)S(1)} %collective-permute-done.12.refs_2_), channel_id=1, source_target_pairs={{0,8},{8,0},{16,24},{24,16},{1,9},{9,1},{17,25},{25,17},{2,10},{10... | collective-permute-start | bytes 786440 | tf_op jit(solution)/shard_map/ppermute | solution.py:940
  73.5 21.2 %collective-permute-start.14 = (bf16[128,1024]{1,0:T(8,128)(2,1)S(1)}, bf16[128,1024]{1,0:T(8,128)(2,1)S(1)}, u32[]{:S(2)}, u32[]{:S(2)}) collective-permute-start(bf16[128,1024]{1,0:T(8,128)(2,1)S(1)} %collective-permute-done.12.refs_2_), channel_id=1, source_target_pairs={{0,16},{8,24},{16,0},{24,8},{1,17},{9,25},{17,1},{25,9},{2,18},{10... | collective-permute-start | bytes 786440 | tf_op jit(solution)/shard_map/ppermute | solution.py:940
  75.0 19.7 %collective-permute-start.15 = (bf16[128,1024]{1,0:T(8,128)(2,1)S(1)}, bf16[128,1024]{1,0:T(8,128)(2,1)}, u32[]{:S(2)}, u32[]{:S(2)}) collective-permute-start(bf16[128,1024]{1,0:T(8,128)(2,1)S(1)} %collective-permute-done.12.refs_2_), channel_id=1, source_target_pairs={{0,24},{8,16},{16,8},{24,0},{1,25},{9,17},{17,9},{25,1},{2,26},{10... | collective-permute-start | bytes 786440 | tf_op jit(solution)/shard_map/ppermute | solution.py:940
  76.5 47.5 %collective-permute-start.17 = (bf16[128,1024]{1,0:T(8,128)(2,1)}, bf16[128,1024]{1,0:T(8,128)(2,1)}, u32[]{:S(2)}, u32[]{:S(2)}) collective-permute-start(bf16[128,1024]{1,0:T(8,128)(2,1)} %collective-permute-done.16.refs_2_), channel_id=1, source_target_pairs={{0,8},{8,0},{16,24},{24,16},{1,9},{9,1},{17,25},{25,17},{2,10},{10... | collective-permute-start | bytes 786440 | tf_op jit(solution)/shard_map/ppermute | solution.py:940
  88.3 1.6 collective-permute-start.21
  89.9 15.6 %collective-permute-start.22 = (bf16[64,1024]{1,0:T(8,128)(2,1)S(1)}, bf16[64,1024]{1,0:T(8,128)(2,1)S(1)}, u32[]{:S(2)}, u32[]{:S(2)}) collective-permute-start(bf16[64,1024]{1,0:T(8,128)(2,1)S(1)} %broadcast_add_fusion.2), channel_id=1, source_target_pairs={{0,2},{2,4},{4,6},{6,0},{1,3},{3,5},{5,7},{7,1},{8,10},{10,12},{12... | collective-permute-start | bytes 393224 | tf_op jit(solution)/shard_map/ppermute | solution.py:934
  93.2 32.8 %collective-permute-start.18 = (bf16[128,1024]{1,0:T(8,128)(2,1)}, bf16[128,1024]{1,0:T(8,128)(2,1)}, u32[]{:S(2)}, u32[]{:S(2)}) collective-permute-start(bf16[128,1024]{1,0:T(8,128)(2,1)} %collective-permute-done.16.refs_2_), channel_id=1, source_target_pairs={{0,16},{8,24},{16,0},{24,8},{1,17},{9,25},{17,1},{25,9},{2,18},{10... | collective-permute-start | bytes 786440 | tf_op jit(solution)/shard_map/ppermute | solution.py:940
  94.7 67.4 %collective-permute-start.20 = (bf16[1024,512]{1,0:T(8,128)(2,1)S(1)}, bf16[1024,512]{1,0:T(8,128)(2,1)S(1)}, u32[]{:S(2)}, u32[]{:S(2)}) collective-permute-start(bf16[1024,512]{1,0:T(8,128)(2,1)S(1)} %broadcast_add_fusion), channel_id=1, source_target_pairs={{0,1},{1,0},{2,3},{3,2},{4,5},{5,4},{6,7},{7,6},{8,9},{9,8},{10,11... | collective-permute-start | bytes 3145736 | tf_op jit(solution)/shard_map/ppermute | solution.py:931
  94.7 23.4 %collective-permute-start.23 = (bf16[64,1024]{1,0:T(8,128)(2,1)S(1)}, bf16[64,1024]{1,0:T(8,128)(2,1)S(1)}, u32[]{:S(2)}, u32[]{:S(2)}) collective-permute-start(bf16[64,1024]{1,0:T(8,128)(2,1)S(1)} %broadcast_add_fusion.2), channel_id=1, source_target_pairs={{0,4},{2,6},{4,0},{6,2},{1,5},{3,7},{5,1},{7,3},{8,12},{10,14},{12... | collective-permute-start | bytes 393224 | tf_op jit(solution)/shard_map/ppermute | solution.py:934
  105.6 16.9 %collective-permute-start.24 = (bf16[64,1024]{1,0:T(8,128)(2,1)S(1)}, bf16[64,1024]{1,0:T(8,128)(2,1)S(1)}, u32[]{:S(2)}, u32[]{:S(2)}) collective-permute-start(bf16[64,1024]{1,0:T(8,128)(2,1)S(1)} %broadcast_add_fusion.2), channel_id=1, source_target_pairs={{0,6},{2,0},{4,2},{6,4},{1,7},{3,1},{5,3},{7,5},{8,14},{10,8},{12,... | collective-permute-start | bytes 393224 | tf_op jit(solution)/shard_map/ppermute | solution.py:934
  118.1 10.5 %collective-permute-start.19 = (bf16[128,1024]{1,0:T(8,128)(2,1)}, bf16[128,1024]{1,0:T(8,128)(2,1)}, u32[]{:S(2)}, u32[]{:S(2)}) collective-permute-start(bf16[128,1024]{1,0:T(8,128)(2,1)} %collective-permute-done.16.refs_2_), channel_id=1, source_target_pairs={{0,24},{8,16},{16,8},{24,0},{1,25},{9,17},{17,9},{25,1},{2,26},{10... | collective-permute-start | bytes 786440 | tf_op jit(solution)/shard_map/ppermute | solution.py:940
  122.5 34.5 %collective-permute-start.25 = (bf16[192,1024]{1,0:T(8,128)(2,1)S(1)}, bf16[192,1024]{1,0:T(8,128)(2,1)S(1)}, u32[]{:S(2)}, u32[]{:S(2)}) collective-permute-start(bf16[192,1024]{1,0:T(8,128)(2,1)S(1)} %constant_dynamic-update-slice_fusion.12.refs_7_), channel_id=1, source_target_pairs={{0,8},{8,0},{16,24},{24,16},{1,9},{9,1},{17,25},{25,17},{2,10},{10... | collective-permute-start | bytes 1179656 | tf_op jit(solution)/shard_map/ppermute | solution.py:940
  124.0 35.3 %collective-permute-start.26 = (bf16[192,1024]{1,0:T(8,128)(2,1)S(1)}, bf16[192,1024]{1,0:T(8,128)(2,1)S(1)}, u32[]{:S(2)}, u32[]{:S(2)}) collective-permute-start(bf16[192,1024]{1,0:T(8,128)(2,1)S(1)} %constant_dynamic-update-slice_fusion.12.refs_7_), channel_id=1, source_target_pairs={{0,16},{8,24},{16,0},{24,8},{1,17},{9,25},{17,1},{25,9},{2,18},{10... | collective-permute-start | bytes 1179656 | tf_op jit(solution)/shard_map/ppermute | solution.py:940
  137.4 24.7 %collective-permute-start.27 = (bf16[192,1024]{1,0:T(8,128)(2,1)S(1)}, bf16[192,1024]{1,0:T(8,128)(2,1)}, u32[]{:S(2)}, u32[]{:S(2)}) collective-permute-start(bf16[192,1024]{1,0:T(8,128)(2,1)S(1)} %constant_dynamic-update-slice_fusion.12.refs_7_), channel_id=1, source_target_pairs={{0,24},{8,16},{16,8},{24,0},{1,25},{9,17},{17,9},{25,1},{2,26},{10... | collective-permute-start | bytes 1179656 | tf_op jit(solution)/shard_map/ppermute | solution.py:940
  138.6 31.4 %collective-permute-start.28 = (bf16[1040,128]{1,0:T(8,128)(2,1)}, bf16[1040,128]{1,0:T(8,128)(2,1)}, u32[]{:S(2)}, u32[]{:S(2)}) collective-permute-start(bf16[1040,128]{1,0:T(8,128)(2,1)} %constant_dynamic-update-slice_fusion.15), channel_id=1, source_target_pairs={{0,2},{2,4},{4,6},{1,3},{3,5},{5,7},{8,10},{10,12},{12,14},{9,11},... | collective-permute-start | bytes 798728 | tf_op jit(solution)/shard_map/ppermute | solution.py:937
  157.0 13.0 %collective-permute-start.29 = (bf16[1040,128]{1,0:T(8,128)(2,1)}, bf16[1040,128]{1,0:T(8,128)(2,1)}, u32[]{:S(2)}, u32[]{:S(2)}) collective-permute-start(bf16[1040,128]{1,0:T(8,128)(2,1)} %constant_dynamic-update-slice_fusion.15), channel_id=1, source_target_pairs={{0,4},{2,6},{1,5},{3,7},{8,12},{10,14},{9,13},{11,15},{16,20},{18,... | collective-permute-start | bytes 798728 | tf_op jit(solution)/shard_map/ppermute | solution.py:937
  159.3 10.7 %collective-permute-start.30 = (bf16[1040,128]{1,0:T(8,128)(2,1)}, bf16[1040,128]{1,0:T(8,128)(2,1)}, u32[]{:S(2)}, u32[]{:S(2)}) collective-permute-start(bf16[1040,128]{1,0:T(8,128)(2,1)} %constant_dynamic-update-slice_fusion.15), channel_id=1, source_target_pairs={{0,6},{1,7},{8,14},{9,15},{16,22},{17,23},{24,30},{25,31}} | collective-permute-start | bytes 798728 | tf_op jit(solution)/shard_map/ppermute | solution.py:937
  189.7 4.1 collective-permute-start.32
  191.8 2.0 collective-permute-start.31
  300.0 46.1 %collective-permute-start.52 = (bf16[128,1024]{1,0:T(8,128)(2,1)}, bf16[128,1024]{1,0:T(8,128)(2,1)S(1)}, u32[]{:S(2)}, u32[]{:S(2)}) collective-permute-start(bf16[128,1024]{1,0:T(8,128)(2,1)} %get-tuple-element.281), channel_id=1, source_target_pairs={{0,8},{8,0},{16,24},{24,16},{1,9},{9,1},{17,25},{25,17},{2,10},{10... | collective-permute-start | bytes 786440 | tf_op jit(solution)/shard_map/ppermute | solution.py:940
  301.5 45.4 %collective-permute-start.53 = (bf16[128,1024]{1,0:T(8,128)(2,1)}, bf16[128,1024]{1,0:T(8,128)(2,1)S(1)}, u32[]{:S(2)}, u32[]{:S(2)}) collective-permute-start(bf16[128,1024]{1,0:T(8,128)(2,1)} %get-tuple-element.282), channel_id=1, source_target_pairs={{0,16},{8,24},{16,0},{24,8},{1,17},{9,25},{17,1},{25,9},{2,18},{10... | collective-permute-start | bytes 786440 | tf_op jit(solution)/shard_map/ppermute | solution.py:940
  307.9 28.5 %collective-permute-start.33 = (bf16[128,1024]{1,0:T(8,128)(2,1)}, bf16[128,1024]{1,0:T(8,128)(2,1)}, u32[]{:S(2)}, u32[]{:S(2)}) collective-permute-start(bf16[128,1024]{1,0:T(8,128)(2,1)} %get-tuple-element.343), channel_id=1, source_target_pairs={{0,6},{2,0},{4,2},{6,4},{1,7},{3,1},{5,3},{7,5},{8,14},{10,8},{12,... | collective-permute-start | bytes 786440 | tf_op jit(solution)/shard_map/ppermute | solution.py:934
  308.6 28.8 %collective-permute-start.34 = (bf16[128,1024]{1,0:T(8,128)(2,1)}, bf16[128,1024]{1,0:T(8,128)(2,1)}, u32[]{:S(2)}, u32[]{:S(2)}) collective-permute-start(bf16[128,1024]{1,0:T(8,128)(2,1)} %get-tuple-element.345), channel_id=1, source_target_pairs={{0,4},{2,6},{4,0},{6,2},{1,5},{3,7},{5,1},{7,3},{8,12},{10,14},{12... | collective-permute-start | bytes 786440 | tf_op jit(solution)/shard_map/ppermute | solution.py:934
  309.9 27.5 %collective-permute-start.35 = (bf16[128,1024]{1,0:T(8,128)(2,1)}, bf16[128,1024]{1,0:T(8,128)(2,1)}, u32[]{:S(2)}, u32[]{:S(2)}) collective-permute-start(bf16[128,1024]{1,0:T(8,128)(2,1)} %get-tuple-element.344), channel_id=1, source_target_pairs={{0,2},{2,4},{4,6},{6,0},{1,3},{3,5},{5,7},{7,1},{8,10},{10,12},{12... | collective-permute-start | bytes 786440 | tf_op jit(solution)/shard_map/ppermute | solution.py:934
  336.4 11.7 %collective-permute-start.54 = (bf16[128,1024]{1,0:T(8,128)(2,1)S(1)}, bf16[128,1024]{1,0:T(8,128)(2,1)S(1)}, u32[]{:S(2)}, u32[]{:S(2)}) collective-permute-start(bf16[128,1024]{1,0:T(8,128)(2,1)S(1)} %copy-done.60), channel_id=1, source_target_pairs={{0,24},{8,16},{16,8},{24,0},{1,25},{9,17},{17,9},{25,1},{2,26},{10... | collective-permute-start | bytes 786440 | tf_op jit(solution)/shard_map/ppermute | solution.py:940
  337.4 65.7 %collective-permute-start.41 = (f32[16,512]{1,0:T(8,128)S(1)}, f32[16,512]{1,0:T(8,128)S(1)}, u32[]{:S(2)}, u32[]{:S(2)}) collective-permute-start(f32[16,512]{1,0:T(8,128)S(1)} %slice.203), channel_id=1, source_target_pairs={{0,1},{1,0},{2,3},{3,2},{4,5},{5,4},{6,7},{7,6},{8,9},{9,8},{10,11... | collective-permute-start | bytes 98312 | tf_op jit(solution)/shard_map/ppermute | solution.py:931
  338.8 38.2 %collective-permute-start.36 = (bf16[128,1024]{1,0:T(8,128)(2,1)S(1)}, bf16[128,1024]{1,0:T(8,128)(2,1)S(1)}, u32[]{:S(2)}, u32[]{:S(2)}) collective-permute-start(bf16[128,1024]{1,0:T(8,128)(2,1)S(1)} %fusion.16.refs_0_), channel_id=1, source_target_pairs={{0,8},{8,0},{16,24},{24,16},{1,9},{9,1},{17,25},{25,17},{2,10},{10... | collective-permute-start | bytes 786440 | tf_op jit(solution)/shard_map/ppermute | solution.py:940
  346.1 27.2 %copy-start.25 = (bf16[208,1024]{1,0:T(8,128)(2,1)S(1)}, bf16[208,1024]{1,0:T(8,128)(2,1)}, u32[]{:S(2)}) copy-start(bf16[208,1024]{1,0:T(8,128)(2,1)} %get-tuple-element.277) | copy-start | bytes 1277956
  346.1 12.9 %collective-permute-start.49 = (bf16[208,1024]{1,0:T(8,128)(2,1)}, bf16[208,1024]{1,0:T(8,128)(2,1)S(1)}, u32[]{:S(2)}, u32[]{:S(2)}) collective-permute-start(bf16[208,1024]{1,0:T(8,128)(2,1)} %get-tuple-element.278), channel_id=1, source_target_pairs={{0,8},{8,0},{16,24},{24,16},{1,9},{9,1},{17,25},{25,17},{2,10},{10... | collective-permute-start | bytes 1277960 | tf_op jit(solution)/shard_map/ppermute | solution.py:940
  346.9 23.1 %collective-permute-start.50 = (bf16[208,1024]{1,0:T(8,128)(2,1)}, bf16[208,1024]{1,0:T(8,128)(2,1)S(1)}, u32[]{:S(2)}, u32[]{:S(2)}) collective-permute-start(bf16[208,1024]{1,0:T(8,128)(2,1)} %get-tuple-element.279), channel_id=1, source_target_pairs={{0,16},{8,24},{16,0},{24,8},{1,17},{9,25},{17,1},{25,9},{2,18},{10... | collective-permute-start | bytes 1277960 | tf_op jit(solution)/shard_map/ppermute | solution.py:940
  348.1 25.2 %collective-permute-start.51 = (bf16[208,1024]{1,0:T(8,128)(2,1)}, bf16[208,1024]{1,0:T(8,128)(2,1)S(1)}, u32[]{:S(2)}, u32[]{:S(2)}) collective-permute-start(bf16[208,1024]{1,0:T(8,128)(2,1)} %get-tuple-element.280), channel_id=1, source_target_pairs={{0,24},{8,16},{16,8},{24,0},{1,25},{9,17},{17,9},{25,1},{2,26},{10... | collective-permute-start | bytes 1277960 | tf_op jit(solution)/shard_map/ppermute | solution.py:940
  359.0 20.4 %collective-permute-start.37 = (bf16[128,1024]{1,0:T(8,128)(2,1)}, bf16[128,1024]{1,0:T(8,128)(2,1)S(1)}, u32[]{:S(2)}, u32[]{:S(2)}) collective-permute-start(bf16[128,1024]{1,0:T(8,128)(2,1)} %copy-done.9), channel_id=1, source_target_pairs={{0,16},{8,24},{16,0},{24,8},{1,17},{9,25},{17,1},{25,9},{2,18},{10... | collective-permute-start | bytes 786440 | tf_op jit(solution)/shard_map/ppermute | solution.py:940
  370.0 12.1 %collective-permute-start.38 = (bf16[128,1024]{1,0:T(8,128)(2,1)}, bf16[128,1024]{1,0:T(8,128)(2,1)S(1)}, u32[]{:S(2)}, u32[]{:S(2)}) collective-permute-start(bf16[128,1024]{1,0:T(8,128)(2,1)} %copy-done.9), channel_id=1, source_target_pairs={{0,24},{8,16},{16,8},{24,0},{1,25},{9,17},{17,9},{25,1},{2,26},{10... | collective-permute-start | bytes 786440 | tf_op jit(solution)/shard_map/ppermute | solution.py:940
  373.7 8.9 %collective-permute-start.55 = (bf16[144,1024]{1,0:T(8,128)(2,1)S(1)}, bf16[144,1024]{1,0:T(8,128)(2,1)S(1)}, u32[]{:S(2)}, u32[]{:S(2)}) collective-permute-start(bf16[144,1024]{1,0:T(8,128)(2,1)S(1)} %get-tuple-element.355), channel_id=1, source_target_pairs={{0,6},{2,0},{4,2},{6,4},{1,7},{3,1},{5,3},{7,5},{8,14},{10,8},{12,... | collective-permute-start | bytes 884744 | tf_op jit(solution)/shard_map/ppermute | solution.py:934
  377.0 20.7 %collective-permute-start.56 = (bf16[144,1024]{1,0:T(8,128)(2,1)S(1)}, bf16[144,1024]{1,0:T(8,128)(2,1)S(1)}, u32[]{:S(2)}, u32[]{:S(2)}) collective-permute-start(bf16[144,1024]{1,0:T(8,128)(2,1)S(1)} %get-tuple-element.356), channel_id=1, source_target_pairs={{0,4},{2,6},{4,0},{6,2},{1,5},{3,7},{5,1},{7,3},{8,12},{10,14},{12... | collective-permute-start | bytes 884744 | tf_op jit(solution)/shard_map/ppermute | solution.py:934
  379.5 18.2 %collective-permute-start.57 = (bf16[144,1024]{1,0:T(8,128)(2,1)S(1)}, bf16[144,1024]{1,0:T(8,128)(2,1)S(1)}, u32[]{:S(2)}, u32[]{:S(2)}) collective-permute-start(bf16[144,1024]{1,0:T(8,128)(2,1)S(1)} %get-tuple-element.357), channel_id=1, source_target_pairs={{0,2},{2,4},{4,6},{6,0},{1,3},{3,5},{5,7},{7,1},{8,10},{10,12},{12... | collective-permute-start | bytes 884744 | tf_op jit(solution)/shard_map/ppermute | solution.py:934
  382.5 22.1 %collective-permute-start.39 = (bf16[4,128,512]{2,1,0:T(8,128)(2,1)S(1)}, bf16[4,128,512]{2,1,0:T(8,128)(2,1)S(1)}, u32[]{:S(2)}, u32[]{:S(2)}) collective-permute-start(bf16[4,128,512]{2,1,0:T(8,128)(2,1)S(1)} %slice.201), channel_id=1, source_target_pairs={{0,1},{1,0},{2,3},{3,2},{4,5},{5,4},{6,7},{7,6},{8,9},{9,8},{10,11... | collective-permute-start | bytes 1572872 | tf_op jit(solution)/shard_map/ppermute | solution.py:931
  397.9 17.7 %collective-permute-start.58 = (bf16[144,1024]{1,0:T(8,128)(2,1)S(1)}, bf16[144,1024]{1,0:T(8,128)(2,1)}, u32[]{:S(2)}, u32[]{:S(2)}) collective-permute-start(bf16[144,1024]{1,0:T(8,128)(2,1)S(1)} %fusion.10), channel_id=1, source_target_pairs={{0,8},{8,0},{16,24},{24,16},{1,9},{9,1},{17,25},{25,17},{2,10},{10... | collective-permute-start | bytes 884744 | tf_op jit(solution)/shard_map/ppermute | solution.py:940
  398.8 16.9 %collective-permute-start.59 = (bf16[144,1024]{1,0:T(8,128)(2,1)S(1)}, bf16[144,1024]{1,0:T(8,128)(2,1)}, u32[]{:S(2)}, u32[]{:S(2)}) collective-permute-start(bf16[144,1024]{1,0:T(8,128)(2,1)S(1)} %fusion.10), channel_id=1, source_target_pairs={{0,16},{8,24},{16,0},{24,8},{1,17},{9,25},{17,1},{25,9},{2,18},{10... | collective-permute-start | bytes 884744 | tf_op jit(solution)/shard_map/ppermute | solution.py:940
  400.1 15.6 %collective-permute-start.60 = (bf16[144,1024]{1,0:T(8,128)(2,1)S(1)}, bf16[144,1024]{1,0:T(8,128)(2,1)}, u32[]{:S(2)}, u32[]{:S(2)}) collective-permute-start(bf16[144,1024]{1,0:T(8,128)(2,1)S(1)} %fusion.10), channel_id=1, source_target_pairs={{0,24},{8,16},{16,8},{24,0},{1,25},{9,17},{17,9},{25,1},{2,26},{10... | collective-permute-start | bytes 884744 | tf_op jit(solution)/shard_map/ppermute | solution.py:940
  403.1 17.3 %collective-permute-start.42 = (f32[16,512]{1,0:T(8,128)S(1)}, f32[16,512]{1,0:T(8,128)S(1)}, u32[]{:S(2)}, u32[]{:S(2)}) collective-permute-start(f32[16,512]{1,0:T(8,128)S(1)} %slice_add_fusion.1), channel_id=1, source_target_pairs={{2,0},{4,2},{6,4},{3,1},{5,3},{7,5},{10,8},{12,10},{14,12},{11,9},... | collective-permute-start | bytes 98312 | tf_op jit(solution)/shard_map/ppermute | solution.py:937
  415.5 4.8 %collective-permute-start.40 = (bf16[1024,512]{1,0:T(8,128)(2,1)}, bf16[1024,512]{1,0:T(8,128)(2,1)S(1)}, u32[]{:S(2)}, u32[]{:S(2)}) collective-permute-start(bf16[1024,512]{1,0:T(8,128)(2,1)} %get-tuple-element.262), channel_id=1, source_target_pairs={{0,1},{1,0},{2,3},{3,2},{4,5},{5,4},{6,7},{7,6},{8,9},{9,8},{10,11... | collective-permute-start | bytes 3145736 | tf_op jit(solution)/shard_map/ppermute | solution.py:931
  417.3 2.2 collective-permute-start.61
  424.5 1.6 collective-permute-start.44
  426.9 4.1 collective-permute-start.45
  430.3 8.7 %collective-permute-start.43 = (f32[1024,1]{0,1:T(1,128)S(1)}, f32[1024,1]{0,1:T(1,128)S(1)}, u32[]{:S(2)}, u32[]{:S(2)}) collective-permute-start(f32[1024,1]{0,1:T(1,128)S(1)} %bitcast.99), channel_id=1, source_target_pairs={{0,1},{1,0},{2,3},{3,2},{4,5},{5,4},{6,7},{7,6},{8,9},{9,8},{10,11... | collective-permute-start | bytes 12296 | tf_op jit(solution)/shard_map/ppermute | solution.py:931
  431.0 5.2 %collective-permute-start.46 = (f32[12384]{0:T(1024)S(1)}, f32[12384]{0:T(1024)S(1)}, u32[]{:S(2)}, u32[]{:S(2)}) collective-permute-start(f32[12384]{0:T(1024)S(1)} %add.214), channel_id=1, source_target_pairs={{0,16},{8,24},{16,0},{24,8},{1,17},{9,25},{17,1},{25,9},{2,18},{10... | collective-permute-start | bytes 148616 | tf_op jit(solution)/shard_map/ppermute | solution.py:940
  436.3 4.8 %collective-permute-start.47 = (f32[12384]{0:T(1024)S(1)}, f32[12384]{0:T(1024)S(1)}, u32[]{:S(2)}, u32[]{:S(2)}) collective-permute-start(f32[12384]{0:T(1024)S(1)} %add.215), channel_id=1, source_target_pairs={{0,2},{2,0},{4,6},{6,4},{1,3},{3,1},{5,7},{7,5},{8,10},{10,8},{12,... | collective-permute-start | bytes 148616 | tf_op jit(solution)/shard_map/ppermute | solution.py:1382
  441.1 5.1 %collective-permute-start.48 = (f32[12384]{0:T(1024)S(1)}, f32[12384]{0:T(1024)S(1)}, u32[]{:S(2)}, u32[]{:S(2)}) collective-permute-start(f32[12384]{0:T(1024)S(1)} %add.216), channel_id=1, source_target_pairs={{0,4},{2,6},{4,0},{6,2},{1,5},{3,7},{5,1},{7,3},{8,12},{10,14},{12... | collective-permute-start | bytes 148616 | tf_op jit(solution)/shard_map/ppermute | solution.py:1382
  (61 other events, 526.0 us)

commit v4 on v3

--- a/solution.py
+++ b/solution.py
@@ -294,11 +294,15 @@
         ):
             head = w * per + jnp.bitwise_xor(di, m)
             v = jnp.transpose(zx[:, pl.ds(pl.multiple_of(head * wide, wide), wide)])
-            if m == 0:
-                whole_o[...] = v
-            else:
-                some_o[m - 1] = v
-            o_o[m] = ow[pl.ds(pl.multiple_of(head * HEADDIM, HEADDIM), HEADDIM), :]
+            for i in range(2):
+                part = v[i * HEADDIM : (i + 1) * HEADDIM, :]
+                if m == 0:
+                    whole_o[i] = part
+                else:
+                    some_o[i, (m - 1) * HEADDIM : m * HEADDIM, :] = part
+            o_o[m * HEADDIM : (m + 1) * HEADDIM, :] = ow[
+                pl.ds(pl.multiple_of(head * HEADDIM, HEADDIM), HEADDIM), :
+            ]
     n = bcdt.shape[1]
     bcdt_o[0:n, :] = jnp.transpose(bcdt[...])
     bcdt_o[n:, :] = jnp.broadcast_to(gain[...], (HALO, gain.shape[1]))
@@ -317,11 +321,9 @@
     table_o[...] = rows
 
 
-def entry_kernel(
-    per, hm, ho, hh, bcdt, table, cbc, sel,
-    xn_o, xnh_o, r_o, raw_o, rawh_o, u_o, b_o, c_o, dt_o, sig_o, cl_o, clt_o, tot_o,
-    dt2_o, e12_o, tl2_o, dttl2_o, ec2_o, edt2_o, rate_o, wdt_o, buf,
-):
+def entry_first(per, hm, ho, hh, bcdt, table, cbc, sel, o, xn_o, buf):
+    xnh_o, r_o, raw_o, rawh_o, dt_o, sig_o = o.xnh, o.r, o.raw, o.rawh, o.dt, o.sig
+    cl_o, clt_o, rate_o, wdt_o, b_o = o.cl, o.clt, o.rate, o.wdt, o.b
     rows = hm.shape[0]
     state = b_o.shape[1]
     per_head = dot(table[...], sel[...], HIGH)
@@ -344,6 +346,7 @@
 
     half = hm.shape[1]
     xnh, _ = norm(hh[:, :half], hh[:, half:])
+    xnh = jnp.where(lax.axis_index("head") > 0, xnh.astype(F32), 0.0).astype(BF)
     xnh_o[...] = xnh
     buf[0:HALO, :] = dot_t(xnh, wbc[...])
     rawh_o[...] = buf[0:HALO, :]
@@ -368,6 +371,13 @@
         return carry
 
     lax.fori_loop(0, blocks, first, 0, unroll=2)
+
+
+def entry_second(cbc, o, tot_o, buf):
+    u_o, b_o, c_o, dt_o, cl_o, clt_o = o.ubc, o.b, o.c, o.dt, o.cl, o.clt
+    dt2_o, e12_o, tl2_o, dttl2_o, ec2_o, edt2_o = o.dt2, o.e12, o.tl2, o.dttl2, o.ec2, o.edt2
+    state = b_o.shape[1]
+    blocks = b_o.shape[0] // Q
 
     def second(i, carry):
         here = pl.ds(pl.multiple_of(i * Q, Q), Q)
@@ -422,62 +432,204 @@
     return low.astype(BF), (1.0 - low).astype(BF)
 
 
-def project_kernel(s, per, *refs):
-    xn, xnh, pieces, cw, dt2, edt2, ex, b, rest = take(refs, 0, 0, per, 0, 0, 0, 0, 0)
-    wz_o, wx_o, z_o, xr_o, xrh_o, u_o, xdt_o, s_o, buf, acc = rest
+def project(s, per, xn, o, w, cw, ex, z_o, xr_o, xrh_o, u_o, xdt_o, msg, buf, acc):
     rows = z_o.shape[0]
     gc = per * HEADDIM
     cols = slice(s * gc, s * gc + gc)
-    wx = jnp.concatenate([v[HEADDIM:, :] for v in pieces], axis=0)
-    wz = jnp.concatenate([v[:HEADDIM, :] for v in pieces], axis=0)
-
-    @pl.when(pl.program_id(0) == 0)
-    def _():
-        wz_o[...] = wz
-        wx_o[...] = wx
-        xh = dot_t(xnh[...], wx)
-        buf[0:HALO, :] = xh
-        xrh_o[...] = xh
-        acc[...] = jnp.zeros_like(acc)
-
-    @pl.when(pl.program_id(0) > 0)
-    def _():
-        buf[0:HALO, :] = buf[rows : rows + HALO, :]
-
-    buf[HALO:, :] = dot_t(xn[...], wx)
-    z_o[...] = dot_t(xn[...], wz)
-    for i in range(rows // Q):
-        here = slice(i * Q, i * Q + Q)
-        win = buf[i * Q : i * Q + Q + HALO, :]
-        u = jnp.zeros((Q, gc), F32)
-        for k in range(4):
-            u = u + cw[k : k + 1, cols] * win[HALO - 3 + k : HALO - 3 + k + Q, :]
-        xr_o[here, :] = win[HALO:, :].astype(BF)
-        u_o[here, :] = u
-        xs = u * sigmoid(u)
-        xdt_o[here, :] = (xs * dot(dt2[here, :], ex[:, cols])).astype(BF)
-        acc[...] += t_dot((xs * dot(edt2[here, :], ex[:, cols])).astype(BF), b[here, :])
-
-    @pl.when(pl.program_id(0) == pl.num_programs(0) - 1)
-    def _():
-        s_o[...] = acc[...].astype(BF)
-
-
-def inside_kernel(s, per, xdt, b, c, cl, clt, y_o):
+    xh = dot_t(o.xnh[...], w[1, cols, :])
+    buf[0:HALO, :] = xh
+    xrh_o[...] = xh
+    acc[...] = jnp.zeros_like(acc)
+    cut = rows // 2 if rows // 2 % Q == 0 else rows
+
+    def part(j, carry):
+        base = j * cut
+        here = pl.ds(pl.multiple_of(base, Q), cut)
+        buf[pl.ds(pl.multiple_of(base + HALO, HALO), cut), :] = dot_t(xn[here, :], w[1, cols, :])
+        z_o[here, :] = dot_t(xn[here, :], w[0, cols, :])
+        for i in range(cut // Q):
+            here = pl.ds(pl.multiple_of(base + i * Q, Q), Q)
+            win = buf[pl.ds(pl.multiple_of(base + i * Q, Q), Q + HALO), :]
+            u = jnp.zeros((Q, gc), F32)
+            for k in range(4):
+                u = u + cw[k : k + 1, cols] * win[HALO - 3 + k : HALO - 3 + k + Q, :]
+            xr_o[here, :] = win[HALO:, :].astype(BF)
+            u_o[here, :] = u
+            xs = u * sigmoid(u)
+            xdt_o[here, :] = (xs * dot(o.dt2[here, :], ex[:, cols])).astype(BF)
+            acc[...] += t_dot((xs * dot(o.edt2[here, :], ex[:, cols])).astype(BF), o.b[here, :])
+        return carry
+
+    lax.fori_loop(0, rows // cut, part, 0)
+    msg[cols, :] = acc[...].astype(BF)
+
+
+def inside(s, per, xdt, o, y_o):
     mask = tri("ge")
     low, high = lane_masks()
-    for i in range(xdt.shape[0] // Q):
-        rows = slice(i * Q, i * Q + Q)
-        g = dot_t(c[rows, :], b[rows, :])
-        clv, cltv = cl[rows, :], clt[:, rows]
-        for p in range(xdt.shape[1] // Q):
-            here = slice(p * Q, p * Q + Q)
-            h = s * per + 2 * p
-            ws = [(g * decay(clv, cltv, j, mask)).astype(BF) for j in (h, h + 1)]
-            x = xdt[rows, here]
-            y_o[rows, here] = dot(
-                jnp.concatenate(ws, axis=1), jnp.concatenate([x * low, x * high], axis=0)
-            ).astype(BF)
+    rows = xdt.shape[0]
+    some = 4 if rows % (4 * Q) == 0 else 1
+
+    def part(j, carry):
+        for i in range(some):
+            here = pl.ds(pl.multiple_of((j * some + i) * Q, Q), Q)
+            g = dot_t(o.c[here, :], o.b[here, :])
+            clv, cltv = o.cl[here, :], o.clt[:, here]
+            for p in range(xdt.shape[1] // Q):
+                lanes = slice(p * Q, p * Q + Q)
+                h = s * per + 2 * p
+                ws = [(g * decay(clv, cltv, k, mask)).astype(BF) for k in (h, h + 1)]
+                x = xdt[here, lanes]
+                y_o[here, lanes] = dot(
+                    jnp.concatenate(ws, axis=1), jnp.concatenate([x * low, x * high], axis=0)
+                ).astype(BF)
+        return carry
+
+    lax.fori_loop(0, rows // (some * Q), part, 0)
+
+
+class Named:
+    def __init__(self, names, refs):
+        for name, ref in zip(names, refs):
+            setattr(self, name, ref)
+
+
+KEPT = (
+    "xnh", "r", "raw", "rawh", "ubc", "b", "c", "dt", "sig", "cl", "clt", "dt2", "e12", "tl2",
+    "dttl2", "ec2", "edt2", "rate", "wdt", "tot", "table",
+)
+
+
+def front_kernel(per, nz, *refs):
+    hidden, first, first2, rest, rest2, bcdt, table, cbc, sel, ex, refs = take(refs, *[0] * 10)
+    out_mine, out2, cot, refs = take(refs, 0, 0, 0)
+    w_o, wo_o, cot_o, xn_o, refs = take(refs, 0, 0, 0, 0)
+    z_o, xr_o, u_o, xdt_o, y_o, messages_o, xrh_o, refs = take(refs, *[nz] * 5, nz - 1, nz)
+    kept, refs = refs[: len(KEPT)], refs[len(KEPT) :]
+    o = Named(KEPT, kept)
+    z_v, xr_v, u_v, xdt_v, y_v, refs = take(refs, *[nz] * 5)
+    w, ho, eh, bc, xn, msg, buf, bcbuf, acc, sends, receives, locals_ = refs
+    rows, half = hidden.shape
+    gc = per * HEADDIM
+    top = nz * gc
+    sibling = {"width": 1 - lax.axis_index("width")}
+    z_peers = line_peers(nz, 1)
+    d_peers = plane_peers(per)
+    used = [0]
+
+    def copy(source, target, peer):
+        i = used[0]
+        used[0] += 1
+        return remote(source, target, sends, receives, i, peer)
+
+    left, right = pl.ds(0, half), pl.ds(half, half)
+    swap_first = copy(first2, w.at[:, pl.ds(0, HEADDIM), right], sibling)
+    swap_rest = copy(rest2, w.at[:, pl.ds(HEADDIM, gc - HEADDIM), right], sibling)
+    swap_hidden = copy(hidden, ho, sibling)
+    swap_bc = copy(bcdt, bc.at[:, right], sibling)
+    swap_out = copy(out2, wo_o.at[pl.ds(0, gc), right], sibling)
+    swap_cot = copy(cot, cot_o, sibling)
+    z_table, z_w, z_out, z_state, z_state2 = [], [], [], [], []
+    for k, peer in enumerate(z_peers):
+        s = k + 1
+        z_table.append(copy(table, o.table.at[:, pl.ds(s * gc, gc)], peer))
+        own = w.at[:, pl.ds(0, HEADDIM), :]
+        z_w.append(copy(own, w.at[:, pl.ds(s * gc, HEADDIM), :], peer))
+        z_out.append(
+            copy(wo_o.at[pl.ds(0, HEADDIM), :], wo_o.at[pl.ds(s * gc, HEADDIM), :], peer)
+        )
+        most = pl.ds(0, top - gc)
+        z_state.append(copy(msg.at[most, :], messages_o[k].at[most, :], peer))
+        more = pl.ds(top - gc, gc + HALO)
+        z_state2.append(copy(msg.at[more, :], messages_o[k].at[more, :], peer))
+    last = pl.ds(rows - HALO, HALO)
+    edge1 = copy(hidden.at[last, :], eh.at[:, left], z_peers[0])
+    edge2 = copy(ho.at[last, :], eh.at[:, right], z_peers[0])
+    p_w = {s: [] for s in range(1, nz)}
+    p_out = {s: [] for s in range(1, nz)}
+    for s in range(1, nz):
+        for k, peer in enumerate(d_peers):
+            mine = pl.ds(s * gc, HEADDIM)
+            there = pl.ds(s * gc + (k + 1) * HEADDIM, HEADDIM)
+            p_w[s].append(copy(w.at[:, mine, :], w.at[:, there, :], peer))
+            p_out[s].append(copy(wo_o.at[mine, :], wo_o.at[there, :], peer))
+
+    places = [0]
+
+    def local(source, target):
+        i = places[0]
+        places[0] += 1
+        found = pltpu.make_async_copy(source, target, locals_.at[i])
+        found.start()
+        return found
+
+    def start(copies):
+        for c in copies:
+            c.start()
+
+    def arrive(copies):
+        for c in copies:
+            c.wait_recv()
+
+    ready = [
+        local(first, w.at[:, pl.ds(0, HEADDIM), left]),
+        local(rest, w.at[:, pl.ds(HEADDIM, gc - HEADDIM), left]),
+        local(bcdt, bc.at[:, left]),
+        local(table, o.table.at[:, pl.ds(0, gc)]),
+        local(out_mine, wo_o.at[pl.ds(0, gc), left]),
+    ]
+    meet([sibling, *z_peers, *line_peers(nz, -1), *d_peers])
+    start([swap_first, *z_table, swap_hidden, swap_bc, edge1, swap_rest, swap_out, swap_cot])
+    ready[0].wait()
+    arrive([swap_first])
+    start(z_w)
+    arrive([swap_hidden])
+    start([edge2])
+    for c in ready[1:]:
+        c.wait()
+    arrive([swap_bc, *z_table, edge1, edge2])
+    entry_first(per, hidden, ho, eh, bc, o.table, cbc, sel, o, xn, bcbuf)
+    arrive([z_w[0]])
+    start(p_w[1])
+    entry_second(cbc, o, o.tot, bcbuf)
+    msg[top:, :] = o.tot[...]
+    pending = [local(xn, xn_o)]
+    arrive([swap_out])
+    start(z_out)
+    arrive([swap_rest])
+    taps = o.table
+    for s in range(nz):
+        if s > 0:
+            arrive(p_w[s])
+        project(
+            s, per, xn, o, w, taps, ex, z_v[s], xr_v[s], xrh_o[s], u_v[s], xdt_v[s], msg, buf, acc
+        )
+        for a, b in ((z_v, z_o), (xr_v, xr_o), (u_v, u_o), (xdt_v, xdt_o)):
+            pending.append(local(a[s], b[s]))
+        if s == 0:
+            for k in range(2, nz):
+                arrive([z_w[k - 1]])
+                start(p_w[k])
+        if s == nz - 2:
+            start(z_state)
+            for k in range(1, nz):
+                arrive([z_out[k - 1]])
+                start(p_out[k])
+        if s == nz - 1:
+            start(z_state2)
+            pending.append(local(w, w_o))
+        inside(s, per, xdt_v[s], o, y_v[s])
+        pending.append(local(y_v[s], y_o[s]))
+    everything = [swap_first, swap_rest, swap_hidden, swap_bc, swap_out, swap_cot, edge1, edge2]
+    everything += [*z_table, *z_w, *z_out, *z_state, *z_state2]
+    for s in range(1, nz):
+        everything += p_w[s] + p_out[s]
+        arrive(p_out[s])
+    arrive([swap_cot, *z_state, *z_state2])
+    for c in everything:
+        c.wait_send()
+    for c in pending:
+        c.wait()
 
 
 def head_scale(clt, first, per, state):
@@ -526,7 +678,8 @@
 
     @pl.when(pl.program_id(0) == 0)
     def _():
-        from_messages(messages, 1, groups, per, s.shape[1], s)
+        z_index = lax.axis_index("head")
+        from_messages(messages, 1, groups, per, s.shape[1], s, lambda k: z_index - k >= 0)
 
     square = jnp.zeros((Q, gc), F32)
     inner = jnp.zeros((Q, gc), F32)
@@ -633,68 +786,6 @@
     )
 
 
-def inside_back_kernel(groups, per, *refs):
-    n = len(groups)
-    xdt, dys, b, c, cl, clt, message, early, rest = take(refs, n, n, 0, 0, 0, 0, 0, per)
-    dx_o, rest = take(rest, n)
-    db_o, dc_o, da_o, rest = take(rest, 0, 0, 0)
-    messages_o, early_o, rest = take(rest, n - 1, per - 1)
-    kt, sends, receives = rest
-    nz = n
-
-    def copies():
-        found = []
-        for i, peer in enumerate(line_peers(nz, -1)):
-            found.append(remote(message, messages_o[i], sends, receives, i, peer))
-        for i, peer in enumerate(plane_peers(per)):
-            found.append(remote(early[i + 1], early_o[i], sends, receives, nz - 1 + i, peer))
-        return found
-
-    @pl.when(pl.program_id(0) == 0)
-    def _():
-        meet(line_peers(nz, -1) + plane_peers(per))
-        for copy in copies():
-            copy.start()
-
-    @pl.when(pl.program_id(0) == pl.num_programs(0) - 1)
-    def _():
-        for copy in copies():
-            copy.wait()
-
-    mask = tri("ge")
-    low, high = lane_masks()
-    g = dot_t(c[...], b[...])
-    clv, cltv = cl[...], clt[...]
-    heads = clt.shape[0]
-    lane = lax.broadcasted_iota(jnp.int32, (Q, heads), 1)
-    dg = jnp.zeros((Q, Q), F32)
-    rsum = jnp.zeros((Q, heads), F32)
-    for s in groups:
-        for p in range(per // 2):
-            here = slice(p * Q, p * Q + Q)
-            x = xdt[s][:, here]
-            dy = dys[s][:, here]
-            pp = dot_t(dy, jnp.concatenate([x * low, x * high], axis=0))
-            ws = []
-            for j in range(2):
-                h = s * per + 2 * p + j
-                ell = decay(clv, cltv, h, mask)
-                ws.append((g * ell).astype(BF))
-                pe = pp[:, j * Q : j * Q + Q] * ell
-                dg = dg + pe
-                m = pe * g
-                rsum = jnp.where(lane == h, jnp.sum(m, axis=1, keepdims=True), rsum)
-                kt[h : h + 1, :] = jnp.sum(m, axis=0, keepdims=True)
-            dx_o[s][:, here] = t_dot(
-                jnp.concatenate(ws, axis=0), jnp.concatenate([dy * low, dy * high], axis=0)
-            )
-    dgb = dg.astype(BF)
-    dc_o[...] = dot(dgb, b[...])
-    db_o[...] = t_dot(dgb, c[...])
-    upper = tri("le").astype(F32)
-    da_o[...] = dot(upper, rsum, HIGH) - dot_t(upper, kt[...], HIGH)
-
-
 def conv_back(d, nxt, taps, raw, rawh, grad_o, out_o, outh_o, last):
     win = jnp.concatenate([d, nxt[...]], axis=0)
     back = jnp.zeros_like(d)
@@ -720,101 +811,208 @@
         outh_o[...] = back_h.astype(BF)
 
 
-def back_kernel(groups, per, final, *refs):
+def scan_back_kernel(groups, per, *refs):
     n = len(groups)
-    dxi, dys, u, xr, xrh, st, rest = take(refs, n, n, n, n, n, n)
-    (b, c, dbi, dci, dai, dti, dt, sig, clt, dt2, e12, tl2), rest = rest[:12], rest[12:]
+    nz = n
+    xdt, dys, u, xr, st, xrh, rest = take(refs, n, n, n, n, n, n)
+    (b, c, cl, clt, dt, sig, dt2, e12, tl2), rest = rest[:9], rest[9:]
     (ubc, braw, brawh, cw, cbc, rate, dsk, ex, er), rest = rest[:9], rest[9:]
-    nz = dt.shape[1] // per
-    messages, _, _, dx_o, dxh_o, gcx_o, rest = take(rest, nz - 1, 0, 0, n, n, n)
-    db_o, dc_o, dt_o, ga_o, gbias_o, bc_o, bch_o, gcb_o, ds, vs = rest[:10]
-    du_next, rest = take(rest[10:], n)
-    (db_next,) = rest
+    message, early, rest = take(rest, 0, per)
+    dx_o, dxh_o, gcx_o, rest = take(rest, n, n, n)
+    dt_o, ga_o, gbias_o, bc_o, bch_o, gcb_o, early_o = rest[:7]
+    messages, got, rest = take(rest[7:], nz - 1, per - 1)
+    du_next, line, rest = take(rest, n, nz - 1)
+    db_next, own, low, dxi, dbi, dci, dai, kt, ds, vs, sends, receives, local = rest
     step = pl.program_id(0)
-    blocks = pl.num_programs(0)
+    blocks = pl.num_programs(0) // 2
     heads = dt.shape[1]
     state = b.shape[1]
     gc = per * HEADDIM
+    line_at, back_at, plane_at = 0, nz - 1, 2 * nz - 2
+
+    def state_copies():
+        return [
+            remote(message, messages[i], sends, receives, line_at + i, peer)
+            for i, peer in enumerate(line_peers(nz, -1))
+        ]
+
+    def plane_copies(s):
+        return [
+            remote(
+                early[i + 1].at[s], got[i].at[s], sends, receives, plane_at + s * (per - 1) + i, peer
+            )
+            for i, peer in enumerate(plane_peers(per))
+        ]
+
+    def line_copy(s):
+        return remote(
+            low.at[s], line[s - 1], sends, receives, back_at + s - 1, line_peers(nz, -1)[s - 1]
+        )
+
+    def own_copy():
+        return pltpu.make_async_copy(early[0], own, local)
 
     @pl.when(step == 0)
     def _():
+        own_copy().start()
+        meet(line_peers(nz, -1) + line_peers(nz, 1) + plane_peers(per))
+        for copy in plane_copies(1) + state_copies():
+            copy.start()
+
+    @pl.when(step < blocks)
+    def _():
+        rows = pl.ds(pl.multiple_of(step * Q, Q), Q)
+        mask = tri("ge")
+        lower, upper_lanes = lane_masks()
+        g = dot_t(c[...], b[...])
+        clv, cltv = cl[...], clt[...]
+        lane = lax.broadcasted_iota(jnp.int32, (Q, heads), 1)
+        dg = jnp.zeros((Q, Q), F32)
+        rsum = jnp.zeros((Q, heads), F32)
+        for s in groups:
+            for p in range(per // 2):
+                here = slice(p * Q, p * Q + Q)
+                x = xdt[s][:, here]
+                dy = dys[s][:, here]
+                pp = dot_t(dy, jnp.concatenate([x * lower, x * upper_lanes], axis=0))
+                ws = []
+                for j in range(2):
+                    h = s * per + 2 * p + j
+                    ell = decay(clv, cltv, h, mask)
+                    ws.append((g * ell).astype(BF))
+                    pe = pp[:, j * Q : j * Q + Q] * ell
+                    dg = dg + pe
+                    m = pe * g
+                    rsum = jnp.where(lane == h, jnp.sum(m, axis=1, keepdims=True), rsum)
+                    kt[h : h + 1, :] = jnp.sum(m, axis=0, keepdims=True)
+                dxi[rows, s * gc + p * Q : s * gc + p * Q + Q] = t_dot(
+                    jnp.concatenate(ws, axis=0),
+                    jnp.concatenate([dy * lower, dy * upper_lanes], axis=0),
+                )
+        dgb = dg.astype(BF)
+        dci[rows, :] = dot(dgb, b[...])
+        dbi[rows, :] = t_dot(dgb, c[...])
+        upper = tri("le").astype(F32)
+        dai[rows, :] = dot(upper, rsum, HIGH) - dot_t(upper, kt[...], HIGH)
+
+    @pl.when(step == blocks)
+    def _():
+        for copy in state_copies():
+            copy.wait()
         z = lax.axis_index("head")
         from_messages(messages, -1, groups, per, state, ds, lambda k: z + k < nz)
         for i in range(n):
             du_next[i][...] = jnp.zeros_like(du_next[i])
             gcx_o[i][...] = jnp.zeros_like(gcx_o[i])
-        vs[...] = jnp.zeros_like(vs)
         db_next[...] = jnp.zeros_like(db_next)
         gcb_o[...] = jnp.zeros_like(gcb_o)
         ga_o[...] = jnp.zeros_like(ga_o)
         gbias_o[...] = jnp.zeros_like(gbias_o)
 
-    last = step == blocks - 1
-    rsum = jnp.zeros((Q, heads), F32)
-    gsum = jnp.zeros((Q, heads), F32)
-    ddt = jnp.zeros((Q, heads), F32)
-    dbs = dbi[...]
-    dcs = dci[...]
-    for i, s in enumerate(groups):
-        here = slice(s * gc, s * gc + gc)
-        mine = slice(i * gc, i * gc + gc)
-        ehere = er[here, :]
-        sb = st[i][0]
-        dsv = ds[mine, :]
-        dsb = dsv.astype(BF)
-        dy = dys[i][...].astype(F32)
-        dye = dy * dot(e12[...], ex[:, here])
-        dyb = dye.astype(BF)
-        rsum = rsum + dot((dye * dot_t(c[...], sb)).astype(BF), ehere)
-        dcs = dcs + dot(dyb, sb)
-        bds = dot_t(b[...], dsb)
-        tail = dot(tl2[...], ex[:, here])
-        dtx = dot(dt2[...], ex[:, here])
-        uu = u[i][...]
-        su = sigmoid(uu)
-        xs = uu * su
-        xt = xs * dtx * tail
-        gsum = gsum + dot((xt * bds).astype(BF), ehere)
-        dbs = dbs + dot(xt.astype(BF), dsb)
-        dxdt = dxi[i][...] + tail * bds
-        ddt = ddt + dot((dxdt * xs).astype(BF), ehere)
-        eds = head_scale(clt, s * per, per, state) * dsv
-        ev = eds * sb.astype(F32)
-        for j in range(per):
-            h = s * per + j
-            vs[h : h + 1, :] = jnp.sum(
-                ev[j * HEADDIM : (j + 1) * HEADDIM, :], axis=0, keepdims=True
+    @pl.when(step >= blocks)
+    def _():
+        rows = pl.ds(pl.multiple_of((2 * blocks - 1 - step) * Q, Q), Q)
+        last = step == 2 * blocks - 1
+        rsum = jnp.zeros((Q, heads), F32)
+        gsum = jnp.zeros((Q, heads), F32)
+        ddt = jnp.zeros((Q, heads), F32)
+        dbs = dbi[rows, :]
+        dcs = dci[rows, :]
+        for s in groups:
+            here = slice(s * gc, s * gc + gc)
+            ehere = er[here, :]
+            sb = st[s][0]
+            dsv = ds[here, :]
+            dsb = dsv.astype(BF)
+            dy = dys[s][...].astype(F32)
+            dye = dy * dot(e12[...], ex[:, here])
+            dyb = dye.astype(BF)
+            rsum = rsum + dot((dye * dot_t(c[...], sb)).astype(BF), ehere)
+            dcs = dcs + dot(dyb, sb)
+            bds = dot_t(b[...], dsb)
+            tail = dot(tl2[...], ex[:, here])
+            dtx = dot(dt2[...], ex[:, here])
+            uu = u[s][...]
+            su = sigmoid(uu)
+            xs = uu * su
+            xt = xs * dtx * tail
+            gsum = gsum + dot((xt * bds).astype(BF), ehere)
+            dbs = dbs + dot(xt.astype(BF), dsb)
+            dxdt = dxi[rows, here] + tail * bds
+            ddt = ddt + dot((dxdt * xs).astype(BF), ehere)
+            eds = head_scale(clt, s * per, per, state) * dsv
+            ev = eds * sb.astype(F32)
+            for j in range(per):
+                h = s * per + j
+                vs[h : h + 1, :] = jnp.sum(
+                    ev[j * HEADDIM : (j + 1) * HEADDIM, :], axis=0, keepdims=True
+                )
+            ds[here, :] = eds + t_dot(dyb, c[...])
+            du = (dxdt * dtx + dsk[:, here] * dy) * (su + xs * (1.0 - su))
+            conv_back(
+                du, du_next[s], cw.at[:, here], xr[s][...].astype(F32), xrh[s], gcx_o[s],
+                dx_o[s], dxh_o[s], last,
             )
-        ds[mine, :] = eds + t_dot(dyb, c[...])
-        du = (dxdt * dtx + dsk[:, here] * dy) * (su + xs * (1.0 - su))
-        conv_back(
-            du, du_next[i], cw.at[:, here], xr[i][...].astype(F32), xrh[i], gcx_o[i], dx_o[i], dxh_o[i], last
+        vrow = dot_t(jnp.ones((8, state), F32), vs[...], HIGH)
+        da = (
+            dai[rows, :]
+            + split_dot(tri("le").astype(BF), rsum)
+            + split_dot(tri("gt").astype(BF), gsum)
+            + vrow[0:1, :]
         )
-    col = lax.broadcasted_iota(jnp.int32, (1, heads), 1)
-    mine = functools.reduce(
-        jnp.logical_or, [(col >= s * per) & (col < s * per + per) for s in groups]
-    )
-    vrow = dot_t(jnp.ones((8, state), F32), vs[...], HIGH)
-    da = (
-        dai[...]
-        + split_dot(tri("le").astype(BF), rsum)
-        + split_dot(tri("gt").astype(BF), gsum)
-        + vrow[0:1, :]
-    )
-    da = jnp.where(mine, da, 0.0)
-    draw = (rate[...] * da + ddt) * sig[...]
-    dt_o[...] = (dti[...] + draw).astype(dt_o.dtype)
-    ga_o[...] += jnp.sum(da * dt[...], axis=0, keepdims=True)
-    gbias_o[...] += jnp.sum(draw, axis=0, keepdims=True)
-    db_o[...] = dbs
-    dc_o[...] = dcs
-    if final:
+        draw = (rate[...] * da + ddt) * sig[...]
+        dt_o[...] = draw.astype(BF)
+        ga_o[...] += jnp.sum(da * dt[...], axis=0, keepdims=True)
+        gbias_o[...] += jnp.sum(draw, axis=0, keepdims=True)
         d = jnp.concatenate([dbs, dcs], axis=1)
         v = ubc[...]
         sv = sigmoid(v)
         conv_back(
-            d * (sv + v * sv * (1.0 - sv)), db_next, cbc, braw[...], brawh, gcb_o, bc_o, bch_o, last
+            d * (sv + v * sv * (1.0 - sv)), db_next, cbc, braw[...], brawh, gcb_o, bc_o, bch_o,
+            last,
         )
+
+    def add(s):
+        for copy in plane_copies(s):
+            copy.wait()
+
+        def piece(i, carry):
+            part = pl.ds(pl.multiple_of(i * HALO, HALO), HALO)
+            total = own[s, part, :].astype(F32)
+            for v in got:
+                total = total + v[s, part, :].astype(F32)
+            low[s, part, :] = total.astype(BF)
+            return carry
+
+        lax.fori_loop(0, low.shape[1] // HALO, piece, 0, unroll=2)
+
+    order = [*range(1, nz), 0]
+    for k, s in enumerate(order):
+        if k > 0:
+
+            @pl.when(step == (blocks * k * 3) // (2 * nz))
+            def _(s=s):
+                for copy in plane_copies(s):
+                    copy.start()
+
+        if s > 0:
+
+            @pl.when(step == blocks + (blocks * 3 * k) // (4 * (nz - 1)) + 1)
+            def _(s=s):
+                if s == 1:
+                    own_copy().wait()
+                add(s)
+                line_copy(s).start()
+
+    @pl.when(step == 2 * blocks - 1)
+    def _():
+        add(0)
+        for s in range(1, nz):
+            line_copy(s).wait()
+        total = low[0].astype(F32)
+        for v in line:
+            total = total + v[...].astype(F32)
+        early_o[...] = total.astype(BF)
 
 
 def sum_products_kernel(n, *refs):
@@ -828,25 +1026,14 @@
     right_o[...] = total[:, half:].astype(BF)
 
 
-def pull_kernel(per, nz, *refs):
-    cot, cot2, limit, own, others, rest = take(refs, 0, 0, 0, per, per)
-    w_o, mask_o, dyn_o = rest
+def pull_kernel(cot, cot2, limit, w, mask_o, dyn_o):
     rows = cot.shape[0]
     half = cot.shape[1]
-
-    @pl.when(pl.program_id(0) == 0)
-    def _():
-        for m in range(per):
-            w_o[m * HEADDIM : (m + 1) * HEADDIM, :] = own[m][...]
-            for s in range(1, nz):
-                at = (s * per + m) * HEADDIM
-                w_o[at : at + HEADDIM, :] = others[m][(s - 1) * HEADDIM : s * HEADDIM, :]
-
     row = lax.broadcasted_iota(jnp.int32, (rows, 1), 0) + pl.program_id(0) * rows
     keep = row < limit[0, 0]
     for i, v in enumerate((cot, cot2)):
         mask_o[:, i * half : i * half + half] = jnp.where(keep, v[...].astype(F32), 0.0).astype(BF)
-    dyn_o[...] = dot_t(mask_o[...], w_o[...])
+    dyn_o[...] = dot_t(mask_o[...], w[...])
 
 
 def early_grad_kernel(per, yn, masked, dz, xn, *outs):
@@ -950,16 +1137,10 @@
     er = jnp.asarray(onehot.T, BF)
     sel = jnp.asarray(onehot.T * (np.arange(channels) % HEADDIM == 0)[:, None], F32)
 
-    def after_that(v, w):
-        return v + (w[(0,) * w.ndim] * 0).astype(v.dtype)
-
-    def beside(mine, other):
-        return jnp.concatenate([mine, swap(other)], axis=-1)
-
     scal = jnp.repeat(jnp.stack([dt_bias, a_log, d_skip]), HEADDIM, axis=1)
-    piece = shape((2 * HEADDIM, half), BF)
-    some = shape((per - 1, 2 * HEADDIM, half), BF)
-    outs = shape((per, HEADDIM, half), BF)
+    piece = shape((2, HEADDIM, half), BF)
+    some = shape((2, gc - HEADDIM, half), BF)
+    outs = shape((gc, half), BF)
     first, first2, rest, rest2, out_mine, out_mine2, bcdt_t, table = pl.pallas_call(
         functools.partial(prep_kernel, per),
         out_shape=[
@@ -973,107 +1154,69 @@
         in_zx.reshape(half, -1), out_w, in_bcdt, norm_gain[None], conv_x, scal,
         gnorm_gain[None],
     )
-    own_first = beside(first, first2)
-    along = [turn(own_first, s) for s in range(1, nz)]
-    hidden_o = swap(hidden)
-    bcdt_t = beside(bcdt_t, bcdt_t)
-    table = jnp.concatenate([table] + [turn(table, s) for s in range(1, nz)], axis=1)
-    rest = beside(rest, rest2)
-    pieces = [[own_first] + [rest[m] for m in range(per - 1)]]
-    for got in along:
-        pieces.append([got] + [cross(got, m) for m in range(1, per)])
-    wbc = bcdt_t[: 2 * STATE]
-    taps, gain_out, skip = table[:4], table[4:5], table[7:8]
     taps_bc = conv_bc.astype(F32)
     slot = jnp.arange(heads)
     slot_head = ((zi - slot // per) % nz) * own_heads + wi * per + ((slot % per) ^ di)
     pick_heads = (slot_head[:, None] == jnp.arange(HEADS)[None, :]).astype(F32)
 
-    edge = jnp.concatenate([hidden[rows - HALO :], hidden_o[rows - HALO :]], axis=1)
-    edge = shift(edge, 1)
-    ext_rows = rows + HALO
-    narrow = shape((rows, 2 * heads), BF)
-    (
-        xn, xnh, r, braw, brawh, ubc, bs, cs, dt, sig, cl, clt, totals,
-        dt2, e12, tl2, dttl2, ec2, edt2, rate, wdt,
-    ) = pl.pallas_call(
-        functools.partial(entry_kernel, per),
-        out_shape=[
-            shape((rows, model), BF), shape((HALO, model), BF), shape((rows, 1)),
-            shape((rows, 2 * STATE)),
-            shape((HALO, 2 * STATE)), shape((rows, 2 * STATE)), shape((rows, STATE), BF),
-            shape((rows, STATE), BF), shape((rows, heads)), shape((rows, heads)),
-            shape((rows, heads)), shape((heads, rows)), shape((heads, STATE), BF),
-            narrow, narrow, narrow, narrow, narrow, narrow, shape((1, heads)),
-            shape((heads, model), BF),
-        ],
-        scratch_shapes=[pltpu.VMEM((ext_rows, 2 * STATE), F32)],
-        compiler_params=params(),
-        cost_estimate=cost(12),
-        name="entry",
-    )(hidden, hidden_o, edge, bcdt_t, table, taps_bc, sel)
-
-    def send_states(local, sign):
-        message = jnp.concatenate([*local, totals], axis=0)
-        return [shift(message, sign * k) for k in range(1, nz)]
-
-    cut = rows // 2 if rows // 2 % Q == 0 else rows
+    step = lambda i: (i, 0)
+    fix = lambda i: (0, 0)
     part = shape((rows, gc), BF)
     full = shape((rows, channels))
-    step = lambda i: (i, 0)
-    fix = lambda i: (0, 0)
-    gspec = pl.BlockSpec((cut, gc), step)
-    wz, wx, z, xr, xrh, u, xdt, s_local, y_in = ([] for _ in range(9))
-    for s in groups:
-        out = pl.pallas_call(
-            functools.partial(project_kernel, s, per),
-            grid=(rows // cut,),
-            in_specs=[
-                pl.BlockSpec((cut, model), step),
-                pl.BlockSpec((HALO, model), fix),
-                *[whole(v) for v in pieces[s]], whole(taps), pl.BlockSpec((cut, 2 * heads), step),
-                pl.BlockSpec((cut, 2 * heads), step), whole(ex), pl.BlockSpec((cut, STATE), step),
-            ],
-            out_specs=[
-                pl.BlockSpec((gc, model), fix), pl.BlockSpec((gc, model), fix), gspec, gspec,
-                pl.BlockSpec((HALO, gc), fix), gspec, gspec, pl.BlockSpec((gc, STATE), fix),
-            ],
-            out_shape=[
-                shape((gc, model), BF), shape((gc, model), BF), shape((rows, gc)), part,
-                shape((HALO, gc)),
-                shape((rows, gc)), part, shape((gc, STATE), BF),
-            ],
-            scratch_shapes=[pltpu.VMEM((cut + HALO, gc), F32), pltpu.VMEM((gc, STATE), F32)],
-            compiler_params=params(),
-            cost_estimate=cost(5),
-            name="project",
-        )(xn, xnh, *pieces[s], taps, dt2, edt2, ex, bs)
-        for keep, v in zip((wz, wx, z, xr, xrh, u, xdt, s_local), out):
-            keep.append(v)
-        y_in.append(
-            pl.pallas_call(
-                functools.partial(inside_kernel, s, per),
-                grid=(rows // cut,),
-                in_specs=[
-                    gspec, pl.BlockSpec((cut, STATE), step), pl.BlockSpec((cut, STATE), step),
-                    pl.BlockSpec((cut, heads), step), pl.BlockSpec((heads, cut), lambda i: (0, i)),
-                ],
-                out_specs=gspec,
-                out_shape=part,
-                compiler_params=params(),
-                cost_estimate=cost(3),
-                name="inside",
-            )(xdt[s], bs, cs, cl, clt)
-        )
-    messages = send_states(s_local, 1)
-
-    out_mine2 = after_that(out_mine2, totals)
-    out_both = beside(out_mine, out_mine2)
-    out_own = [out_both[m] for m in range(per)]
-    out_first = after_that(out_own[0], s_local[1])
-    out_along = jnp.concatenate([turn(out_first, s) for s in range(1, nz)], axis=0)
-    out_cross = [out_along] + [cross(out_along, m) for m in range(1, per)]
-    cot_o = swap(after_that(cotangent, totals))
+    anywhere = pl.BlockSpec(memory_space=pl.ANY)
+    vmem = pl.BlockSpec(memory_space=pltpu.VMEM)
+    narrow = shape((rows, 2 * heads), BF)
+    kept = dict(
+        xnh=shape((HALO, model), BF), r=shape((rows, 1)), raw=shape((rows, 2 * STATE)),
+        rawh=shape((HALO, 2 * STATE)), ubc=shape((rows, 2 * STATE)), b=shape((rows, STATE), BF),
+        c=shape((rows, STATE), BF), dt=shape((rows, heads)), sig=shape((rows, heads)),
+        cl=shape((rows, heads)), clt=shape((heads, rows)), dt2=narrow, e12=narrow, tl2=narrow,
+        dttl2=narrow, ec2=narrow, edt2=narrow, rate=shape((1, heads)),
+        wdt=shape((heads, model), BF), tot=shape((heads, STATE), BF), table=shape((8, channels)),
+    )
+    wide_part = shape((rows, gc))
+    message_shape = shape((channels + HALO, STATE), BF)
+    out_shapes = [
+        shape((2, channels, model), BF), shape((channels, model), BF), shape((rows, half), BF),
+        shape((rows, model), BF), *[wide_part] * nz, *[part] * nz, *[wide_part] * nz,
+        *[part] * nz, *[part] * nz, *[message_shape] * (nz - 1), *[shape((HALO, gc))] * nz,
+        *[kept[name] for name in KEPT],
+    ]
+    held = lambda v: pltpu.VMEM(v.shape, v.dtype)
+    remotes = 6 + 5 * (nz - 1) + 2 + 2 * (nz - 1) * (per - 1)
+    out = pl.pallas_call(
+        functools.partial(front_kernel, per, nz),
+        in_specs=[vmem] * 10 + [anywhere] * 3,
+        out_specs=[anywhere] * (4 + 5 * nz + nz - 1) + [vmem] * (nz + len(KEPT)),
+        out_shape=out_shapes,
+        scratch_shapes=[
+            *[held(wide_part)] * nz, *[held(part)] * nz, *[held(wide_part)] * nz,
+            *[held(part)] * nz, *[held(part)] * nz, pltpu.VMEM((2, channels, model), BF),
+            pltpu.VMEM((rows, half), BF), pltpu.VMEM((HALO, model), BF),
+            pltpu.VMEM((2 * STATE + HEADS + HALO, model), BF), pltpu.VMEM((rows, model), BF),
+            held(message_shape), pltpu.VMEM((rows + HALO, gc), F32),
+            pltpu.VMEM((rows + HALO, 2 * STATE), F32), pltpu.VMEM((gc, STATE), F32),
+            pltpu.SemaphoreType.DMA((remotes,)), pltpu.SemaphoreType.DMA((remotes,)),
+            pltpu.SemaphoreType.DMA((7 + 5 * nz,)),
+        ],
+        compiler_params=pltpu.CompilerParams(
+            vmem_limit_bytes=VMEM, collective_id=1, has_side_effects=True
+        ),
+        cost_estimate=cost(90),
+        name="front",
+    )(
+        hidden, first, first2, rest, rest2, bcdt_t, table, taps_bc, sel, ex, out_mine, out_mine2,
+        cotangent,
+    )
+    weights, wout, cot_o, xn, out = out[0], out[1], out[2], out[3], out[4:]
+    z, xr, u, xdt, y_in, messages, xrh, out = take(out, *[nz] * 5, nz - 1, nz)
+    o = Named(KEPT, out)
+    xnh, r, braw, brawh, ubc, bs, cs = o.xnh, o.r, o.raw, o.rawh, o.ubc, o.b, o.c
+    dt, sig, cl, clt, rate, wdt, totals, table = o.dt, o.sig, o.cl, o.clt, o.rate, o.wdt, o.tot, o.table
+    dt2, e12, tl2, dttl2, ec2, edt2 = o.dt2, o.e12, o.tl2, o.dttl2, o.ec2, o.edt2
+    taps, gain_out, skip = table[:4], table[4:5], table[7:8]
+    bcdt_t = jnp.concatenate([bcdt_t, swap(bcdt_t)], axis=-1)
+    wbc = bcdt_t[: 2 * STATE]
     limit = (lengths[0] - zi * rows).reshape(1, 1)
 
     wide = pl.BlockSpec((Q, channels), step)
@@ -1084,22 +1227,18 @@
     tspec = pl.BlockSpec((heads, Q), lambda i: (0, i))
     tile = 2 * Q if rows % (2 * Q) == 0 else Q
     smem = pl.BlockSpec(memory_space=pltpu.SMEM)
-    wout, masked, dyn = pl.pallas_call(
-        functools.partial(pull_kernel, per, nz),
+    masked, dyn = pl.pallas_call(
+        pull_kernel,
         grid=(rows // tile,),
         in_specs=[
-            pl.BlockSpec((tile, half), step), pl.BlockSpec((tile, half), step), smem,
-            *[whole(v) for v in out_own + out_cross],
+            pl.BlockSpec((tile, half), step), pl.BlockSpec((tile, half), step), smem, whole(wout),
         ],
-        out_specs=[
-            pl.BlockSpec((channels, model), fix), pl.BlockSpec((tile, model), step),
-            pl.BlockSpec((tile, channels), step),
-        ],
-        out_shape=[shape((channels, model), BF), shape((rows, model), BF), full],
+        out_specs=[pl.BlockSpec((tile, model), step), pl.BlockSpec((tile, channels), step)],
+        out_shape=[shape((rows, model), BF), full],
         compiler_params=params(),
         cost_estimate=cost(5),
         name="pull",
-    )(cotangent, cot_o, limit, *out_own, *out_cross)
+    )(cotangent, cot_o, limit, wout)
     out = pl.pallas_call(
         functools.partial(carry_kernel, groups, per),
         grid=(blocks,),
@@ -1189,7 +1328,6 @@
         high_w = jnp.where(wi == 0, other, mine)
         return jnp.concatenate([low_w, high_w], axis=0)
 
-    anywhere = pl.BlockSpec(memory_space=pl.ANY)
     gcol = pl.BlockSpec((rows, gc), lambda s: (0, s))
     early = pl.pallas_call(
         functools.partial(early_grad_kernel, per),
@@ -1201,121 +1339,87 @@
         cost_estimate=cost(6),
         name="early_grad",
     )(yn, masked, dz, xn)
+    one = lambda i: (jnp.minimum(i, blocks - 1), 0)
+    two = lambda i: (jnp.minimum(blocks - 1, 2 * blocks - 1 - i), 0)
+    both = lambda i: (jnp.minimum(i, 2 * blocks - 1 - i), 0)
+    head_columns = lambda v: pl.BlockSpec((Q, v), two)
+    early_shape = early[0].shape
+    exchange = 2 * (nz - 1) + nz * (per - 1)
     out = pl.pallas_call(
-        functools.partial(inside_back_kernel, groups, per),
-        grid=(blocks,),
+        functools.partial(scan_back_kernel, groups, per),
+        grid=(2 * blocks,),
         in_specs=[
-            *[gwide] * (2 * nz), bspec, bspec, hspec, tspec, *[anywhere] * (1 + per)
+            *[pl.BlockSpec((Q, gc), one)] * nz, *[pl.BlockSpec((Q, gc), both)] * nz,
+            *[pl.BlockSpec((Q, gc), two)] * (2 * nz),
+            *[
+                pl.BlockSpec(
+                    (1, gc, STATE), lambda i: (jnp.minimum(blocks - 1, 2 * blocks - 1 - i), 0, 0)
+                )
+            ] * nz,
+            *[pl.BlockSpec((HALO, gc), fix)] * nz,
+            pl.BlockSpec((Q, STATE), both), pl.BlockSpec((Q, STATE), both),
+            pl.BlockSpec((Q, heads), one),
+            pl.BlockSpec((heads, Q), lambda i: (0, jnp.minimum(i, 2 * blocks - 1 - i))),
+            head_columns(heads), head_columns(heads), head_columns(2 * heads),
+            head_columns(2 * heads), head_columns(2 * heads), head_columns(2 * STATE),
+            head_columns(2 * STATE), whole(brawh), whole(taps), whole(taps_bc), whole(rate),
+            whole(skip), whole(ex), whole(er), *[anywhere] * (1 + per),
         ],
-        out_specs=[*[gwide] * nz, bspec, bspec, hspec, *[anywhere] * (nz - 1 + per - 1)],
+        out_specs=[
+            *[pl.BlockSpec((Q, gc), two)] * nz, *[pl.BlockSpec((HALO, gc), fix)] * nz,
+            *[pl.BlockSpec((4, gc), fix)] * nz, head_columns(heads),
+            pl.BlockSpec((1, heads), fix), pl.BlockSpec((1, heads), fix),
+            head_columns(2 * STATE), pl.BlockSpec((HALO, 2 * STATE), fix),
+            pl.BlockSpec((4, 2 * STATE), fix), pl.BlockSpec((2 * HEADDIM, model), fix),
+        ],
         out_shape=[
-            *[shape((rows, gc))] * nz, shape((rows, STATE)), shape((rows, STATE)),
-            shape((rows, heads)), *[shape(message.shape, BF)] * (nz - 1),
-            *[shape(early[0].shape, BF)] * (per - 1),
+            *[shape((rows, gc), BF)] * nz, *[shape((HALO, gc), BF)] * nz, *[shape((4, gc))] * nz,
+            shape((rows, heads), BF), shape((1, heads)), shape((1, heads)),
+            shape((rows, 2 * STATE), BF), shape((HALO, 2 * STATE), BF), shape((4, 2 * STATE)),
+            shape((2 * HEADDIM, model), BF),
         ],
         scratch_shapes=[
-            pltpu.VMEM((heads, Q), F32), pltpu.SemaphoreType.DMA((nz + per - 2,)),
-            pltpu.SemaphoreType.DMA((nz + per - 2,)),
+            *[pltpu.VMEM(message.shape, BF)] * (nz - 1), *[pltpu.VMEM(early_shape, BF)] * (per - 1),
+            *[pltpu.VMEM((8, gc), F32)] * nz, *[pltpu.VMEM((2 * HEADDIM, model), BF)] * (nz - 1),
+            pltpu.VMEM((8, 2 * STATE), F32), pltpu.VMEM(early_shape, BF),
+            pltpu.VMEM(early_shape, BF), pltpu.VMEM((rows, channels), F32),
+            pltpu.VMEM((rows, STATE), F32), pltpu.VMEM((rows, STATE), F32),
+            pltpu.VMEM((rows, heads), F32), pltpu.VMEM((heads, Q), F32),
+            pltpu.VMEM((channels, STATE), F32), pltpu.VMEM((heads, STATE), F32),
+            pltpu.SemaphoreType.DMA((exchange,)), pltpu.SemaphoreType.DMA((exchange,)),
+            pltpu.SemaphoreType.DMA,
         ],
         compiler_params=pltpu.CompilerParams(
             vmem_limit_bytes=VMEM, collective_id=0, has_side_effects=True
         ),
-        cost_estimate=cost(15),
-        name="inside_back",
-    )(*xdt, *dys, bs, cs, cl, clt, message, *early)
-    dxi = out[:nz]
-    dbi, dci, dai = out[nz : nz + 3]
-    messages = out[nz + 3 : 2 * nz + 2]
-    early_sum = sum(v.astype(F32) for v in [early[0], *out[2 * nz + 2 :]])
-    early_low = early_sum.astype(BF)
-    early_total = early_sum[0]
-    for s in range(1, nz):
-        early_total = early_total + turn(early_low[s], -s).astype(F32)
-    early_total = early_total.astype(BF)
+        cost_estimate=cost(50),
+        name="scan_back",
+    )(
+        *xdt, *dys, *u, *xr, *states, *xrh, bs, cs, cl, clt, dt, sig, dt2, e12, tl2, ubc, braw,
+        brawh, taps, taps_bc, rate, skip, ex, er, message, *early,
+    )
+    dx, dxh, g_taps = list(out[:nz]), list(out[nz : 2 * nz]), out[2 * nz : 3 * nz]
+    dti, g_rate, g_bias, dbc, dbch, g_taps_bc, early_total = out[3 * nz :]
+    g_taps = jnp.concatenate(g_taps, axis=1)
     early_own, early_other = to_owner(early_total)
-    rev = lambda i: (blocks - 1 - i, 0)
-    rg = pl.BlockSpec((Q, gc), rev)
-    rb = pl.BlockSpec((Q, STATE), rev)
-    rh = pl.BlockSpec((Q, heads), rev)
-    rh2 = pl.BlockSpec((Q, 2 * heads), rev)
-    rbc = pl.BlockSpec((Q, 2 * STATE), rev)
-
-    def back(some, final, dbi, dci, dti, wait):
-        n = len(some)
-        of = lambda values: [values[s] for s in some]
-        out = pl.pallas_call(
-            functools.partial(back_kernel, some, per, final),
-            grid=(blocks,),
-            in_specs=[
-                *[rg] * (4 * n), *[pl.BlockSpec((HALO, gc), fix)] * n,
-                *[pl.BlockSpec((1, gc, STATE), lambda i: (blocks - 1 - i, 0, 0))] * n,
-                rb, rb, rb, rb, rh, rh, rh, rh,
-                pl.BlockSpec((heads, Q), lambda i: (0, blocks - 1 - i)), rh2, rh2, rh2,
-                rbc, rbc, whole(brawh), whole(taps), whole(taps_bc), whole(rate), whole(skip),
-                whole(ex), whole(er), *[whole(v) for v in messages],
-                pl.BlockSpec(memory_space=pl.ANY), pl.BlockSpec(memory_space=pl.ANY),
-            ],
-            out_specs=[
-                *[rg] * n, *[pl.BlockSpec((HALO, gc), fix)] * n, *[pl.BlockSpec((4, gc), fix)] * n,
-                rb, rb, rh, pl.BlockSpec((1, heads), fix), pl.BlockSpec((1, heads), fix),
-                rbc, pl.BlockSpec((HALO, 2 * STATE), fix), pl.BlockSpec((4, 2 * STATE), fix),
-            ],
-            out_shape=[
-                *[shape((rows, gc), BF)] * n, *[shape((HALO, gc), BF)] * n, *[shape((4, gc))] * n,
-                shape((rows, STATE)), shape((rows, STATE)),
-                shape((rows, heads), BF if final else F32), shape((1, heads)), shape((1, heads)),
-                shape((rows, 2 * STATE), BF), shape((HALO, 2 * STATE), BF), shape((4, 2 * STATE)),
-            ],
-            scratch_shapes=[
-                pltpu.VMEM((n * gc, STATE), F32), pltpu.VMEM((heads, STATE), F32),
-                *[pltpu.VMEM((8, gc), F32)] * n, pltpu.VMEM((8, 2 * STATE), F32),
-            ],
-            compiler_params=params(),
-            cost_estimate=cost(7 * n),
-            name="back",
-        )(
-            *of(dxi), *of(dys), *of(u), *of(xr), *of(xrh), *of(states), bs, cs, dbi, dci, dai, dti,
-            dt, sig, clt, dt2, e12, tl2, ubc, braw, brawh, taps, taps_bc, rate, skip, ex, er,
-            *messages, *wait,
-        )
-        return out[:n], out[n : 2 * n], out[2 * n : 3 * n], *out[3 * n :]
-
-    halves = (groups[1 : nz // 2 + 1], groups[nz // 2 + 1 :] + groups[:1])
-    dx, dxh, g_taps = [None] * nz, [None] * nz, [None] * nz
-    dti = jnp.zeros((rows, heads), F32)
-    g_rate, g_bias, late, wait = 0.0, 0.0, [], (dti, dti)
+    spread_heads = pick_heads.T.astype(BF)
     bc_rows = 2 * STATE // per
-    for number, some in enumerate(halves):
-        final = number == len(halves) - 1
-        got, got_h, got_taps, dbi, dci, dti, one, two, dbc, dbch, g_taps_bc = back(
-            some, final, dbi, dci, dti, wait
-        )
-        g_rate, g_bias = g_rate + one, g_bias + two
-        for i, s in enumerate(some):
-            dx[s], dxh[s], g_taps[s] = got[i], got_h[i], got_taps[i]
-        n = len(some)
-        spread_heads = pick_heads.T.astype(BF)
-        more = [dbc, dbch, dti, spread_heads] if final else []
-        out_rows = n * HEADDIM + (bc_rows + HALO if final else 0)
-        g = pl.pallas_call(
-            functools.partial(late_grad_kernel, n, per, final),
-            in_specs=[
-                pl.BlockSpec(memory_space=pl.ANY),
-                *[whole(v) for v in [*got, *got_h, xn, xnh, *more]],
-            ],
-            out_shape=[shape((out_rows, model), BF)] * per,
-            scratch_shapes=(
-                [pltpu.VMEM((2 * STATE, model), F32), pltpu.VMEM((HEADS, model), F32)]
-                if final
-                else []
-            ),
-            compiler_params=params(),
-            cost_estimate=cost(3),
-            name="late_grad",
-        )(early_total if final else dti, *got, *got_h, xn, xnh, *more)
-        late.append(plane_sum(g))
-        wait = (early_low, g[0])
-    g_taps = jnp.concatenate(g_taps, axis=1)
+    order = groups[1:] + groups[:1]
+    operands = [
+        early_total, *[dx[s] for s in order], *[dxh[s] for s in order], xn, xnh, dbc, dbch, dti,
+        spread_heads,
+    ]
+    late = pl.pallas_call(
+        functools.partial(late_grad_kernel, nz, per, True),
+        in_specs=[anywhere, *[whole(v) for v in operands[1:]]],
+        out_shape=[shape((nz * HEADDIM + bc_rows + HALO, model), BF)] * per,
+        scratch_shapes=[pltpu.VMEM((2 * STATE, model), F32), pltpu.VMEM((HEADS, model), F32)],
+        compiler_params=params(),
+        cost_estimate=cost(8),
+        name="late_grad",
+    )(*operands)
+    halves = (order,)
+    late = [plane_sum(late)]
 
     share = late[-1][len(halves[-1]) * HEADDIM :]
     addend = {}
@@ -1340,6 +1444,8 @@
         )
     )
 
+    wz = [weights[0, s * gc : (s + 1) * gc] for s in groups]
+    wx = [weights[1, s * gc : (s + 1) * gc] for s in groups]
     lhs = [dz] * nz + dx + [dbc, dti]
     dxn, dxn_o = sum_products(
         lhs, [*groups] + [0] * (nz + 2), wz + wx + [wbc, wdt], rows, early_other

time: 455 us -> 366 us (0.80)
  starting transfers between devices: 88.6 us -> 25.7 us
  local copies, waits for them, and re-layouts: 46.7 us -> 26.8 us
  Pallas kernels: 223 us -> 228 us
  other arithmetic: 25.9 us -> 21.3 us
    ppermute x15 -> x3, starting transfers between devices: 38 us -> 4.52 us  [turn(): return lax.ppermute(v, 'head', [(i, (i + s) % nz) for i in range(nz)])]
    ppermute x26 -> x11, starting transfers between devices: 32.2 us -> 12.5 us  [cross(): return lax.ppermute(v, 'dp', [(i, i ^ m) for i in range(ndp)])]
    ppermute x26 -> x11, waiting for transfers between devices: 24.5 us -> 41.5 us  [cross(): return lax.ppermute(v, 'dp', [(i, i ^ m) for i in range(ndp)])]
    ppermute x15 -> x3, waiting for transfers between devices: 28.2 us -> 11.6 us  [turn(): return lax.ppermute(v, 'head', [(i, (i + s) % nz) for i in range(nz)])]
    unnamed x144 -> x93, local copies, waits for them, and re-layouts: 25.1 us -> 11.7 us
    ppermute x5 -> x1, starting transfers between devices: 11.4 us -> 1.28 us  [shift(): lax.ppermute(v, 'head', [(i, i + s) for i in range(nz) if 0 <= i + s < nz])]
    convert_element_type x2 -> x0, other arithmetic: 5.5 us -> none  [the longest x1 4.09 us: sequence_device(): early_low = early_sum.astype(BF)]
    pallas_call x15 -> x4, Pallas kernels: 166 us -> 172 us  [the longest x1 90 us: sequence_device(): pl.pallas_call(functools.partial(front_kernel, per, nz), in_specs=[vmem]...]
  transfers between devices with their start and end apart: 62 -> 26, of which waited for: 15 -> 9; matrix products, arithmetic and copies ran while one was open for 12% -> 10% of each run, Pallas kernels for 22% -> 37%
where the time goes in v4:
time: 366 us; the launch traced here: 364 us
  Pallas kernels  228 us (62%)
  waiting for transfers between devices  55.2 us (15%)
  local copies, waits for them, and re-layouts  26.8 us (7%)
  starting transfers between devices  25.7 us (7%)
  other arithmetic  21.3 us (6%)
  matrix products  5.39 us (1%)
    pallas_call x1, Pallas kernels, sequence_device(): pl.pallas_call(functools.partial(front_kernel, per, nz), in_specs=[vmem]...  90 us
    pallas_call x1, Pallas kernels, sequence_device(): pl.pallas_call(functools.partial(scan_back_kernel, groups, per), grid=(2...  66.9 us
    ppermute x11, waiting for transfers between devices, cross(): return lax.ppermute(v, 'dp', [(i, i ^ m) for i in range(ndp)])  41.5 us
    pallas_call x2, Pallas kernels, sum_products(): pl.pallas_call(functools.partial(sum_products_kernel, len(a)), grid=(coun...  16.2 us
    pallas_call x1, Pallas kernels, sequence_device(): pl.pallas_call(functools.partial(gate_kernel, groups, per), grid=(blocks,...  14.5 us
    pallas_call x1, Pallas kernels, sequence_device(): pl.pallas_call(functools.partial(carry_kernel, groups, per), grid=(blocks...  13.7 us
    ppermute x11, starting transfers between devices, cross(): return lax.ppermute(v, 'dp', [(i, i ^ m) for i in range(ndp)])  12.5 us
    unnamed x93, local copies, waits for them, and re-layouts  11.7 us
  transfers between devices with their start and end apart: 26, of which 9 were waited for; matrix products, arithmetic and copies ran while one was open for 10% of the time, Pallas kernels for 37%

profile of v4, /device:TPU:0, one launch (start us, length us, event | category | flops | bytes accessed | tf_op | source)
XLA Modules:
  0.0 364.4 jit_solution(1370746089272263666)
XLA Ops:
  0.7 2.6 copy.53
  3.3 0.9 copy.41.bcdt
  4.3 0.7 reshape.135.scal
  6.2 3.0 prep.1
  10.9 90.0 %front.1 = (bf16[2,1024,1024]{2,1,0:T(8,128)(2,1)}, bf16[1024,1024]{1,0:T(8,128)(2,1)}, bf16[1024,512]{1,0:T(8,128)(2,1)}, bf16[1024,1024]{1,0:T(8,128)(2,1)}, f...) custom-call(bf16[1024,512]{1,0:T(8,128)(2,1)} %refs_19_.1, ...), custom_call_target="tpu_custom_call" | custom-call | flops 8999999488 | bytes 90000 | tf_op jit(solution)/shard_map/front/pallas_call | solution.py:1187
  100.9 1.4 fusion.24
  102.4 6.6 %pull.1 = (bf16[1024,1024]{1,0:T(8,128)(2,1)}, f32[1024,1024]{1,0:T(8,128)}) custom-call(bf16[1024,512]{1,0:T(8,128)(2,1)} %cot.1, bf16[1024,512]{1,0:T(8,128)(2,1)} %get-tuple-element.144.cot2, s32[1,1]{1,0:T(1,128)} %bitcast.4.limit.refs_22_, bf16[1024,1024]{1,0:T(8,128)(2,1)} %get-tuple-element.145.w.refs_1_), custom_call_target="tpu_custom_call" | custom-call | flops 500000000 | bytes 5000 | tf_op jit(solution)/shard_map/pull/pallas_call | solution.py:1230
  109.0 13.7 %carry.1 = (f32[1024,256]{1,0:T(8,128)}, f32[1024,256]{1,0:T(8,128)}, f32[1024,256]{1,0:T(8,128)}, f32[1024,256]{1,0:T(8,128)}, bf16[8,256,128]{2,1,0:T(8,128)(2...) custom-call(bf16[1024,256]{1,0:T(8,128)(2,1)} %get-tuple-element.132, ...), custom_call_target="tpu_custom_call" | custom-call | flops 1000000000 | bytes 10000 | tf_op jit(solution)/shard_map/carry/pallas_call | solution.py:1242
  122.7 5.9 %products.2 = (f32[1024,512]{1,0:T(8,128)}, bf16[1024,512]{1,0:T(8,128)(2,1)}) custom-call(bf16[1024,1024]{1,0:T(8,128)(2,1)} %get-tuple-element.162.refs_0_, bf16[1024,1024]{1,0:T(8,128)(2,1)} %get-tuple-element.145.w.refs_1_, f32[1024,2]{1,0:T(8,128)} %get-tuple-element.160.refs_2_.refs_13_), custom_call_target="tpu_custom_call" | custom-call | flops 400000000 | bytes 4000 | tf_op jit(solution)/shard_map/products/pallas_call | solution.py:1267
  130.7 4.2 %slice_bitcast_fusion = (bf16[256,1024]{1,0:T(8,128)(2,1)}, bf16[256,1024]{1,0:T(8,128)(2,1)}, bf16[256,1024]{1,0:T(8,128)(2,1)}, bf16[256,1024]{1,0:T(8,128)(2,...) fusion(bf16[2,1024,1024]{2,1,0:T(8,128)(2,1)} %get-tuple-elemen, ...), kind=kLoop, calls=%fused_computation.35 | loop fusion | bytes 8388608 | tf_op jit(solution)/shard_map/squeeze | solution.py:1448
  135.0 0.8 copy-done.17
  136.2 14.5 %gate.1 = (bf16[1024,256]{1,0:T(8,128)(2,1)}, bf16[1024,256]{1,0:T(8,128)(2,1)}, bf16[1024,256]{1,0:T(8,128)(2,1)}, bf16[1024,256]{1,0:T(8,128)(2,1)}, bf16[1024...) custom-call(f32[1024,256]{1,0:T(8,128)} %get-tuple-element.156.refs_, ...), custom_call_target="tpu_custom_call" | custom-call | flops 1000000000 | bytes 10000 | tf_op jit(solution)/shard_map/gate/pallas_call | solution.py:1288
  150.7 1.7 pad_maximum_fusion.9.refs_42_
  152.4 9.0 %early_grad.1 = (bf16[4,128,1024]{2,1,0:T(8,128)(2,1)}, bf16[4,128,1024]{2,1,0:T(8,128)(2,1)}, bf16[4,128,1024]{2,1,0:T(8,128)(2,1)}, bf16[4,128,1024]{2,1,0:T(8,128)(2,1)}) custom-call(bf16[1024,1024]{1,0:T(8,128)(2,1)} %get-tuple-element.199.yn, bf16[1024,1024]{1,0:T(8,128)(2,1)} %get-tuple-element.200.masked, ...), custom_call_target="tpu_custom_call" | custom-call | flops 600000000 | bytes 6000 | tf_op jit(solution)/shard_map/early_grad/pallas_call | solution.py:1332
  161.4 66.9 %scan_back.1 = (bf16[1024,256]{1,0:T(8,128)(2,1)}, bf16[1024,256]{1,0:T(8,128)(2,1)}, bf16[1024,256]{1,0:T(8,128)(2,1)}, bf16[1024,256]{1,0:T(8,128)(2,1)}, bf16...) custom-call(bf16[1024,256]{1,0:T(8,128)(2,1)} %get-tuple-element.168, ...), custom_call_target="tpu_custom_call" | custom-call | flops 5000000000 | bytes 50000 | tf_op jit(solution)/shard_map/scan_back/pallas_call | solution.py:1348
  228.7 1.3 collective-permute-start.4
  230.1 1.8 collective-permute-start.5
  231.9 1.2 fusion.19
  233.1 8.0 %late_grad.1 = (bf16[336,1024]{1,0:T(8,128)(2,1)}, bf16[336,1024]{1,0:T(8,128)(2,1)}, bf16[336,1024]{1,0:T(8,128)(2,1)}, bf16[336,1024]{1,0:T(8,128)(2,1)}) custom-call(bf16[128,1024]{1,0:T(8,128)(2,1)} %get-tuple-element.214.refs_0_, bf16[1024,256]{1,0:T(8,128)(2,1)} %get-tuple-element.207.refs_5_.refs_1_, ...), custom_call_target="tpu_custom_call" | custom-call | flops 800000000 | bytes 8000 | tf_op jit(solution)/shard_map/late_grad/pallas_call | solution.py:1412
  241.7 1.2 convolution_add_fusion.3
  242.9 1.2 convolution_add_fusion.2
  244.1 1.2 convolution_add_fusion.1
  248.3 1.4 collective-permute-start.17
  249.8 1.8 collective-permute-start.18
  253.2 1.3 collective-permute-start.9
  255.0 4.8 %collective-permute-done.16 = bf16[336,1024]{1,0:T(8,128)(2,1)S(1)} collective-permute-done((bf16[336,1024]{1,0:T(8,128)(2,1)}, bf16[336,1024]{1,0:T(8,128)(2,1)S(1)}, u32[]{:S(2)}, u32[]{:S(2)}) %collective-permute-start.16) | collective-permute-done | bytes 688160 | tf_op jit(solution)/shard_map/ppermute | solution.py:1127
  259.9 21.3 %collective-permute-done.17 = bf16[336,1024]{1,0:T(8,128)(2,1)S(1)} collective-permute-done((bf16[336,1024]{1,0:T(8,128)(2,1)}, bf16[336,1024]{1,0:T(8,128)(2,1)S(1)}, u32[]{:S(2)}, u32[]{:S(2)}) %collective-permute-start.17) | collective-permute-done | bytes 688160 | tf_op jit(solution)/shard_map/ppermute | solution.py:1127
  281.2 0.8 copy-done.15
  282.0 0.8 copy-done.16
  282.9 1.8 fusion.21
  284.8 1.0 pad_maximum_fusion.8
  285.8 3.3 collective-permute-start.19
  289.1 1.2 collective-permute-start.21
  290.3 0.8 copy-done.10
  291.1 10.4 %products.3 = (f32[1024,512]{1,0:T(8,128)}, bf16[1024,512]{1,0:T(8,128)(2,1)}) custom-call(bf16[1024,1024]{1,0:T(8,128)(2,1)} %get-tuple-element.167.dz.refs_0_.refs_1_.refs_2_.refs_3_, bf16[1024,1024]{1,0:T(8,128)(2,1)} %get-tuple-element.167.dz.refs_0_.refs_1_.refs_2_.refs_3_, bf16[1024,1024]{1,0:T(8,128)(2,1)} %get-tuple-element.167.dz.refs_0_.refs_1_.refs_2_.refs_3_, ...), custom_call_target="tpu_custom_call" | custom-call | flops 400000000 | bytes 4000 | tf_op jit(solution)/shard_map/products/pallas_call | solution.py:1267
  301.5 1.1 broadcast_select_fusion
  302.7 11.6 %collective-permute-done.20 = bf16[144,1024]{1,0:T(8,128)(2,1)S(1)} collective-permute-done((bf16[144,1024]{1,0:T(8,128)(2,1)}, bf16[144,1024]{1,0:T(8,128)(2,1)S(1)}, u32[]{:S(2)}, u32[]{:S(2)}) %collective-permute-start.20) | collective-permute-done | bytes 294944 | tf_op jit(solution)/shard_map/ppermute | solution.py:1121
  314.5 0.9 collective-permute-start.22
  315.3 1.2 collective-permute-start.23
  316.6 1.5 collective-permute-start.24
  318.0 0.9 pad_maximum_fusion.4
  318.9 1.1 bitcast_convert_fusion
  320.0 4.4 %collective-permute-done.22 = bf16[144,1024]{1,0:T(8,128)(2,1)S(1)} collective-permute-done((bf16[144,1024]{1,0:T(8,128)(2,1)S(1)}, bf16[144,1024]{1,0:T(8,128)(2,1)S(1)}, u32[]{:S(2)}, u32[]{:S(2)}) %collective-permute-start.22) | collective-permute-done | bytes 294944 | tf_op jit(solution)/shard_map/ppermute | solution.py:1127
  324.5 3.7 %collective-permute-done.23 = bf16[144,1024]{1,0:T(8,128)(2,1)S(1)} collective-permute-done((bf16[144,1024]{1,0:T(8,128)(2,1)S(1)}, bf16[144,1024]{1,0:T(8,128)(2,1)S(1)}, u32[]{:S(2)}, u32[]{:S(2)}) %collective-permute-start.23) | collective-permute-done | bytes 294944 | tf_op jit(solution)/shard_map/ppermute | solution.py:1127
  328.2 1.6 collective-permute-done.24
  330.9 0.9 slice.167
  332.5 0.9 fusion.5
  334.1 0.8 concatenate.46
  335.4 0.7 add_multiply_fusion
  336.1 3.2 fusion.2
  339.4 1.1 convert_add_fusion.1
  340.5 1.1 broadcast_select_fusion.3
  341.6 0.9 collective-permute-start.12
  342.5 1.0 broadcast_select_fusion.2
  343.5 2.3 collective-permute-done.12
  345.8 0.9 collective-permute-start.13
  346.8 3.3 collective-permute-done.13
  350.1 1.9 collective-permute-start.14
  352.2 2.0 collective-permute-done.14
  354.3 3.7 %collective-permute-start.15 = (f32[12384]{0:T(1024)S(1)}, f32[12384]{0:T(1024)S(1)}, u32[]{:S(2)}, u32[]{:S(2)}) collective-permute-start(f32[12384]{0:T(1024)S(1)} %add.151), channel_id=1, source_target_pairs={{0,4},{2,6},{4,0},{6,2},{1,5},{3,7},{5,1},{7,3},{8,12},{10,14},{12... | collective-permute-start | bytes 148616 | tf_op jit(solution)/shard_map/ppermute | solution.py:1488
  357.9 0.9 maximum_bitcast_fusion
  358.8 1.8 copy.47
  361.0 0.7 reshape.150
  363.0 0.7 dynamic-slice_reduce_fusion
  (177 shorter events, 16.7 us)
Async XLA Ops:
  0.6 2.7 copy-start.20
  0.7 3.6 copy-start.41
  0.7 3.6 copy-start.40
  0.7 3.6 copy-start.39
  0.7 4.3 %copy-start.28 = (bf16[512]{0:T(512)(128)(2,1)S(1)}, bf16[512]{0:T(512)(128)(2,1)}, u32[]{:S(2)}) copy-start(bf16[512]{0:T(512)(128)(2,1)} %param.19) | copy-start | bytes 3076
  0.7 4.9 %copy-start.37 = (bf16[512]{0:T(512)(128)(2,1)S(1)}, bf16[512]{0:T(512)(128)(2,1)}, u32[]{:S(2)}) copy-start(bf16[512]{0:T(512)(128)(2,1)} %param.27) | copy-start | bytes 3076
  0.7 8.9 %copy-start.36 = (bf16[4,256]{1,0:T(4,128)(2,1)S(1)}, bf16[4,256]{1,0:T(4,128)(2,1)}, u32[]{:S(2)}) copy-start(bf16[4,256]{1,0:T(4,128)(2,1)} %param.23) | copy-start | bytes 6148
  9.2 125.7 %collective-permute-start.2 = (bf16[304,512]{1,0:T(8,128)(2,1)}, bf16[304,512]{1,0:T(8,128)(2,1)S(1)}, u32[]{:S(2)}, u32[]{:S(2)}) collective-permute-start(bf16[304,512]{1,0:T(8,128)(2,1)} %get-tuple-element.128.refs_5_), channel_id=1, source_target_pairs={{0,1},{1,0},{2,3},{3,2},{4,5},{5,4},{6,7},{7,6},{8,9},{9,8},{10,11... | collective-permute-start | bytes 933896 | tf_op jit(solution)/shard_map/ppermute | solution.py:1118
  122.6 12.3 %collective-permute-start = (f32[1024,2]{1,0:T(8,128)}, f32[1024,2]{1,0:T(8,128)S(1)}, u32[]{:S(2)}, u32[]{:S(2)}) collective-permute-start(f32[1024,2]{1,0:T(8,128)} %get-tuple-element.160.refs_2_.refs_13_), channel_id=1, source_target_pairs={{0,1},{1,0},{2,3},{3,2},{4,5},{5,4},{6,7},{7,6},{8,9},{9,8},{10,11... | collective-permute-start | bytes 24584 | tf_op jit(solution)/shard_map/ppermute | solution.py:1118
  122.7 6.4 %copy-start.26 = (f32[8,1024]{1,0:T(8,128)S(1)}, f32[8,1024]{1,0:T(8,128)}, u32[]{:S(2)}) copy-start(f32[8,1024]{1,0:T(8,128)} %get-tuple-element.155) | copy-start | bytes 98308
  122.7 7.0 %copy-start.18 = (f32[1024,1]{1,0:T(8,128)S(1)}, f32[1024,1]{1,0:T(8,128)}, u32[]{:S(2)}) copy-start(f32[1024,1]{1,0:T(8,128)} %get-tuple-element.166) | copy-start | bytes 12292
  128.6 6.4 %collective-permute-start.1 = (bf16[1024,512]{1,0:T(8,128)(2,1)}, bf16[1024,512]{1,0:T(8,128)(2,1)S(1)}, u32[]{:S(2)}, u32[]{:S(2)}) collective-permute-start(bf16[1024,512]{1,0:T(8,128)(2,1)} %get-tuple-element.164), channel_id=1, source_target_pairs={{0,1},{1,0},{2,3},{3,2},{4,5},{5,4},{6,7},{7,6},{8,9},{9,8},{10,11... | collective-permute-start | bytes 3145736 | tf_op jit(solution)/shard_map/ppermute | solution.py:1118
  130.7 4.2 %copy-start.19 = (bf16[304,512]{1,0:T(8,128)(2,1)S(1)}, bf16[304,512]{1,0:T(8,128)(2,1)}, u32[]{:S(2)}) copy-start(bf16[304,512]{1,0:T(8,128)(2,1)} %get-tuple-element.128.refs_5_) | copy-start | bytes 933892
  134.9 110.4 %copy-start.2 = (bf16[256,1024]{1,0:T(8,128)(2,1)}, bf16[256,1024]{1,0:T(8,128)(2,1)S(1)}, u32[]{:S(2)}) copy-start(bf16[256,1024]{1,0:T(8,128)(2,1)S(1)} %pad_maximum_fusion.5.refs_18_) | copy-start | bytes 1572868
  135.0 1.2 copy-start.13
  136.2 14.5 %copy-start.27 = (bf16[16,128]{1,0:T(8,128)(2,1)S(1)}, bf16[16,128]{1,0:T(8,128)(2,1)}, u32[]{:S(2)}) copy-start(bf16[16,128]{1,0:T(8,128)(2,1)} %get-tuple-element.198) | copy-start | bytes 12292
  228.3 21.4 %collective-permute-start.3 = (bf16[128,1024]{1,0:T(8,128)(2,1)}, bf16[128,1024]{1,0:T(8,128)(2,1)S(1)}, u32[]{:S(2)}, u32[]{:S(2)}) collective-permute-start(bf16[128,1024]{1,0:T(8,128)(2,1)} %get-tuple-element.214.refs_0_), channel_id=1, source_target_pairs={{0,8},{8,0},{16,24},{24,16},{1,9},{9,1},{17,25},{25,17},{2,10},{10... | collective-permute-start | bytes 786440 | tf_op jit(solution)/shard_map/ppermute | solution.py:1127
  228.7 24.5 %collective-permute-start.4 = (bf16[128,1024]{1,0:T(8,128)(2,1)}, bf16[128,1024]{1,0:T(8,128)(2,1)S(1)}, u32[]{:S(2)}, u32[]{:S(2)}) collective-permute-start(bf16[128,1024]{1,0:T(8,128)(2,1)} %get-tuple-element.214.refs_0_), channel_id=1, source_target_pairs={{0,16},{8,24},{16,0},{24,8},{1,17},{9,25},{17,1},{25,9},{2,18},{10... | collective-permute-start | bytes 786440 | tf_op jit(solution)/shard_map/ppermute | solution.py:1127
  230.1 24.4 %collective-permute-start.5 = (bf16[128,1024]{1,0:T(8,128)(2,1)}, bf16[128,1024]{1,0:T(8,128)(2,1)S(1)}, u32[]{:S(2)}, u32[]{:S(2)}) collective-permute-start(bf16[128,1024]{1,0:T(8,128)(2,1)} %get-tuple-element.214.refs_0_), channel_id=1, source_target_pairs={{0,24},{8,16},{16,8},{24,0},{1,25},{9,17},{17,9},{25,1},{2,26},{10... | collective-permute-start | bytes 786440 | tf_op jit(solution)/shard_map/ppermute | solution.py:1127
  233.1 8.5 %copy-start.25 = (bf16[16,256]{1,0:T(8,128)(2,1)S(1)}, bf16[16,256]{1,0:T(8,128)(2,1)}, u32[]{:S(2)}) copy-start(bf16[16,256]{1,0:T(8,128)(2,1)} %get-tuple-element.217.refs_8_) | copy-start | bytes 24580
  233.1 9.8 %copy-start.24 = (bf16[16,256]{1,0:T(8,128)(2,1)S(1)}, bf16[16,256]{1,0:T(8,128)(2,1)}, u32[]{:S(2)}) copy-start(bf16[16,256]{1,0:T(8,128)(2,1)} %get-tuple-element.219.refs_6_) | copy-start | bytes 24580
  233.1 11.0 %copy-start.23 = (bf16[16,256]{1,0:T(8,128)(2,1)S(1)}, bf16[16,256]{1,0:T(8,128)(2,1)}, u32[]{:S(2)}) copy-start(bf16[16,256]{1,0:T(8,128)(2,1)} %get-tuple-element.220.refs_7_) | copy-start | bytes 24580
  233.1 12.2 %copy-start.22 = (bf16[16,256]{1,0:T(8,128)(2,1)S(1)}, bf16[16,256]{1,0:T(8,128)(2,1)}, u32[]{:S(2)}) copy-start(bf16[16,256]{1,0:T(8,128)(2,1)} %get-tuple-element.221.refs_12_) | copy-start | bytes 24580
  241.1 4.5 %copy-start.38 = (f32[1,16]{1,0:T(1,128)S(1)}, f32[1,16]{1,0:T(1,128)}, u32[]{:S(2)}) copy-start(f32[1,16]{1,0:T(1,128)} %get-tuple-element.196.refs_38_) | copy-start | bytes 196
  241.1 4.5 %copy-start.43 = (f32[1,16]{1,0:T(1,128)S(1)}, f32[1,16]{1,0:T(1,128)}, u32[]{:S(2)}) copy-start(f32[1,16]{1,0:T(1,128)} %get-tuple-element.223) | copy-start | bytes 196
  241.1 4.5 %copy-start.32 = (f32[4,256]{1,0:T(4,128)S(1)}, f32[4,256]{1,0:T(4,128)}, u32[]{:S(2)}) copy-start(f32[4,256]{1,0:T(4,128)} %get-tuple-element.225) | copy-start | bytes 12292
  241.2 4.5 %copy-start.33 = (f32[4,256]{1,0:T(4,128)S(1)}, f32[4,256]{1,0:T(4,128)}, u32[]{:S(2)}) copy-start(f32[4,256]{1,0:T(4,128)} %get-tuple-element.226) | copy-start | bytes 12292
  241.2 4.5 %copy-start.34 = (f32[4,256]{1,0:T(4,128)S(1)}, f32[4,256]{1,0:T(4,128)}, u32[]{:S(2)}) copy-start(f32[4,256]{1,0:T(4,128)} %get-tuple-element.227) | copy-start | bytes 12292
  241.2 4.5 %copy-start.35 = (f32[4,256]{1,0:T(4,128)S(1)}, f32[4,256]{1,0:T(4,128)}, u32[]{:S(2)}) copy-start(f32[4,256]{1,0:T(4,128)} %get-tuple-element.228) | copy-start | bytes 12292
  241.2 4.8 %copy-start.42 = (f32[1,16]{1,0:T(1,128)S(1)}, f32[1,16]{1,0:T(1,128)}, u32[]{:S(2)}) copy-start(f32[1,16]{1,0:T(1,128)} %get-tuple-element.222) | copy-start | bytes 196
  241.2 5.4 %copy-start.30 = (f32[1,1024]{1,0:T(1,128)S(1)}, f32[1,1024]{1,0:T(1,128)}, u32[]{:S(2)}) copy-start(f32[1,1024]{1,0:T(1,128)} %get-tuple-element.224) | copy-start | bytes 12292
  241.2 6.3 %copy-start.29 = (f32[1,1024]{1,0:T(1,128)S(1)}, f32[1,1024]{1,0:T(1,128)}, u32[]{:S(2)}) copy-start(f32[1,1024]{1,0:T(1,128)} %get-tuple-element.229) | copy-start | bytes 12292
  241.2 10.8 %copy-start.31 = (f32[4,256]{1,0:T(4,128)S(1)}, f32[4,256]{1,0:T(4,128)}, u32[]{:S(2)}) copy-start(f32[4,256]{1,0:T(4,128)} %get-tuple-element.230) | copy-start | bytes 12292
  241.2 13.3 %copy-start.12 = (bf16[128,1024]{1,0:T(8,128)(2,1)S(1)}, bf16[128,1024]{1,0:T(8,128)(2,1)}, u32[]{:S(2)}) copy-start(bf16[128,1024]{1,0:T(8,128)(2,1)} %get-tuple-element.214.refs_0_) | copy-start | bytes 786436
  241.2 18.6 %collective-permute-start.16 = (bf16[336,1024]{1,0:T(8,128)(2,1)}, bf16[336,1024]{1,0:T(8,128)(2,1)S(1)}, u32[]{:S(2)}, u32[]{:S(2)}) collective-permute-start(bf16[336,1024]{1,0:T(8,128)(2,1)} %get-tuple-element.233), channel_id=1, source_target_pairs={{0,8},{8,0},{16,24},{24,16},{1,9},{9,1},{17,25},{25,17},{2,10},{10... | collective-permute-start | bytes 2064392 | tf_op jit(solution)/shard_map/ppermute | solution.py:1127
  245.5 2.8 collective-permute-start.8
  248.3 32.8 %collective-permute-start.17 = (bf16[336,1024]{1,0:T(8,128)(2,1)}, bf16[336,1024]{1,0:T(8,128)(2,1)S(1)}, u32[]{:S(2)}, u32[]{:S(2)}) collective-permute-start(bf16[336,1024]{1,0:T(8,128)(2,1)} %get-tuple-element.234), channel_id=1, source_target_pairs={{0,16},{8,24},{16,0},{24,8},{1,17},{9,25},{17,1},{25,9},{2,18},{10... | collective-permute-start | bytes 2064392 | tf_op jit(solution)/shard_map/ppermute | solution.py:1127
  249.8 31.4 %collective-permute-start.18 = (bf16[336,1024]{1,0:T(8,128)(2,1)}, bf16[336,1024]{1,0:T(8,128)(2,1)S(1)}, u32[]{:S(2)}, u32[]{:S(2)}) collective-permute-start(bf16[336,1024]{1,0:T(8,128)(2,1)} %get-tuple-element.235), channel_id=1, source_target_pairs={{0,24},{8,16},{16,8},{24,0},{1,25},{9,17},{17,9},{25,1},{2,26},{10... | collective-permute-start | bytes 2064392 | tf_op jit(solution)/shard_map/ppermute | solution.py:1127
  253.2 78.6 %collective-permute-start.9 = (f32[16,512]{1,0:T(8,128)}, f32[16,512]{1,0:T(8,128)S(1)}, u32[]{:S(2)}, u32[]{:S(2)}) collective-permute-start(f32[16,512]{1,0:T(8,128)} %slice_add_fusion.1), channel_id=1, source_target_pairs={{2,0},{4,2},{6,4},{3,1},{5,3},{7,5},{10,8},{12,10},{14,12},{11,9},... | collective-permute-start | bytes 98312 | tf_op jit(solution)/shard_map/ppermute | solution.py:1124
  254.8 28.1 %copy-start.14 = (bf16[336,1024]{1,0:T(8,128)(2,1)S(1)}, bf16[336,1024]{1,0:T(8,128)(2,1)}, u32[]{:S(2)}) copy-start(bf16[336,1024]{1,0:T(8,128)(2,1)} %get-tuple-element.232) | copy-start | bytes 2064388
  255.0 35.3 %collective-permute-start.6 = (bf16[4,128,512]{2,1,0:T(8,128)(2,1)S(1)}, bf16[4,128,512]{2,1,0:T(8,128)(2,1)S(1)}, u32[]{:S(2)}, u32[]{:S(2)}) collective-permute-start(bf16[4,128,512]{2,1,0:T(8,128)(2,1)S(1)} %slice.156), channel_id=1, source_target_pairs={{0,1},{1,0},{2,3},{3,2},{4,5},{5,4},{6,7},{7,6},{8,9},{9,8},{10,11... | collective-permute-start | bytes 1572872 | tf_op jit(solution)/shard_map/ppermute | solution.py:1118
  285.8 16.9 %collective-permute-start.19 = (bf16[144,1024]{1,0:T(8,128)(2,1)}, bf16[144,1024]{1,0:T(8,128)(2,1)S(1)}, u32[]{:S(2)}, u32[]{:S(2)}) collective-permute-start(bf16[144,1024]{1,0:T(8,128)(2,1)} %get-tuple-element.306), channel_id=1, source_target_pairs={{0,6},{2,0},{4,2},{6,4},{1,7},{3,1},{5,3},{7,5},{8,14},{10,8},{12,... | collective-permute-start | bytes 884744 | tf_op jit(solution)/shard_map/ppermute | solution.py:1121
  289.1 25.2 %collective-permute-start.20 = (bf16[144,1024]{1,0:T(8,128)(2,1)}, bf16[144,1024]{1,0:T(8,128)(2,1)S(1)}, u32[]{:S(2)}, u32[]{:S(2)}) collective-permute-start(bf16[144,1024]{1,0:T(8,128)(2,1)} %get-tuple-element.307), channel_id=1, source_target_pairs={{0,4},{2,6},{4,0},{6,2},{1,5},{3,7},{5,1},{7,3},{8,12},{10,14},{12... | collective-permute-start | bytes 884744 | tf_op jit(solution)/shard_map/ppermute | solution.py:1121
  289.1 25.2 %collective-permute-start.21 = (bf16[144,1024]{1,0:T(8,128)(2,1)}, bf16[144,1024]{1,0:T(8,128)(2,1)S(1)}, u32[]{:S(2)}, u32[]{:S(2)}) collective-permute-start(bf16[144,1024]{1,0:T(8,128)(2,1)} %get-tuple-element.308), channel_id=1, source_target_pairs={{0,2},{2,4},{4,6},{6,0},{1,3},{3,5},{5,7},{7,1},{8,10},{10,12},{12... | collective-permute-start | bytes 884744 | tf_op jit(solution)/shard_map/ppermute | solution.py:1121
  301.4 30.4 %collective-permute-start.7 = (bf16[1024,512]{1,0:T(8,128)(2,1)}, bf16[1024,512]{1,0:T(8,128)(2,1)S(1)}, u32[]{:S(2)}, u32[]{:S(2)}) collective-permute-start(bf16[1024,512]{1,0:T(8,128)(2,1)} %get-tuple-element.216), channel_id=1, source_target_pairs={{0,1},{1,0},{2,3},{3,2},{4,5},{5,4},{6,7},{7,6},{8,9},{9,8},{10,11... | collective-permute-start | bytes 3145736 | tf_op jit(solution)/shard_map/ppermute | solution.py:1118
  314.5 10.0 %collective-permute-start.22 = (bf16[144,1024]{1,0:T(8,128)(2,1)S(1)}, bf16[144,1024]{1,0:T(8,128)(2,1)S(1)}, u32[]{:S(2)}, u32[]{:S(2)}) collective-permute-start(bf16[144,1024]{1,0:T(8,128)(2,1)S(1)} %fusion.8), channel_id=1, source_target_pairs={{0,8},{8,0},{16,24},{24,16},{1,9},{9,1},{17,25},{25,17},{2,10},{10... | collective-permute-start | bytes 884744 | tf_op jit(solution)/shard_map/ppermute | solution.py:1127
  315.3 12.8 %collective-permute-start.23 = (bf16[144,1024]{1,0:T(8,128)(2,1)S(1)}, bf16[144,1024]{1,0:T(8,128)(2,1)S(1)}, u32[]{:S(2)}, u32[]{:S(2)}) collective-permute-start(bf16[144,1024]{1,0:T(8,128)(2,1)S(1)} %fusion.8), channel_id=1, source_target_pairs={{0,16},{8,24},{16,0},{24,8},{1,17},{9,25},{17,1},{25,9},{2,18},{10... | collective-permute-start | bytes 884744 | tf_op jit(solution)/shard_map/ppermute | solution.py:1127
  316.6 13.2 %collective-permute-start.24 = (bf16[144,1024]{1,0:T(8,128)(2,1)S(1)}, bf16[144,1024]{1,0:T(8,128)(2,1)S(1)}, u32[]{:S(2)}, u32[]{:S(2)}) collective-permute-start(bf16[144,1024]{1,0:T(8,128)(2,1)S(1)} %fusion.8), channel_id=1, source_target_pairs={{0,24},{8,16},{16,8},{24,0},{1,25},{9,17},{17,9},{25,1},{2,26},{10... | collective-permute-start | bytes 884744 | tf_op jit(solution)/shard_map/ppermute | solution.py:1127
  330.1 1.7 copy-start.7
  330.1 1.8 copy-start
  330.1 2.4 copy-start.1
  331.8 7.6 %collective-permute-start.25 = (bf16[4,144,512]{2,1,0:T(8,128)(2,1)}, bf16[4,144,512]{2,1,0:T(8,128)(2,1)}, u32[]{:S(2)}, u32[]{:S(2)}) collective-permute-start(bf16[4,144,512]{2,1,0:T(8,128)(2,1)} %slice.167), channel_id=1, source_target_pairs={{0,1},{1,0},{2,3},{3,2},{4,5},{5,4},{6,7},{7,6},{8,9},{9,8},{10,11... | collective-permute-start | bytes 1769480 | tf_op jit(solution)/shard_map/ppermute | solution.py:1118
  331.8 1.6 copy-start.21
  331.8 1.6 copy-start.9
  333.4 2.0 collective-permute-start.10
  334.9 6.7 %collective-permute-start.11 = (f32[12384]{0:T(1024)S(1)}, f32[12384]{0:T(1024)S(1)}, u32[]{:S(2)}, u32[]{:S(2)}) collective-permute-start(f32[12384]{0:T(1024)S(1)} %concatenate.46), channel_id=1, source_target_pairs={{0,1},{1,0},{2,3},{3,2},{4,5},{5,4},{6,7},{7,6},{8,9},{9,8},{10,11... | collective-permute-start | bytes 148616 | tf_op jit(solution)/shard_map/ppermute | solution.py:1118
  336.1 3.3 copy-start.4
  336.1 3.3 copy-start.6
  336.1 3.3 copy-start.8
  340.5 11.4 %copy-start.11 = (bf16[8,64,512]{2,1,0:T(8,128)(2,1)S(1)}, bf16[8,64,512]{2,1,0:T(8,128)(2,1)}, u32[]{:S(2)}) copy-start(bf16[8,64,512]{2,1,0:T(8,128)(2,1)} %get-tuple-element.298) | copy-start | bytes 1572868
  341.6 4.2 %collective-permute-start.12 = (f32[12384]{0:T(1024)S(1)}, f32[12384]{0:T(1024)S(1)}, u32[]{:S(2)}, u32[]{:S(2)}) collective-permute-start(f32[12384]{0:T(1024)S(1)} %add.148), channel_id=1, source_target_pairs={{0,8},{8,0},{16,24},{24,16},{1,9},{9,1},{17,25},{25,17},{2,10},{10... | collective-permute-start | bytes 148616 | tf_op jit(solution)/shard_map/ppermute | solution.py:1127
  345.8 4.2 %collective-permute-start.13 = (f32[12384]{0:T(1024)S(1)}, f32[12384]{0:T(1024)S(1)}, u32[]{:S(2)}, u32[]{:S(2)}) collective-permute-start(f32[12384]{0:T(1024)S(1)} %add.149), channel_id=1, source_target_pairs={{0,16},{8,24},{16,0},{24,8},{1,17},{9,25},{17,1},{25,9},{2,18},{10... | collective-permute-start | bytes 148616 | tf_op jit(solution)/shard_map/ppermute | solution.py:1127
  350.1 4.2 %collective-permute-start.14 = (f32[12384]{0:T(1024)S(1)}, f32[12384]{0:T(1024)S(1)}, u32[]{:S(2)}, u32[]{:S(2)}) collective-permute-start(f32[12384]{0:T(1024)S(1)} %add.150), channel_id=1, source_target_pairs={{0,2},{2,0},{4,6},{6,4},{1,3},{3,1},{5,7},{7,5},{8,10},{10,8},{12,... | collective-permute-start | bytes 148616 | tf_op jit(solution)/shard_map/ppermute | solution.py:1488
  354.3 6.4 %collective-permute-start.15 = (f32[12384]{0:T(1024)S(1)}, f32[12384]{0:T(1024)S(1)}, u32[]{:S(2)}, u32[]{:S(2)}) collective-permute-start(f32[12384]{0:T(1024)S(1)} %add.151), channel_id=1, source_target_pairs={{0,4},{2,6},{4,0},{6,2},{1,5},{3,7},{5,1},{7,3},{8,12},{10,14},{12... | collective-permute-start | bytes 148616 | tf_op jit(solution)/shard_map/ppermute | solution.py:1488
  (6 other events, 4.9 us)

commit v5 on v4

--- a/solution.py
+++ b/solution.py
@@ -496,7 +496,7 @@
 
 KEPT = (
     "xnh", "r", "raw", "rawh", "ubc", "b", "c", "dt", "sig", "cl", "clt", "dt2", "e12", "tl2",
-    "dttl2", "ec2", "edt2", "rate", "wdt", "tot", "table",
+    "dttl2", "ec2", "edt2", "rate", "wdt", "tot", "table", "bcdt",
 )
 
 
@@ -508,7 +508,8 @@
     kept, refs = refs[: len(KEPT)], refs[len(KEPT) :]
     o = Named(KEPT, kept)
     z_v, xr_v, u_v, xdt_v, y_v, refs = take(refs, *[nz] * 5)
-    w, ho, eh, bc, xn, msg, buf, bcbuf, acc, sends, receives, locals_ = refs
+    w, ho, eh, xn, msg, buf, bcbuf, acc, sends, receives, locals_ = refs
+    bc = o.bcdt
     rows, half = hidden.shape
     gc = per * HEADDIM
     top = nz * gc
@@ -562,14 +563,6 @@
         found = pltpu.make_async_copy(source, target, locals_.at[i])
         found.start()
         return found
-
-    def start(copies):
-        for c in copies:
-            c.start()
-
-    def arrive(copies):
-        for c in copies:
-            c.wait_recv()
 
     ready = [
         local(first, w.at[:, pl.ds(0, HEADDIM), left]),
@@ -1045,31 +1038,318 @@
         outs[m][0, HEADDIM:, :] = g_z[here, :]
 
 
-def late_grad_kernel(n, per, final, *refs):
-    _, dx, dxh, xn, xnh, rest = take(refs, 0, n, n, 0, 0)
-    if final:
-        dbc, dbch, ddt, spread, rest = take(rest, 0, 0, 0, 0)
-        outs, rest = take(rest, per)
-        gbc, gdt = rest
-        bc_rows = gbc.shape[0] // per
-        dt_rows = gdt.shape[0] // per
-        gbc[...] = t_dot(dbc[...], xn[...]) + t_dot(dbch[...], xnh[...])
-        gdt[...] = split_dot(spread[...], t_dot(ddt[...], xn[...]))
-    else:
-        outs, rest = take(rest, per)
-    for i in range(n):
-        g = (t_dot(dx[i][...], xn[...]) + t_dot(dxh[i][...], xnh[...])).astype(BF)
+class Copies:
+    def __init__(self, sends, receives):
+        self.sends, self.receives, self.all = sends, receives, []
+
+    def __call__(self, source, target, peer):
+        copy = remote(source, target, self.sends, self.receives, len(self.all), peer)
+        self.all.append(copy)
+        return copy
+
+
+def start(copies):
+    for c in copies:
+        c.start()
+
+
+def arrive(copies):
+    for c in copies:
+        c.wait_recv()
+
+
+def tail_kernel(per, nz, *refs):
+    dx, dxh, taps, refs = take(refs, nz, nz, nz)
+    (dz, dbc, dbch, dti, xn, xnh, w, bc, wdt, early, hidden, cot, r), refs = refs[:13], refs[13:]
+    (gain, gbc, grate, gbias, gskip, ggain, rate, ex), refs = refs[:8], refs[8:]
+    zx_o, ow_o, bcdt_o, hid_o, norm_o, tbc_o, small_o, refs = take(refs, *[0] * 7)
+    ea, la, gx, gs, gdt, lx, ls, sw_out, sw_in, dxn, dxn_out, dxn_in, refs = take(refs, *[0] * 12)
+    edge_out, edge_in, edge_sum, edge_next, across, across_in, nrm, nrm2, sums, refs = take(
+        refs, *[0] * 9
+    )
+    rx, rs, zx, zs, nr, nz_r, refs = take(refs, per - 1, per - 1, nz - 1, nz - 1, per - 1, nz - 1)
+    stage, sends, receives = refs
+    copy = Copies(sends, receives)
+    rows, half = hidden.shape
+    gc = per * HEADDIM
+    channels = nz * gc
+    state2 = dbc.shape[1]
+    quarter = state2 // per
+    share = quarter + HALO
+    some_dt = HEADS // per
+    wi, di, zi = lax.axis_index("width"), lax.axis_index("dp"), lax.axis_index("head")
+    sibling = {"width": 1 - wi}
+    d_peers, z_back = plane_peers(per), line_peers(nz, -1)
+    left, right = pl.ds(0, half), pl.ds(half, half)
+    block = rows // nz
+
+    early_swap = copy(early.at[:, right], ea.at[0, wi], sibling)
+    late_swap = copy(sw_out, sw_in, sibling)
+    dxn_swap = [
+        copy(dxn_out.at[pl.ds(i * block, block), :], dxn_in.at[pl.ds(i * block, block), :], sibling)
+        for i in range(nz)
+    ]
+    edge_swap = copy(edge_out, edge_in, sibling)
+    across_swap = copy(across, across_in, sibling)
+    p_share, p_x, p_early, p_norm, p_late = [], {s: [] for s in range(nz)}, [], [], []
+    for k, peer in enumerate(d_peers):
+        m = k + 1
+        p_share.append(copy(gs.at[m], rs[k], peer))
+        for s in range(nz):
+            p_x[s].append(copy(gx.at[s, m], rx[k].at[s], peer))
+        p_early.append(copy(ea.at[0], ea.at[m], peer))
+        p_norm.append(copy(nrm, nr[k], peer))
+        p_late.append(copy(la.at[0], la.at[m], peer))
+    z_x, z_share, z_norm = [], [], []
+    for k, peer in enumerate(z_back):
+        z_x.append(copy(lx.at[k + 1], zx[k], peer))
+        z_share.append(copy(ls, zs[k], peer))
+        z_norm.append(copy(nrm2, nz_r[k], peer))
+    z_edge = copy(edge_sum, edge_next, z_back[0])
+
+    meet([sibling, *z_back, *line_peers(nz, 1), *d_peers])
+    start([early_swap])
+    ea[0, wi] = early[:, :half]
+
+    g = t_dot(dbc[...], xn[...]) + t_dot(dbch[...], xnh[...])
+    stage[0:state2, :] = g
+    gdt[...] = split_dot_tr(slot_heads(dti.shape[1], per), t_dot(dti[...], xn[...]))
+    per_head = jnp.concatenate([gbias[...], grate[...] * rate[...]], axis=0)
+    small = jnp.concatenate(
+        [
+            jnp.concatenate([v[...] for v in taps], axis=1),
+            ggain[...],
+            gskip[...],
+            dot(split2(per_head), ex[...]),
+        ],
+        axis=0,
+    )
+    both = split2(gbc[...])
+    both = jnp.concatenate([both, jnp.zeros((4, 2 * state2), BF)], axis=0)
+    for m in range(per):
+        at = jnp.bitwise_xor(di, m)
+        gs[m, 0:quarter, :] = stage[pl.ds(pl.multiple_of(at * quarter, quarter), quarter), :].astype(
+            BF
+        )
+        lanes = jnp.concatenate(
+            [
+                small[:, (s * per + m) * HEADDIM : (s * per + m + 1) * HEADDIM]
+                for s in range(nz)
+            ],
+            axis=1,
+        )
+        lower = jnp.concatenate([split2(lanes), both], axis=1)
+        upper = gdt[pl.ds(pl.multiple_of(at * some_dt, some_dt), some_dt), :].astype(BF)
+        gs[m, quarter:, :] = jnp.concatenate(
+            [upper.astype(F32), lower.astype(F32)], axis=0
+        ).astype(BF)
+    start(p_share)
+    order = [*range(1, nz), 0]
+    for s in order:
+        g = t_dot(dx[s][...], xn[...]) + t_dot(dxh[s][...], xnh[...])
         for m in range(per):
-            outs[m][i * HEADDIM : (i + 1) * HEADDIM, :] = g[m * HEADDIM : (m + 1) * HEADDIM, :]
-    if final:
-        me = lax.axis_index("dp")
-        for m in range(per):
-            at = jnp.bitwise_xor(me, m)
-            v = gbc[pl.ds(pl.multiple_of(at * bc_rows, bc_rows), bc_rows), :]
-            w = gdt[pl.ds(pl.multiple_of(at * dt_rows, dt_rows), dt_rows), :]
-            w = jnp.concatenate([w, jnp.zeros((HALO - dt_rows, w.shape[1]), F32)], axis=0)
-            outs[m][n * HEADDIM : n * HEADDIM + bc_rows, :] = v.astype(BF)
-            outs[m][n * HEADDIM + bc_rows :, :] = w.astype(BF)
+            gx[s, m] = g[m * HEADDIM : (m + 1) * HEADDIM, :].astype(BF)
+        start(p_x[s])
+    arrive([early_swap])
+    start(p_early)
+
+    def add_share():
+        arrive(p_share)
+        for i in range(share // HALO):
+            here = slice(i * HALO, i * HALO + HALO)
+            total = gs[0, here, :].astype(F32)
+            for v in rs:
+                total = total + v[here, :].astype(F32)
+            sums[here, :] = total
+        pack(sums)
+        start(z_share)
+
+    def pack(v):
+        ls[0:quarter, :] = v[0:quarter, :].astype(BF)
+        n = nz * HEADDIM
+        rest = v[quarter:, :]
+        a = rest[:, 0:n] + rest[:, n : 2 * n]
+        b = rest[:, 2 * n : 2 * n + state2] + rest[:, 2 * n + state2 :]
+        low_rows = jnp.concatenate([split2(a), split2(b)], axis=1)
+        row = lax.broadcasted_iota(jnp.int32, (HALO, 1), 0)
+        ls[quarter:, :] = jnp.where(row < some_dt, rest, low_rows.astype(F32)).astype(BF)
+
+    def add_x(s):
+        arrive(p_x[s])
+        for i in range(HEADDIM // HALO):
+            here = slice(i * HALO, i * HALO + HALO)
+            total = gx[s, 0, here, :].astype(F32)
+            for v in rx:
+                total = total + v[s, here, :].astype(F32)
+            lx[s, here, :] = total.astype(BF)
+        if s > 0:
+            start([z_x[s - 1]])
+
+    for i in range(nz):
+        here = slice(i * block, i * block + block)
+        total = dot(dz[here, :], w[0])
+        for s in range(nz):
+            total = total + dot(dx[s][here, :], w[1, s * gc : (s + 1) * gc, :])
+        total = total + dot(dbc[here, :], bc[0:state2, :]) + dot(dti[here, :], wdt[...])
+        dxn[here, :] = total[:, :half]
+        dxn_out[here, :] = total[:, half:].astype(BF)
+        start([dxn_swap[i]])
+        if i == 0:
+            add_share()
+            total = dot(dbch[...], bc[0:state2, :])
+            for s in range(nz):
+                total = total + dot(dxh[s][...], w[1, s * gc : (s + 1) * gc, :])
+            edge_sum[...] = total[:, :half]
+            edge_out[...] = total[:, half:]
+            start([edge_swap])
+        if i == 1:
+            add_x(order[0])
+            arrive([edge_swap])
+            edge_sum[...] = edge_sum[...] + edge_in[...]
+            start([z_edge])
+    if nz > 2:
+        add_x(order[1])
+
+    arrive([*dxn_swap, z_edge])
+    late_edge = jnp.where(zi < nz - 1, edge_next[...], 0.0)
+    gain_v = gain[...]
+    norm_sum = jnp.zeros((8, half), F32)
+    ones = jnp.ones((8, half), BF)
+    for i in range(rows // Q):
+        here = slice(i * Q, i * Q + Q)
+        v = dxn[here, :] + dxn_in[here, :].astype(F32)
+        if i == rows // Q - 1:
+            v = v + jnp.concatenate([jnp.zeros((Q - HALO, half), F32), late_edge], axis=0)
+        dxn[here, :] = v
+        h = hidden[here, :].astype(F32)
+        vh = v * h
+        norm_sum = norm_sum + jnp.sum(
+            (vh * r[here, :]).reshape(Q // 8, 8, half), axis=0
+        )
+        across[:, here] = split_dot_t(ones, vh * gain_v)
+    start([across_swap])
+    nrm[...] = norm_sum
+    start(p_norm)
+    for s in order[2:]:
+        add_x(s)
+    arrive([across_swap])
+    eighth = jnp.full((8, Q), 0.125, F32)
+    for i in range(rows // Q):
+        here = slice(i * Q, i * Q + Q)
+        total = across[:, here] + across_in[:, here]
+        total = t_dot(total, eighth, HIGH)
+        rr = r[here, :]
+        scale = rr * rr * rr / (2 * half)
+        rg = rr * gain_v
+        for j in range(half // Q):
+            lanes = slice(j * Q, j * Q + Q)
+            hid_o[here, lanes] = (
+                cot[here, lanes].astype(F32)
+                + rg[:, lanes] * dxn[here, lanes]
+                - hidden[here, lanes].astype(F32) * (scale * total)
+            ).astype(BF)
+    arrive(p_norm)
+    total = nrm[...]
+    for v in nr:
+        total = total + v[...]
+    nrm2[...] = total
+    start(z_norm)
+
+    arrive([*z_x, *z_share])
+    total = lx[0].astype(F32)
+    for v in zx:
+        total = total + v[...].astype(F32)
+    mine = total.astype(BF)
+    la[0, pl.ds(pl.multiple_of(wi * HEADDIM, HEADDIM), HEADDIM), :] = mine[:, :half]
+    sw_out[0:HEADDIM, :] = mine[:, half:]
+    n = nz * HEADDIM
+    total = ls[0:quarter, :].astype(F32)
+    for v in zs:
+        total = total + v[0:quarter, :].astype(F32)
+    sums[0:quarter, :] = total
+    sw_out[HEADDIM : HEADDIM + quarter, :] = total[:, half:].astype(BF)
+    total = ls[quarter:, :].astype(F32)
+    own_small = total[:, 0:HEADDIM] + total[:, n : n + HEADDIM]
+    for k, v in enumerate(zs):
+        part = v[quarter:, :].astype(F32)
+        total = total + part
+        at = (k + 1) * HEADDIM
+        own_small = own_small + (
+            part[:, at : at + HEADDIM] + part[:, n + at : n + at + HEADDIM]
+        )
+    sums[quarter:, :] = total
+    taps_bc = total[:, 2 * n : 2 * n + state2] + total[:, 2 * n + state2 :]
+    at = HEADDIM + quarter
+    sw_out[at : at + HALO, :] = total[:, half:].astype(BF)
+    own_small = split2(own_small)
+    own_small = jnp.concatenate(
+        [own_small, jnp.zeros((HALO, half - 2 * HEADDIM), BF)], axis=1
+    )
+    taps_bc2 = split2(taps_bc)
+    sw_out[at + HALO : at + 2 * HALO, :] = own_small
+    sw_out[at + 2 * HALO : at + 3 * HALO, :] = taps_bc2
+    start([late_swap])
+    arrive([late_swap])
+    there = pl.ds(pl.multiple_of((1 - wi) * HEADDIM, HEADDIM), HEADDIM)
+    la[0, there, :] = sw_in[0:HEADDIM, :]
+    base = 2 * HEADDIM
+    la[0, base : base + share, :] = (
+        sums[:, :half] + sw_in[HEADDIM : HEADDIM + share, :].astype(F32)
+    ).astype(BF)
+    base = base + share
+    la[0, pl.ds(pl.multiple_of(base + wi * HALO, HALO), HALO), :] = own_small
+    la[0, pl.ds(pl.multiple_of(base + (1 - wi) * HALO, HALO), HALO), :] = sw_in[
+        at + HALO : at + 2 * HALO, :
+    ]
+    start(p_late)
+    got = sw_in[at + 2 * HALO : at + 3 * HALO, :].astype(F32)
+    taps_bc = taps_bc + got[:, :state2] + got[:, state2:]
+    tbc_o[...] = taps_bc[some_dt : some_dt + 4, :]
+    arrive(z_norm)
+    total = nrm2[...]
+    for v in nz_r:
+        total = total + v[...]
+    norm_o[...] = jnp.sum(total, axis=0, keepdims=True)
+
+    arrive(p_early)
+    for m in range(per):
+        for k in range(2):
+            head = k * per + jnp.bitwise_xor(di, m)
+            v = ea[m, k].astype(F32)
+            ow_o[pl.ds(pl.multiple_of(head * HEADDIM, HEADDIM), HEADDIM), :] = v[:HEADDIM, :]
+    arrive(p_late)
+    for m in range(per):
+        at = jnp.bitwise_xor(di, m)
+        for k in range(2):
+            head = k * per + at
+            z_part = ea[m, k, HEADDIM:, :].astype(F32)
+            x_part = la[m, k * HEADDIM : (k + 1) * HEADDIM, :].astype(F32)
+            zx_o[:, pl.ds(pl.multiple_of(head * 2 * HEADDIM, 2 * HEADDIM), 2 * HEADDIM)] = (
+                jnp.transpose(jnp.concatenate([z_part, x_part], axis=0))
+            )
+            v = la[m, base + k * HALO : base + (k + 1) * HALO, :].astype(F32)
+            small_o[head] = (v[:, :HEADDIM] + v[:, HEADDIM : 2 * HEADDIM])[some_dt:, :]
+        v = la[m, 2 * HEADDIM : base, :].astype(F32)
+        stage[pl.ds(pl.multiple_of(at * quarter, quarter), quarter), left] = v[:quarter, :]
+        stage[pl.ds(pl.multiple_of(state2 + at * some_dt, some_dt), some_dt), left] = v[
+            quarter : quarter + some_dt, :
+        ]
+    bcdt_o[...] = jnp.transpose(stage[:, :half])
+    for c in copy.all:
+        c.wait_send()
+
+
+def split_dot_tr(m, v):
+    hi = v.astype(BF)
+    lo = (v - hi.astype(F32)).astype(BF)
+    m = m.astype(BF)
+    return t_dot(m, hi) + t_dot(m, lo)
+
+
+def split_dot_t(m, v):
+    hi = v.astype(BF)
+    lo = (v - hi.astype(F32)).astype(BF)
+    return dot_t(m, hi) + dot_t(m, lo)
 
 
 def shape(dims, dtype=F32):
@@ -1117,18 +1397,6 @@
     def swap(v):
         return lax.ppermute(v, "width", [(0, 1), (1, 0)])
 
-    def turn(v, s):
-        return lax.ppermute(v, "head", [(i, (i + s) % nz) for i in range(nz)])
-
-    def shift(v, s):
-        return lax.ppermute(v, "head", [(i, i + s) for i in range(nz) if 0 <= i + s < nz])
-
-    def cross(v, m):
-        return lax.ppermute(v, "dp", [(i, i ^ m) for i in range(ndp)])
-
-    def pick(v, index):
-        return lax.dynamic_index_in_dim(v, index, 0, keepdims=False)
-
     gc = per * HEADDIM
     groups = tuple(range(nz))
 
@@ -1155,9 +1423,6 @@
         gnorm_gain[None],
     )
     taps_bc = conv_bc.astype(F32)
-    slot = jnp.arange(heads)
-    slot_head = ((zi - slot // per) % nz) * own_heads + wi * per + ((slot % per) ^ di)
-    pick_heads = (slot_head[:, None] == jnp.arange(HEADS)[None, :]).astype(F32)
 
     step = lambda i: (i, 0)
     fix = lambda i: (0, 0)
@@ -1172,7 +1437,8 @@
         c=shape((rows, STATE), BF), dt=shape((rows, heads)), sig=shape((rows, heads)),
         cl=shape((rows, heads)), clt=shape((heads, rows)), dt2=narrow, e12=narrow, tl2=narrow,
         dttl2=narrow, ec2=narrow, edt2=narrow, rate=shape((1, heads)),
-        wdt=shape((heads, model), BF), tot=shape((heads, STATE), BF), table=shape((8, channels)),
+        wdt=shape((heads, model), BF),
+        bcdt=shape((2 * STATE + HEADS + HALO, model), BF), tot=shape((heads, STATE), BF), table=shape((8, channels)),
     )
     wide_part = shape((rows, gc))
     message_shape = shape((channels + HALO, STATE), BF)
@@ -1193,7 +1459,7 @@
             *[held(wide_part)] * nz, *[held(part)] * nz, *[held(wide_part)] * nz,
             *[held(part)] * nz, *[held(part)] * nz, pltpu.VMEM((2, channels, model), BF),
             pltpu.VMEM((rows, half), BF), pltpu.VMEM((HALO, model), BF),
-            pltpu.VMEM((2 * STATE + HEADS + HALO, model), BF), pltpu.VMEM((rows, model), BF),
+            pltpu.VMEM((rows, model), BF),
             held(message_shape), pltpu.VMEM((rows + HALO, gc), F32),
             pltpu.VMEM((rows + HALO, 2 * STATE), F32), pltpu.VMEM((gc, STATE), F32),
             pltpu.SemaphoreType.DMA((remotes,)), pltpu.SemaphoreType.DMA((remotes,)),
@@ -1215,8 +1481,6 @@
     dt, sig, cl, clt, rate, wdt, totals, table = o.dt, o.sig, o.cl, o.clt, o.rate, o.wdt, o.tot, o.table
     dt2, e12, tl2, dttl2, ec2, edt2 = o.dt2, o.e12, o.tl2, o.dttl2, o.ec2, o.edt2
     taps, gain_out, skip = table[:4], table[4:5], table[7:8]
-    bcdt_t = jnp.concatenate([bcdt_t, swap(bcdt_t)], axis=-1)
-    wbc = bcdt_t[: 2 * STATE]
     limit = (lengths[0] - zi * rows).reshape(1, 1)
 
     wide = pl.BlockSpec((Q, channels), step)
@@ -1311,22 +1575,6 @@
     dys = out[:nz]
     dz, yn, ds_local, g_gain, g_skip, out_hidden = out[nz:]
     message = jnp.concatenate([ds_local, totals], axis=0)
-
-    def plane_sum(parts):
-        total = parts[0].astype(F32)
-        for m in range(1, per):
-            total = total + cross(parts[m], m).astype(F32)
-        return total
-
-    def to_owner(total):
-        v = jnp.stack([total] + [cross(total, m) for m in range(1, per)])
-        v = jnp.stack([pick(v, di ^ m) for m in range(per)])
-        return v[:, :, :half], swap(v[:, :, half:])
-
-    def by_head(mine, other):
-        low_w = jnp.where(wi == 0, mine, other)
-        high_w = jnp.where(wi == 0, other, mine)
-        return jnp.concatenate([low_w, high_w], axis=0)
 
     gcol = pl.BlockSpec((rows, gc), lambda s: (0, s))
     early = pl.pallas_call(
@@ -1400,114 +1648,62 @@
     )
     dx, dxh, g_taps = list(out[:nz]), list(out[nz : 2 * nz]), out[2 * nz : 3 * nz]
     dti, g_rate, g_bias, dbc, dbch, g_taps_bc, early_total = out[3 * nz :]
-    g_taps = jnp.concatenate(g_taps, axis=1)
-    early_own, early_other = to_owner(early_total)
-    spread_heads = pick_heads.T.astype(BF)
-    bc_rows = 2 * STATE // per
-    order = groups[1:] + groups[:1]
+    quarter = 2 * STATE // per
+    share = quarter + HALO
+    late_rows = 2 * HEADDIM + share + 2 * HALO
+    swap_rows = HEADDIM + share + 2 * HALO
+    tail_copies = 4 + nz + (per - 1) * (4 + nz) + 3 * (nz - 1) + 1
     operands = [
-        early_total, *[dx[s] for s in order], *[dxh[s] for s in order], xn, xnh, dbc, dbch, dti,
-        spread_heads,
+        *dx, *dxh, *g_taps, dz, dbc, dbch, dti, xn, xnh, weights, o.bcdt, wdt, early_total, hidden,
+        cotangent, r, norm_gain[None].astype(F32), g_taps_bc, g_rate, g_bias, g_skip, g_gain, rate,
+        ex,
     ]
-    late = pl.pallas_call(
-        functools.partial(late_grad_kernel, nz, per, True),
-        in_specs=[anywhere, *[whole(v) for v in operands[1:]]],
-        out_shape=[shape((nz * HEADDIM + bc_rows + HALO, model), BF)] * per,
-        scratch_shapes=[pltpu.VMEM((2 * STATE, model), F32), pltpu.VMEM((HEADS, model), F32)],
-        compiler_params=params(),
-        cost_estimate=cost(8),
-        name="late_grad",
+    line16 = pltpu.VMEM((HALO, half), F32)
+    line8 = pltpu.VMEM((8, half), F32)
+    g_zx, g_out, grad_in_bcdt, grad_hidden, g_norm, g_taps_bc, small = pl.pallas_call(
+        functools.partial(tail_kernel, per, nz),
+        in_specs=[vmem] * len(operands),
+        out_specs=[vmem] * 7,
+        out_shape=[
+            shape((half, own_heads * 2 * HEADDIM)), shape((own_heads * HEADDIM, half)),
+            shape((half, 2 * STATE + HEADS)), shape((rows, half), BF), shape((1, half)),
+            shape((4, 2 * STATE)), shape((own_heads, 8, HEADDIM)),
+        ],
+        scratch_shapes=[
+            pltpu.VMEM((per, 2, 2 * HEADDIM, half), BF), pltpu.VMEM((per, late_rows, half), BF),
+            pltpu.VMEM((nz, per, HEADDIM, model), BF), pltpu.VMEM((per, share, model), BF),
+            pltpu.VMEM((HEADS, model), F32), pltpu.VMEM((nz, HEADDIM, model), BF),
+            pltpu.VMEM((share, model), BF), pltpu.VMEM((swap_rows, half), BF),
+            pltpu.VMEM((swap_rows, half), BF), pltpu.VMEM((rows, half), F32),
+            pltpu.VMEM((rows, half), BF), pltpu.VMEM((rows, half), BF), line16, line16, line16,
+            line16, pltpu.VMEM((8, rows), F32), pltpu.VMEM((8, rows), F32), line8, line8,
+            pltpu.VMEM((share, model), F32),
+            *[pltpu.VMEM((nz, HEADDIM, model), BF)] * (per - 1),
+            *[pltpu.VMEM((share, model), BF)] * (per - 1),
+            *[pltpu.VMEM((HEADDIM, model), BF)] * (nz - 1),
+            *[pltpu.VMEM((share, model), BF)] * (nz - 1), *[line8] * (per - 1),
+            *[line8] * (nz - 1), pltpu.VMEM((2 * STATE + HEADS, model), F32),
+            pltpu.SemaphoreType.DMA((tail_copies,)), pltpu.SemaphoreType.DMA((tail_copies,)),
+        ],
+        compiler_params=pltpu.CompilerParams(
+            vmem_limit_bytes=VMEM, collective_id=2, has_side_effects=True
+        ),
+        cost_estimate=cost(60),
+        name="tail",
     )(*operands)
-    halves = (order,)
-    late = [plane_sum(late)]
-
-    share = late[-1][len(halves[-1]) * HEADDIM :]
-    addend = {}
-    for some, v in zip(halves, late):
-        for i, s in enumerate(some):
-            addend[s] = jnp.concatenate([v[i * HEADDIM : (i + 1) * HEADDIM], share], axis=0)
-    total = addend[0]
-    for s in range(1, nz):
-        total = total + turn(addend[s].astype(BF), -s).astype(F32)
-    late_own, late_other = to_owner(total.astype(BF))
-    g_early = by_head(early_own, early_other)
-    g_late = by_head(late_own[:, :HEADDIM], late_other[:, :HEADDIM])
-    g_zx = jnp.concatenate([g_early[:, HEADDIM:], g_late], axis=1)
-    g_bcdt = late_own[:, HEADDIM:].astype(F32) + late_other[:, HEADDIM:].astype(F32)
-    grad_in_bcdt = jnp.transpose(
-        jnp.concatenate(
-            [
-                g_bcdt[:, :bc_rows].reshape(2 * STATE, half),
-                g_bcdt[:, bc_rows : bc_rows + HEADS // per].reshape(HEADS, half),
-            ],
-            axis=0,
-        )
-    )
-
-    wz = [weights[0, s * gc : (s + 1) * gc] for s in groups]
-    wx = [weights[1, s * gc : (s + 1) * gc] for s in groups]
-    lhs = [dz] * nz + dx + [dbc, dti]
-    dxn, dxn_o = sum_products(
-        lhs, [*groups] + [0] * (nz + 2), wz + wx + [wbc, wdt], rows, early_other
-    )
-    edge = sum(dot(v, w) for v, w in zip(dxh + [dbch], wx + [wbc]))
-    edge = edge[:, :half] + swap(edge[:, half:])
-    edge = shift(edge, -1)
-    dxn = dxn + swap(dxn_o).astype(F32) + jnp.pad(edge, ((rows - HALO, 0), (0, 0)))
-    source = hidden.astype(F32)
-    gain_half = norm_gain[None].astype(F32)
-    across = jnp.sum(dxn * gain_half * source, axis=1, keepdims=True)
-    across = across + swap(across)
-    grad_hidden = (
-        cotangent.astype(F32)
-        + r * gain_half * dxn
-        - source * (r * r * r) / model * across
-    ).astype(BF)
-    g_norm = jnp.sum(dxn * source * r, axis=0)
-
-    table = jnp.concatenate(
-        [
-            g_bias.reshape(heads, 1),
-            (g_rate * rate).reshape(heads, 1),
-            jnp.sum(g_skip.reshape(heads, HEADDIM), axis=1, keepdims=True),
-            jnp.transpose(g_taps.reshape(4, heads, HEADDIM), (1, 0, 2)).reshape(heads, 4 * HEADDIM),
-            g_gain.reshape(heads, HEADDIM),
-        ],
-        axis=1,
-    )
-    table = jnp.dot(pick_heads.T, table, precision=HIGH)
-    side = (jnp.arange(2) == wi).astype(F32)[:, None] * g_norm[None]
-    small = jnp.concatenate([table.reshape(-1), g_taps_bc.reshape(-1), side.reshape(-1)])
-    small = small + swap(small)
-    flip = 1
-    while flip < ndp:
-        small = small + cross(small, flip)
-        flip *= 2
-    flip = 1
-    while flip < nz:
-        small = small + lax.ppermute(small, "head", [(i, i ^ flip) for i in range(nz)])
-        flip *= 2
-    size = table.size
-    table = lax.dynamic_slice_in_dim(
-        small[:size].reshape(HEADS, -1), zi * own_heads, own_heads, 0
-    )
-    g_taps_bc = small[size : size + 8 * STATE].reshape(4, 2 * STATE)
-    g_norm = pick(small[size + 8 * STATE :].reshape(2, half), wi)
     return (
         out_hidden,
         grad_hidden,
-        g_norm,
-        jnp.transpose(g_zx, (2, 0, 1)).astype(F32),
+        g_norm.reshape(half),
+        g_zx.reshape(half, own_heads, 2 * HEADDIM),
         grad_in_bcdt,
-        jnp.transpose(
-            table[:, 3 : 3 + 4 * HEADDIM].reshape(own_heads, 4, HEADDIM), (1, 0, 2)
-        ).reshape(4, own_heads * HEADDIM),
+        jnp.transpose(small[:, :4], (1, 0, 2)).reshape(4, own_heads * HEADDIM),
         g_taps_bc,
-        table[:, 0],
-        table[:, 1],
-        table[:, 2],
-        table[:, 3 + 4 * HEADDIM :].reshape(-1),
-        g_early[:, :HEADDIM].reshape(own_heads * HEADDIM, half).astype(F32),
+        small[:, 6, 0],
+        small[:, 7, 0],
+        jnp.sum(small[:, 5], axis=1),
+        small[:, 4].reshape(-1),
+        g_out,
     )
 
 
@@ -1521,7 +1717,7 @@
         and LEN % (nz * Q) == 0
         and SEQS == ndp
         and HEADS // nw * HEADDIM % Q == 0
-        and HEADS // ndp <= HALO
+        and HEADS // ndp == 8
     )
 
 

time: 366 us -> 314 us (0.86)
  waiting for transfers between devices: 55.2 us -> 1.92 us
  Pallas kernels: 228 us -> 280 us
  starting transfers between devices: 25.7 us -> 0.51 us
  other arithmetic: 21.3 us -> 5.71 us
  matrix products: 5.39 us -> 0 us
  local copies, waits for them, and re-layouts: 26.8 us -> 23.1 us
    pallas_call x1, Pallas kernels: 7.99 us -> 69.9 us  [sequence_device(): pl.pallas_call(functools.partial(tail_kernel, per, nz), in_specs=[vmem] *...]
    ppermute x17 -> x0, waiting for transfers between devices: 55.1 us -> none  [the longest x11 41.5 us: cross(): return lax.ppermute(v, 'dp', [(i, i ^ m) for i in range(ndp)])]
    ppermute x17 -> x0, starting transfers between devices: 23.9 us -> none  [the longest x11 12.5 us: cross(): return lax.ppermute(v, 'dp', [(i, i ^ m) for i in range(ndp)])]
    pallas_call x2 -> x1, Pallas kernels: 16.2 us -> 5.86 us  [sum_products(): pl.pallas_call(functools.partial(sum_products_kernel, len(a)), grid=(coun...]
    dot_general x6 -> x0, matrix products: 5.39 us -> none  [the longest x5 5.11 us: dot(): lax.dot_general(a, b, (((1,), (0,)), ((), ())), precision=prec, preferred...]
    convert_element_type x7 -> x1, other arithmetic: 5.44 us -> 0.58 us  [sequence_device(): norm_gain[None].astype(F32)]
    squeeze x1 -> x0, local copies, waits for them, and re-layouts: 4.21 us -> none  [sequence_device(): wx = [weights[1, s * gc:(s + 1) * gc] for s in groups]]
    unnamed x93 -> x28, local copies, waits for them, and re-layouts: 11.7 us -> 14.2 us
  transfers between devices with their start and end apart: 26 -> 2, of which waited for: 9 -> 2; matrix products, arithmetic and copies ran while one was open for 10% -> 0% of each run, Pallas kernels for 37% -> 0%
where the time goes in v5:
time: 314 us; the launch traced here: 313 us
  Pallas kernels  280 us (89%)
  local copies, waits for them, and re-layouts  23.1 us (7%)
  other arithmetic  5.71 us (2%)
    pallas_call x1, Pallas kernels, sequence_device(): pl.pallas_call(functools.partial(front_kernel, per, nz), in_specs=[vmem]...  91.1 us
    pallas_call x1, Pallas kernels, sequence_device(): pl.pallas_call(functools.partial(tail_kernel, per, nz), in_specs=[vmem] *...  69.9 us
    pallas_call x1, Pallas kernels, sequence_device(): pl.pallas_call(functools.partial(scan_back_kernel, groups, per), grid=(2...  66.6 us
    pallas_call x1, Pallas kernels, sequence_device(): pl.pallas_call(functools.partial(gate_kernel, groups, per), grid=(blocks,...  14.5 us
    unnamed x28, local copies, waits for them, and re-layouts  14.2 us
    pallas_call x1, Pallas kernels, sequence_device(): pl.pallas_call(functools.partial(carry_kernel, groups, per), grid=(blocks...  13.7 us
    pallas_call x1, Pallas kernels, sequence_device(): pl.pallas_call(functools.partial(early_grad_kernel, per), grid=(nz,), in_...  8.99 us
    pallas_call x1, Pallas kernels, sequence_device(): pl.pallas_call(pull_kernel, grid=(rows // tile,), in_specs=[pl.BlockSpec(...  6.54 us
  transfers between devices with their start and end apart: 2, of which 2 were waited for; matrix products, arithmetic and copies ran while one was open for 0% of the time, Pallas kernels for 0%

profile of v5, /device:TPU:0, one launch (start us, length us, event | category | flops | bytes accessed | tf_op | source)
XLA Modules:
  0.0 313.0 jit_solution(5731488073042602726)
XLA Ops:
  1.3 1.3 broadcast_in_dim.12.gn
  2.6 1.3 broadcast_in_dim.10.gain
  3.8 1.3 convert_element_type.6.refs_7_.refs_37_
  5.1 0.7 pad_maximum_fusion.1
  5.8 0.1 broadcast_in_dim.11
  5.9 0.7 reshape.45.scal
  6.5 1.9 copy.30.bcdt
  8.4 2.5 copy.36
  10.9 3.0 prep.1
  13.9 91.1 %front.1 = (bf16[2,1024,1024]{2,1,0:T(8,128)(2,1)}, bf16[1024,1024]{1,0:T(8,128)(2,1)}, bf16[1024,512]{1,0:T(8,128)(2,1)}, bf16[1024,1024]{1,0:T(8,128)(2,1)}, f...) custom-call(bf16[1024,512]{1,0:T(8,128)(2,1)} %refs_22_.1, ...), custom_call_target="tpu_custom_call" | custom-call | flops 8999999488 | bytes 90000 | tf_op jit(solution)/shard_map/front/pallas_call | solution.py:1453
  105.1 1.4 fusion
  106.5 6.5 %pull.1 = (bf16[1024,1024]{1,0:T(8,128)(2,1)}, f32[1024,1024]{1,0:T(8,128)}) custom-call(bf16[1024,512]{1,0:T(8,128)(2,1)} %refs_23_.2, bf16[1024,512]{1,0:T(8,128)(2,1)} %get-tuple-element.146.cot2, s32[1,1]{1,0:T(1,128)} %bitcast.4.limit.refs_22_, bf16[1024,1024]{1,0:T(8,128)(2,1)} %get-tuple-element.147.w.refs_1_), custom_call_target="tpu_custom_call" | custom-call | flops 500000000 | bytes 5000 | tf_op jit(solution)/shard_map/pull/pallas_call | solution.py:1494
  113.0 13.7 %carry.1 = (f32[1024,256]{1,0:T(8,128)}, f32[1024,256]{1,0:T(8,128)}, f32[1024,256]{1,0:T(8,128)}, f32[1024,256]{1,0:T(8,128)}, bf16[8,256,128]{2,1,0:T(8,128)(2...) custom-call(bf16[1024,256]{1,0:T(8,128)(2,1)} %get-tuple-element.134, ...), custom_call_target="tpu_custom_call" | custom-call | flops 1000000000 | bytes 10000 | tf_op jit(solution)/shard_map/carry/pallas_call | solution.py:1506
  126.7 0.0 copy-start
  126.7 0.0 copy-start.7
  126.7 0.0 copy-start.5
  126.7 5.9 %products.1 = (f32[1024,512]{1,0:T(8,128)}, bf16[1024,512]{1,0:T(8,128)(2,1)}) custom-call(bf16[1024,1024]{1,0:T(8,128)(2,1)} %get-tuple-element.164.refs_0_, bf16[1024,1024]{1,0:T(8,128)(2,1)} %get-tuple-element.147.w.refs_1_, f32[1024,2]{1,0:T(8,128)} %get-tuple-element.162.refs_2_.refs_13_), custom_call_target="tpu_custom_call" | custom-call | flops 400000000 | bytes 4000 | tf_op jit(solution)/shard_map/products/pallas_call | solution.py:1531
  132.6 0.0 collective-permute-start.1
  132.6 0.0 copy-done
  132.6 0.5 collective-permute-start
  133.1 0.0 copy-done.7
  133.1 0.6 reshape_convert_fusion.refs_25_
  133.7 0.0 copy-done.5
  133.7 0.6 slice.26.refs_36_
  134.3 1.7 collective-permute-done.refs_14_
  136.0 0.0 copy-start.4
  136.0 0.2 collective-permute-done.1.refs_21_
  136.2 0.0 copy-start.3
  136.2 0.6 copy-done.4
  136.8 0.5 copy-done.3
  137.3 0.0 copy-start.6
  137.3 14.5 %gate.1 = (bf16[1024,256]{1,0:T(8,128)(2,1)}, bf16[1024,256]{1,0:T(8,128)(2,1)}, bf16[1024,256]{1,0:T(8,128)(2,1)}, bf16[1024,256]{1,0:T(8,128)(2,1)}, bf16[1024...) custom-call(f32[1024,256]{1,0:T(8,128)} %get-tuple-element.158.refs_, ...), custom_call_target="tpu_custom_call" | custom-call | flops 1000000000 | bytes 10000 | tf_op jit(solution)/shard_map/gate/pallas_call | solution.py:1552
  151.8 0.0 copy-done.6
  151.8 1.7 pad_maximum_fusion.refs_42_
  153.5 9.0 %early_grad.1 = (bf16[4,128,1024]{2,1,0:T(8,128)(2,1)}, bf16[4,128,1024]{2,1,0:T(8,128)(2,1)}, bf16[4,128,1024]{2,1,0:T(8,128)(2,1)}, bf16[4,128,1024]{2,1,0:T(8,128)(2,1)}) custom-call(bf16[1024,1024]{1,0:T(8,128)(2,1)} %get-tuple-element.199.yn, bf16[1024,1024]{1,0:T(8,128)(2,1)} %get-tuple-element.200.masked, ...), custom_call_target="tpu_custom_call" | custom-call | flops 600000000 | bytes 6000 | tf_op jit(solution)/shard_map/early_grad/pallas_call | solution.py:1580
  162.5 66.6 %scan_back.1 = (bf16[1024,256]{1,0:T(8,128)(2,1)}, bf16[1024,256]{1,0:T(8,128)(2,1)}, bf16[1024,256]{1,0:T(8,128)(2,1)}, bf16[1024,256]{1,0:T(8,128)(2,1)}, bf16...) custom-call(bf16[1024,256]{1,0:T(8,128)(2,1)} %get-tuple-element.168, ...), custom_call_target="tpu_custom_call" | custom-call | flops 5000000000 | bytes 50000 | tf_op jit(solution)/shard_map/scan_back/pallas_call | solution.py:1596
  229.1 69.9 %tail.1 = (f32[512,1024]{1,0:T(8,128)}, f32[512,512]{1,0:T(8,128)}, f32[512,288]{1,0:T(8,128)}, bf16[1024,512]{1,0:T(8,128)(2,1)}, f32[1,512]{1,0:T(1,128)}, /*index=5*/f32[4,256]{1,0:T(4,128)}, f32[8,8,64]{2,1,0:T(8,128)}) custom-call(bf16[1024,256]{1,0:T(8,128)(2,1)} %get-tuple-element.207.refs_0_, bf16[1024,256]{1,0:T(8,128)(2,1)} %get-tuple-element.208.refs_1_, ...), custom_call_target="tpu_custom_call" | custom-call | flops 6000000000 | bytes 60000 | tf_op jit(solution)/shard_map/tail/pallas_call | solution.py:1663
  299.1 1.5 slice_reduce_fusion.2
  300.6 1.5 slice_reduce_fusion
  302.1 0.8 slice_bitcast_fusion
  302.8 0.7 reshape.49
  303.5 0.7 reshape_squeeze.3
  304.2 2.2 copy.32
  306.4 0.0 copy-start.2
  306.4 3.5 %copy.34 = f32[64,8,8,128]{3,2,1,0:T(8,128)} copy(f32[64,8,8,128]{3,1,2,0:T(8,128)} %bitcast.16) | data formatting | bytes 4194304
  309.8 0.0 copy-start.9
  309.8 0.0 copy-start.8
  309.8 0.0 copy-start.1
  309.8 0.0 copy-done.2
  309.8 1.0 copy.42
  310.8 0.0 copy-done.9
  310.8 0.6 copy.43
  311.4 0.0 copy-done.8
  311.4 0.6 copy.44
  312.0 0.0 copy-done.1
  312.0 1.0 copy.45
  (1 shorter events, 0.0 us)
Async XLA Ops:
  126.7 5.9 %copy-start = (f32[1024,2]{1,0:T(8,128)S(1)}, f32[1024,2]{1,0:T(8,128)}, u32[]{:S(2)}) copy-start(f32[1024,2]{1,0:T(8,128)} %get-tuple-element.162.refs_2_.refs_13_) | copy-start | bytes 24580
  126.7 6.4 %copy-start.7 = (bf16[512]{0:T(512)(128)(2,1)S(1)}, bf16[512]{0:T(512)(128)(2,1)}, u32[]{:S(2)}) copy-start(bf16[512]{0:T(512)(128)(2,1)} %param.19) | copy-start | bytes 3076
  126.7 7.0 %copy-start.5 = (f32[8,1024]{1,0:T(8,128)S(1)}, f32[8,1024]{1,0:T(8,128)}, u32[]{:S(2)}) copy-start(f32[8,1024]{1,0:T(8,128)} %get-tuple-element.157) | copy-start | bytes 98308
  132.6 3.6 %collective-permute-start.1 = (bf16[1024,512]{1,0:T(8,128)(2,1)}, bf16[1024,512]{1,0:T(8,128)(2,1)S(1)}, u32[]{:S(2)}, u32[]{:S(2)}) collective-permute-start(bf16[1024,512]{1,0:T(8,128)(2,1)} %get-tuple-element.166), channel_id=1, source_target_pairs={{0,1},{1,0},{2,3},{3,2},{4,5},{5,4},{6,7},{7,6},{8,9},{9,8},{10,11... | collective-permute-start | bytes 3145736 | tf_op jit(solution)/shard_map/ppermute | solution.py:1398
  132.6 3.4 %collective-permute-start = (f32[1024,2]{1,0:T(8,128)S(1)}, f32[1024,2]{1,0:T(8,128)S(1)}, u32[]{:S(2)}, u32[]{:S(2)}) collective-permute-start(f32[1024,2]{1,0:T(8,128)S(1)} %copy-done), channel_id=1, source_target_pairs={{0,1},{1,0},{2,3},{3,2},{4,5},{5,4},{6,7},{7,6},{8,9},{9,8},{10,11... | collective-permute-start | bytes 24584 | tf_op jit(solution)/shard_map/ppermute | solution.py:1398
  136.0 0.8 copy-start.4
  136.2 1.1 copy-start.3
  137.3 14.5 %copy-start.6 = (bf16[16,128]{1,0:T(8,128)(2,1)S(1)}, bf16[16,128]{1,0:T(8,128)(2,1)}, u32[]{:S(2)}) copy-start(bf16[16,128]{1,0:T(8,128)(2,1)} %get-tuple-element.198) | copy-start | bytes 12292
  306.4 3.5 %copy-start.2 = (bf16[1024,512]{1,0:T(8,128)(2,1)S(1)}, bf16[1024,512]{1,0:T(8,128)(2,1)}, u32[]{:S(2)}) copy-start(bf16[1024,512]{1,0:T(8,128)(2,1)} %get-tuple-element.283) | copy-start | bytes 3145732
  309.8 1.0 copy-start.9
  309.8 1.6 copy-start.8
  309.8 2.2 copy-start.1

commit v6 on v5

--- a/solution.py
+++ b/solution.py
@@ -282,7 +282,7 @@
 
 
 def prep_kernel(
-    per, zx, ow, bcdt, gain, cx, scal, gn,
+    per, zx, ow, bcdt, rows_in,
     first_o, first2_o, rest_o, rest2_o, out_o, out2_o, bcdt_o, table_o,
 ):
     di = lax.axis_index("dp")
@@ -303,12 +303,10 @@
             o_o[m * HEADDIM : (m + 1) * HEADDIM, :] = ow[
                 pl.ds(pl.multiple_of(head * HEADDIM, HEADDIM), HEADDIM), :
             ]
-    n = bcdt.shape[1]
-    bcdt_o[0:n, :] = jnp.transpose(bcdt[...])
-    bcdt_o[n:, :] = jnp.broadcast_to(gain[...], (HALO, gain.shape[1]))
-    rows = jnp.concatenate(
-        [cx[...].astype(F32), gn[...].astype(F32), scal[...]], axis=0
-    )
+    n = bcdt.shape[0]
+    bcdt_o[0:n, :] = bcdt[...]
+    bcdt_o[n:, :] = jnp.broadcast_to(rows_in[8:9, :], (HALO, bcdt.shape[1])).astype(BF)
+    rows = rows_in[0:8, :]
     half = rows.shape[1] // 2
     rows = jnp.where(wi == 0, rows[:, :half], rows[:, half:])
     step = 1
@@ -321,7 +319,7 @@
     table_o[...] = rows
 
 
-def entry_first(per, hm, ho, hh, bcdt, table, cbc, sel, o, xn_o, buf):
+def entry_first(per, hm, ho, hh, bcdt, table, sel, o, xn_o, buf, between, edges):
     xnh_o, r_o, raw_o, rawh_o, dt_o, sig_o = o.xnh, o.r, o.raw, o.rawh, o.dt, o.sig
     cl_o, clt_o, rate_o, wdt_o, b_o = o.cl, o.clt, o.rate, o.wdt, o.b
     rows = hm.shape[0]
@@ -343,13 +341,6 @@
         h = jnp.concatenate([left, right], axis=1).astype(F32)
         r = lax.rsqrt(jnp.mean(h * h, axis=1, keepdims=True) + EPS)
         return (h * r * gain).astype(BF), r
-
-    half = hm.shape[1]
-    xnh, _ = norm(hh[:, :half], hh[:, half:])
-    xnh = jnp.where(lax.axis_index("head") > 0, xnh.astype(F32), 0.0).astype(BF)
-    xnh_o[...] = xnh
-    buf[0:HALO, :] = dot_t(xnh, wbc[...])
-    rawh_o[...] = buf[0:HALO, :]
 
     def first(i, carry):
         here = pl.ds(pl.multiple_of(i * Q, Q), Q)
@@ -370,7 +361,16 @@
         )
         return carry
 
-    lax.fori_loop(0, blocks, first, 0, unroll=2)
+    lax.fori_loop(0, blocks // 2, first, 0, unroll=2)
+    between()
+    lax.fori_loop(blocks // 2, blocks, first, 0, unroll=2)
+    edges()
+    half = hm.shape[1]
+    xnh, _ = norm(hh[:, :half], hh[:, half:])
+    xnh = jnp.where(lax.axis_index("head") > 0, xnh.astype(F32), 0.0).astype(BF)
+    xnh_o[...] = xnh
+    buf[0:HALO, :] = dot_t(xnh, wbc[...])
+    rawh_o[...] = buf[0:HALO, :]
 
 
 def entry_second(cbc, o, tot_o, buf):
@@ -552,8 +552,13 @@
         for k, peer in enumerate(d_peers):
             mine = pl.ds(s * gc, HEADDIM)
             there = pl.ds(s * gc + (k + 1) * HEADDIM, HEADDIM)
-            p_w[s].append(copy(w.at[:, mine, :], w.at[:, there, :], peer))
-            p_out[s].append(copy(wo_o.at[mine, :], wo_o.at[there, :], peer))
+            via, to = k, peer
+            if k + 1 == per - 1:
+                first_hop = s % 2
+                mine = pl.ds(s * gc + (first_hop + 1) * HEADDIM, HEADDIM)
+                to = d_peers[1 - first_hop]
+            p_w[s].append(copy(w.at[:, mine, :], w.at[:, there, :], to))
+            p_out[s].append(copy(wo_o.at[mine, :], wo_o.at[there, :], to))
 
     places = [0]
 
@@ -572,52 +577,76 @@
         local(out_mine, wo_o.at[pl.ds(0, gc), left]),
     ]
     meet([sibling, *z_peers, *line_peers(nz, -1), *d_peers])
-    start([swap_first, *z_table, swap_hidden, swap_bc, edge1, swap_rest, swap_out, swap_cot])
+    start([swap_first, *z_table, swap_hidden, swap_bc, edge1])
     ready[0].wait()
     arrive([swap_first])
-    start(z_w)
+    start([z_w[0], swap_rest, swap_out, swap_cot])
+    for c in ready[1:]:
+        c.wait()
     arrive([swap_hidden])
     start([edge2])
-    for c in ready[1:]:
-        c.wait()
-    arrive([swap_bc, *z_table, edge1, edge2])
-    entry_first(per, hidden, ho, eh, bc, o.table, cbc, sel, o, xn, bcbuf)
-    arrive([z_w[0]])
-    start(p_w[1])
+    arrive([swap_bc, *z_table])
+    pending = []
+
+    def pass_on(copies, s):
+        arrive([copies[s % 2]])
+        start([copies[2]])
+
+    def between():
+        arrive([z_w[0]])
+        start([*p_w[1][:2], *z_w[1:]])
+
+    def edges():
+        arrive([edge1, edge2])
+
+    entry_first(per, hidden, ho, eh, bc, o.table, sel, o, xn, bcbuf, between, edges)
+    pass_on(p_w[1], 1)
+    arrive([z_w[1], swap_rest])
+    start(p_w[2][:2])
     entry_second(cbc, o, o.tot, bcbuf)
     msg[top:, :] = o.tot[...]
-    pending = [local(xn, xn_o)]
+    pending.append(local(xn, xn_o))
+    for k in range(3, nz):
+        arrive([z_w[k - 1]])
+        start(p_w[k][:2])
     arrive([swap_out])
     start(z_out)
-    arrive([swap_rest])
     taps = o.table
-    for s in range(nz):
-        if s > 0:
-            arrive(p_w[s])
+
+    def project_group(s):
         project(
             s, per, xn, o, w, taps, ex, z_v[s], xr_v[s], xrh_o[s], u_v[s], xdt_v[s], msg, buf, acc
         )
         for a, b in ((z_v, z_o), (xr_v, xr_o), (u_v, u_o), (xdt_v, xdt_o)):
             pending.append(local(a[s], b[s]))
-        if s == 0:
-            for k in range(2, nz):
-                arrive([z_w[k - 1]])
-                start(p_w[k])
+
+    def inside_group(s):
+        inside(s, per, xdt_v[s], o, y_v[s])
+        pending.append(local(y_v[s], y_o[s]))
+
+    project_group(0)
+    for k in range(2, nz):
+        pass_on(p_w[k], k)
+    inside_group(0)
+    for k in range(1, nz):
+        arrive([z_out[k - 1]])
+        start(p_out[k][:2])
+    for s in range(1, nz):
+        arrive([p_w[s][1 - s % 2], p_w[s][2]])
+        project_group(s)
         if s == nz - 2:
             start(z_state)
             for k in range(1, nz):
-                arrive([z_out[k - 1]])
-                start(p_out[k])
-        if s == nz - 1:
-            start(z_state2)
-            pending.append(local(w, w_o))
-        inside(s, per, xdt_v[s], o, y_v[s])
-        pending.append(local(y_v[s], y_o[s]))
+                pass_on(p_out[k], k)
+    start(z_state2)
+    pending.append(local(w, w_o))
+    for s in range(1, nz):
+        inside_group(s)
     everything = [swap_first, swap_rest, swap_hidden, swap_bc, swap_out, swap_cot, edge1, edge2]
     everything += [*z_table, *z_w, *z_out, *z_state, *z_state2]
     for s in range(1, nz):
         everything += p_w[s] + p_out[s]
-        arrive(p_out[s])
+        arrive([p_out[s][1 - s % 2], p_out[s][2]])
     arrive([swap_cot, *z_state, *z_state2])
     for c in everything:
         c.wait_send()
@@ -660,95 +689,129 @@
         store[at * gc : at * gc + gc, :] = total
 
 
-def carry_kernel(groups, per, *refs):
-    n = len(groups)
-    y_in, us, z, dyn, b, c, clt, e12, dttl2, messages, dsk, gain, ex, rest = take(
-        refs, n, n, n, 0, 0, 0, 0, 0, 0, n - 1, 0, 0, 0
-    )
-    ys_o, st_o, rest = take(rest, n, n)
-    gg_o, sum_o, s = rest
+def mid_kernel(groups, per, *refs):
+    nz = len(groups)
+    y_in, u, z, cot, cot2, b, c, clt, e12, dttl2, refs = take(refs, nz, nz, nz, *[0] * 7)
+    u2, z2, ec2, c2, hidden, refs = take(refs, nz, nz, 0, 0, 0)
+    messages, tot, table, ex, wout, limit, refs = take(refs, nz - 1, *[0] * 5)
+    gain, dsk = table.at[4:5, :], table.at[7:8, :]
+    st_o, mask_o, dys_o, dz_o, yn_o, out_o, msg_o, gn_o, sk_o, refs = take(
+        refs, nz, 0, nz, *[0] * 6
+    )
+    s, acc, yv, dv, br, br_out, br_in, sm_out, sm_in, gg, sends, receives = refs
+    step = pl.program_id(0)
+    tiles = pl.num_programs(0) - 1
+    rows, half = cot.shape
     gc = per * HEADDIM
-
-    @pl.when(pl.program_id(0) == 0)
+    state = s.shape[1]
+    sibling = {"width": 1 - lax.axis_index("width")}
+
+    def copies(k):
+        return [
+            remote(sm_out.at[k], sm_in.at[k], sends, receives, 2 * k, sibling),
+            remote(br_out.at[k], br_in.at[k], sends, receives, 2 * k + 1, sibling),
+        ]
+
+    @pl.when(step == 0)
     def _():
+        meet([sibling])
         z_index = lax.axis_index("head")
-        from_messages(messages, 1, groups, per, s.shape[1], s, lambda k: z_index - k >= 0)
-
-    square = jnp.zeros((Q, gc), F32)
-    inner = jnp.zeros((Q, gc), F32)
-    for j in groups:
-        here = slice(j * gc, j * gc + gc)
-        sv = s[here, :]
-        sb = sv.astype(BF)
-        st_o[j][0] = sb
-        x = us[j][...]
-        x = x * sigmoid(x)
-        e1 = dot(e12[...], ex[:, here])
-        y = y_in[j][...].astype(F32) + e1 * dot_t(c[...], sb) + dsk[:, here] * x
-        ys_o[j][...] = y
-        xt = (x * dot(dttl2[...], ex[:, here])).astype(BF)
-        s[here, :] = head_scale(clt, j * per, per, sv.shape[1]) * sv + t_dot(xt, b[...])
-        zz = z[j][...]
-        gz = y * (zz * sigmoid(zz))
-        gg = gz * gain[:, here]
-        gg_o[:, here] = gg.astype(BF)
-        square = square + gz * gz
-        inner = inner + gg * dyn[:, here]
-    lane = lax.broadcasted_iota(jnp.int32, (Q, 2), 1)
-    sum_o[...] = jnp.where(
-        lane == 0,
-        jnp.sum(square, axis=1, keepdims=True),
-        jnp.sum(inner, axis=1, keepdims=True),
-    )
-
-
-def gate_kernel(groups, per, *refs):
-    n = len(groups)
-    ys, z, us, dyn, sums, sums2, gain, ec2, ex, c, rest = take(refs, n, n, n, *[0] * 7)
-    hidden, branch, branch2, limit, rest = take(rest, 0, 0, 0, 0)
-    dys_o, rest = take(rest, n)
-    dz_o, yn_o, ds_o, gn_o, sk_o, out_o, acc = rest
-    gc = per * HEADDIM
-
-    @pl.when(pl.program_id(0) == 0)
-    def _():
+        from_messages(messages, 1, groups, per, state, s, lambda k: z_index - k >= 0)
         acc[...] = jnp.zeros_like(acc)
         gn_o[...] = jnp.zeros_like(gn_o)
         sk_o[...] = jnp.zeros_like(sk_o)
 
-    count = n * gc * 2
-    both = sums[...] + sums2[...]
-    r2 = lax.rsqrt(both[:, 0:1] / count + EPS)
-    pull = both[:, 1:2] * (r2 * r2 * r2) / count
-    row = lax.broadcasted_iota(jnp.int32, (Q, 1), 0) + pl.program_id(0) * Q
-    keep = jnp.where(row < limit[0, 0], r2, 0.0)
-    out_o[...] = (
-        hidden[...].astype(F32) + keep * (branch[...] + branch2[...].astype(F32))
-    ).astype(BF)
-    for j in groups:
-        here = slice(j * gc, j * gc + gc)
-        gn = gain[:, here]
-        zz = z[j][...]
-        sz = sigmoid(zz)
-        silu = zz * sz
-        y = ys[j][...]
-        gz = y * silu
-        dy_n = dyn[:, here]
-        gr = gz * r2
-        yn_o[:, here] = (gr * gn).astype(BF)
-        gn_o[:, here] += jnp.sum(dy_n * gr, axis=0, keepdims=True)
-        dgz = r2 * gn * dy_n - gz * pull
-        dys = dgz * silu
-        dys_o[j][...] = dys.astype(BF)
-        dz_o[:, here] = (dgz * y * (sz + silu * (1.0 - sz))).astype(BF)
-        x = us[j][...]
-        x = x * sigmoid(x)
-        sk_o[:, here] += jnp.sum(dys * x, axis=0, keepdims=True)
-        acc[here, :] += t_dot((dys * dot(ec2[...], ex[:, here])).astype(BF), c[...])
-
-    @pl.when(pl.program_id(0) == pl.num_programs(0) - 1)
+    @pl.when(step < tiles)
     def _():
-        ds_o[...] = acc[...].astype(BF)
+        slot = lax.rem(step, 2)
+        row = lax.broadcasted_iota(jnp.int32, (rows, 1), 0) + step * rows
+        keep = row < limit[0, 0]
+        for i, v in enumerate((cot, cot2)):
+            mask_o[:, i * half : i * half + half] = jnp.where(keep, v[...].astype(F32), 0.0).astype(
+                BF
+            )
+        dv[slot] = dot_t(mask_o[...], wout[...])
+        lane = lax.broadcasted_iota(jnp.int32, (Q, Q), 1)
+        for i in range(rows // Q):
+            part = slice(i * Q, i * Q + Q)
+            cc, bb = c[part, :], b[part, :]
+            square = jnp.zeros((Q, gc), F32)
+            inner = jnp.zeros((Q, gc), F32)
+            for j in groups:
+                here = slice(j * gc, j * gc + gc)
+                sv = s[here, :]
+                sb = sv.astype(BF)
+                st_o[j][i] = sb
+                x = u[j][part, :]
+                x = x * sigmoid(x)
+                e1 = dot(e12[part, :], ex[:, here])
+                y = y_in[j][part, :].astype(F32) + e1 * dot_t(cc, sb) + dsk[:, here] * x
+                yv[slot, part, here] = y
+                xt = (x * dot(dttl2[part, :], ex[:, here])).astype(BF)
+                s[here, :] = head_scale(clt.at[:, part], j * per, per, state) * sv + t_dot(xt, bb)
+                zz = z[j][part, :]
+                gz = y * (zz * sigmoid(zz))
+                g = gz * gain[:, here]
+                gg[part, here] = g.astype(BF)
+                square = square + gz * gz
+                inner = inner + g * dv[slot, part, here]
+            sm_out[step, part, :] = jnp.where(
+                lane == 0,
+                jnp.sum(square, axis=1, keepdims=True),
+                jnp.sum(inner, axis=1, keepdims=True),
+            )
+        branch = dot(gg[...], wout[...])
+        br[slot] = branch[:, :half]
+        br_out[step] = branch[:, half:].astype(BF)
+        for copy in copies(step):
+            copy.start()
+
+    @pl.when(step > 0)
+    def _():
+        k = step - 1
+        slot = lax.rem(k, 2)
+        for copy in copies(k):
+            copy.wait()
+        count = nz * gc * 2
+        for i in range(rows // Q):
+            part = slice(i * Q, i * Q + Q)
+            both = sm_out[k, part, :] + sm_in[k, part, :]
+            r2 = lax.rsqrt(both[:, 0:1] / count + EPS)
+            pull = both[:, 1:2] * (r2 * r2 * r2) / count
+            row = lax.broadcasted_iota(jnp.int32, (Q, 1), 0) + k * rows + i * Q
+            keep = jnp.where(row < limit[0, 0], r2, 0.0)
+            out_o[part, :] = (
+                hidden[part, :].astype(F32)
+                + keep * (br[slot, part, :] + br_in[k, part, :].astype(F32))
+            ).astype(BF)
+            for j in groups:
+                here = slice(j * gc, j * gc + gc)
+                gn = gain[:, here]
+                zz = z2[j][part, :]
+                sz = sigmoid(zz)
+                silu = zz * sz
+                y = yv[slot, part, here]
+                gz = y * silu
+                dy_n = dv[slot, part, here]
+                gr = gz * r2
+                yn_o[part, here] = (gr * gn).astype(BF)
+                gn_o[:, here] += jnp.sum(dy_n * gr, axis=0, keepdims=True)
+                dgz = r2 * gn * dy_n - gz * pull
+                dys = dgz * silu
+                dys_o[j][part, :] = dys.astype(BF)
+                dz_o[part, here] = (dgz * y * (sz + silu * (1.0 - sz))).astype(BF)
+                x = u2[j][part, :]
+                x = x * sigmoid(x)
+                sk_o[:, here] += jnp.sum(dys * x, axis=0, keepdims=True)
+                acc[here, :] += t_dot(
+                    (dys * dot(ec2[part, :], ex[:, here])).astype(BF), c2[part, :]
+                )
+
+    @pl.when(step == tiles)
+    def _():
+        top = nz * gc
+        msg_o[0:top, :] = acc[...].astype(BF)
+        msg_o[top:, :] = tot[...]
 
 
 def line_peers(count, sign):
@@ -809,19 +872,20 @@
     nz = n
     xdt, dys, u, xr, st, xrh, rest = take(refs, n, n, n, n, n, n)
     (b, c, cl, clt, dt, sig, dt2, e12, tl2), rest = rest[:9], rest[9:]
-    (ubc, braw, brawh, cw, cbc, rate, dsk, ex, er), rest = rest[:9], rest[9:]
+    (ubc, braw, brawh, table, cbc, rate, ex, er), rest = rest[:8], rest[8:]
+    cw, dsk = table.at[0:4, :], table.at[7:8, :]
     message, early, rest = take(rest, 0, per)
     dx_o, dxh_o, gcx_o, rest = take(rest, n, n, n)
-    dt_o, ga_o, gbias_o, bc_o, bch_o, gcb_o, early_o = rest[:7]
+    dt_o, ga_o, gbias_o, bc_o, bch_o, gcb_o, low = rest[:7]
     messages, got, rest = take(rest[7:], nz - 1, per - 1)
-    du_next, line, rest = take(rest, n, nz - 1)
-    db_next, own, low, dxi, dbi, dci, dai, kt, ds, vs, sends, receives, local = rest
+    du_next, rest = take(rest, n)
+    db_next, own, dxi, dbi, dci, dai, kt, ds, vs, sends, receives, local = rest
     step = pl.program_id(0)
     blocks = pl.num_programs(0) // 2
     heads = dt.shape[1]
     state = b.shape[1]
     gc = per * HEADDIM
-    line_at, back_at, plane_at = 0, nz - 1, 2 * nz - 2
+    line_at, plane_at = 0, nz - 1
 
     def state_copies():
         return [
@@ -836,11 +900,6 @@
             )
             for i, peer in enumerate(plane_peers(per))
         ]
-
-    def line_copy(s):
-        return remote(
-            low.at[s], line[s - 1], sends, receives, back_at + s - 1, line_peers(nz, -1)[s - 1]
-        )
 
     def own_copy():
         return pltpu.make_async_copy(early[0], own, local)
@@ -995,38 +1054,10 @@
                 if s == 1:
                     own_copy().wait()
                 add(s)
-                line_copy(s).start()
 
     @pl.when(step == 2 * blocks - 1)
     def _():
         add(0)
-        for s in range(1, nz):
-            line_copy(s).wait()
-        total = low[0].astype(F32)
-        for v in line:
-            total = total + v[...].astype(F32)
-        early_o[...] = total.astype(BF)
-
-
-def sum_products_kernel(n, *refs):
-    a, w, _, rest = take(refs, n, n, 0)
-    left_o, right_o = rest
-    total = dot(a[0][...], w[0][...])
-    for i in range(1, n):
-        total = total + dot(a[i][...], w[i][...])
-    half = left_o.shape[1]
-    left_o[...] = total[:, :half]
-    right_o[...] = total[:, half:].astype(BF)
-
-
-def pull_kernel(cot, cot2, limit, w, mask_o, dyn_o):
-    rows = cot.shape[0]
-    half = cot.shape[1]
-    row = lax.broadcasted_iota(jnp.int32, (rows, 1), 0) + pl.program_id(0) * rows
-    keep = row < limit[0, 0]
-    for i, v in enumerate((cot, cot2)):
-        mask_o[:, i * half : i * half + half] = jnp.where(keep, v[...].astype(F32), 0.0).astype(BF)
-    dyn_o[...] = dot_t(mask_o[...], w[...])
 
 
 def early_grad_kernel(per, yn, masked, dz, xn, *outs):
@@ -1062,12 +1093,14 @@
     dx, dxh, taps, refs = take(refs, nz, nz, nz)
     (dz, dbc, dbch, dti, xn, xnh, w, bc, wdt, early, hidden, cot, r), refs = refs[:13], refs[13:]
     (gain, gbc, grate, gbias, gskip, ggain, rate, ex), refs = refs[:8], refs[8:]
-    zx_o, ow_o, bcdt_o, hid_o, norm_o, tbc_o, small_o, refs = take(refs, *[0] * 7)
-    ea, la, gx, gs, gdt, lx, ls, sw_out, sw_in, dxn, dxn_out, dxn_in, refs = take(refs, *[0] * 12)
+    ea, la, hid_o, norm_o, tbc_o, refs = take(refs, *[0] * 5)
+    etot, gx, gs, gdt, lx, ls, sw_out, sw_in, dxn, dxn_out, dxn_in, refs = take(refs, *[0] * 11)
     edge_out, edge_in, edge_sum, edge_next, across, across_in, nrm, nrm2, sums, refs = take(
         refs, *[0] * 9
     )
-    rx, rs, zx, zs, nr, nz_r, refs = take(refs, per - 1, per - 1, nz - 1, nz - 1, per - 1, nz - 1)
+    rx, rs, zx, zs, nr, nz_r, ze, refs = take(
+        refs, per - 1, per - 1, nz - 1, nz - 1, per - 1, nz - 1, nz - 1
+    )
     stage, sends, receives = refs
     copy = Copies(sends, receives)
     rows, half = hidden.shape
@@ -1083,7 +1116,7 @@
     left, right = pl.ds(0, half), pl.ds(half, half)
     block = rows // nz
 
-    early_swap = copy(early.at[:, right], ea.at[0, wi], sibling)
+    early_swap = copy(etot.at[:, right], ea.at[0, wi], sibling)
     late_swap = copy(sw_out, sw_in, sibling)
     dxn_swap = [
         copy(dxn_out.at[pl.ds(i * block, block), :], dxn_in.at[pl.ds(i * block, block), :], sibling)
@@ -1100,16 +1133,16 @@
         p_early.append(copy(ea.at[0], ea.at[m], peer))
         p_norm.append(copy(nrm, nr[k], peer))
         p_late.append(copy(la.at[0], la.at[m], peer))
-    z_x, z_share, z_norm = [], [], []
+    z_x, z_share, z_norm, z_early = [], [], [], []
     for k, peer in enumerate(z_back):
         z_x.append(copy(lx.at[k + 1], zx[k], peer))
+        z_early.append(copy(early.at[k + 1], ze[k], peer))
         z_share.append(copy(ls, zs[k], peer))
         z_norm.append(copy(nrm2, nz_r[k], peer))
     z_edge = copy(edge_sum, edge_next, z_back[0])
 
     meet([sibling, *z_back, *line_peers(nz, 1), *d_peers])
-    start([early_swap])
-    ea[0, wi] = early[:, :half]
+    start(z_early)
 
     g = t_dot(dbc[...], xn[...]) + t_dot(dbch[...], xnh[...])
     stage[0:state2, :] = g
@@ -1150,9 +1183,6 @@
         for m in range(per):
             gx[s, m] = g[m * HEADDIM : (m + 1) * HEADDIM, :].astype(BF)
         start(p_x[s])
-    arrive([early_swap])
-    start(p_early)
-
     def add_share():
         arrive(p_share)
         for i in range(share // HALO):
@@ -1203,10 +1233,22 @@
             edge_out[...] = total[:, half:]
             start([edge_swap])
         if i == 1:
+            arrive(z_early)
+            for j in range(early.shape[1] // HALO):
+                part = slice(j * HALO, j * HALO + HALO)
+                total = early[0, part, :].astype(F32)
+                for v in ze:
+                    total = total + v[part, :].astype(F32)
+                etot[part, :] = total.astype(BF)
+            start([early_swap])
+            ea[0, wi] = etot[:, :half]
             add_x(order[0])
             arrive([edge_swap])
             edge_sum[...] = edge_sum[...] + edge_in[...]
             start([z_edge])
+        if i == 2:
+            arrive([early_swap])
+            start(p_early)
     if nz > 2:
         add_x(order[1])
 
@@ -1311,32 +1353,42 @@
         total = total + v[...]
     norm_o[...] = jnp.sum(total, axis=0, keepdims=True)
 
-    arrive(p_early)
-    for m in range(per):
-        for k in range(2):
-            head = k * per + jnp.bitwise_xor(di, m)
-            v = ea[m, k].astype(F32)
-            ow_o[pl.ds(pl.multiple_of(head * HEADDIM, HEADDIM), HEADDIM), :] = v[:HEADDIM, :]
-    arrive(p_late)
-    for m in range(per):
-        at = jnp.bitwise_xor(di, m)
-        for k in range(2):
-            head = k * per + at
-            z_part = ea[m, k, HEADDIM:, :].astype(F32)
-            x_part = la[m, k * HEADDIM : (k + 1) * HEADDIM, :].astype(F32)
-            zx_o[:, pl.ds(pl.multiple_of(head * 2 * HEADDIM, 2 * HEADDIM), 2 * HEADDIM)] = (
-                jnp.transpose(jnp.concatenate([z_part, x_part], axis=0))
-            )
-            v = la[m, base + k * HALO : base + (k + 1) * HALO, :].astype(F32)
-            small_o[head] = (v[:, :HEADDIM] + v[:, HEADDIM : 2 * HEADDIM])[some_dt:, :]
-        v = la[m, 2 * HEADDIM : base, :].astype(F32)
-        stage[pl.ds(pl.multiple_of(at * quarter, quarter), quarter), left] = v[:quarter, :]
-        stage[pl.ds(pl.multiple_of(state2 + at * some_dt, some_dt), some_dt), left] = v[
-            quarter : quarter + some_dt, :
-        ]
-    bcdt_o[...] = jnp.transpose(stage[:, :half])
+    arrive([*p_early, *p_late])
     for c in copy.all:
         c.wait_send()
+
+
+def finish_kernel(per, ea, la, las, ones, zx_o, ow_o, bcdt_o, cx_o, gn_o, sk_o, bias_o, rate_o):
+    di = lax.axis_index("dp")
+    some_dt = HEADS // per
+    quarter = (bcdt_o.shape[0] - HEADS) // per
+    base = 2 * HEADDIM + quarter + HALO
+    small = []
+    for h in range(2 * per):
+        k, j = h // per, h % per
+        m = jnp.bitwise_xor(di, j)
+        z_part = ea[m, k, HEADDIM:, :].astype(F32)
+        x_part = la[m, k * HEADDIM : (k + 1) * HEADDIM, :].astype(F32)
+        zx_o[:, h, :] = jnp.transpose(jnp.concatenate([z_part, x_part], axis=0))
+        ow_o[h * HEADDIM : (h + 1) * HEADDIM, :] = ea[m, k, :HEADDIM, :].astype(F32)
+        v = las[m, base + k * HALO : base + (k + 1) * HALO, :].astype(F32)
+        small.append((v[:, :HEADDIM] + v[:, HEADDIM : 2 * HEADDIM])[some_dt:, :])
+    for j in range(per):
+        m = jnp.bitwise_xor(di, j)
+        v = la[m, 2 * HEADDIM : base, :].astype(F32)
+        bcdt_o[j * quarter : (j + 1) * quarter, :] = v[:quarter, :]
+        at = per * quarter + j * some_dt
+        bcdt_o[at : at + some_dt, :] = v[quarter : quarter + some_dt, :]
+
+    @pl.when(pl.program_id(0) == 0)
+    def _():
+        rows = jnp.concatenate(small, axis=1)
+        cx_o[...] = rows[0:4, :]
+        gn_o[...] = rows[4:5, :]
+        total = dot(rows, ones[...], HIGH)
+        sk_o[...] = total[5:6, :]
+        bias_o[...] = total[6:7, :] / HEADDIM
+        rate_o[...] = total[7:8, :] / HEADDIM
 
 
 def split_dot_tr(m, v):
@@ -1405,7 +1457,14 @@
     er = jnp.asarray(onehot.T, BF)
     sel = jnp.asarray(onehot.T * (np.arange(channels) % HEADDIM == 0)[:, None], F32)
 
-    scal = jnp.repeat(jnp.stack([dt_bias, a_log, d_skip]), HEADDIM, axis=1)
+    each = lambda v: jnp.broadcast_to(v[:, None], (own_heads, HEADDIM)).reshape(1, -1)
+    parameter_rows = jnp.concatenate(
+        [
+            conv_x.astype(F32), gnorm_gain[None].astype(F32), each(dt_bias), each(a_log),
+            each(d_skip), jnp.broadcast_to(norm_gain[None].astype(F32), (8, half)),
+        ],
+        axis=0,
+    )
     piece = shape((2, HEADDIM, half), BF)
     some = shape((2, gc - HEADDIM, half), BF)
     outs = shape((gc, half), BF)
@@ -1419,8 +1478,7 @@
         cost_estimate=cost(4),
         name="prep",
     )(
-        in_zx.reshape(half, -1), out_w, in_bcdt, norm_gain[None], conv_x, scal,
-        gnorm_gain[None],
+        in_zx.reshape(half, -1), out_w, jnp.transpose(in_bcdt), parameter_rows
     )
     taps_bc = conv_bc.astype(F32)
 
@@ -1480,101 +1538,55 @@
     xnh, r, braw, brawh, ubc, bs, cs = o.xnh, o.r, o.raw, o.rawh, o.ubc, o.b, o.c
     dt, sig, cl, clt, rate, wdt, totals, table = o.dt, o.sig, o.cl, o.clt, o.rate, o.wdt, o.tot, o.table
     dt2, e12, tl2, dttl2, ec2, edt2 = o.dt2, o.e12, o.tl2, o.dttl2, o.ec2, o.edt2
-    taps, gain_out, skip = table[:4], table[4:5], table[7:8]
     limit = (lengths[0] - zi * rows).reshape(1, 1)
 
-    wide = pl.BlockSpec((Q, channels), step)
-    gwide = pl.BlockSpec((Q, gc), step)
-    bspec = pl.BlockSpec((Q, STATE), step)
-    hspec = pl.BlockSpec((Q, heads), step)
-    h2spec = pl.BlockSpec((Q, 2 * heads), step)
-    tspec = pl.BlockSpec((heads, Q), lambda i: (0, i))
+    smem = pl.BlockSpec(memory_space=pltpu.SMEM)
     tile = 2 * Q if rows % (2 * Q) == 0 else Q
-    smem = pl.BlockSpec(memory_space=pltpu.SMEM)
-    masked, dyn = pl.pallas_call(
-        pull_kernel,
-        grid=(rows // tile,),
+    tiles = rows // tile
+    now = lambda columns: pl.BlockSpec((tile, columns), lambda i: (jnp.minimum(i, tiles - 1), 0))
+    then = lambda columns: pl.BlockSpec((tile, columns), lambda i: (jnp.maximum(i - 1, 0), 0))
+    out = pl.pallas_call(
+        functools.partial(mid_kernel, groups, per),
+        grid=(tiles + 1,),
         in_specs=[
-            pl.BlockSpec((tile, half), step), pl.BlockSpec((tile, half), step), smem, whole(wout),
-        ],
-        out_specs=[pl.BlockSpec((tile, model), step), pl.BlockSpec((tile, channels), step)],
-        out_shape=[shape((rows, model), BF), full],
-        compiler_params=params(),
-        cost_estimate=cost(5),
-        name="pull",
-    )(cotangent, cot_o, limit, wout)
-    out = pl.pallas_call(
-        functools.partial(carry_kernel, groups, per),
-        grid=(blocks,),
-        in_specs=[
-            *[gwide] * (3 * nz), wide, bspec, bspec, tspec, h2spec, h2spec, *[whole(v) for v in messages],
-            whole(skip), whole(gain_out), whole(ex),
+            *[now(gc)] * (3 * nz), now(half), now(half), now(STATE), now(STATE),
+            pl.BlockSpec((heads, tile), lambda i: (0, jnp.minimum(i, tiles - 1))),
+            now(2 * heads), now(2 * heads), *[then(gc)] * (2 * nz), then(2 * heads), then(STATE),
+            then(half), *[whole(v) for v in messages], whole(totals), whole(table),
+            whole(ex), whole(wout), smem,
         ],
         out_specs=[
-            *[gwide] * nz, *[pl.BlockSpec((1, gc, STATE), lambda i: (i, 0, 0))] * nz, wide,
-            pl.BlockSpec((Q, 2), step),
+            *[
+                pl.BlockSpec((tile // Q, gc, STATE), lambda i: (jnp.minimum(i, tiles - 1), 0, 0))
+            ] * nz,
+            now(model), *[then(gc)] * nz, then(channels), then(channels), then(half),
+            pl.BlockSpec((channels + HALO, STATE), fix), pl.BlockSpec((1, channels), fix),
+            pl.BlockSpec((1, channels), fix),
         ],
         out_shape=[
-            *[shape((rows, gc))] * nz, *[shape((blocks, gc, STATE), BF)] * nz, shape((rows, channels), BF),
-            shape((rows, 2)),
+            *[shape((blocks, gc, STATE), BF)] * nz, shape((rows, model), BF), *[part] * nz,
+            shape((rows, channels), BF), shape((rows, channels), BF), shape((rows, half), BF),
+            message_shape, shape((1, channels)), shape((1, channels)),
         ],
-        scratch_shapes=[pltpu.VMEM((channels, STATE), F32)],
-        compiler_params=params(),
-        cost_estimate=cost(10),
-        name="carry",
-    )(*y_in, *u, *z, dyn, bs, cs, clt, e12, dttl2, *messages, skip, gain_out, ex)
-    ys, states, gg, sums = out[:nz], out[nz : 2 * nz], out[2 * nz], out[2 * nz + 1]
-    sums2 = swap(sums)
-
-    def sum_products(a, columns, w, count, wait):
-        tile = 2 * Q if count % (2 * Q) == 0 else count
-        return pl.pallas_call(
-            functools.partial(sum_products_kernel, len(a)),
-            grid=(count // tile,),
-            in_specs=[
-                *[
-                    pl.BlockSpec((tile, v.shape[0]), lambda i, j=j: (i, j))
-                    for v, j in zip(w, columns)
-                ],
-                *[whole(v) for v in w],
-                pl.BlockSpec(memory_space=pl.ANY),
-            ],
-            out_specs=[pl.BlockSpec((tile, half), step)] * 2,
-            out_shape=[shape((count, half)), shape((count, half), BF)],
-            compiler_params=params(),
-            cost_estimate=cost(4),
-            name="products",
-        )(*a, *w, wait)
-
-    branch, branch_o = sum_products([gg], [0], [wout], rows, sums)
-    branch_o = swap(branch_o)
-    hhalf = pl.BlockSpec((Q, half), step)
-    out = pl.pallas_call(
-        functools.partial(gate_kernel, groups, per),
-        grid=(blocks,),
-        in_specs=[
-            *[gwide] * (3 * nz), wide, pl.BlockSpec((Q, 2), step), pl.BlockSpec((Q, 2), step),
-            whole(gain_out), h2spec, whole(ex), bspec, hhalf, hhalf, hhalf, smem,
+        scratch_shapes=[
+            pltpu.VMEM((channels, STATE), F32), pltpu.VMEM((channels, STATE), F32),
+            pltpu.VMEM((2, tile, channels), F32), pltpu.VMEM((2, tile, channels), F32),
+            pltpu.VMEM((2, tile, half), F32), pltpu.VMEM((tiles, tile, half), BF),
+            pltpu.VMEM((tiles, tile, half), BF), pltpu.VMEM((tiles, tile, Q), F32),
+            pltpu.VMEM((tiles, tile, Q), F32), pltpu.VMEM((tile, channels), BF),
+            pltpu.SemaphoreType.DMA((2 * tiles,)), pltpu.SemaphoreType.DMA((2 * tiles,)),
         ],
-        out_specs=[
-            *[gwide] * nz, wide, wide, pl.BlockSpec((channels, STATE), fix),
-            pl.BlockSpec((1, channels), fix), pl.BlockSpec((1, channels), fix), hhalf,
-        ],
-        out_shape=[
-            *[part] * nz, shape((rows, channels), BF), shape((rows, channels), BF),
-            shape((channels, STATE), BF), shape((1, channels)), shape((1, channels)),
-            shape((rows, half), BF),
-        ],
-        scratch_shapes=[pltpu.VMEM((channels, STATE), F32)],
-        compiler_params=params(),
-        cost_estimate=cost(10),
-        name="gate",
+        compiler_params=pltpu.CompilerParams(
+            vmem_limit_bytes=VMEM, collective_id=3, has_side_effects=True
+        ),
+        cost_estimate=cost(30),
+        name="mid",
     )(
-        *ys, *z, *u, dyn, sums, sums2, gain_out, ec2, ex, cs, hidden, branch, branch_o, limit
-    )
-    dys = out[:nz]
-    dz, yn, ds_local, g_gain, g_skip, out_hidden = out[nz:]
-    message = jnp.concatenate([ds_local, totals], axis=0)
+        *y_in, *u, *z, cotangent, cot_o, bs, cs, clt, e12, dttl2, *u, *z, ec2, cs, hidden,
+        *messages, totals, table, ex, wout, limit,
+    )
+    states, masked, dys, out = take(out, nz, 0, nz)
+    dz, yn, out_hidden, message, g_gain, g_skip = out
 
     gcol = pl.BlockSpec((rows, gc), lambda s: (0, s))
     early = pl.pallas_call(
@@ -1592,7 +1604,7 @@
     both = lambda i: (jnp.minimum(i, 2 * blocks - 1 - i), 0)
     head_columns = lambda v: pl.BlockSpec((Q, v), two)
     early_shape = early[0].shape
-    exchange = 2 * (nz - 1) + nz * (per - 1)
+    exchange = nz - 1 + nz * (per - 1)
     out = pl.pallas_call(
         functools.partial(scan_back_kernel, groups, per),
         grid=(2 * blocks,),
@@ -1610,27 +1622,26 @@
             pl.BlockSpec((heads, Q), lambda i: (0, jnp.minimum(i, 2 * blocks - 1 - i))),
             head_columns(heads), head_columns(heads), head_columns(2 * heads),
             head_columns(2 * heads), head_columns(2 * heads), head_columns(2 * STATE),
-            head_columns(2 * STATE), whole(brawh), whole(taps), whole(taps_bc), whole(rate),
-            whole(skip), whole(ex), whole(er), *[anywhere] * (1 + per),
+            head_columns(2 * STATE), whole(brawh), whole(table), whole(taps_bc), whole(rate),
+            whole(ex), whole(er), *[anywhere] * (1 + per),
         ],
         out_specs=[
             *[pl.BlockSpec((Q, gc), two)] * nz, *[pl.BlockSpec((HALO, gc), fix)] * nz,
             *[pl.BlockSpec((4, gc), fix)] * nz, head_columns(heads),
             pl.BlockSpec((1, heads), fix), pl.BlockSpec((1, heads), fix),
             head_columns(2 * STATE), pl.BlockSpec((HALO, 2 * STATE), fix),
-            pl.BlockSpec((4, 2 * STATE), fix), pl.BlockSpec((2 * HEADDIM, model), fix),
+            pl.BlockSpec((4, 2 * STATE), fix), pl.BlockSpec(early_shape, lambda i: (0, 0, 0)),
         ],
         out_shape=[
             *[shape((rows, gc), BF)] * nz, *[shape((HALO, gc), BF)] * nz, *[shape((4, gc))] * nz,
             shape((rows, heads), BF), shape((1, heads)), shape((1, heads)),
             shape((rows, 2 * STATE), BF), shape((HALO, 2 * STATE), BF), shape((4, 2 * STATE)),
-            shape((2 * HEADDIM, model), BF),
+            shape(early_shape, BF),
         ],
         scratch_shapes=[
             *[pltpu.VMEM(message.shape, BF)] * (nz - 1), *[pltpu.VMEM(early_shape, BF)] * (per - 1),
-            *[pltpu.VMEM((8, gc), F32)] * nz, *[pltpu.VMEM((2 * HEADDIM, model), BF)] * (nz - 1),
-            pltpu.VMEM((8, 2 * STATE), F32), pltpu.VMEM(early_shape, BF),
-            pltpu.VMEM(early_shape, BF), pltpu.VMEM((rows, channels), F32),
+            *[pltpu.VMEM((8, gc), F32)] * nz,
+            pltpu.VMEM((8, 2 * STATE), F32), pltpu.VMEM(early_shape, BF), pltpu.VMEM((rows, channels), F32),
             pltpu.VMEM((rows, STATE), F32), pltpu.VMEM((rows, STATE), F32),
             pltpu.VMEM((rows, heads), F32), pltpu.VMEM((heads, Q), F32),
             pltpu.VMEM((channels, STATE), F32), pltpu.VMEM((heads, STATE), F32),
@@ -1644,33 +1655,32 @@
         name="scan_back",
     )(
         *xdt, *dys, *u, *xr, *states, *xrh, bs, cs, cl, clt, dt, sig, dt2, e12, tl2, ubc, braw,
-        brawh, taps, taps_bc, rate, skip, ex, er, message, *early,
+        brawh, table, taps_bc, rate, ex, er, message, *early,
     )
     dx, dxh, g_taps = list(out[:nz]), list(out[nz : 2 * nz]), out[2 * nz : 3 * nz]
-    dti, g_rate, g_bias, dbc, dbch, g_taps_bc, early_total = out[3 * nz :]
+    dti, g_rate, g_bias, dbc, dbch, g_taps_bc, early_low = out[3 * nz :]
     quarter = 2 * STATE // per
     share = quarter + HALO
     late_rows = 2 * HEADDIM + share + 2 * HALO
     swap_rows = HEADDIM + share + 2 * HALO
-    tail_copies = 4 + nz + (per - 1) * (4 + nz) + 3 * (nz - 1) + 1
+    tail_copies = 4 + nz + (per - 1) * (4 + nz) + 4 * (nz - 1) + 1
     operands = [
-        *dx, *dxh, *g_taps, dz, dbc, dbch, dti, xn, xnh, weights, o.bcdt, wdt, early_total, hidden,
+        *dx, *dxh, *g_taps, dz, dbc, dbch, dti, xn, xnh, weights, o.bcdt, wdt, early_low, hidden,
         cotangent, r, norm_gain[None].astype(F32), g_taps_bc, g_rate, g_bias, g_skip, g_gain, rate,
         ex,
     ]
     line16 = pltpu.VMEM((HALO, half), F32)
     line8 = pltpu.VMEM((8, half), F32)
-    g_zx, g_out, grad_in_bcdt, grad_hidden, g_norm, g_taps_bc, small = pl.pallas_call(
+    early_all, late_all, grad_hidden, g_norm, g_taps_bc = pl.pallas_call(
         functools.partial(tail_kernel, per, nz),
         in_specs=[vmem] * len(operands),
-        out_specs=[vmem] * 7,
+        out_specs=[vmem] * 5,
         out_shape=[
-            shape((half, own_heads * 2 * HEADDIM)), shape((own_heads * HEADDIM, half)),
-            shape((half, 2 * STATE + HEADS)), shape((rows, half), BF), shape((1, half)),
-            shape((4, 2 * STATE)), shape((own_heads, 8, HEADDIM)),
+            shape((per, 2, 2 * HEADDIM, half), BF), shape((per, late_rows, half), BF),
+            shape((rows, half), BF), shape((1, half)), shape((4, 2 * STATE)),
         ],
         scratch_shapes=[
-            pltpu.VMEM((per, 2, 2 * HEADDIM, half), BF), pltpu.VMEM((per, late_rows, half), BF),
+            pltpu.VMEM((2 * HEADDIM, model), BF),
             pltpu.VMEM((nz, per, HEADDIM, model), BF), pltpu.VMEM((per, share, model), BF),
             pltpu.VMEM((HEADS, model), F32), pltpu.VMEM((nz, HEADDIM, model), BF),
             pltpu.VMEM((share, model), BF), pltpu.VMEM((swap_rows, half), BF),
@@ -1682,7 +1692,8 @@
             *[pltpu.VMEM((share, model), BF)] * (per - 1),
             *[pltpu.VMEM((HEADDIM, model), BF)] * (nz - 1),
             *[pltpu.VMEM((share, model), BF)] * (nz - 1), *[line8] * (per - 1),
-            *[line8] * (nz - 1), pltpu.VMEM((2 * STATE + HEADS, model), F32),
+            *[line8] * (nz - 1), *[pltpu.VMEM((2 * HEADDIM, model), BF)] * (nz - 1),
+            pltpu.VMEM((2 * STATE, model), F32),
             pltpu.SemaphoreType.DMA((tail_copies,)), pltpu.SemaphoreType.DMA((tail_copies,)),
         ],
         compiler_params=pltpu.CompilerParams(
@@ -1691,18 +1702,44 @@
         cost_estimate=cost(60),
         name="tail",
     )(*operands)
+    inner = own_heads * HEADDIM
+    each_head = jnp.asarray(np.kron(np.eye(own_heads), np.ones((HEADDIM, 1))), F32)
+    row_heads = shape((1, own_heads))
+    g_zx, g_out, g_bcdt, g_cx, g_gain, g_skip, g_bias, g_rate = pl.pallas_call(
+        functools.partial(finish_kernel, per),
+        grid=(half // Q,),
+        in_specs=[
+            pl.BlockSpec((per, 2, 2 * HEADDIM, Q), lambda i: (0, 0, 0, i)),
+            pl.BlockSpec((per, late_rows, Q), lambda i: (0, 0, i)),
+            pl.BlockSpec((per, late_rows, Q), lambda i: (0, 0, 0)), whole(each_head),
+        ],
+        out_specs=[
+            pl.BlockSpec((Q, own_heads, 2 * HEADDIM), lambda i: (i, 0, 0)),
+            pl.BlockSpec((inner, Q), lambda i: (0, i)),
+            pl.BlockSpec((2 * STATE + HEADS, Q), lambda i: (0, i)), pl.BlockSpec((4, inner), fix),
+            pl.BlockSpec((1, inner), fix), *[pl.BlockSpec((1, own_heads), fix)] * 3,
+        ],
+        out_shape=[
+            shape((half, own_heads, 2 * HEADDIM)), shape((inner, half)),
+            shape((2 * STATE + HEADS, half)), shape((4, inner)), shape((1, inner)), row_heads,
+            row_heads, row_heads,
+        ],
+        compiler_params=params(),
+        cost_estimate=cost(5),
+        name="finish",
+    )(early_all, late_all, late_all, each_head)
     return (
         out_hidden,
         grad_hidden,
-        g_norm.reshape(half),
-        g_zx.reshape(half, own_heads, 2 * HEADDIM),
-        grad_in_bcdt,
-        jnp.transpose(small[:, :4], (1, 0, 2)).reshape(4, own_heads * HEADDIM),
+        g_norm.reshape(-1),
+        g_zx,
+        jnp.transpose(g_bcdt),
+        g_cx,
         g_taps_bc,
-        small[:, 6, 0],
-        small[:, 7, 0],
-        jnp.sum(small[:, 5], axis=1),
-        small[:, 4].reshape(-1),
+        g_bias.reshape(-1),
+        g_rate.reshape(-1),
+        g_skip.reshape(-1),
+        g_gain.reshape(-1),
         g_out,
     )
 

time: 314 us -> 271 us (0.86)
  Pallas kernels: 280 us -> 260 us
  local copies, waits for them, and re-layouts: 23.1 us -> 7.35 us
  other arithmetic: 5.71 us -> 1.18 us
    pallas_call x4 -> x2, Pallas kernels: 40.6 us -> 28.4 us  [the longest x1 23 us: sequence_device(): pl.pallas_call(functools.partial(mid_kernel, groups, per), grid=(tiles +...]
    pallas_call x1, Pallas kernels: 91.1 us -> 82.5 us  [sequence_device(): pl.pallas_call(functools.partial(front_kernel, per, nz), in_specs=[vmem]...]
    unnamed x28 -> x27, local copies, waits for them, and re-layouts: 14.2 us -> 5.67 us
    pallas_call x1, Pallas kernels: 69.9 us -> 75.3 us  [sequence_device(): pl.pallas_call(functools.partial(tail_kernel, per, nz), in_specs=[vmem] *...]
    pallas_call x1, Pallas kernels: 66.6 us -> 61.7 us  [sequence_device(): pl.pallas_call(functools.partial(scan_back_kernel, groups, per), grid=(2...]
    slice x3 -> x0, local copies, waits for them, and re-layouts: 3.52 us -> none  [the longest x2 2.03 us: sequence_device(): taps, gain_out, skip = (table[:4], table[4:5], table[7:8])]
  transfers between devices with their start and end apart: 2 -> 0, of which waited for: 2 -> 0; matrix products, arithmetic and copies ran while one was open for 0% -> 0% of each run, Pallas kernels for 0% -> 0%
where the time goes in v6:
time: 271 us; the launch traced here: 270 us
  Pallas kernels  260 us (96%)
  local copies, waits for them, and re-layouts  7.35 us (3%)
    pallas_call x1, Pallas kernels, sequence_device(): pl.pallas_call(functools.partial(front_kernel, per, nz), in_specs=[vmem]...  82.5 us
    pallas_call x1, Pallas kernels, sequence_device(): pl.pallas_call(functools.partial(tail_kernel, per, nz), in_specs=[vmem] *...  75.3 us
    pallas_call x1, Pallas kernels, sequence_device(): pl.pallas_call(functools.partial(scan_back_kernel, groups, per), grid=(2...  61.7 us
    pallas_call x1, Pallas kernels, sequence_device(): pl.pallas_call(functools.partial(mid_kernel, groups, per), grid=(tiles +...  23 us
    pallas_call x1, Pallas kernels, sequence_device(): pl.pallas_call(functools.partial(early_grad_kernel, per), grid=(nz,), in_...  9 us
    unnamed x27, local copies, waits for them, and re-layouts  5.67 us
    pallas_call x1, Pallas kernels, sequence_device(): pl.pallas_call(functools.partial(finish_kernel, per), grid=(half // Q,),...  5.46 us

profile of v6, /device:TPU:0, one launch (start us, length us, event | category | flops | bytes accessed | tf_op | source)
XLA Modules:
  0.0 269.8 jit_solution(1355454984430401680)
XLA Ops:
  0.6 0.0 copy-start.2
  0.7 0.0 copy-start.8
  0.7 0.0 copy-start.9
  0.7 0.0 copy-start.10
  0.7 0.0 copy-start.7
  0.7 0.0 copy-start.4
  0.7 0.0 copy-start.5
  0.7 2.5 copy.31
  3.2 0.0 copy-done.2
  3.2 0.0 copy-done.8
  3.2 0.1 broadcast_in_dim.8
  3.3 0.1 reshape.62
  3.4 0.0 copy-done.9
  3.4 0.1 broadcast_in_dim.9
  3.5 0.1 reshape.63
  3.5 0.0 copy-done.10
  3.5 0.1 broadcast_in_dim.10
  3.6 0.1 reshape.64
  3.7 0.0 copy-done.7
  3.7 0.0 copy-done.4
  3.7 1.2 concatenate.3.rows_in
  4.9 2.9 %prep.1 = (bf16[2,64,512]{2,1,0:T(8,128)(2,1)}, bf16[2,64,512]{2,1,0:T(8,128)(2,1)}, bf16[2,192,512]{2,1,0:T(8,128)(2,1)}, bf16[2,192,512]{2,1,0:T(8,128)(2,1)},...) custom-call(bf16[512,1024]{1,0:T(8,128)(2,1)} %bitcast.16, ...), custom_call_target="tpu_custom_call" | custom-call | flops 400000000 | bytes 4000 | tf_op jit(solution)/shard_map/prep/pallas_call | solution.py:1471
  7.9 0.0 copy-done.5
  7.9 0.6 convert_element_type.22.refs_7_.refs_37_
  8.5 82.5 %front.1 = (bf16[2,1024,1024]{2,1,0:T(8,128)(2,1)}, bf16[1024,1024]{1,0:T(8,128)(2,1)}, bf16[1024,512]{1,0:T(8,128)(2,1)}, bf16[1024,1024]{1,0:T(8,128)(2,1)}, f...) custom-call(bf16[1024,512]{1,0:T(8,128)(2,1)} %refs_22_.1, ...), custom_call_target="tpu_custom_call" | custom-call | flops 8999999488 | bytes 90000 | tf_op jit(solution)/shard_map/front/pallas_call | solution.py:1511
  91.6 23.0 %mid.1 = (bf16[8,256,128]{2,1,0:T(8,128)(2,1)}, bf16[8,256,128]{2,1,0:T(8,128)(2,1)}, bf16[8,256,128]{2,1,0:T(8,128)(2,1)}, bf16[8,256,128]{2,1,0:T(8,128)(2,1)}...) custom-call(bf16[1024,256]{1,0:T(8,128)(2,1)} %get-tuple-element.131, ...), custom_call_target="tpu_custom_call" | custom-call | flops 3000000000 | bytes 30000 | tf_op jit(solution)/shard_map/mid/pallas_call | solution.py:1548
  114.6 9.0 %early_grad.1 = (bf16[4,128,1024]{2,1,0:T(8,128)(2,1)}, bf16[4,128,1024]{2,1,0:T(8,128)(2,1)}, bf16[4,128,1024]{2,1,0:T(8,128)(2,1)}, bf16[4,128,1024]{2,1,0:T(8,128)(2,1)}) custom-call(bf16[1024,1024]{1,0:T(8,128)(2,1)} %get-tuple-element.187.yn, bf16[1024,1024]{1,0:T(8,128)(2,1)} %get-tuple-element.188.masked, ...), custom_call_target="tpu_custom_call" | custom-call | flops 600000000 | bytes 6000 | tf_op jit(solution)/shard_map/early_grad/pallas_call | solution.py:1592
  123.6 61.7 %scan_back.1 = (bf16[1024,256]{1,0:T(8,128)(2,1)}, bf16[1024,256]{1,0:T(8,128)(2,1)}, bf16[1024,256]{1,0:T(8,128)(2,1)}, bf16[1024,256]{1,0:T(8,128)(2,1)}, bf16...) custom-call(bf16[1024,256]{1,0:T(8,128)(2,1)} %get-tuple-element.157, ...), custom_call_target="tpu_custom_call" | custom-call | flops 5000000000 | bytes 50000 | tf_op jit(solution)/shard_map/scan_back/pallas_call | solution.py:1608
  185.3 0.6 convert_element_type.21
  185.9 75.3 %tail.1 = (bf16[4,2,128,512]{3,2,1,0:T(8,128)(2,1)}, bf16[4,240,512]{2,1,0:T(8,128)(2,1)}, bf16[1024,512]{1,0:T(8,128)(2,1)}, f32[1,512]{1,0:T(1,128)}, f32[4,256]{1,0:T(4,128)}) custom-call(bf16[1024,256]{1,0:T(8,128)(2,1)} %get-tuple-element.195.refs_0_, bf16[1024,256]{1,0:T(8,128)(2,1)} %get-tuple-element.196.refs_1_, ...), custom_call_target="tpu_custom_call" | custom-call | flops 6000000000 | bytes 60000 | tf_op jit(solution)/shard_map/tail/pallas_call | solution.py:1674
  261.2 0.0 copy-start
  261.2 0.0 copy-start.1
  261.2 5.5 %finish.1 = (f32[512,8,128]{2,1,0:T(8,128)}, f32[512,512]{1,0:T(8,128)}, f32[288,512]{1,0:T(8,128)}, f32[4,512]{1,0:T(4,128)}, f32[1,512]{1,0:T(1,128)}, /*index...) custom-call(bf16[4,2,128,512]{3,2,1,0:T(8,128)(2,1)} %get-tuple-element.223.ea, ...), custom_call_target="tpu_custom_call" | custom-call | flops 500000000 | bytes 5000 | tf_op jit(solution)/shard_map/finish/pallas_call | solution.py:1708
  266.7 0.0 copy-done
  266.7 0.0 copy-start.6
  266.7 0.0 copy-start.3
  266.7 1.0 copy.37
  267.7 0.0 copy-done.1
  267.7 1.0 copy.38
  268.7 0.0 copy-done.6
  268.7 0.6 copy.39
  269.2 0.0 copy-done.3
  269.2 0.6 copy.40
  (2 shorter events, 0.0 us)
Async XLA Ops:
  0.6 2.6 copy-start.2
  0.7 2.6 copy-start.8
  0.7 2.7 %copy-start.9 = (f32[8]{0:T(128)S(1)}, f32[8]{0:T(128)}, u32[]{:S(2)}) copy-start(f32[8]{0:T(128)} %param.26) | copy-start | bytes 100
  0.7 2.9 %copy-start.10 = (f32[8]{0:T(128)S(1)}, f32[8]{0:T(128)}, u32[]{:S(2)}) copy-start(f32[8]{0:T(128)} %param.27) | copy-start | bytes 100
  0.7 3.0 %copy-start.7 = (bf16[512]{0:T(512)(128)(2,1)S(1)}, bf16[512]{0:T(512)(128)(2,1)}, u32[]{:S(2)}) copy-start(bf16[512]{0:T(512)(128)(2,1)} %param.28) | copy-start | bytes 3076
  0.7 3.0 %copy-start.4 = (bf16[4,512]{1,0:T(4,128)(2,1)S(1)}, bf16[4,512]{1,0:T(4,128)(2,1)}, u32[]{:S(2)}) copy-start(bf16[4,512]{1,0:T(4,128)(2,1)} %param.23) | copy-start | bytes 12292
  0.7 7.2 %copy-start.5 = (bf16[4,256]{1,0:T(4,128)(2,1)S(1)}, bf16[4,256]{1,0:T(4,128)(2,1)}, u32[]{:S(2)}) copy-start(bf16[4,256]{1,0:T(4,128)(2,1)} %param.24) | copy-start | bytes 6148
  261.2 5.5 %copy-start = (bf16[1024,512]{1,0:T(8,128)(2,1)S(1)}, bf16[1024,512]{1,0:T(8,128)(2,1)}, u32[]{:S(2)}) copy-start(bf16[1024,512]{1,0:T(8,128)(2,1)} %get-tuple-element.246) | copy-start | bytes 3145732
  261.2 6.5 %copy-start.1 = (bf16[1024,512]{1,0:T(8,128)(2,1)S(1)}, bf16[1024,512]{1,0:T(8,128)(2,1)}, u32[]{:S(2)}) copy-start(bf16[1024,512]{1,0:T(8,128)(2,1)} %get-tuple-element.247) | copy-start | bytes 3145732
  266.7 2.0 copy-start.6
  266.7 2.5 copy-start.3

commit v7 on v6

--- a/solution.py
+++ b/solution.py
@@ -842,7 +842,7 @@
     )
 
 
-def conv_back(d, nxt, taps, raw, rawh, grad_o, out_o, outh_o, last):
+def conv_back(d, nxt, taps, raw, grad_o, out_o):
     win = jnp.concatenate([d, nxt[...]], axis=0)
     back = jnp.zeros_like(d)
     sums = []
@@ -854,17 +854,18 @@
     out_o[...] = back.astype(BF)
     nxt[...] = d[0:8, :]
 
-    @pl.when(last)
-    def _():
-        win_h = jnp.concatenate([jnp.zeros((HALO, d.shape[1]), F32), d[0:8, :]], axis=0)
-        back_h = jnp.zeros((HALO, d.shape[1]), F32)
-        sums_h = []
-        for k in range(4):
-            part = win_h[3 - k : 3 - k + HALO, :]
-            back_h = back_h + taps[k : k + 1, :] * part
-            sums_h.append(jnp.sum(rawh[...] * part, axis=0, keepdims=True))
-        grad_o[...] += jnp.concatenate(sums_h, axis=0)
-        outh_o[...] = back_h.astype(BF)
+
+def conv_edge(first, taps, rawh, grad_o, outh_o):
+    first = first[...]
+    win = jnp.concatenate([jnp.zeros((HALO, first.shape[1]), F32), first], axis=0)
+    back = jnp.zeros((HALO, first.shape[1]), F32)
+    sums = []
+    for k in range(4):
+        part = win[3 - k : 3 - k + HALO, :]
+        back = back + taps[k : k + 1, :] * part
+        sums.append(jnp.sum(rawh[...] * part, axis=0, keepdims=True))
+    grad_o[...] += jnp.concatenate(sums, axis=0)
+    outh_o[...] = back.astype(BF)
 
 
 def scan_back_kernel(groups, per, *refs):
@@ -874,18 +875,20 @@
     (b, c, cl, clt, dt, sig, dt2, e12, tl2), rest = rest[:9], rest[9:]
     (ubc, braw, brawh, table, cbc, rate, ex, er), rest = rest[:8], rest[8:]
     cw, dsk = table.at[0:4, :], table.at[7:8, :]
-    message, early, rest = take(rest, 0, per)
+    message, yn, masked, dz, xn, rest = take(rest, *[0] * 5)
     dx_o, dxh_o, gcx_o, rest = take(rest, n, n, n)
-    dt_o, ga_o, gbias_o, bc_o, bch_o, gcb_o, low = rest[:7]
-    messages, got, rest = take(rest[7:], nz - 1, per - 1)
+    dt_o, ga_o, gbias_o, bc_o, bch_o, gcb_o, etot = rest[:7]
+    messages, got, line, rest = take(rest[7:], nz - 1, per - 1, nz - 1)
     du_next, rest = take(rest, n)
-    db_next, own, dxi, dbi, dci, dai, kt, ds, vs, sends, receives, local = rest
-    step = pl.program_id(0)
-    blocks = pl.num_programs(0) // 2
+    db_next, early, low, dxi, dbi, dci, dai, kt, ds, vs, sends, receives = rest
+    turn = pl.program_id(0)
+    step = turn - nz
+    blocks = (pl.num_programs(0) - nz) // 2
     heads = dt.shape[1]
     state = b.shape[1]
     gc = per * HEADDIM
     line_at, plane_at = 0, nz - 1
+    back_at = plane_at + nz * (per - 1)
 
     def state_copies():
         return [
@@ -896,22 +899,44 @@
     def plane_copies(s):
         return [
             remote(
-                early[i + 1].at[s], got[i].at[s], sends, receives, plane_at + s * (per - 1) + i, peer
+                early.at[i + 1, s], got[i].at[s], sends, receives, plane_at + s * (per - 1) + i, peer
             )
             for i, peer in enumerate(plane_peers(per))
         ]
 
-    def own_copy():
-        return pltpu.make_async_copy(early[0], own, local)
-
-    @pl.when(step == 0)
+    def line_copy(s):
+        return remote(
+            low.at[s], line[s - 1], sends, receives, back_at + s - 1, line_peers(nz, -1)[s - 1]
+        )
+
+    order = [*range(1, nz), 0]
+    leave = [0, nz + blocks // 4, nz + blocks - 1, nz + blocks + blocks // 4]
+    added = [nz + blocks // 2, nz + blocks, nz + blocks + 3 * blocks // 8, nz + 2 * blocks - 1]
+
+    @pl.when(turn == 0)
     def _():
-        own_copy().start()
-        meet(line_peers(nz, -1) + line_peers(nz, 1) + plane_peers(per))
-        for copy in plane_copies(1) + state_copies():
+        meet([*line_peers(nz, -1), *line_peers(nz, 1), *plane_peers(per)])
+        for copy in state_copies():
             copy.start()
 
-    @pl.when(step < blocks)
+    @pl.when(turn < nz)
+    def _():
+        s = lax.rem(turn + 1, nz)
+        g = t_dot(yn[...], masked[...]).astype(BF)
+        for m in range(per):
+            early[m, s, :HEADDIM, :] = g[m * HEADDIM : (m + 1) * HEADDIM, :]
+        g = t_dot(dz[...], xn[...]).astype(BF)
+        for m in range(per):
+            early[m, s, HEADDIM:, :] = g[m * HEADDIM : (m + 1) * HEADDIM, :]
+
+    for s, when in zip(order, leave):
+
+        @pl.when(turn == when)
+        def _(s=s):
+            for copy in plane_copies(s):
+                copy.start()
+
+    @pl.when(jnp.logical_and(step >= 0, step < blocks))
     def _():
         rows = pl.ds(pl.multiple_of(step * Q, Q), Q)
         mask = tri("ge")
@@ -964,7 +989,6 @@
     @pl.when(step >= blocks)
     def _():
         rows = pl.ds(pl.multiple_of((2 * blocks - 1 - step) * Q, Q), Q)
-        last = step == 2 * blocks - 1
         rsum = jnp.zeros((Q, heads), F32)
         gsum = jnp.zeros((Q, heads), F32)
         ddt = jnp.zeros((Q, heads), F32)
@@ -1002,8 +1026,7 @@
             ds[here, :] = eds + t_dot(dyb, c[...])
             du = (dxdt * dtx + dsk[:, here] * dy) * (su + xs * (1.0 - su))
             conv_back(
-                du, du_next[s], cw.at[:, here], xr[s][...].astype(F32), xrh[s], gcx_o[s],
-                dx_o[s], dxh_o[s], last,
+                du, du_next[s], cw.at[:, here], xr[s][...].astype(F32), gcx_o[s], dx_o[s]
             )
         vrow = dot_t(jnp.ones((8, state), F32), vs[...], HIGH)
         da = (
@@ -1019,10 +1042,14 @@
         d = jnp.concatenate([dbs, dcs], axis=1)
         v = ubc[...]
         sv = sigmoid(v)
-        conv_back(
-            d * (sv + v * sv * (1.0 - sv)), db_next, cbc, braw[...], brawh, gcb_o, bc_o, bch_o,
-            last,
-        )
+        conv_back(d * (sv + v * sv * (1.0 - sv)), db_next, cbc, braw[...], gcb_o, bc_o)
+
+    @pl.when(step == 2 * blocks - 1)
+    def _():
+        for s in groups:
+            here = slice(s * gc, s * gc + gc)
+            conv_edge(du_next[s], cw.at[:, here], xrh[s], gcx_o[s], dxh_o[s])
+        conv_edge(db_next, cbc, brawh, gcb_o, bch_o)
 
     def add(s):
         for copy in plane_copies(s):
@@ -1030,7 +1057,7 @@
 
         def piece(i, carry):
             part = pl.ds(pl.multiple_of(i * HALO, HALO), HALO)
-            total = own[s, part, :].astype(F32)
+            total = early[0, s, part, :].astype(F32)
             for v in got:
                 total = total + v[s, part, :].astype(F32)
             low[s, part, :] = total.astype(BF)
@@ -1038,35 +1065,24 @@
 
         lax.fori_loop(0, low.shape[1] // HALO, piece, 0, unroll=2)
 
-    order = [*range(1, nz), 0]
-    for k, s in enumerate(order):
-        if k > 0:
-
-            @pl.when(step == (blocks * k * 3) // (2 * nz))
-            def _(s=s):
-                for copy in plane_copies(s):
-                    copy.start()
-
-        if s > 0:
-
-            @pl.when(step == blocks + (blocks * 3 * k) // (4 * (nz - 1)) + 1)
-            def _(s=s):
-                if s == 1:
-                    own_copy().wait()
-                add(s)
+    for s, when in zip(order, added):
+
+        @pl.when(turn == when)
+        def _(s=s):
+            add(s)
+            if s > 0:
+                line_copy(s).start()
 
     @pl.when(step == 2 * blocks - 1)
     def _():
-        add(0)
-
-
-def early_grad_kernel(per, yn, masked, dz, xn, *outs):
-    g_out = t_dot(yn[...], masked[...]).astype(BF)
-    g_z = t_dot(dz[...], xn[...]).astype(BF)
-    for m in range(per):
-        here = slice(m * HEADDIM, (m + 1) * HEADDIM)
-        outs[m][0, :HEADDIM, :] = g_out[here, :]
-        outs[m][0, HEADDIM:, :] = g_z[here, :]
+        for s in range(1, nz):
+            line_copy(s).wait()
+        for i in range(low.shape[1] // HALO):
+            part = slice(i * HALO, i * HALO + HALO)
+            total = low[0, part, :].astype(F32)
+            for v in line:
+                total = total + v[part, :].astype(F32)
+            etot[part, :] = total.astype(BF)
 
 
 class Copies:
@@ -1094,13 +1110,11 @@
     (dz, dbc, dbch, dti, xn, xnh, w, bc, wdt, early, hidden, cot, r), refs = refs[:13], refs[13:]
     (gain, gbc, grate, gbias, gskip, ggain, rate, ex), refs = refs[:8], refs[8:]
     ea, la, hid_o, norm_o, tbc_o, refs = take(refs, *[0] * 5)
-    etot, gx, gs, gdt, lx, ls, sw_out, sw_in, dxn, dxn_out, dxn_in, refs = take(refs, *[0] * 11)
+    gx, gs, gdt, lx, ls, sw_out, sw_in, dxn, dxn_out, dxn_in, refs = take(refs, *[0] * 10)
     edge_out, edge_in, edge_sum, edge_next, across, across_in, nrm, nrm2, sums, refs = take(
         refs, *[0] * 9
     )
-    rx, rs, zx, zs, nr, nz_r, ze, refs = take(
-        refs, per - 1, per - 1, nz - 1, nz - 1, per - 1, nz - 1, nz - 1
-    )
+    rx, rs, zx, zs, nr, nz_r, refs = take(refs, per - 1, per - 1, nz - 1, nz - 1, per - 1, nz - 1)
     stage, sends, receives = refs
     copy = Copies(sends, receives)
     rows, half = hidden.shape
@@ -1116,7 +1130,7 @@
     left, right = pl.ds(0, half), pl.ds(half, half)
     block = rows // nz
 
-    early_swap = copy(etot.at[:, right], ea.at[0, wi], sibling)
+    early_swap = copy(early.at[:, right], ea.at[0, wi], sibling)
     late_swap = copy(sw_out, sw_in, sibling)
     dxn_swap = [
         copy(dxn_out.at[pl.ds(i * block, block), :], dxn_in.at[pl.ds(i * block, block), :], sibling)
@@ -1133,16 +1147,17 @@
         p_early.append(copy(ea.at[0], ea.at[m], peer))
         p_norm.append(copy(nrm, nr[k], peer))
         p_late.append(copy(la.at[0], la.at[m], peer))
-    z_x, z_share, z_norm, z_early = [], [], [], []
+    z_x, z_share, z_norm = [], [], []
     for k, peer in enumerate(z_back):
         z_x.append(copy(lx.at[k + 1], zx[k], peer))
-        z_early.append(copy(early.at[k + 1], ze[k], peer))
         z_share.append(copy(ls, zs[k], peer))
         z_norm.append(copy(nrm2, nz_r[k], peer))
     z_edge = copy(edge_sum, edge_next, z_back[0])
 
     meet([sibling, *z_back, *line_peers(nz, 1), *d_peers])
-    start(z_early)
+
+    start([early_swap])
+    ea[0, wi] = early[:, :half]
 
     g = t_dot(dbc[...], xn[...]) + t_dot(dbch[...], xnh[...])
     stage[0:state2, :] = g
@@ -1177,12 +1192,15 @@
             [upper.astype(F32), lower.astype(F32)], axis=0
         ).astype(BF)
     start(p_share)
+    arrive([early_swap])
     order = [*range(1, nz), 0]
     for s in order:
         g = t_dot(dx[s][...], xn[...]) + t_dot(dxh[s][...], xnh[...])
         for m in range(per):
             gx[s, m] = g[m * HEADDIM : (m + 1) * HEADDIM, :].astype(BF)
         start(p_x[s])
+    start(p_early)
+
     def add_share():
         arrive(p_share)
         for i in range(share // HALO):
@@ -1233,22 +1251,10 @@
             edge_out[...] = total[:, half:]
             start([edge_swap])
         if i == 1:
-            arrive(z_early)
-            for j in range(early.shape[1] // HALO):
-                part = slice(j * HALO, j * HALO + HALO)
-                total = early[0, part, :].astype(F32)
-                for v in ze:
-                    total = total + v[part, :].astype(F32)
-                etot[part, :] = total.astype(BF)
-            start([early_swap])
-            ea[0, wi] = etot[:, :half]
             add_x(order[0])
             arrive([edge_swap])
             edge_sum[...] = edge_sum[...] + edge_in[...]
             start([z_edge])
-        if i == 2:
-            arrive([early_swap])
-            start(p_early)
     if nz > 2:
         add_x(order[1])
 
@@ -1588,65 +1594,61 @@
     states, masked, dys, out = take(out, nz, 0, nz)
     dz, yn, out_hidden, message, g_gain, g_skip = out
 
-    gcol = pl.BlockSpec((rows, gc), lambda s: (0, s))
-    early = pl.pallas_call(
-        functools.partial(early_grad_kernel, per),
-        grid=(nz,),
-        in_specs=[gcol, whole(masked), gcol, whole(xn)],
-        out_specs=[pl.BlockSpec((1, 2 * HEADDIM, model), lambda s: (s, 0, 0))] * per,
-        out_shape=[shape((nz, 2 * HEADDIM, model), BF)] * per,
-        compiler_params=params(),
-        cost_estimate=cost(6),
-        name="early_grad",
-    )(yn, masked, dz, xn)
-    one = lambda i: (jnp.minimum(i, blocks - 1), 0)
-    two = lambda i: (jnp.minimum(blocks - 1, 2 * blocks - 1 - i), 0)
-    both = lambda i: (jnp.minimum(i, 2 * blocks - 1 - i), 0)
+    begin = lambda i: jnp.maximum(i - nz, 0)
+    first_pass = lambda i: jnp.minimum(begin(i), blocks - 1)
+    second_pass = lambda i: jnp.minimum(blocks - 1, 2 * blocks - 1 - begin(i))
+    either = lambda i: jnp.minimum(begin(i), 2 * blocks - 1 - begin(i))
+    one = lambda i: (first_pass(i), 0)
+    two = lambda i: (second_pass(i), 0)
+    both = lambda i: (either(i), 0)
+    gcol = pl.BlockSpec((rows, gc), lambda i: (0, lax.rem(jnp.minimum(i, nz - 1) + 1, nz)))
     head_columns = lambda v: pl.BlockSpec((Q, v), two)
-    early_shape = early[0].shape
-    exchange = nz - 1 + nz * (per - 1)
+    early_shape = (nz, 2 * HEADDIM, model)
+    exchange = 2 * (nz - 1) + nz * (per - 1)
     out = pl.pallas_call(
         functools.partial(scan_back_kernel, groups, per),
-        grid=(2 * blocks,),
+        grid=(nz + 2 * blocks,),
         in_specs=[
             *[pl.BlockSpec((Q, gc), one)] * nz, *[pl.BlockSpec((Q, gc), both)] * nz,
             *[pl.BlockSpec((Q, gc), two)] * (2 * nz),
             *[
                 pl.BlockSpec(
-                    (1, gc, STATE), lambda i: (jnp.minimum(blocks - 1, 2 * blocks - 1 - i), 0, 0)
+                    (1, gc, STATE), lambda i: (second_pass(i), 0, 0)
                 )
             ] * nz,
             *[pl.BlockSpec((HALO, gc), fix)] * nz,
             pl.BlockSpec((Q, STATE), both), pl.BlockSpec((Q, STATE), both),
             pl.BlockSpec((Q, heads), one),
-            pl.BlockSpec((heads, Q), lambda i: (0, jnp.minimum(i, 2 * blocks - 1 - i))),
+            pl.BlockSpec((heads, Q), lambda i: (0, either(i))),
             head_columns(heads), head_columns(heads), head_columns(2 * heads),
             head_columns(2 * heads), head_columns(2 * heads), head_columns(2 * STATE),
             head_columns(2 * STATE), whole(brawh), whole(table), whole(taps_bc), whole(rate),
-            whole(ex), whole(er), *[anywhere] * (1 + per),
+            whole(ex), whole(er), anywhere, gcol, whole(masked), gcol, whole(xn),
         ],
         out_specs=[
             *[pl.BlockSpec((Q, gc), two)] * nz, *[pl.BlockSpec((HALO, gc), fix)] * nz,
             *[pl.BlockSpec((4, gc), fix)] * nz, head_columns(heads),
             pl.BlockSpec((1, heads), fix), pl.BlockSpec((1, heads), fix),
             head_columns(2 * STATE), pl.BlockSpec((HALO, 2 * STATE), fix),
-            pl.BlockSpec((4, 2 * STATE), fix), pl.BlockSpec(early_shape, lambda i: (0, 0, 0)),
+            pl.BlockSpec((4, 2 * STATE), fix),
+            pl.BlockSpec((2 * HEADDIM, model), fix),
         ],
         out_shape=[
             *[shape((rows, gc), BF)] * nz, *[shape((HALO, gc), BF)] * nz, *[shape((4, gc))] * nz,
             shape((rows, heads), BF), shape((1, heads)), shape((1, heads)),
             shape((rows, 2 * STATE), BF), shape((HALO, 2 * STATE), BF), shape((4, 2 * STATE)),
-            shape(early_shape, BF),
+            shape((2 * HEADDIM, model), BF),
         ],
         scratch_shapes=[
             *[pltpu.VMEM(message.shape, BF)] * (nz - 1), *[pltpu.VMEM(early_shape, BF)] * (per - 1),
-            *[pltpu.VMEM((8, gc), F32)] * nz,
-            pltpu.VMEM((8, 2 * STATE), F32), pltpu.VMEM(early_shape, BF), pltpu.VMEM((rows, channels), F32),
+            *[pltpu.VMEM(early_shape[1:], BF)] * (nz - 1), *[pltpu.VMEM((8, gc), F32)] * nz,
+            pltpu.VMEM((8, 2 * STATE), F32), pltpu.VMEM((per, *early_shape), BF),
+            pltpu.VMEM(early_shape, BF),
+            pltpu.VMEM((rows, channels), F32),
             pltpu.VMEM((rows, STATE), F32), pltpu.VMEM((rows, STATE), F32),
             pltpu.VMEM((rows, heads), F32), pltpu.VMEM((heads, Q), F32),
             pltpu.VMEM((channels, STATE), F32), pltpu.VMEM((heads, STATE), F32),
             pltpu.SemaphoreType.DMA((exchange,)), pltpu.SemaphoreType.DMA((exchange,)),
-            pltpu.SemaphoreType.DMA,
         ],
         compiler_params=pltpu.CompilerParams(
             vmem_limit_bytes=VMEM, collective_id=0, has_side_effects=True
@@ -1655,17 +1657,18 @@
         name="scan_back",
     )(
         *xdt, *dys, *u, *xr, *states, *xrh, bs, cs, cl, clt, dt, sig, dt2, e12, tl2, ubc, braw,
-        brawh, table, taps_bc, rate, ex, er, message, *early,
+        brawh, table, taps_bc, rate, ex, er, message, yn, masked,
+        dz, xn,
     )
     dx, dxh, g_taps = list(out[:nz]), list(out[nz : 2 * nz]), out[2 * nz : 3 * nz]
-    dti, g_rate, g_bias, dbc, dbch, g_taps_bc, early_low = out[3 * nz :]
+    dti, g_rate, g_bias, dbc, dbch, g_taps_bc, early_total = out[3 * nz :]
     quarter = 2 * STATE // per
     share = quarter + HALO
     late_rows = 2 * HEADDIM + share + 2 * HALO
     swap_rows = HEADDIM + share + 2 * HALO
-    tail_copies = 4 + nz + (per - 1) * (4 + nz) + 4 * (nz - 1) + 1
+    tail_copies = 4 + nz + (per - 1) * (4 + nz) + 3 * (nz - 1) + 1
     operands = [
-        *dx, *dxh, *g_taps, dz, dbc, dbch, dti, xn, xnh, weights, o.bcdt, wdt, early_low, hidden,
+        *dx, *dxh, *g_taps, dz, dbc, dbch, dti, xn, xnh, weights, o.bcdt, wdt, early_total, hidden,
         cotangent, r, norm_gain[None].astype(F32), g_taps_bc, g_rate, g_bias, g_skip, g_gain, rate,
         ex,
     ]
@@ -1680,7 +1683,6 @@
             shape((rows, half), BF), shape((1, half)), shape((4, 2 * STATE)),
         ],
         scratch_shapes=[
-            pltpu.VMEM((2 * HEADDIM, model), BF),
             pltpu.VMEM((nz, per, HEADDIM, model), BF), pltpu.VMEM((per, share, model), BF),
             pltpu.VMEM((HEADS, model), F32), pltpu.VMEM((nz, HEADDIM, model), BF),
             pltpu.VMEM((share, model), BF), pltpu.VMEM((swap_rows, half), BF),
@@ -1692,7 +1694,7 @@
             *[pltpu.VMEM((share, model), BF)] * (per - 1),
             *[pltpu.VMEM((HEADDIM, model), BF)] * (nz - 1),
             *[pltpu.VMEM((share, model), BF)] * (nz - 1), *[line8] * (per - 1),
-            *[line8] * (nz - 1), *[pltpu.VMEM((2 * HEADDIM, model), BF)] * (nz - 1),
+            *[line8] * (nz - 1),
             pltpu.VMEM((2 * STATE, model), F32),
             pltpu.SemaphoreType.DMA((tail_copies,)), pltpu.SemaphoreType.DMA((tail_copies,)),
         ],

time: 271 us -> 258 us (0.952)
  Pallas kernels: 260 us -> 248 us
    pallas_call x2 -> x1, Pallas kernels: 70.7 us -> 62.2 us  [sequence_device(): pl.pallas_call(functools.partial(scan_back_kernel, groups, per), grid=(nz...]
    pallas_call x1, Pallas kernels: 75.3 us -> 71.5 us  [sequence_device(): pl.pallas_call(functools.partial(tail_kernel, per, nz), in_specs=[vmem] *...]
where the time goes in v7:
time: 258 us
  Pallas kernels  248 us (96%)
  local copies, waits for them, and re-layouts  7.34 us (3%)
    pallas_call x1, Pallas kernels, sequence_device(): pl.pallas_call(functools.partial(front_kernel, per, nz), in_specs=[vmem]...  82.5 us
    pallas_call x1, Pallas kernels, sequence_device(): pl.pallas_call(functools.partial(tail_kernel, per, nz), in_specs=[vmem] *...  71.5 us
    pallas_call x1, Pallas kernels, sequence_device(): pl.pallas_call(functools.partial(scan_back_kernel, groups, per), grid=(nz...  62.2 us
    pallas_call x1, Pallas kernels, sequence_device(): pl.pallas_call(functools.partial(mid_kernel, groups, per), grid=(tiles +...  23 us
    unnamed x27, local copies, waits for them, and re-layouts  5.67 us
    pallas_call x1, Pallas kernels, sequence_device(): pl.pallas_call(functools.partial(finish_kernel, per), grid=(half // Q,),...  5.46 us

profile of v7, /device:TPU:0, one launch (start us, length us, event | category | flops | bytes accessed | tf_op | source)
XLA Modules:
  0.0 257.6 jit_solution(15640698209853729531)
XLA Ops:
  0.6 0.0 copy-start.2
  0.7 0.0 copy-start.8
  0.7 0.0 copy-start.9
  0.7 0.0 copy-start.10
  0.7 0.0 copy-start.7
  0.7 0.0 copy-start.4
  0.7 0.0 copy-start.5
  0.7 2.5 copy.31
  3.2 0.0 copy-done.2
  3.2 0.0 copy-done.8
  3.2 0.1 broadcast_in_dim.8
  3.3 0.1 reshape.62
  3.4 0.0 copy-done.9
  3.4 0.1 broadcast_in_dim.9
  3.5 0.1 reshape.63
  3.5 0.0 copy-done.10
  3.5 0.1 broadcast_in_dim.10
  3.6 0.1 reshape.64
  3.7 0.0 copy-done.7
  3.7 0.0 copy-done.4
  3.7 1.2 concatenate.3.rows_in
  4.9 2.9 %prep.1 = (bf16[2,64,512]{2,1,0:T(8,128)(2,1)}, bf16[2,64,512]{2,1,0:T(8,128)(2,1)}, bf16[2,192,512]{2,1,0:T(8,128)(2,1)}, bf16[2,192,512]{2,1,0:T(8,128)(2,1)},...) custom-call(bf16[512,1024]{1,0:T(8,128)(2,1)} %bitcast.16, ...), custom_call_target="tpu_custom_call" | custom-call | flops 400000000 | bytes 4000 | tf_op jit(solution)/shard_map/prep/pallas_call | solution.py:1477
  7.9 0.0 copy-done.5
  7.9 0.6 convert_element_type.22.refs_7_.refs_37_
  8.5 82.5 %front.1 = (bf16[2,1024,1024]{2,1,0:T(8,128)(2,1)}, bf16[1024,1024]{1,0:T(8,128)(2,1)}, bf16[1024,512]{1,0:T(8,128)(2,1)}, bf16[1024,1024]{1,0:T(8,128)(2,1)}, f...) custom-call(bf16[1024,512]{1,0:T(8,128)(2,1)} %refs_22_.1, ...), custom_call_target="tpu_custom_call" | custom-call | flops 8999999488 | bytes 90000 | tf_op jit(solution)/shard_map/front/pallas_call | solution.py:1517
  91.6 23.0 %mid.1 = (bf16[8,256,128]{2,1,0:T(8,128)(2,1)}, bf16[8,256,128]{2,1,0:T(8,128)(2,1)}, bf16[8,256,128]{2,1,0:T(8,128)(2,1)}, bf16[8,256,128]{2,1,0:T(8,128)(2,1)}...) custom-call(bf16[1024,256]{1,0:T(8,128)(2,1)} %get-tuple-element.127, ...), custom_call_target="tpu_custom_call" | custom-call | flops 3000000000 | bytes 30000 | tf_op jit(solution)/shard_map/mid/pallas_call | solution.py:1554
  114.6 62.2 %scan_back.1 = (bf16[1024,256]{1,0:T(8,128)(2,1)}, bf16[1024,256]{1,0:T(8,128)(2,1)}, bf16[1024,256]{1,0:T(8,128)(2,1)}, bf16[1024,256]{1,0:T(8,128)(2,1)}, bf16...) custom-call(bf16[1024,256]{1,0:T(8,128)(2,1)} %get-tuple-element.153, ...), custom_call_target="tpu_custom_call" | custom-call | flops 5000000000 | bytes 50000 | tf_op jit(solution)/shard_map/scan_back/pallas_call | solution.py:1608
  176.9 0.6 convert_element_type.21
  177.4 71.5 %tail.1 = (bf16[4,2,128,512]{3,2,1,0:T(8,128)(2,1)}, bf16[4,240,512]{2,1,0:T(8,128)(2,1)}, bf16[1024,512]{1,0:T(8,128)(2,1)}, f32[1,512]{1,0:T(1,128)}, f32[4,256]{1,0:T(4,128)}) custom-call(bf16[1024,256]{1,0:T(8,128)(2,1)} %get-tuple-element.187.refs_0_, bf16[1024,256]{1,0:T(8,128)(2,1)} %get-tuple-element.188.refs_1_, ...), custom_call_target="tpu_custom_call" | custom-call | flops 6000000000 | bytes 60000 | tf_op jit(solution)/shard_map/tail/pallas_call | solution.py:1677
  248.9 0.0 copy-start
  248.9 0.0 copy-start.1
  248.9 5.5 %finish.1 = (f32[512,8,128]{2,1,0:T(8,128)}, f32[512,512]{1,0:T(8,128)}, f32[288,512]{1,0:T(8,128)}, f32[4,512]{1,0:T(4,128)}, f32[1,512]{1,0:T(1,128)}, /*index...) custom-call(bf16[4,2,128,512]{3,2,1,0:T(8,128)(2,1)} %get-tuple-element.215.ea, ...), custom_call_target="tpu_custom_call" | custom-call | flops 500000000 | bytes 5000 | tf_op jit(solution)/shard_map/finish/pallas_call | solution.py:1710
  254.4 0.0 copy-done
  254.4 0.0 copy-start.6
  254.4 0.0 copy-start.3
  254.4 1.0 copy.37
  255.4 0.0 copy-done.1
  255.4 1.0 copy.38
  256.4 0.0 copy-done.6
  256.4 0.6 copy.39
  257.0 0.0 copy-done.3
  257.0 0.6 copy.40
  (2 shorter events, 0.0 us)
Async XLA Ops:
  0.6 2.6 %copy-start.2 = (bf16[512]{0:T(512)(128)(2,1)S(1)}, bf16[512]{0:T(512)(128)(2,1)}, u32[]{:S(2)}) copy-start(bf16[512]{0:T(512)(128)(2,1)} %param.20) | copy-start | bytes 3076
  0.7 2.6 %copy-start.8 = (f32[8]{0:T(128)S(1)}, f32[8]{0:T(128)}, u32[]{:S(2)}) copy-start(f32[8]{0:T(128)} %param.25) | copy-start | bytes 100
  0.7 2.7 %copy-start.9 = (f32[8]{0:T(128)S(1)}, f32[8]{0:T(128)}, u32[]{:S(2)}) copy-start(f32[8]{0:T(128)} %param.26) | copy-start | bytes 100
  0.7 2.9 %copy-start.10 = (f32[8]{0:T(128)S(1)}, f32[8]{0:T(128)}, u32[]{:S(2)}) copy-start(f32[8]{0:T(128)} %param.27) | copy-start | bytes 100
  0.7 3.0 %copy-start.7 = (bf16[512]{0:T(512)(128)(2,1)S(1)}, bf16[512]{0:T(512)(128)(2,1)}, u32[]{:S(2)}) copy-start(bf16[512]{0:T(512)(128)(2,1)} %param.28) | copy-start | bytes 3076
  0.7 3.0 %copy-start.4 = (bf16[4,512]{1,0:T(4,128)(2,1)S(1)}, bf16[4,512]{1,0:T(4,128)(2,1)}, u32[]{:S(2)}) copy-start(bf16[4,512]{1,0:T(4,128)(2,1)} %param.23) | copy-start | bytes 12292
  0.7 7.2 %copy-start.5 = (bf16[4,256]{1,0:T(4,128)(2,1)S(1)}, bf16[4,256]{1,0:T(4,128)(2,1)}, u32[]{:S(2)}) copy-start(bf16[4,256]{1,0:T(4,128)(2,1)} %param.24) | copy-start | bytes 6148
  248.9 5.5 %copy-start = (bf16[1024,512]{1,0:T(8,128)(2,1)S(1)}, bf16[1024,512]{1,0:T(8,128)(2,1)}, u32[]{:S(2)}) copy-start(bf16[1024,512]{1,0:T(8,128)(2,1)} %get-tuple-element.238) | copy-start | bytes 3145732
  248.9 6.5 %copy-start.1 = (bf16[1024,512]{1,0:T(8,128)(2,1)S(1)}, bf16[1024,512]{1,0:T(8,128)(2,1)}, u32[]{:S(2)}) copy-start(bf16[1024,512]{1,0:T(8,128)(2,1)} %get-tuple-element.239) | copy-start | bytes 3145732
  254.4 2.0 copy-start.6
  254.4 2.5 copy-start.3

commit v8 on v7

--- a/solution.py
+++ b/solution.py
@@ -530,7 +530,7 @@
     swap_bc = copy(bcdt, bc.at[:, right], sibling)
     swap_out = copy(out2, wo_o.at[pl.ds(0, gc), right], sibling)
     swap_cot = copy(cot, cot_o, sibling)
-    z_table, z_w, z_out, z_state, z_state2 = [], [], [], [], []
+    z_table, z_w, z_out, z_state = [], [], [], {s: [] for s in range(nz)}
     for k, peer in enumerate(z_peers):
         s = k + 1
         z_table.append(copy(table, o.table.at[:, pl.ds(s * gc, gc)], peer))
@@ -539,10 +539,9 @@
         z_out.append(
             copy(wo_o.at[pl.ds(0, HEADDIM), :], wo_o.at[pl.ds(s * gc, HEADDIM), :], peer)
         )
-        most = pl.ds(0, top - gc)
-        z_state.append(copy(msg.at[most, :], messages_o[k].at[most, :], peer))
-        more = pl.ds(top - gc, gc + HALO)
-        z_state2.append(copy(msg.at[more, :], messages_o[k].at[more, :], peer))
+        for j in range(nz):
+            some = pl.ds(j * gc, gc + HALO if j == nz - 1 else gc)
+            z_state[j].append(copy(msg.at[some, :], messages_o[k].at[some, :], peer))
     last = pl.ds(rows - HALO, HALO)
     edge1 = copy(hidden.at[last, :], eh.at[:, left], z_peers[0])
     edge2 = copy(ho.at[last, :], eh.at[:, right], z_peers[0])
@@ -617,6 +616,7 @@
         project(
             s, per, xn, o, w, taps, ex, z_v[s], xr_v[s], xrh_o[s], u_v[s], xdt_v[s], msg, buf, acc
         )
+        start(z_state[s])
         for a, b in ((z_v, z_o), (xr_v, xr_o), (u_v, u_o), (xdt_v, xdt_o)):
             pending.append(local(a[s], b[s]))
 
@@ -635,19 +635,19 @@
         arrive([p_w[s][1 - s % 2], p_w[s][2]])
         project_group(s)
         if s == nz - 2:
-            start(z_state)
             for k in range(1, nz):
                 pass_on(p_out[k], k)
-    start(z_state2)
     pending.append(local(w, w_o))
     for s in range(1, nz):
         inside_group(s)
     everything = [swap_first, swap_rest, swap_hidden, swap_bc, swap_out, swap_cot, edge1, edge2]
-    everything += [*z_table, *z_w, *z_out, *z_state, *z_state2]
+    everything += [*z_table, *z_w, *z_out]
+    states = [c for s in range(nz) for c in z_state[s]]
+    everything += states
     for s in range(1, nz):
         everything += p_w[s] + p_out[s]
         arrive([p_out[s][1 - s % 2], p_out[s][2]])
-    arrive([swap_cot, *z_state, *z_state2])
+    arrive([swap_cot, *states])
     for c in everything:
         c.wait_send()
     for c in pending:
@@ -1513,7 +1513,7 @@
         *[kept[name] for name in KEPT],
     ]
     held = lambda v: pltpu.VMEM(v.shape, v.dtype)
-    remotes = 6 + 5 * (nz - 1) + 2 + 2 * (nz - 1) * (per - 1)
+    remotes = 6 + (3 + nz) * (nz - 1) + 2 + 2 * (nz - 1) * (per - 1)
     out = pl.pallas_call(
         functools.partial(front_kernel, per, nz),
         in_specs=[vmem] * 10 + [anywhere] * 3,

time: 258 us -> 250 us (0.969)
  Pallas kernels: 248 us -> 240 us
    pallas_call x1, Pallas kernels: 82.5 us -> 76.3 us  [sequence_device(): pl.pallas_call(functools.partial(front_kernel, per, nz), in_specs=[vmem]...]
where the time goes in v8:
time: 250 us
  Pallas kernels  240 us (96%)
  local copies, waits for them, and re-layouts  7.34 us (3%)
    pallas_call x1, Pallas kernels, sequence_device(): pl.pallas_call(functools.partial(front_kernel, per, nz), in_specs=[vmem]...  76.3 us
    pallas_call x1, Pallas kernels, sequence_device(): pl.pallas_call(functools.partial(tail_kernel, per, nz), in_specs=[vmem] *...  70.5 us
    pallas_call x1, Pallas kernels, sequence_device(): pl.pallas_call(functools.partial(scan_back_kernel, groups, per), grid=(nz...  61.9 us
    pallas_call x1, Pallas kernels, sequence_device(): pl.pallas_call(functools.partial(mid_kernel, groups, per), grid=(tiles +...  23 us
    unnamed x27, local copies, waits for them, and re-layouts  5.67 us
    pallas_call x1, Pallas kernels, sequence_device(): pl.pallas_call(functools.partial(finish_kernel, per), grid=(half // Q,),...  5.46 us

profile of v8, /device:TPU:0, one launch (start us, length us, event | category | flops | bytes accessed | tf_op | source)
XLA Modules:
  0.0 250.1 jit_solution(3464358050387220579)
XLA Ops:
  0.6 0.0 copy-start.2
  0.7 0.0 copy-start.8
  0.7 0.0 copy-start.9
  0.7 0.0 copy-start.10
  0.7 0.0 copy-start.7
  0.7 0.0 copy-start.4
  0.7 0.0 copy-start.5
  0.7 2.5 %copy.31 = bf16[64,8,8,128]{3,1,2,0:T(8,128)(2,1)} copy(bf16[64,8,8,128]{3,2,1,0:T(8,128)(2,1)} %bitcast.17) | data formatting | bytes 2097152
  3.2 0.0 copy-done.2
  3.2 0.0 copy-done.8
  3.2 0.1 broadcast_in_dim.8
  3.3 0.1 reshape.62
  3.4 0.0 copy-done.9
  3.4 0.1 broadcast_in_dim.9
  3.5 0.1 reshape.63
  3.5 0.0 copy-done.10
  3.5 0.1 broadcast_in_dim.10
  3.6 0.1 reshape.64
  3.7 0.0 copy-done.7
  3.7 0.0 copy-done.4
  3.7 1.2 concatenate.3.rows_in
  4.9 2.9 %prep.1 = (bf16[2,64,512]{2,1,0:T(8,128)(2,1)}, bf16[2,64,512]{2,1,0:T(8,128)(2,1)}, bf16[2,192,512]{2,1,0:T(8,128)(2,1)}, bf16[2,192,512]{2,1,0:T(8,128)(2,1)},...) custom-call(bf16[512,1024]{1,0:T(8,128)(2,1)} %bitcast.16, ...), custom_call_target="tpu_custom_call" | custom-call | flops 400000000 | bytes 4000 | tf_op jit(solution)/shard_map/prep/pallas_call | solution.py:1477
  7.9 0.0 copy-done.5
  7.9 0.6 convert_element_type.22.refs_7_.refs_37_
  8.5 76.3 %front.1 = (bf16[2,1024,1024]{2,1,0:T(8,128)(2,1)}, bf16[1024,1024]{1,0:T(8,128)(2,1)}, bf16[1024,512]{1,0:T(8,128)(2,1)}, bf16[1024,1024]{1,0:T(8,128)(2,1)}, f...) custom-call(bf16[1024,512]{1,0:T(8,128)(2,1)} %refs_22_.1, ...), custom_call_target="tpu_custom_call" | custom-call | flops 8999999488 | bytes 90000 | tf_op jit(solution)/shard_map/front/pallas_call | solution.py:1517
  85.5 23.0 %mid.1 = (bf16[8,256,128]{2,1,0:T(8,128)(2,1)}, bf16[8,256,128]{2,1,0:T(8,128)(2,1)}, bf16[8,256,128]{2,1,0:T(8,128)(2,1)}, bf16[8,256,128]{2,1,0:T(8,128)(2,1)}...) custom-call(bf16[1024,256]{1,0:T(8,128)(2,1)} %get-tuple-element.127, ...), custom_call_target="tpu_custom_call" | custom-call | flops 3000000000 | bytes 30000 | tf_op jit(solution)/shard_map/mid/pallas_call | solution.py:1554
  108.5 61.9 %scan_back.1 = (bf16[1024,256]{1,0:T(8,128)(2,1)}, bf16[1024,256]{1,0:T(8,128)(2,1)}, bf16[1024,256]{1,0:T(8,128)(2,1)}, bf16[1024,256]{1,0:T(8,128)(2,1)}, bf16...) custom-call(bf16[1024,256]{1,0:T(8,128)(2,1)} %get-tuple-element.153, ...), custom_call_target="tpu_custom_call" | custom-call | flops 5000000000 | bytes 50000 | tf_op jit(solution)/shard_map/scan_back/pallas_call | solution.py:1608
  170.4 0.6 convert_element_type.21
  171.0 70.5 %tail.1 = (bf16[4,2,128,512]{3,2,1,0:T(8,128)(2,1)}, bf16[4,240,512]{2,1,0:T(8,128)(2,1)}, bf16[1024,512]{1,0:T(8,128)(2,1)}, f32[1,512]{1,0:T(1,128)}, f32[4,256]{1,0:T(4,128)}) custom-call(bf16[1024,256]{1,0:T(8,128)(2,1)} %get-tuple-element.187.refs_0_, bf16[1024,256]{1,0:T(8,128)(2,1)} %get-tuple-element.188.refs_1_, ...), custom_call_target="tpu_custom_call" | custom-call | flops 6000000000 | bytes 60000 | tf_op jit(solution)/shard_map/tail/pallas_call | solution.py:1677
  241.4 0.0 copy-start
  241.5 0.0 copy-start.1
  241.5 5.5 %finish.1 = (f32[512,8,128]{2,1,0:T(8,128)}, f32[512,512]{1,0:T(8,128)}, f32[288,512]{1,0:T(8,128)}, f32[4,512]{1,0:T(4,128)}, f32[1,512]{1,0:T(1,128)}, /*index...) custom-call(bf16[4,2,128,512]{3,2,1,0:T(8,128)(2,1)} %get-tuple-element.215.ea, ...), custom_call_target="tpu_custom_call" | custom-call | flops 500000000 | bytes 5000 | tf_op jit(solution)/shard_map/finish/pallas_call | solution.py:1710
  246.9 0.0 copy-done
  246.9 0.0 copy-start.6
  246.9 0.0 copy-start.3
  247.0 1.0 copy.37
  247.9 0.0 copy-done.1
  247.9 1.0 copy.38
  248.9 0.0 copy-done.6
  248.9 0.6 copy.39
  249.5 0.0 copy-done.3
  249.5 0.6 copy.40
  (2 shorter events, 0.0 us)
Async XLA Ops:
  0.6 2.6 %copy-start.2 = (bf16[512]{0:T(512)(128)(2,1)S(1)}, bf16[512]{0:T(512)(128)(2,1)}, u32[]{:S(2)}) copy-start(bf16[512]{0:T(512)(128)(2,1)} %param.20) | copy-start | bytes 3076
  0.7 2.6 %copy-start.8 = (f32[8]{0:T(128)S(1)}, f32[8]{0:T(128)}, u32[]{:S(2)}) copy-start(f32[8]{0:T(128)} %param.25) | copy-start | bytes 100
  0.7 2.7 %copy-start.9 = (f32[8]{0:T(128)S(1)}, f32[8]{0:T(128)}, u32[]{:S(2)}) copy-start(f32[8]{0:T(128)} %param.26) | copy-start | bytes 100
  0.7 2.9 %copy-start.10 = (f32[8]{0:T(128)S(1)}, f32[8]{0:T(128)}, u32[]{:S(2)}) copy-start(f32[8]{0:T(128)} %param.27) | copy-start | bytes 100
  0.7 3.0 %copy-start.7 = (bf16[512]{0:T(512)(128)(2,1)S(1)}, bf16[512]{0:T(512)(128)(2,1)}, u32[]{:S(2)}) copy-start(bf16[512]{0:T(512)(128)(2,1)} %param.28) | copy-start | bytes 3076
  0.7 3.0 %copy-start.4 = (bf16[4,512]{1,0:T(4,128)(2,1)S(1)}, bf16[4,512]{1,0:T(4,128)(2,1)}, u32[]{:S(2)}) copy-start(bf16[4,512]{1,0:T(4,128)(2,1)} %param.23) | copy-start | bytes 12292
  0.7 7.2 %copy-start.5 = (bf16[4,256]{1,0:T(4,128)(2,1)S(1)}, bf16[4,256]{1,0:T(4,128)(2,1)}, u32[]{:S(2)}) copy-start(bf16[4,256]{1,0:T(4,128)(2,1)} %param.24) | copy-start | bytes 6148
  241.4 5.5 %copy-start = (bf16[1024,512]{1,0:T(8,128)(2,1)S(1)}, bf16[1024,512]{1,0:T(8,128)(2,1)}, u32[]{:S(2)}) copy-start(bf16[1024,512]{1,0:T(8,128)(2,1)} %get-tuple-element.238) | copy-start | bytes 3145732
  241.5 6.5 %copy-start.1 = (bf16[1024,512]{1,0:T(8,128)(2,1)S(1)}, bf16[1024,512]{1,0:T(8,128)(2,1)}, u32[]{:S(2)}) copy-start(bf16[1024,512]{1,0:T(8,128)(2,1)} %get-tuple-element.239) | copy-start | bytes 3145732
  246.9 2.0 copy-start.6
  246.9 2.5 %copy-start.3 = (f32[4,256]{1,0:T(4,128)S(1)}, f32[4,256]{1,0:T(4,128)}, u32[]{:S(2)}) copy-start(f32[4,256]{1,0:T(4,128)} %get-tuple-element.244) | copy-start | bytes 12292

commit v9 on v8

--- a/solution.py
+++ b/solution.py
@@ -1144,7 +1144,8 @@
         p_share.append(copy(gs.at[m], rs[k], peer))
         for s in range(nz):
             p_x[s].append(copy(gx.at[s, m], rx[k].at[s], peer))
-        p_early.append(copy(ea.at[0], ea.at[m], peer))
+        if m < per - 1:
+            p_early.append(copy(ea.at[0], ea.at[m], peer))
         p_norm.append(copy(nrm, nr[k], peer))
         p_late.append(copy(la.at[0], la.at[m], peer))
     z_x, z_share, z_norm = [], [], []
@@ -1152,6 +1153,10 @@
         z_x.append(copy(lx.at[k + 1], zx[k], peer))
         z_share.append(copy(ls, zs[k], peer))
         z_norm.append(copy(nrm2, nz_r[k], peer))
+    p_relay = [
+        copy(ea.at[1, 0], ea.at[per - 1, 0], d_peers[1]),
+        copy(ea.at[2, 1], ea.at[per - 1, 1], d_peers[0]),
+    ]
     z_edge = copy(edge_sum, edge_next, z_back[0])
 
     meet([sibling, *z_back, *line_peers(nz, 1), *d_peers])
@@ -1280,6 +1285,8 @@
     start(p_norm)
     for s in order[2:]:
         add_x(s)
+    arrive(p_early)
+    start(p_relay)
     arrive([across_swap])
     eighth = jnp.full((8, Q), 0.125, F32)
     for i in range(rows // Q):
@@ -1359,7 +1366,7 @@
         total = total + v[...]
     norm_o[...] = jnp.sum(total, axis=0, keepdims=True)
 
-    arrive([*p_early, *p_late])
+    arrive([*p_relay, *p_late])
     for c in copy.all:
         c.wait_send()
 
@@ -1666,7 +1673,7 @@
     share = quarter + HALO
     late_rows = 2 * HEADDIM + share + 2 * HALO
     swap_rows = HEADDIM + share + 2 * HALO
-    tail_copies = 4 + nz + (per - 1) * (4 + nz) + 3 * (nz - 1) + 1
+    tail_copies = 5 + nz + (per - 1) * (4 + nz) + 3 * (nz - 1) + 1
     operands = [
         *dx, *dxh, *g_taps, dz, dbc, dbch, dti, xn, xnh, weights, o.bcdt, wdt, early_total, hidden,
         cotangent, r, norm_gain[None].astype(F32), g_taps_bc, g_rate, g_bias, g_skip, g_gain, rate,

time: 250 us -> 245 us (0.980)
  Pallas kernels: 240 us -> 235 us
    pallas_call x1, Pallas kernels: 70.5 us -> 65.3 us  [sequence_device(): pl.pallas_call(functools.partial(tail_kernel, per, nz), in_specs=[vmem] *...]
where the time goes in v9:
time: 245 us
  Pallas kernels  235 us (96%)
  local copies, waits for them, and re-layouts  7.34 us (3%)
    pallas_call x1, Pallas kernels, sequence_device(): pl.pallas_call(functools.partial(front_kernel, per, nz), in_specs=[vmem]...  76.3 us
    pallas_call x1, Pallas kernels, sequence_device(): pl.pallas_call(functools.partial(tail_kernel, per, nz), in_specs=[vmem] *...  65.3 us
    pallas_call x1, Pallas kernels, sequence_device(): pl.pallas_call(functools.partial(scan_back_kernel, groups, per), grid=(nz...  61.9 us
    pallas_call x1, Pallas kernels, sequence_device(): pl.pallas_call(functools.partial(mid_kernel, groups, per), grid=(tiles +...  23 us
    unnamed x27, local copies, waits for them, and re-layouts  5.67 us
    pallas_call x1, Pallas kernels, sequence_device(): pl.pallas_call(functools.partial(finish_kernel, per), grid=(half // Q,),...  5.46 us

profile of v9, /device:TPU:0, one launch (start us, length us, event | category | flops | bytes accessed | tf_op | source)
XLA Modules:
  0.0 244.9 jit_solution(7144553772436255926)
XLA Ops:
  0.6 0.0 copy-start.2
  0.7 0.0 copy-start.8
  0.7 0.0 copy-start.9
  0.7 0.0 copy-start.10
  0.7 0.0 copy-start.7
  0.7 0.0 copy-start.4
  0.7 0.0 copy-start.5
  0.7 2.5 %copy.31 = bf16[64,8,8,128]{3,1,2,0:T(8,128)(2,1)} copy(bf16[64,8,8,128]{3,2,1,0:T(8,128)(2,1)} %bitcast.17) | data formatting | bytes 2097152
  3.2 0.0 copy-done.2
  3.2 0.0 copy-done.8
  3.2 0.1 broadcast_in_dim.8
  3.3 0.1 reshape.62
  3.4 0.0 copy-done.9
  3.4 0.1 broadcast_in_dim.9
  3.5 0.1 reshape.63
  3.5 0.0 copy-done.10
  3.5 0.1 broadcast_in_dim.10
  3.6 0.1 reshape.64
  3.7 0.0 copy-done.7
  3.7 0.0 copy-done.4
  3.7 1.2 concatenate.3.rows_in
  4.9 2.9 %prep.1 = (bf16[2,64,512]{2,1,0:T(8,128)(2,1)}, bf16[2,64,512]{2,1,0:T(8,128)(2,1)}, bf16[2,192,512]{2,1,0:T(8,128)(2,1)}, bf16[2,192,512]{2,1,0:T(8,128)(2,1)},...) custom-call(bf16[512,1024]{1,0:T(8,128)(2,1)} %bitcast.16, ...), custom_call_target="tpu_custom_call" | custom-call | flops 400000000 | bytes 4000 | tf_op jit(solution)/shard_map/prep/pallas_call | solution.py:1484
  7.9 0.0 copy-done.5
  7.9 0.6 convert_element_type.22.refs_7_.refs_37_
  8.5 76.3 %front.1 = (bf16[2,1024,1024]{2,1,0:T(8,128)(2,1)}, bf16[1024,1024]{1,0:T(8,128)(2,1)}, bf16[1024,512]{1,0:T(8,128)(2,1)}, bf16[1024,1024]{1,0:T(8,128)(2,1)}, f...) custom-call(bf16[1024,512]{1,0:T(8,128)(2,1)} %refs_22_.1, ...), custom_call_target="tpu_custom_call" | custom-call | flops 8999999488 | bytes 90000 | tf_op jit(solution)/shard_map/front/pallas_call | solution.py:1524
  85.5 23.0 %mid.1 = (bf16[8,256,128]{2,1,0:T(8,128)(2,1)}, bf16[8,256,128]{2,1,0:T(8,128)(2,1)}, bf16[8,256,128]{2,1,0:T(8,128)(2,1)}, bf16[8,256,128]{2,1,0:T(8,128)(2,1)}...) custom-call(bf16[1024,256]{1,0:T(8,128)(2,1)} %get-tuple-element.127, ...), custom_call_target="tpu_custom_call" | custom-call | flops 3000000000 | bytes 30000 | tf_op jit(solution)/shard_map/mid/pallas_call | solution.py:1561
  108.5 61.9 %scan_back.1 = (bf16[1024,256]{1,0:T(8,128)(2,1)}, bf16[1024,256]{1,0:T(8,128)(2,1)}, bf16[1024,256]{1,0:T(8,128)(2,1)}, bf16[1024,256]{1,0:T(8,128)(2,1)}, bf16...) custom-call(bf16[1024,256]{1,0:T(8,128)(2,1)} %get-tuple-element.153, ...), custom_call_target="tpu_custom_call" | custom-call | flops 5000000000 | bytes 50000 | tf_op jit(solution)/shard_map/scan_back/pallas_call | solution.py:1615
  170.4 0.6 convert_element_type.21
  171.0 65.3 %tail.1 = (bf16[4,2,128,512]{3,2,1,0:T(8,128)(2,1)}, bf16[4,240,512]{2,1,0:T(8,128)(2,1)}, bf16[1024,512]{1,0:T(8,128)(2,1)}, f32[1,512]{1,0:T(1,128)}, f32[4,256]{1,0:T(4,128)}) custom-call(bf16[1024,256]{1,0:T(8,128)(2,1)} %get-tuple-element.187.refs_0_, bf16[1024,256]{1,0:T(8,128)(2,1)} %get-tuple-element.188.refs_1_, ...), custom_call_target="tpu_custom_call" | custom-call | flops 6000000000 | bytes 60000 | tf_op jit(solution)/shard_map/tail/pallas_call | solution.py:1684
  236.3 0.0 copy-start
  236.3 0.0 copy-start.1
  236.3 5.5 %finish.1 = (f32[512,8,128]{2,1,0:T(8,128)}, f32[512,512]{1,0:T(8,128)}, f32[288,512]{1,0:T(8,128)}, f32[4,512]{1,0:T(4,128)}, f32[1,512]{1,0:T(1,128)}, /*index...) custom-call(bf16[4,2,128,512]{3,2,1,0:T(8,128)(2,1)} %get-tuple-element.215.ea, ...), custom_call_target="tpu_custom_call" | custom-call | flops 500000000 | bytes 5000 | tf_op jit(solution)/shard_map/finish/pallas_call | solution.py:1717
  241.7 0.0 copy-done
  241.8 0.0 copy-start.6
  241.8 0.0 copy-start.3
  241.8 1.0 copy.37
  242.8 0.0 copy-done.1
  242.8 1.0 copy.38
  243.7 0.0 copy-done.6
  243.7 0.6 copy.39
  244.3 0.0 copy-done.3
  244.3 0.6 copy.40
  (2 shorter events, 0.0 us)
Async XLA Ops:
  0.6 2.6 %copy-start.2 = (bf16[512]{0:T(512)(128)(2,1)S(1)}, bf16[512]{0:T(512)(128)(2,1)}, u32[]{:S(2)}) copy-start(bf16[512]{0:T(512)(128)(2,1)} %param.20) | copy-start | bytes 3076
  0.7 2.6 %copy-start.8 = (f32[8]{0:T(128)S(1)}, f32[8]{0:T(128)}, u32[]{:S(2)}) copy-start(f32[8]{0:T(128)} %param.25) | copy-start | bytes 100
  0.7 2.7 %copy-start.9 = (f32[8]{0:T(128)S(1)}, f32[8]{0:T(128)}, u32[]{:S(2)}) copy-start(f32[8]{0:T(128)} %param.26) | copy-start | bytes 100
  0.7 2.9 %copy-start.10 = (f32[8]{0:T(128)S(1)}, f32[8]{0:T(128)}, u32[]{:S(2)}) copy-start(f32[8]{0:T(128)} %param.27) | copy-start | bytes 100
  0.7 3.0 %copy-start.7 = (bf16[512]{0:T(512)(128)(2,1)S(1)}, bf16[512]{0:T(512)(128)(2,1)}, u32[]{:S(2)}) copy-start(bf16[512]{0:T(512)(128)(2,1)} %param.28) | copy-start | bytes 3076
  0.7 3.0 %copy-start.4 = (bf16[4,512]{1,0:T(4,128)(2,1)S(1)}, bf16[4,512]{1,0:T(4,128)(2,1)}, u32[]{:S(2)}) copy-start(bf16[4,512]{1,0:T(4,128)(2,1)} %param.23) | copy-start | bytes 12292
  0.7 7.2 %copy-start.5 = (bf16[4,256]{1,0:T(4,128)(2,1)S(1)}, bf16[4,256]{1,0:T(4,128)(2,1)}, u32[]{:S(2)}) copy-start(bf16[4,256]{1,0:T(4,128)(2,1)} %param.24) | copy-start | bytes 6148
  236.3 5.5 %copy-start = (bf16[1024,512]{1,0:T(8,128)(2,1)S(1)}, bf16[1024,512]{1,0:T(8,128)(2,1)}, u32[]{:S(2)}) copy-start(bf16[1024,512]{1,0:T(8,128)(2,1)} %get-tuple-element.238) | copy-start | bytes 3145732
  236.3 6.5 %copy-start.1 = (bf16[1024,512]{1,0:T(8,128)(2,1)S(1)}, bf16[1024,512]{1,0:T(8,128)(2,1)}, u32[]{:S(2)}) copy-start(bf16[1024,512]{1,0:T(8,128)(2,1)} %get-tuple-element.239) | copy-start | bytes 3145732
  241.8 2.0 copy-start.6
  241.8 2.5 %copy-start.3 = (f32[4,256]{1,0:T(4,128)S(1)}, f32[4,256]{1,0:T(4,128)}, u32[]{:S(2)}) copy-start(f32[4,256]{1,0:T(4,128)} %get-tuple-element.244) | copy-start | bytes 12292
